TPU v7x, 32 devices: a whole 2x2x4 slice. The times are simulated.
32 devices in a mesh: groups: 2 (over x), morton: 16 (over z, y, core).
Axes of the slice: x: 2, y: 2, z: 4, core: 2. Of those that a mesh axis runs over, the one named last changes fastest.
Arguments:
- features: bfloat16 [32768, 256], P(('groups', 'morton')), parts along dimension 0, may hold values from -6 to 6
- norm_gain: float32 [256], replicated, may hold values from 0.1 to 1.9
- conv_weight: bfloat16 [6912, 256], replicated, may hold values from -0.078125 to 0.078125
- recv_slot: int32 [64, 26], P(('groups', 'morton')), parts along dimension 0, may hold values from -1 to 63, as said below
- send_face: int32 [32, 64], P(('groups', 'morton')), parts along dimension 0, may hold values from 0 to 11
- cotangent: bfloat16 [32768, 256], P(('groups', 'morton')), parts along dimension 0, may hold values from -6 to 6
Outputs:
- mixed: bfloat16 [32768, 256], P(('groups', 'morton')), parts along dimension 0
- grad_features: bfloat16 [32768, 256], P(('groups', 'morton')), parts along dimension 0
- grad_weight: float32 [13824, 256], P(('groups', 'morton')), parts along dimension 0
There are 2 independent parts, one for each index of `groups`. A program takes and returns all parts, laid end to end along the dimension named above; an argument that names none is the same for every part. Nothing has to cross between parts.
Inputs may be any that keep to these rules, and one draw needn't show every extreme that they name: `recv_slot`: on a device no slot is named twice; -1 marks a missing neighbour; on every device all 4 slots from some device are named.
All inputs are finite; a program needn't handle non-finite values.
Results may differ from a plain program's by a relative error of at most 0.0033.
Values may be sent and summed in bfloat16 or wider, within the bound.
No kernel may reach another device: no remote copies, remote signals or barrier semaphores. Data moves between devices by JAX's collectives and lax.ppermute only.
A program may use at most 128 MiB of HBM per device.

v0:
```python
import functools
import math

import jax
import jax.numpy as jnp
import numpy as np
from jax import lax
from jax.experimental import pallas as pl
from jax.experimental.pallas import tpu as pltpu
from jax.sharding import PartitionSpec as P

F32 = jnp.float32
BF16 = jnp.bfloat16
C = 256
C_LINES = 128
B_LINES = 256
ROWS = 352
HB = 24
VMEM_LIMIT = 56 * 1024 * 1024
DIRECTIONS = [
    (i, j, l)
    for i in (-1, 0, 1)
    for j in (-1, 0, 1)
    for l in (-1, 0, 1)
    if (i, j, l) != (0, 0, 0)
]

VMEM = pl.BlockSpec(memory_space=pltpu.VMEM)
SMEM = pl.BlockSpec(memory_space=pltpu.SMEM)


def call(body, out_shape, in_specs, scratch=(), flops=0, nbytes=0, name=None):
    return pl.pallas_call(
        body,
        out_shape=out_shape,
        in_specs=in_specs,
        out_specs=jax.tree.map(lambda _: VMEM, out_shape),
        scratch_shapes=list(scratch),
        compiler_params=pltpu.CompilerParams(vmem_limit_bytes=VMEM_LIMIT),
        cost_estimate=pl.CostEstimate(flops=flops, bytes_accessed=nbytes, transcendentals=0),
        name=name,
    )


def put_boundary(rows, brick, a, out_ref, stage):
    wide = rows.astype(F32)
    for half in range(2):
        stage[half] = wide[:, half * 128 : half * 128 + 128]
    for edge, at in ((0, 0), (7, 64)):

        @pl.when(a == edge)
        def _():
            out_ref[brick, at : at + 64, :] = rows

    for half in range(2):
        lanes = slice(half * 128, half * 128 + 128)
        first = stage[half, pl.ds(0, 8, stride=8), :]
        last = stage[half, pl.ds(7, 8, stride=8), :]
        pair = jnp.concatenate([first, last], axis=0).astype(BF16)
        out_ref[brick, pl.ds(pl.multiple_of(C_LINES + 16 * a, 16), 16), lanes] = pair
    pair = jnp.concatenate([wide[:8], wide[56:]], axis=0).astype(BF16)

    @pl.when((a > 0) & (a < 7))
    def _():
        out_ref[brick, pl.ds(pl.multiple_of(B_LINES - 16 + 16 * a, 16), 16), :] = pair


def norm_body(x_ref, gain_ref, hidden_ref, out_ref, stage):
    bricks = out_ref.shape[0]
    gain = gain_ref[...]

    def step(k, _):
        at = pl.ds(pl.multiple_of(k * 64, 64), 64)
        x = x_ref[at, :].astype(F32)
        inverse = lax.rsqrt(jnp.mean(x * x, axis=-1, keepdims=True) + 1e-6)
        v = x * inverse * gain
        rows = (v / (1.0 + jnp.exp(-v))).astype(BF16)
        hidden_ref[at, :] = rows
        put_boundary(rows, k // 8, k % 8, out_ref, stage)
        return 0

    lax.fori_loop(0, bricks * 8, step, 0)


def extract_body(x_ref, out_ref, stage):
    bricks = out_ref.shape[0]

    def step(k, _):
        at = pl.ds(pl.multiple_of(k * 64, 64), 64)
        put_boundary(x_ref[at, :], k // 8, k % 8, out_ref, stage)
        return 0

    lax.fori_loop(0, bricks * 8, step, 0)


def start_padded(own_ref, cells, halo, bricks):
    zero = jnp.zeros((8, C), F32)

    def clear(k, _):
        for b in range(10):
            cells[k * 10 + b] = zero
        for side in range(2):
            for part in range(HB // 8):
                halo[side, k, part * 8 : part * 8 + 8, :] = zero
        return 0

    lax.fori_loop(0, bricks * 10, clear, 0)

    def fill(k, _):
        plane = (k // 8) * 10 + k % 8 + 1
        rows = own_ref[pl.ds(pl.multiple_of(k * 64, 64), 64), :].astype(F32)
        for b in range(8):
            cells[plane * 10 + b + 1] = rows[b * 8 : b * 8 + 8]
        return 0

    lax.fori_loop(0, bricks * 8, fill, 0)


def add_line(ref, index, line):
    ref[index] = ref[index] + line


def place(kind, e, keep, source, brick, share, cells, halo):
    flags = [t == -1 for t in e]
    pads = [jnp.where(f, 0, 9) for f in flags]
    take = [jnp.where(f, 1, 0) for f in flags]

    def rows(at, size):
        got = share[source, pl.ds(at, size), :].astype(F32)
        return got if keep is None else jnp.where(keep, got, 0.0)

    def half(pair, axis):
        return jnp.where(flags[axis], pair[8:], pair[:8])

    side = jnp.where(flags[2], 0, 1)
    base = brick * 10
    if kind == (1, 0, 0):
        got = rows(pl.multiple_of(take[0] * 64, 64), 64)
        first = (base + pads[0]) * 10 + 1
        for b in range(8):
            add_line(cells, first + b, got[b * 8 : b * 8 + 8])
    elif kind == (0, 1, 0):
        for a in range(8):
            if a in (0, 7):
                plane = rows(0 if a == 0 else 64, 64)
                line = jnp.where(flags[1], plane[56:], plane[:8])
            else:
                line = half(rows(B_LINES - 16 + 16 * a, 16), 1)
            add_line(cells, (base + a + 1) * 10 + pads[1], line)
    elif kind == (0, 0, 1):
        for a in range(8):
            line = half(rows(C_LINES + 16 * a, 16), 2)
            halo[side, base + a + 1, 8:16, :] = halo[side, base + a + 1, 8:16, :] + line
    elif kind == (1, 1, 0):
        plane = rows(pl.multiple_of(take[0] * 64, 64), 64)
        line = jnp.where(flags[1], plane[56:], plane[:8])
        add_line(cells, (base + pads[0]) * 10 + pads[1], line)
    elif kind == (1, 0, 1):
        line = half(rows(pl.multiple_of(C_LINES + 112 * take[0], 16), 16), 2)
        at = base + pads[0]
        halo[side, at, 8:16, :] = halo[side, at, 8:16, :] + line
    else:
        spot = pl.ds(jnp.where(flags[1], 7, 16), 1)
        planes = range(8) if kind == (0, 1, 1) else (None,)
        for a in planes:
            if a is None:
                line = half(rows(pl.multiple_of(C_LINES + 112 * take[0], 16), 16), 2)
                at = base + pads[0]
            else:
                line = half(rows(C_LINES + 16 * a, 16), 2)
                at = base + a + 1
            cell = jnp.where(flags[1], line[7:8], line[0:1])
            halo[side, at, spot, :] = halo[side, at, spot, :] + cell


def windows(cells, halo, cols, bricks):
    row = lax.broadcasted_iota(jnp.int32, (8, C), 0)

    def step(k, _):
        shifted = [[], [], []]
        for b in range(10):
            x = cells[k * 10 + b]
            before = halo[0, k, pl.ds(b + 7, 1), :]
            after = halo[1, k, pl.ds(b + 7, 1), :]
            shifted[0].append(jnp.where(row == 0, before, pltpu.roll(x, 1, 0)))
            shifted[1].append(x)
            shifted[2].append(jnp.where(row == 7, after, pltpu.roll(x, 7, 0)))
        for j in range(3):
            for l in range(3):
                block = jnp.concatenate(shifted[l][j : j + 8], axis=0).astype(BF16)
                at = (3 * j + l) * C
                cols[k, :, at : at + C] = block
        return 0

    lax.fori_loop(0, bricks * 10, step, 0)


def weight_grad_body(slots, factor, recv, codes, own_ref, share, cot_ref, gw_ref, cols, cells, halo):
    bricks = own_ref.shape[0] // 512
    start_padded(own_ref, cells, halo, bricks)
    for brick in range(bricks):
        for number, e in enumerate(DIRECTIONS):
            slot = recv[brick * 26 + number]
            safe = jnp.maximum(slot, 0)
            source = (safe // slots) * bricks + codes[safe] // 6
            kind = tuple(abs(t) for t in e)
            place(kind, e, slot >= 0, source, brick, share, cells, halo)
    windows(cells, halo, cols, bricks)

    def step(t, _):
        i = t // 9
        for jl in range(9):
            total = None
            for brick in range(bricks):
                left = cols[pl.ds(brick * 10 + t, 8), :, jl * C : jl * C + C].reshape(512, C)
                right = cot_ref[brick * 512 : brick * 512 + 512, :]
                term = lax.dot_general(
                    left, right, (((0,), (0,)), ((), ())), preferred_element_type=F32
                )
                total = term if total is None else total + term
            at = pl.multiple_of((t * 9 + jl) * C, C)
            gw_ref[pl.ds(at, C), :] = total * factor
        return 0

    lax.fori_loop(0, 3, step, 0)


def tap_sum(cols, weight_ref, brick):
    total = None
    for i in range(3):
        left = cols[brick * 10 + i : brick * 10 + i + 8].reshape(512, 9 * C)
        right = weight_ref[i * 9 * C : (i + 1) * 9 * C, :]
        term = jnp.dot(left, right, preferred_element_type=F32)
        total = term if total is None else total + term
    return total


def mix_body(cols, weight_ref, x_ref, out_ref):
    for brick in range(x_ref.shape[0] // 512):
        at = slice(brick * 512, brick * 512 + 512)
        out_ref[at, :] = (x_ref[at, :].astype(F32) + tap_sum(cols, weight_ref, brick)).astype(BF16)


def input_grad_body(
    slots, returned, code_here, cot_ref, share, weight_ref, x_ref, gain_ref, out_ref, cells, halo, cols
):
    bricks = cot_ref.shape[0] // 512
    start_padded(cot_ref, cells, halo, bricks)

    def one(k, _):
        info = returned[k]

        @pl.when(info > 0)
        def _():
            entry = info - 1
            brick = code_here[k] // 6
            source = (k // slots) * bricks + entry // 26
            number = 25 - entry % 26
            tap = jnp.where(number >= 13, number + 1, number)
            e = (tap // 9 - 1, (tap // 3) % 3 - 1, tap % 3 - 1)
            on = [t != 0 for t in e]
            for kind in ((1, 0, 0), (0, 1, 0), (0, 0, 1), (1, 1, 0), (1, 0, 1), (0, 1, 1), (1, 1, 1)):
                match = functools.reduce(
                    jnp.logical_and, [f if w else jnp.logical_not(f) for f, w in zip(on, kind)]
                )

                @pl.when(match)
                def _():
                    place(kind, e, None, source, brick, share, cells, halo)

        return 0

    lax.fori_loop(0, returned.shape[0], one, 0)
    windows(cells, halo, cols, bricks)
    gain = gain_ref[...]
    for brick in range(bricks):
        at = slice(brick * 512, brick * 512 + 512)
        grad = tap_sum(cols, weight_ref, brick)
        x = x_ref[at, :].astype(F32)
        inverse = lax.rsqrt(jnp.mean(x * x, axis=-1, keepdims=True) + 1e-6)
        unit = x * inverse
        v = unit * gain
        gate = 1.0 / (1.0 + jnp.exp(-v))
        grad = grad * (gate * (1.0 + v * (1.0 - gate))) * gain
        grad = inverse * (grad - unit * jnp.mean(grad * unit, axis=-1, keepdims=True))
        out_ref[at, :] = (cot_ref[at, :].astype(F32) + grad).astype(BF16)


def local(features, norm_gain, conv_weight, recv_slot, send_face, cotangent):
    channels = features.shape[1]
    per_device = features.shape[0]
    bricks = per_device // 512
    peers = lax.axis_size("morton")
    slots = send_face.shape[1] // peers
    factor = 1.0 / math.sqrt(peers * per_device)
    gain = norm_gain.reshape(1, channels)
    sds = jax.ShapeDtypeStruct
    stage = pltpu.VMEM((2, 64, 128), F32)
    padded = [
        pltpu.VMEM((bricks * 100, 8, channels), F32),
        pltpu.VMEM((2, bricks * 10, HB, channels), F32),
    ]
    cols_shape = (bricks * 10, 64, 9 * channels)
    conv_flops = 2 * per_device * 27 * channels * channels

    recv = recv_slot.reshape(-1)
    order = jnp.arange(peers * slots, dtype=jnp.int32)
    numbers = jnp.arange(1, bricks * 26 + 1, dtype=jnp.int32)
    served = jnp.sum(jnp.where(recv[:, None] == order[None, :], numbers[:, None], 0), axis=0)
    notes = jnp.concatenate(
        [send_face.reshape(peers, slots), served.astype(jnp.int32).reshape(peers, slots)], axis=1
    )
    notes = lax.all_to_all(notes, "morton", split_axis=0, concat_axis=0, tiled=True)
    codes = notes[:, :slots].reshape(-1)
    returned = notes[:, slots:].reshape(-1)

    hidden, share = call(
        norm_body,
        (sds((per_device, channels), BF16), sds((bricks, ROWS, channels), BF16)),
        [VMEM, VMEM],
        [stage],
        name="norm",
    )(features, gain)
    hidden_all = lax.all_gather(share, "morton", axis=0, tiled=True)

    cot_share = call(
        extract_body,
        sds((bricks, ROWS, channels), BF16),
        [VMEM],
        [stage],
        name="extract",
    )(cotangent)
    cot_all = lax.all_gather(cot_share, "morton", axis=0, tiled=True)

    whole_term, cols = call(
        functools.partial(weight_grad_body, slots, factor),
        (sds((27 * channels, channels), F32), sds(cols_shape, BF16)),
        [SMEM, SMEM, VMEM, VMEM, VMEM],
        padded,
        flops=conv_flops,
        nbytes=2**24,
        name="weight_grad",
    )(recv, codes, hidden, hidden_all, cotangent)
    grad_weight = lax.psum_scatter(whole_term, "morton", scatter_dimension=0, tiled=True)

    mixed = call(
        mix_body,
        sds((per_device, channels), BF16),
        [VMEM, VMEM, VMEM],
        flops=conv_flops,
        nbytes=2**23,
        name="mix",
    )(cols, conv_weight, features)

    turned = conv_weight.reshape(27, channels, channels)[::-1].transpose(0, 2, 1)
    grad_features = call(
        functools.partial(input_grad_body, slots),
        sds((per_device, channels), BF16),
        [SMEM, SMEM, VMEM, VMEM, VMEM, VMEM, VMEM],
        padded + [pltpu.VMEM(cols_shape, BF16)],
        flops=conv_flops,
        nbytes=2**24,
        name="input_grad",
    )(
        returned,
        send_face.reshape(-1),
        cotangent,
        cot_all,
        turned.reshape(27 * channels, channels),
        features,
        gain,
    )
    return (mixed, grad_features, grad_weight)


def solution(mesh):
    rows = P(("groups", "morton"), None)
    return jax.shard_map(
        local,
        mesh=mesh,
        in_specs=(rows, P(), P(), rows, rows, rows),
        out_specs=(rows, rows, rows),
        check_vma=False,
    )
```

profile of v0, /device:TPU:0, one launch (start us, length us, event | category | flops | bytes accessed | tf_op | source)
XLA Modules:
  0.0 232.9 jit_solution(2761376835623715783)
XLA Ops:
  7.2 4.1 %norm.1 = (bf16[1024,256]{1,0:T(8,128)(2,1)}, bf16[2,352,256]{2,1,0:T(8,128)(2,1)}) custom-call(bf16[1024,256]{1,0:T(8,128)(2,1)} %x_ref.7, f32[1,256]{1,0:T(1,128)} %bitcast.14), custom_call_target="tpu_custom_call" | custom-call | tf_op jit(solution)/shard_map/norm/pallas_call | solution.py:317
  11.4 0.0 all-gather.5.cloned.1.call-start
  11.4 2.2 extract.1
  13.7 0.8 reshape.40.recv
  14.5 0.1 select_reduce_fusion
  14.6 0.1 reshape.42
  14.7 0.5 broadcast.7
  15.2 1.3 reduce.3
  16.5 0.1 reshape.41
  16.6 0.1 pad_add_fusion
  16.7 13.7 %all_to_all.12 = s32[16,1,8]{2,1,0:T(1,128)S(1)} all-to-all(s32[16,1,8]{2,1,0:T(1,128)S(1)} %bitcast.12), channel_id=1, replica_groups=mesh['groups'=2,'morton'=16] {'morton'}, dimensions={0} | all-to-all | bytes 1024 | tf_op jit(solution)/shard_map/all_to_all | solution.py:313
  30.4 0.1 copy.25
  30.4 0.1 copy.26
  30.5 0.7 reshape.43.codes
  31.2 41.9 %all-gather.3.cloned.1.call-done.share = bf16[32,352,256]{2,1,0:T(8,128)(2,1)} async-done(((bf16[2,352,256]{2,1,0:T(8,128)(2,1)}), bf16[32,352,256]{2,1,0:T(8,128)(2,1)}) %all-gather.3.cloned.1.call-update) | async-done | bytes 5767184 | tf_op jit(solution)/shard_map/all_gather | solution.py:324
  73.1 12.9 %weight_grad.1 = (f32[6912,256]{1,0:T(8,128)}, bf16[20,64,2304]{2,1,0:T(8,128)(2,1)}) custom-call(s32[52]{0:T(128)} %copy-done, s32[64]{0:T(128)} %reshape.43.codes, bf16[1024,256]{1,0:T(8,128)(2,1)} %get-tuple-element.7.own_ref, bf16[32,352,256]{2,1,0:T(8,128)(2,1)} %all-gather.3.cloned.1.call-done.share, bf16[1024,256]{1,0:T(8,128)(2,1)} %cot_ref.3), custom_call_target="tpu_custom_call" | custom-call | flops 3623878656 | bytes 16777216 | tf_op jit(solution)/shard_map/weight_grad/pallas_call | solution.py:335
  86.1 4.5 %copy.28 = bf16[27,256,256]{1,2,0:T(8,128)(2,1)S(1)} copy(bf16[27,256,256]{2,1,0:T(8,128)(2,1)} %bitcast.10) | data formatting | bytes 7077888 | tf_op jit(solution)/shard_map/reshape | solution.py:355
  90.6 2.0 rev.3
  92.6 0.1 copy.27
  92.7 0.7 reshape.45.returned
  93.4 8.4 %mix.1 = bf16[1024,256]{1,0:T(8,128)(2,1)} custom-call(bf16[20,64,2304]{2,1,0:T(8,128)(2,1)} %get-tuple-element.9.cols, bf16[6912,256]{1,0:T(8,128)(2,1)} %weight_ref.1, bf16[1024,256]{1,0:T(8,128)(2,1)} %x_ref.7), custom_call_target="tpu_custom_call" | custom-call | flops 3623878656 | bytes 8388608 | tf_op jit(solution)/shard_map/mix/pallas_call | solution.py:346
  101.8 31.3 %all-gather.5.cloned.1.call-done.share = bf16[32,352,256]{2,1,0:T(8,128)(2,1)} async-done(((bf16[2,352,256]{2,1,0:T(8,128)(2,1)}), bf16[32,352,256]{2,1,0:T(8,128)(2,1)}) %all-gather.5.cloned.1.call-update) | async-done | bytes 5767184 | tf_op jit(solution)/shard_map/all_gather | solution.py:333
  133.1 14.0 %input_grad.1 = bf16[1024,256]{1,0:T(8,128)(2,1)} custom-call(s32[64]{0:T(128)} %reshape.45.returned, s32[64]{0:T(128)} %bitcast.16, bf16[1024,256]{1,0:T(8,128)(2,1)} %cot_ref.3, bf16[32,352,256]{2,1,0:T(8,128)(2,1)} %all-gather.5.cloned.1.call-done.share, bf16[6912,256]{1,0:T(8,128)(2,1)} %bitcast.11, bf16[1024,256]{1,0:T(8,128)(2,1)} %x_ref.7, ...), custom_call_target="tpu_custom_call" | custom-call | flops 3623878656 | bytes 16777216 | tf_op jit(solution)/shard_map/input_grad/pallas_call | solution.py:356
  147.1 79.3 %reduce-scatter.2.cloned.1.call-done = f32[432,256]{1,0:T(8,128)} async-done(((f32[6912,256]{1,0:T(8,128)}), f32[432,256]{1,0:T(8,128)}) %reduce-scatter.2.cloned.1.call-update) | async-done | bytes 442384 | tf_op jit(solution)/shard_map/reduce_scatter | solution.py:344
  (9 shorter events, 0.1 us)
Async XLA Ops:
  7.2 66.0 %all-gather.3.cloned.1.call-start = ((), (), s32[]{:S(2)}) async-start(), calls=%async_computation.2 | async-start | bytes 6127616 | tf_op jit(solution)/shard_map/all_gather | solution.py:324
  11.4 121.7 %all-gather.5.cloned.1.call-start = ((), (), s32[]{:S(2)}) async-start(), calls=%async_computation.3 | async-start | bytes 6127616 | tf_op jit(solution)/shard_map/all_gather | solution.py:333
  13.7 212.7 %reduce-scatter.2.cloned.1.call-start = ((), (), s32[]{:S(2)}) async-start(), calls=%async_computation.4 | async-start | bytes 7520256 | tf_op jit(solution)/shard_map/reduce_scatter | solution.py:344
  14.5 58.6 %copy-start = (s32[52]{0:T(128)}, s32[52]{0:T(128)S(1)}, u32[]{:S(2)}) copy-start(s32[52]{0:T(128)S(1)} %reshape.40.recv) | copy-start | bytes 628
Sparse Core Ops, SparseCore 0:
  11.5 61.6 all-gather.2
  75.4 57.6 all-gather.4
  137.7 88.6 reduce-scatter.1
where the time goes:
time: 233 us
  waiting for transfers between devices  153 us (66%)
  Pallas kernels  41.7 us (18%)
  between operations  13.8 us (6%)
  blocking collectives  13.7 us (6%)
  local copies, waits for them, and re-layouts  9.57 us (4%)
    reduce_scatter x1, waiting for transfers between devices, local(): lax.psum_scatter(whole_term, 'morton', scatter_dimension=0, tiled=True)  79.3 us
    all_gather x1, waiting for transfers between devices, local(): hidden_all = lax.all_gather(share, 'morton', axis=0, tiled=True)  41.9 us
    all_gather x1, waiting for transfers between devices, local(): cot_all = lax.all_gather(cot_share, 'morton', axis=0, tiled=True)  31.3 us
    pallas_call x1, Pallas kernels, local(): call(functools.partial(input_grad_body, slots), sds((per_device, channels...  14 us
    all_to_all x1, blocking collectives, local(): lax.all_to_all(notes, 'morton', split_axis=0, concat_axis=0, tiled=True)  13.7 us
    pallas_call x1, Pallas kernels, local(): call(functools.partial(weight_grad_body, slots, factor), (sds((27 * chann...  12.9 us
    pallas_call x1, Pallas kernels, local(): call(mix_body, sds((per_device, channels), BF16), [VMEM, VMEM, VMEM], flo...  8.41 us
  transfers between devices with their start and end apart: 3, of which 3 were waited for; matrix products, arithmetic and copies ran while one was open for 5% of the time, Pallas kernels for 16%

commit v1 on v0

--- a/solution.py
+++ b/solution.py
@@ -27,14 +27,80 @@
 
 VMEM = pl.BlockSpec(memory_space=pltpu.VMEM)
 SMEM = pl.BlockSpec(memory_space=pltpu.SMEM)
-
-
-def call(body, out_shape, in_specs, scratch=(), flops=0, nbytes=0, name=None):
+ANY = pl.BlockSpec(memory_space=pl.ANY)
+
+
+def ring_order(chips):
+    if chips == 8:
+        return [0, 2, 4, 6, 7, 5, 3, 1]
+    return list(range(chips))
+
+
+def ring_tables(peers):
+    chips = peers // 2
+    spot = np.argsort(np.array(ring_order(chips)))
+    device = np.arange(peers)
+    behind = (spot[device // 2][:, None] - spot[None, :]) % chips
+    place_of = behind[:, device // 2] + chips * (device[:, None] % 2 != device[None, :] % 2)
+    if chips > 8:
+        place_of = np.broadcast_to(device, (peers, peers))
+    return behind.astype(np.int32), place_of.astype(np.int32)
+
+
+def ring_step(x, peers, step):
+    order = ring_order(peers // 2)
+    pairs = [
+        (2 * order[i] + core, 2 * order[(i + step) % len(order)] + core)
+        for i in range(len(order))
+        for core in range(2)
+    ]
+    return lax.ppermute(x, "morton", pairs)
+
+
+def swap_cores(x, peers):
+    return lax.ppermute(x, "morton", [(m, m ^ 1) for m in range(peers)])
+
+
+def gather_ring(x, peers):
+    chips = peers // 2
+    if chips > 8:
+        return [lax.all_gather(x, "morton", axis=0, tiled=True)]
+    ups, downs = [x], []
+    for hop in range(chips // 2):
+        ups.append(ring_step(ups[-1], peers, 1))
+        if hop < (chips - 1) // 2:
+            downs.append(ring_step((downs or [x])[-1], peers, -1))
+    mine = ups + downs[::-1]
+    return mine + [swap_cores(t, peers) for t in mine]
+
+
+def scatter_ring(keep, give, peers):
+    chips = peers // 2
+    other = swap_cores(give, peers)
+
+    def term(k):
+        return keep[k] + other[k].astype(F32)
+
+    ups, downs = chips // 2, (chips - 1) // 2
+    total = term(0)
+    for count, step in ((ups, 1), (downs, -1)):
+        held = None
+        for hop in range(count, 0, -1):
+            part = term((-step * hop) % chips)
+            if held is not None:
+                part = part + held.astype(F32)
+            held = ring_step(part.astype(BF16), peers, step)
+        if held is not None:
+            total = total + held.astype(F32)
+    return total
+
+
+def call(body, out_shape, in_specs, scratch=(), flops=0, nbytes=0, name=None, out_specs=None):
     return pl.pallas_call(
         body,
         out_shape=out_shape,
         in_specs=in_specs,
-        out_specs=jax.tree.map(lambda _: VMEM, out_shape),
+        out_specs=out_specs or jax.tree.map(lambda _: VMEM, out_shape),
         scratch_shapes=list(scratch),
         compiler_params=pltpu.CompilerParams(vmem_limit_bytes=VMEM_LIMIT),
         cost_estimate=pl.CostEstimate(flops=flops, bytes_accessed=nbytes, transcendentals=0),
@@ -195,34 +261,65 @@
     lax.fori_loop(0, bricks * 10, step, 0)
 
 
-def weight_grad_body(slots, factor, recv, codes, own_ref, share, cot_ref, gw_ref, cols, cells, halo):
+def fetch(parts, share, sems):
+    size = parts[0].shape[0]
+    copies = [
+        pltpu.make_async_copy(part, share.at[pl.ds(k * size, size)], sems.at[k])
+        for k, part in enumerate(parts)
+    ]
+    for copy in copies:
+        copy.start()
+    return copies
+
+
+def weight_grad_body(slots, factor, peers, count, *refs):
+    recv, codes, place_of, behind, core, own_ref, cot_ref = refs[:7]
+    parts = refs[7 : 7 + count]
+    keep_ref, give_ref, cols, cells, halo, share, sums, sems, out_sems = refs[7 + count :]
     bricks = own_ref.shape[0] // 512
+    copies = fetch(parts, share, sems)
     start_padded(own_ref, cells, halo, bricks)
+    for copy in copies:
+        copy.wait()
     for brick in range(bricks):
         for number, e in enumerate(DIRECTIONS):
             slot = recv[brick * 26 + number]
             safe = jnp.maximum(slot, 0)
-            source = (safe // slots) * bricks + codes[safe] // 6
+            source = place_of[safe // slots] * bricks + codes[safe] // 6
             kind = tuple(abs(t) for t in e)
             place(kind, e, slot >= 0, source, brick, share, cells, halo)
     windows(cells, halo, cols, bricks)
 
-    def step(t, _):
-        i = t // 9
-        for jl in range(9):
-            total = None
-            for brick in range(bricks):
-                left = cols[pl.ds(brick * 10 + t, 8), :, jl * C : jl * C + C].reshape(512, C)
-                right = cot_ref[brick * 512 : brick * 512 + 512, :]
-                term = lax.dot_general(
-                    left, right, (((0,), (0,)), ((), ())), preferred_element_type=F32
-                )
-                total = term if total is None else total + term
-            at = pl.multiple_of((t * 9 + jl) * C, C)
-            gw_ref[pl.ds(at, C), :] = total * factor
-        return 0
-
-    lax.fori_loop(0, 3, step, 0)
+    rows = 27 * C // peers
+    mine = core[0]
+    for tap in range(27):
+        i, jl = divmod(tap, 9)
+        total = None
+        for brick in range(bricks):
+            left = cols[brick * 10 + i : brick * 10 + i + 8, :, jl * C : jl * C + C].reshape(512, C)
+            right = cot_ref[brick * 512 : brick * 512 + 512, :]
+            term = lax.dot_general(left, right, (((0,), (0,)), ((), ())), preferred_element_type=F32)
+            total = term if total is None else total + term
+        total = total * factor
+        start = tap * C
+        while start < (tap + 1) * C:
+            owner = start // rows
+            stop = min((tap + 1) * C, (owner + 1) * rows)
+            piece = total[start - tap * C : stop - tap * C]
+            bucket = jnp.bitwise_xor(mine, owner % 2)
+            where = slice(start - owner * rows, stop - owner * rows)
+            sums[bucket, behind[owner // 2], where, :] = piece
+            start = stop
+    keep_copy = pltpu.make_async_copy(sums.at[0], keep_ref, out_sems.at[0])
+    keep_copy.start()
+    half = sums.shape[1]
+
+    def narrow(k, _):
+        give_ref[k] = sums[1, k].astype(BF16)
+        return 0
+
+    lax.fori_loop(0, half, narrow, 0)
+    keep_copy.wait()
 
 
 def tap_sum(cols, weight_ref, brick):
@@ -241,11 +338,15 @@
         out_ref[at, :] = (x_ref[at, :].astype(F32) + tap_sum(cols, weight_ref, brick)).astype(BF16)
 
 
-def input_grad_body(
-    slots, returned, code_here, cot_ref, share, weight_ref, x_ref, gain_ref, out_ref, cells, halo, cols
-):
+def input_grad_body(slots, count, *refs):
+    returned, code_here, place_of, cot_ref, weight_ref, x_ref, gain_ref = refs[:7]
+    parts = refs[7 : 7 + count]
+    out_ref, cells, halo, cols, share, sems = refs[7 + count :]
     bricks = cot_ref.shape[0] // 512
+    copies = fetch(parts, share, sems)
     start_padded(cot_ref, cells, halo, bricks)
+    for copy in copies:
+        copy.wait()
 
     def one(k, _):
         info = returned[k]
@@ -254,7 +355,7 @@
         def _():
             entry = info - 1
             brick = code_here[k] // 6
-            source = (k // slots) * bricks + entry // 26
+            source = place_of[k // slots] * bricks + entry // 26
             number = 25 - entry % 26
             tap = jnp.where(number >= 13, number + 1, number)
             e = (tap // 9 - 1, (tap // 3) % 3 - 1, tap % 3 - 1)
@@ -303,16 +404,21 @@
     cols_shape = (bricks * 10, 64, 9 * channels)
     conv_flops = 2 * per_device * 27 * channels * channels
 
+    me = lax.axis_index("morton")
+    behind_all, place_all = ring_tables(peers)
+    behind = jnp.asarray(behind_all)[me]
+    place_of = jnp.asarray(place_all)[me]
+    core = (me % 2).astype(jnp.int32).reshape(1)
+
     recv = recv_slot.reshape(-1)
     order = jnp.arange(peers * slots, dtype=jnp.int32)
     numbers = jnp.arange(1, bricks * 26 + 1, dtype=jnp.int32)
     served = jnp.sum(jnp.where(recv[:, None] == order[None, :], numbers[:, None], 0), axis=0)
-    notes = jnp.concatenate(
-        [send_face.reshape(peers, slots), served.astype(jnp.int32).reshape(peers, slots)], axis=1
-    )
-    notes = lax.all_to_all(notes, "morton", split_axis=0, concat_axis=0, tiled=True)
-    codes = notes[:, :slots].reshape(-1)
-    returned = notes[:, slots:].reshape(-1)
+    notes = jnp.concatenate([send_face, served.astype(jnp.int32)[None]], axis=0)
+    notes = lax.all_gather(notes, "morton", axis=0, tiled=False)
+    notes = lax.dynamic_slice_in_dim(notes, me * slots, slots, 2)
+    codes = notes[:, 0].reshape(-1)
+    returned = notes[:, 1].reshape(-1)
 
     hidden, share = call(
         norm_body,
@@ -321,7 +427,7 @@
         [stage],
         name="norm",
     )(features, gain)
-    hidden_all = lax.all_gather(share, "morton", axis=0, tiled=True)
+    hidden_parts = gather_ring(share, peers)
 
     cot_share = call(
         extract_body,
@@ -330,18 +436,33 @@
         [stage],
         name="extract",
     )(cotangent)
-    cot_all = lax.all_gather(cot_share, "morton", axis=0, tiled=True)
-
-    whole_term, cols = call(
-        functools.partial(weight_grad_body, slots, factor),
-        (sds((27 * channels, channels), F32), sds(cols_shape, BF16)),
-        [SMEM, SMEM, VMEM, VMEM, VMEM],
-        padded,
+    cot_share, _ = lax.optimization_barrier((cot_share, hidden_parts[len(hidden_parts) // 4]))
+    cot_parts = gather_ring(cot_share, peers)
+
+    gathered = [
+        pltpu.VMEM((peers * bricks, ROWS, channels), BF16),
+        pltpu.SemaphoreType.DMA((len(hidden_parts),)),
+    ]
+    rows = 27 * channels // peers
+    keep, give, cols = call(
+        functools.partial(weight_grad_body, slots, factor, peers, len(hidden_parts)),
+        (
+            sds((peers // 2, rows, channels), F32),
+            sds((peers // 2, rows, channels), BF16),
+            sds(cols_shape, BF16),
+        ),
+        [SMEM] * 5 + [VMEM] * 2 + [ANY] * len(hidden_parts),
+        padded
+        + gathered[:1]
+        + [pltpu.VMEM((2, peers // 2, rows, channels), F32)]
+        + gathered[1:]
+        + [pltpu.SemaphoreType.DMA((1,))],
         flops=conv_flops,
         nbytes=2**24,
         name="weight_grad",
-    )(recv, codes, hidden, hidden_all, cotangent)
-    grad_weight = lax.psum_scatter(whole_term, "morton", scatter_dimension=0, tiled=True)
+        out_specs=(ANY, VMEM, VMEM),
+    )(recv, codes, place_of, behind, core, hidden, cotangent, *hidden_parts)
+    grad_weight = scatter_ring(keep, give, peers)
 
     mixed = call(
         mix_body,
@@ -354,21 +475,22 @@
 
     turned = conv_weight.reshape(27, channels, channels)[::-1].transpose(0, 2, 1)
     grad_features = call(
-        functools.partial(input_grad_body, slots),
+        functools.partial(input_grad_body, slots, len(cot_parts)),
         sds((per_device, channels), BF16),
-        [SMEM, SMEM, VMEM, VMEM, VMEM, VMEM, VMEM],
-        padded + [pltpu.VMEM(cols_shape, BF16)],
+        [SMEM] * 3 + [VMEM] * 4 + [ANY] * len(cot_parts),
+        padded + [pltpu.VMEM(cols_shape, BF16)] + gathered,
         flops=conv_flops,
         nbytes=2**24,
         name="input_grad",
     )(
         returned,
         send_face.reshape(-1),
+        place_of,
         cotangent,
-        cot_all,
         turned.reshape(27 * channels, channels),
         features,
         gain,
+        *cot_parts,
     )
     return (mixed, grad_features, grad_weight)
 

time: 233 us -> 168 us (0.72)
  waiting for transfers between devices: 153 us -> 56.7 us
  starting transfers between devices: 0.12 us -> 22.1 us
  between operations: 13.8 us -> 0.98 us
  other arithmetic: 1.47 us -> 10.1 us
  blocking collectives: 13.7 us -> 21.2 us
  local copies, waits for them, and re-layouts: 9.57 us -> 13 us
    reduce_scatter x1 -> x0, waiting for transfers between devices: 79.3 us -> none  [local(): lax.psum_scatter(whole_term, 'morton', scatter_dimension=0, tiled=True)]
    all_gather x2 -> x0, waiting for transfers between devices: 73.2 us -> none  [the longest x1 41.9 us: local(): hidden_all = lax.all_gather(share, 'morton', axis=0, tiled=True)]
    ppermute x0 -> x38, waiting for transfers between devices: none -> 56.7 us  [the longest x21 55.3 us: ring_step(): return lax.ppermute(x, 'morton', pairs)]
    ppermute x0 -> x38, starting transfers between devices: none -> 22.1 us  [the longest x21 18.9 us: ring_step(): return lax.ppermute(x, 'morton', pairs)]
    all_gather x0 -> x1, blocking collectives: none -> 21.2 us  [local(): notes = lax.all_gather(notes, 'morton', axis=0, tiled=False)]
    all_to_all x1 -> x0, blocking collectives: 13.7 us -> none  [local(): lax.all_to_all(notes, 'morton', split_axis=0, concat_axis=0, tiled=True)]
    convert_element_type x0 -> x5, other arithmetic: none -> 7.35 us  [scatter_ring(): held = ring_step(part.astype(BF16), peers, step)]
    squeeze x0 -> x2, local copies, waits for them, and re-layouts: none -> 2.48 us  [the longest x1 1.27 us: local(): place_of = jnp.asarray(place_all)[me]]
  transfers between devices with their start and end apart: 3 -> 38, of which waited for: 3 -> 12; matrix products, arithmetic and copies ran while one was open for 5% -> 12% of each run, Pallas kernels for 16% -> 15%
where the time goes in v1:
time: 168 us
  waiting for transfers between devices  56.7 us (34%)
  Pallas kernels  43.7 us (26%)
  starting transfers between devices  22.1 us (13%)
  blocking collectives  21.2 us (13%)
  local copies, waits for them, and re-layouts  13 us (8%)
  other arithmetic  10.1 us (6%)
    ppermute x21, waiting for transfers between devices, ring_step(): return lax.ppermute(x, 'morton', pairs)  55.3 us
    all_gather x1, blocking collectives, local(): notes = lax.all_gather(notes, 'morton', axis=0, tiled=False)  21.2 us
    ppermute x21, starting transfers between devices, ring_step(): return lax.ppermute(x, 'morton', pairs)  18.9 us
    pallas_call x1, Pallas kernels, local(): call(functools.partial(input_grad_body, slots, len(cot_parts)), sds((per_...  15.1 us
    pallas_call x1, Pallas kernels, local(): call(functools.partial(weight_grad_body, slots, factor, peers, len(hidden...  13.8 us
    pallas_call x1, Pallas kernels, local(): call(mix_body, sds((per_device, channels), BF16), [VMEM, VMEM, VMEM], flo...  8.43 us
    convert_element_type x5, other arithmetic, scatter_ring(): held = ring_step(part.astype(BF16), peers, step)  7.35 us
    reshape x1, local copies, waits for them, and re-layouts, local(): conv_weight.reshape(27, channels, channels)[::-1].transpose(0, 2, 1)  4.44 us
  transfers between devices with their start and end apart: 38, of which 12 were waited for; matrix products, arithmetic and copies ran while one was open for 12% of the time, Pallas kernels for 15%

profile of v1, /device:TPU:0, one launch (start us, length us, event | category | flops | bytes accessed | tf_op | source)
XLA Modules:
  0.0 167.8 jit_solution(13417509918260249991)
XLA Ops:
  0.6 4.1 %norm.1 = (bf16[1024,256]{1,0:T(8,128)(2,1)}, bf16[2,352,256]{2,1,0:T(8,128)(2,1)}) custom-call(bf16[1024,256]{1,0:T(8,128)(2,1)} %refs_5_.1, f32[1,256]{1,0:T(1,128)} %bitcast.44), custom_call_target="tpu_custom_call" | custom-call | tf_op jit(solution)/shard_map/norm/pallas_call | solution.py:423
  4.8 3.0 %collective-permute-start = (bf16[2,352,256]{2,1,0:T(8,128)(2,1)}, bf16[2,352,256]{2,1,0:T(8,128)(2,1)S(1)}, u32[]{:S(2)}, u32[]{:S(2)}) collective-permute-start(bf16[2,352,256]{2,1,0:T(8,128)(2,1)} %get-tuple-element.10.refs_7_), channel_id=1, source_target_pairs={{0,4},{1,5},{4,8},{5,9},{8,12},{9,13},{12,14},{13,15},{14,10},{15,... | collective-permute-start | bytes 1081352 | tf_op jit(solution)/shard_map/ppermute | solution.py:57
  7.8 8.6 %collective-permute-done.refs_8_ = bf16[2,352,256]{2,1,0:T(8,128)(2,1)S(1)} collective-permute-done((bf16[2,352,256]{2,1,0:T(8,128)(2,1)}, bf16[2,352,256]{2,1,0:T(8,128)(2,1)S(1)}, u32[]{:S(2)}, u32[]{:S(2)}) %collective-permute-start) | collective-permute-done | bytes 360480 | tf_op jit(solution)/shard_map/ppermute | solution.py:57
  18.4 7.6 %collective-permute-done.1.refs_9_ = bf16[2,352,256]{2,1,0:T(8,128)(2,1)S(1)} collective-permute-done((bf16[2,352,256]{2,1,0:T(8,128)(2,1)S(1)}, bf16[2,352,256]{2,1,0:T(8,128)(2,1)S(1)}, u32[]{:S(2)}, u32[]{:S(2)}) %collective-permute-start.1) | collective-permute-done | bytes 360480 | tf_op jit(solution)/shard_map/ppermute | solution.py:57
  28.5 6.1 %collective-permute-done.2.refs_10_ = bf16[2,352,256]{2,1,0:T(8,128)(2,1)S(1)} collective-permute-done((bf16[2,352,256]{2,1,0:T(8,128)(2,1)S(1)}, bf16[2,352,256]{2,1,0:T(8,128)(2,1)S(1)}, u32[]{:S(2)}, u32[]{:S(2)}) %collective-permute-start.2) | collective-permute-done | bytes 360480 | tf_op jit(solution)/shard_map/ppermute | solution.py:57
  38.8 3.7 %collective-permute-done.3.refs_11_ = bf16[2,352,256]{2,1,0:T(8,128)(2,1)} collective-permute-done((bf16[2,352,256]{2,1,0:T(8,128)(2,1)S(1)}, bf16[2,352,256]{2,1,0:T(8,128)(2,1)}, u32[]{:S(2)}, u32[]{:S(2)}) %collective-permute-start.3) | collective-permute-done | bytes 360480 | tf_op jit(solution)/shard_map/ppermute | solution.py:57
  43.3 21.2 %all-gather.1 = s32[16,2,64]{2,1,0:T(2,128)S(1)} all-gather(s32[1,2,64]{2,1,0:T(2,128)S(1)} %add_bitcast_fusion), channel_id=2, replica_groups=mesh['groups'=2,'morton'=16] {'morton'}, dimensions={0}, use_global_device_ids=true | all-gather | bytes 8704 | tf_op jit(solution)/shard_map/all_gather | solution.py:418
  67.8 13.8 %weight_grad.1 = (f32[8,432,256]{2,1,0:T(8,128)}, bf16[8,432,256]{2,1,0:T(8,128)(2,1)}, bf16[20,64,2304]{2,1,0:T(8,128)(2,1)}) custom-call(s32[52]{0:T(128)} %copy-done.19, s32[64]{0:T(128)} %reshape_squeeze.6.refs_1_, s32[16]{0:T(128)} %fusion.8.refs_2_, s32[8]{0:T(128)} %fusion.9.refs_3_, s32[1]{0:T(128)} %bitcast.4.refs_4_, ...), custom_call_target="tpu_custom_call" | custom-call | flops 3623878656 | bytes 16777216 | tf_op jit(solution)/shard_map/weight_grad/pallas_call | solution.py:447
  82.0 2.2 %extract.1.refs_7_ = bf16[2,352,256]{2,1,0:T(8,128)(2,1)} custom-call(bf16[1024,256]{1,0:T(8,128)(2,1)} %refs_3_.1), custom_call_target="tpu_custom_call" | custom-call | tf_op jit(solution)/shard_map/extract/pallas_call | solution.py:432
  87.6 2.0 %collective-permute-start.19 = (bf16[2,352,256]{2,1,0:T(8,128)(2,1)}, bf16[2,352,256]{2,1,0:T(8,128)(2,1)}, u32[]{:S(2)}, u32[]{:S(2)}) collective-permute-start(bf16[2,352,256]{2,1,0:T(8,128)(2,1)} %extract.1.refs_7_), channel_id=1, source_target_pairs={{0,2},{1,3},{4,0},{5,1},{8,4},{9,5},{12,8},{13,9},{14,12},{15,13},... | collective-permute-start | bytes 1081352 | tf_op jit(solution)/shard_map/ppermute | solution.py:57
  89.6 6.3 %collective-permute-done.15.refs_8_ = bf16[2,352,256]{2,1,0:T(8,128)(2,1)} collective-permute-done((bf16[2,352,256]{2,1,0:T(8,128)(2,1)}, bf16[2,352,256]{2,1,0:T(8,128)(2,1)}, u32[]{:S(2)}, u32[]{:S(2)}) %collective-permute-start.15) | collective-permute-done | bytes 360480 | tf_op jit(solution)/shard_map/ppermute | solution.py:57
  95.9 4.6 %collective-permute-done.31 = bf16[432,256]{1,0:T(8,128)(2,1)S(1)} collective-permute-done((bf16[432,256]{1,0:T(8,128)(2,1)S(1)}, bf16[432,256]{1,0:T(8,128)(2,1)S(1)}, u32[]{:S(2)}, u32[]{:S(2)}) %collective-permute-start.31) | collective-permute-done | bytes 221216 | tf_op jit(solution)/shard_map/ppermute | solution.py:57
  101.7 2.0 %collective-permute-start.20 = (bf16[2,352,256]{2,1,0:T(8,128)(2,1)}, bf16[2,352,256]{2,1,0:T(8,128)(2,1)}, u32[]{:S(2)}, u32[]{:S(2)}) collective-permute-start(bf16[2,352,256]{2,1,0:T(8,128)(2,1)} %collective-permute-done.19.refs_14_), channel_id=1, source_target_pairs={{0,2},{1,3},{4,0},{5,1},{8,4},{9,5},{12,8},{13,9},{14,12},{15,13},... | collective-permute-start | bytes 1081352 | tf_op jit(solution)/shard_map/ppermute | solution.py:57
  103.7 4.5 %collective-permute-done.16.refs_9_ = bf16[2,352,256]{2,1,0:T(8,128)(2,1)S(1)} collective-permute-done((bf16[2,352,256]{2,1,0:T(8,128)(2,1)}, bf16[2,352,256]{2,1,0:T(8,128)(2,1)S(1)}, u32[]{:S(2)}, u32[]{:S(2)}) %collective-permute-start.16) | collective-permute-done | bytes 360480 | tf_op jit(solution)/shard_map/ppermute | solution.py:57
  108.2 2.0 %collective-permute-start.35 = (bf16[432,256]{1,0:T(8,128)(2,1)S(1)}, bf16[432,256]{1,0:T(8,128)(2,1)S(1)}, u32[]{:S(2)}, u32[]{:S(2)}) collective-permute-start(bf16[432,256]{1,0:T(8,128)(2,1)S(1)} %get-tuple-element.20), channel_id=1, source_target_pairs={{0,2},{1,3},{4,0},{5,1},{8,4},{9,5},{12,8},{13,9},{14,12},{15,13},... | collective-permute-start | bytes 663560 | tf_op jit(solution)/shard_map/ppermute | solution.py:57
  110.2 2.7 %collective-permute-done.32 = bf16[432,256]{1,0:T(8,128)(2,1)S(1)} collective-permute-done((bf16[432,256]{1,0:T(8,128)(2,1)S(1)}, bf16[432,256]{1,0:T(8,128)(2,1)S(1)}, u32[]{:S(2)}, u32[]{:S(2)}) %collective-permute-start.32) | collective-permute-done | bytes 221216 | tf_op jit(solution)/shard_map/ppermute | solution.py:57
  114.7 6.1 %collective-permute-done.17.refs_10_ = bf16[2,352,256]{2,1,0:T(8,128)(2,1)} collective-permute-done((bf16[2,352,256]{2,1,0:T(8,128)(2,1)S(1)}, bf16[2,352,256]{2,1,0:T(8,128)(2,1)}, u32[]{:S(2)}, u32[]{:S(2)}) %collective-permute-start.17) | collective-permute-done | bytes 360480 | tf_op jit(solution)/shard_map/ppermute | solution.py:57
  120.8 3.9 %collective-permute-done.33 = bf16[432,256]{1,0:T(8,128)(2,1)S(1)} collective-permute-done((bf16[432,256]{1,0:T(8,128)(2,1)S(1)}, bf16[432,256]{1,0:T(8,128)(2,1)S(1)}, u32[]{:S(2)}, u32[]{:S(2)}) %collective-permute-start.33) | collective-permute-done | bytes 221216 | tf_op jit(solution)/shard_map/ppermute | solution.py:57
  125.0 2.1 %fusion.4 = (bf16[432,256]{1,0:T(8,128)(2,1)}, bf16[432,256]{1,0:T(8,128)(2,1)}) fusion(bf16[432,256]{1,0:T(8,128)(2,1)S(1)} %collective-permute-done.33, f32[8,432,256]{2,1,0:T(8,128)} %get-tuple-element.13, bf16[8,432,256]{2,1,0:T(8,128)(2,1)S(1)} %collective-permute-done.30, bf16[432,256]{1,0:T(8,128)(2,1)S(1)} %collective-permute-done.35), kind=kLoop, calls=%fused_computation.9 | loop fusion | flops 1105920 | bytes 2211840 | tf_op jit(solution)/shard_map/convert_element_type | solution.py:92
  130.2 4.4 %copy.14 = bf16[27,256,256]{1,2,0:T(8,128)(2,1)S(1)} copy(bf16[27,256,256]{2,1,0:T(8,128)(2,1)} %bitcast.42) | data formatting | bytes 7077888 | tf_op jit(solution)/shard_map/reshape | solution.py:476
  134.6 2.1 %rev.3 = bf16[27,256,256]{1,2,0:T(8,128)(2,1)} reverse(bf16[27,256,256]{1,2,0:T(8,128)(2,1)S(1)} %copy.14), dimensions={0} | reverse | bytes 7077888 | tf_op jit(solution)/shard_map/rev | solution.py:476
  137.9 8.4 %mix.1 = bf16[1024,256]{1,0:T(8,128)(2,1)} custom-call(bf16[20,64,2304]{2,1,0:T(8,128)(2,1)} %get-tuple-element.11.cols, bf16[6912,256]{1,0:T(8,128)(2,1)} %weight_ref.1, bf16[1024,256]{1,0:T(8,128)(2,1)} %refs_5_.1), custom_call_target="tpu_custom_call" | custom-call | flops 3623878656 | bytes 8388608 | tf_op jit(solution)/shard_map/mix/pallas_call | solution.py:467
  150.7 15.1 %input_grad.1 = bf16[1024,256]{1,0:T(8,128)(2,1)} custom-call(s32[64]{0:T(128)} %reshape_squeeze.7.refs_0_, s32[64]{0:T(128)} %bitcast.46, s32[16]{0:T(128)} %fusion.8.refs_2_, bf16[1024,256]{1,0:T(8,128)(2,1)} %refs_3_.1, bf16[6912,256]{1,0:T(8,128)(2,1)} %bitcast.43, bf16[1024,256]{1,0:T(8,128)(2,1)} %refs_5_.1, f32[1,256]{1,0:T(1,128)} %bitcast.45, ...), custom_call_target="tpu_custom_call" | custom-call | flops 3623878656 | bytes 16777216 | tf_op jit(solution)/shard_map/input_grad/pallas_call | solution.py:477
  165.8 1.9 %fusion.5 = f32[432,256]{1,0:T(8,128)} fusion(bf16[432,256]{1,0:T(8,128)(2,1)S(1)} %collective-permute-done.37, bf16[432,256]{1,0:T(8,128)(2,1)S(1)} %collective-permute-done.34, f32[8,432,256]{2,1,0:T(8,128)} %get-tuple-element.13, bf16[8,432,256]{2,1,0:T(8,128)(2,1)} %copy-done), kind=kLoop, calls=%fused_computation.11 | loop fusion | flops 663552 | bytes 1548288 | tf_op jit(solution)/shard_map/add | solution.py:94
  (115 shorter events, 28.3 us)
Async XLA Ops:
  4.8 11.6 %collective-permute-start = (bf16[2,352,256]{2,1,0:T(8,128)(2,1)}, bf16[2,352,256]{2,1,0:T(8,128)(2,1)S(1)}, u32[]{:S(2)}, u32[]{:S(2)}) collective-permute-start(bf16[2,352,256]{2,1,0:T(8,128)(2,1)} %get-tuple-element.10.refs_7_), channel_id=1, source_target_pairs={{0,4},{1,5},{4,8},{5,9},{8,12},{9,13},{12,14},{13,15},{14,10},{15,... | collective-permute-start | bytes 1081352 | tf_op jit(solution)/shard_map/ppermute | solution.py:57
  36.8 30.9 %collective-permute-start.9 = (bf16[2,352,256]{2,1,0:T(8,128)(2,1)S(1)}, bf16[2,352,256]{2,1,0:T(8,128)(2,1)}, u32[]{:S(2)}, u32[]{:S(2)}) collective-permute-start(bf16[2,352,256]{2,1,0:T(8,128)(2,1)S(1)} %collective-permute-done.1.refs_9_), channel_id=1, source_target_pairs={{0,1},{1,0},{2,3},{3,2},{4,5},{5,4},{6,7},{7,6},{8,9},{9,8},{10,11... | collective-permute-start | bytes 1081352 | tf_op jit(solution)/shard_map/ppermute | solution.py:61
  36.9 30.8 %collective-permute-start.13 = (bf16[2,352,256]{2,1,0:T(8,128)(2,1)S(1)}, bf16[2,352,256]{2,1,0:T(8,128)(2,1)}, u32[]{:S(2)}, u32[]{:S(2)}) collective-permute-start(bf16[2,352,256]{2,1,0:T(8,128)(2,1)S(1)} %collective-permute-done.5.refs_13_), channel_id=1, source_target_pairs={{0,1},{1,0},{2,3},{3,2},{4,5},{5,4},{6,7},{7,6},{8,9},{9,8},{10,11... | collective-permute-start | bytes 1081352 | tf_op jit(solution)/shard_map/ppermute | solution.py:61
  37.4 30.3 %collective-permute-start.10 = (bf16[2,352,256]{2,1,0:T(8,128)(2,1)S(1)}, bf16[2,352,256]{2,1,0:T(8,128)(2,1)}, u32[]{:S(2)}, u32[]{:S(2)}) collective-permute-start(bf16[2,352,256]{2,1,0:T(8,128)(2,1)S(1)} %collective-permute-done.2.refs_10_), channel_id=1, source_target_pairs={{0,1},{1,0},{2,3},{3,2},{4,5},{5,4},{6,7},{7,6},{8,9},{9,8},{10,11... | collective-permute-start | bytes 1081352 | tf_op jit(solution)/shard_map/ppermute | solution.py:61
  38.8 28.9 %collective-permute-start.12 = (bf16[2,352,256]{2,1,0:T(8,128)(2,1)S(1)}, bf16[2,352,256]{2,1,0:T(8,128)(2,1)}, u32[]{:S(2)}, u32[]{:S(2)}) collective-permute-start(bf16[2,352,256]{2,1,0:T(8,128)(2,1)S(1)} %collective-permute-done.6.refs_12_), channel_id=1, source_target_pairs={{0,1},{1,0},{2,3},{3,2},{4,5},{5,4},{6,7},{7,6},{8,9},{9,8},{10,11... | collective-permute-start | bytes 1081352 | tf_op jit(solution)/shard_map/ppermute | solution.py:61
  42.5 25.2 %collective-permute-start.11 = (bf16[2,352,256]{2,1,0:T(8,128)(2,1)}, bf16[2,352,256]{2,1,0:T(8,128)(2,1)}, u32[]{:S(2)}, u32[]{:S(2)}) collective-permute-start(bf16[2,352,256]{2,1,0:T(8,128)(2,1)} %collective-permute-done.3.refs_11_), channel_id=1, source_target_pairs={{0,1},{1,0},{2,3},{3,2},{4,5},{5,4},{6,7},{7,6},{8,9},{9,8},{10,11... | collective-permute-start | bytes 1081352 | tf_op jit(solution)/shard_map/ppermute | solution.py:61
  84.3 11.6 %collective-permute-start.15 = (bf16[2,352,256]{2,1,0:T(8,128)(2,1)}, bf16[2,352,256]{2,1,0:T(8,128)(2,1)}, u32[]{:S(2)}, u32[]{:S(2)}) collective-permute-start(bf16[2,352,256]{2,1,0:T(8,128)(2,1)} %extract.1.refs_7_), channel_id=1, source_target_pairs={{0,4},{1,5},{4,8},{5,9},{8,12},{9,13},{12,14},{13,15},{14,10},{15,... | collective-permute-start | bytes 1081352 | tf_op jit(solution)/shard_map/ppermute | solution.py:57
  87.5 13.0 %collective-permute-start.31 = (bf16[432,256]{1,0:T(8,128)(2,1)S(1)}, bf16[432,256]{1,0:T(8,128)(2,1)S(1)}, u32[]{:S(2)}, u32[]{:S(2)}) collective-permute-start(bf16[432,256]{1,0:T(8,128)(2,1)S(1)} %get-tuple-element.19), channel_id=1, source_target_pairs={{0,4},{1,5},{4,8},{5,9},{8,12},{9,13},{12,14},{13,15},{14,10},{15,... | collective-permute-start | bytes 663560 | tf_op jit(solution)/shard_map/ppermute | solution.py:57
  87.6 14.1 %collective-permute-start.19 = (bf16[2,352,256]{2,1,0:T(8,128)(2,1)}, bf16[2,352,256]{2,1,0:T(8,128)(2,1)}, u32[]{:S(2)}, u32[]{:S(2)}) collective-permute-start(bf16[2,352,256]{2,1,0:T(8,128)(2,1)} %extract.1.refs_7_), channel_id=1, source_target_pairs={{0,2},{1,3},{4,0},{5,1},{8,4},{9,5},{12,8},{13,9},{14,12},{15,13},... | collective-permute-start | bytes 1081352 | tf_op jit(solution)/shard_map/ppermute | solution.py:57
  95.8 12.4 %collective-permute-start.16 = (bf16[2,352,256]{2,1,0:T(8,128)(2,1)}, bf16[2,352,256]{2,1,0:T(8,128)(2,1)S(1)}, u32[]{:S(2)}, u32[]{:S(2)}) collective-permute-start(bf16[2,352,256]{2,1,0:T(8,128)(2,1)} %collective-permute-done.15.refs_8_), channel_id=1, source_target_pairs={{0,4},{1,5},{4,8},{5,9},{8,12},{9,13},{12,14},{13,15},{14,10},{15,... | collective-permute-start | bytes 1081352 | tf_op jit(solution)/shard_map/ppermute | solution.py:57
  101.6 11.4 %collective-permute-start.32 = (bf16[432,256]{1,0:T(8,128)(2,1)S(1)}, bf16[432,256]{1,0:T(8,128)(2,1)S(1)}, u32[]{:S(2)}, u32[]{:S(2)}) collective-permute-start(bf16[432,256]{1,0:T(8,128)(2,1)S(1)} %fusion.2), channel_id=1, source_target_pairs={{0,4},{1,5},{4,8},{5,9},{8,12},{9,13},{12,14},{13,15},{14,10},{15,... | collective-permute-start | bytes 663560 | tf_op jit(solution)/shard_map/ppermute | solution.py:57
  101.7 12.5 %collective-permute-start.20 = (bf16[2,352,256]{2,1,0:T(8,128)(2,1)}, bf16[2,352,256]{2,1,0:T(8,128)(2,1)}, u32[]{:S(2)}, u32[]{:S(2)}) collective-permute-start(bf16[2,352,256]{2,1,0:T(8,128)(2,1)} %collective-permute-done.19.refs_14_), channel_id=1, source_target_pairs={{0,2},{1,3},{4,0},{5,1},{8,4},{9,5},{12,8},{13,9},{14,12},{15,13},... | collective-permute-start | bytes 1081352 | tf_op jit(solution)/shard_map/ppermute | solution.py:57
  108.2 12.6 %collective-permute-start.17 = (bf16[2,352,256]{2,1,0:T(8,128)(2,1)S(1)}, bf16[2,352,256]{2,1,0:T(8,128)(2,1)}, u32[]{:S(2)}, u32[]{:S(2)}) collective-permute-start(bf16[2,352,256]{2,1,0:T(8,128)(2,1)S(1)} %collective-permute-done.16.refs_9_), channel_id=1, source_target_pairs={{0,4},{1,5},{4,8},{5,9},{8,12},{9,13},{12,14},{13,15},{14,10},{15,... | collective-permute-start | bytes 1081352 | tf_op jit(solution)/shard_map/ppermute | solution.py:57
  108.2 12.5 %collective-permute-start.35 = (bf16[432,256]{1,0:T(8,128)(2,1)S(1)}, bf16[432,256]{1,0:T(8,128)(2,1)S(1)}, u32[]{:S(2)}, u32[]{:S(2)}) collective-permute-start(bf16[432,256]{1,0:T(8,128)(2,1)S(1)} %get-tuple-element.20), channel_id=1, source_target_pairs={{0,2},{1,3},{4,0},{5,1},{8,4},{9,5},{12,8},{13,9},{14,12},{15,13},... | collective-permute-start | bytes 663560 | tf_op jit(solution)/shard_map/ppermute | solution.py:57
  114.1 13.0 %collective-permute-start.22 = (bf16[2,352,256]{2,1,0:T(8,128)(2,1)S(1)}, bf16[2,352,256]{2,1,0:T(8,128)(2,1)S(1)}, u32[]{:S(2)}, u32[]{:S(2)}) collective-permute-start(bf16[2,352,256]{2,1,0:T(8,128)(2,1)S(1)} %copy-done.1), channel_id=1, source_target_pairs={{0,1},{1,0},{2,3},{3,2},{4,5},{5,4},{6,7},{7,6},{8,9},{9,8},{10,11... | collective-permute-start | bytes 1081352 | tf_op jit(solution)/shard_map/ppermute | solution.py:61
  114.2 22.6 %collective-permute-start.23 = (bf16[2,352,256]{2,1,0:T(8,128)(2,1)}, bf16[2,352,256]{2,1,0:T(8,128)(2,1)}, u32[]{:S(2)}, u32[]{:S(2)}) collective-permute-start(bf16[2,352,256]{2,1,0:T(8,128)(2,1)} %collective-permute-done.15.refs_8_), channel_id=1, source_target_pairs={{0,1},{1,0},{2,3},{3,2},{4,5},{5,4},{6,7},{7,6},{8,9},{9,8},{10,11... | collective-permute-start | bytes 1081352 | tf_op jit(solution)/shard_map/ppermute | solution.py:61
  120.8 16.0 %collective-permute-start.29 = (bf16[2,352,256]{2,1,0:T(8,128)(2,1)}, bf16[2,352,256]{2,1,0:T(8,128)(2,1)}, u32[]{:S(2)}, u32[]{:S(2)}) collective-permute-start(bf16[2,352,256]{2,1,0:T(8,128)(2,1)} %collective-permute-done.19.refs_14_), channel_id=1, source_target_pairs={{0,1},{1,0},{2,3},{3,2},{4,5},{5,4},{6,7},{7,6},{8,9},{9,8},{10,11... | collective-permute-start | bytes 1081352 | tf_op jit(solution)/shard_map/ppermute | solution.py:61
  120.8 16.5 %collective-permute-start.21 = (bf16[2,352,256]{2,1,0:T(8,128)(2,1)}, bf16[2,352,256]{2,1,0:T(8,128)(2,1)}, u32[]{:S(2)}, u32[]{:S(2)}) collective-permute-start(bf16[2,352,256]{2,1,0:T(8,128)(2,1)} %collective-permute-done.20.refs_13_), channel_id=1, source_target_pairs={{0,2},{1,3},{4,0},{5,1},{8,4},{9,5},{12,8},{13,9},{14,12},{15,13},... | collective-permute-start | bytes 1081352 | tf_op jit(solution)/shard_map/ppermute | solution.py:57
  124.7 12.7 %collective-permute-start.18 = (bf16[2,352,256]{2,1,0:T(8,128)(2,1)}, bf16[2,352,256]{2,1,0:T(8,128)(2,1)}, u32[]{:S(2)}, u32[]{:S(2)}) collective-permute-start(bf16[2,352,256]{2,1,0:T(8,128)(2,1)} %collective-permute-done.17.refs_10_), channel_id=1, source_target_pairs={{0,4},{1,5},{4,8},{5,9},{8,12},{9,13},{12,14},{13,15},{14,10},{15,... | collective-permute-start | bytes 1081352 | tf_op jit(solution)/shard_map/ppermute | solution.py:57
  137.3 12.4 %collective-permute-start.25 = (bf16[2,352,256]{2,1,0:T(8,128)(2,1)}, bf16[2,352,256]{2,1,0:T(8,128)(2,1)S(1)}, u32[]{:S(2)}, u32[]{:S(2)}) collective-permute-start(bf16[2,352,256]{2,1,0:T(8,128)(2,1)} %collective-permute-done.17.refs_10_), channel_id=1, source_target_pairs={{0,1},{1,0},{2,3},{3,2},{4,5},{5,4},{6,7},{7,6},{8,9},{9,8},{10,11... | collective-permute-start | bytes 1081352 | tf_op jit(solution)/shard_map/ppermute | solution.py:61
  137.4 12.3 %collective-permute-start.27 = (bf16[2,352,256]{2,1,0:T(8,128)(2,1)}, bf16[2,352,256]{2,1,0:T(8,128)(2,1)S(1)}, u32[]{:S(2)}, u32[]{:S(2)}) collective-permute-start(bf16[2,352,256]{2,1,0:T(8,128)(2,1)} %collective-permute-done.21.refs_12_), channel_id=1, source_target_pairs={{0,1},{1,0},{2,3},{3,2},{4,5},{5,4},{6,7},{7,6},{8,9},{9,8},{10,11... | collective-permute-start | bytes 1081352 | tf_op jit(solution)/shard_map/ppermute | solution.py:61
  137.8 11.9 %collective-permute-start.26 = (bf16[2,352,256]{2,1,0:T(8,128)(2,1)}, bf16[2,352,256]{2,1,0:T(8,128)(2,1)S(1)}, u32[]{:S(2)}, u32[]{:S(2)}) collective-permute-start(bf16[2,352,256]{2,1,0:T(8,128)(2,1)} %collective-permute-done.18.refs_11_), channel_id=1, source_target_pairs={{0,1},{1,0},{2,3},{3,2},{4,5},{5,4},{6,7},{7,6},{8,9},{9,8},{10,11... | collective-permute-start | bytes 1081352 | tf_op jit(solution)/shard_map/ppermute | solution.py:61
  147.6 18.2 %collective-permute-start.34 = (bf16[432,256]{1,0:T(8,128)(2,1)S(1)}, bf16[432,256]{1,0:T(8,128)(2,1)S(1)}, u32[]{:S(2)}, u32[]{:S(2)}) collective-permute-start(bf16[432,256]{1,0:T(8,128)(2,1)S(1)} %copy-done.2), channel_id=1, source_target_pairs={{0,4},{1,5},{4,8},{5,9},{8,12},{9,13},{12,14},{13,15},{14,10},{15,... | collective-permute-start | bytes 663560 | tf_op jit(solution)/shard_map/ppermute | solution.py:57
  148.0 17.8 %collective-permute-start.37 = (bf16[432,256]{1,0:T(8,128)(2,1)S(1)}, bf16[432,256]{1,0:T(8,128)(2,1)S(1)}, u32[]{:S(2)}, u32[]{:S(2)}) collective-permute-start(bf16[432,256]{1,0:T(8,128)(2,1)S(1)} %fusion.1), channel_id=1, source_target_pairs={{0,2},{1,3},{4,0},{5,1},{8,4},{9,5},{12,8},{13,9},{14,12},{15,13},... | collective-permute-start | bytes 663560 | tf_op jit(solution)/shard_map/ppermute | solution.py:57
  (34 other events, 605.0 us)

commit v2 on v1

v2 whole, which is shorter than its diff:
```python
import functools
import math

import jax
import jax.numpy as jnp
import numpy as np
from jax import lax
from jax.experimental import pallas as pl
from jax.experimental.pallas import tpu as pltpu
from jax.sharding import PartitionSpec as P

F32 = jnp.float32
BF16 = jnp.bfloat16
C = 256
C_LINES = 128
B_LINES = 224
ROWS = 320
NOTES = 16
HB = 24
VMEM_LIMIT = 40 * 1024 * 1024
DIRECTIONS = [
    (i, j, l)
    for i in (-1, 0, 1)
    for j in (-1, 0, 1)
    for l in (-1, 0, 1)
    if (i, j, l) != (0, 0, 0)
]

VMEM = pl.BlockSpec(memory_space=pltpu.VMEM)
SMEM = pl.BlockSpec(memory_space=pltpu.SMEM)
ANY = pl.BlockSpec(memory_space=pl.ANY)


def ring_order(chips):
    if chips == 8:
        return [0, 2, 4, 6, 7, 5, 3, 1]
    return list(range(chips))


def ring_tables(peers):
    chips = peers // 2
    spot = np.argsort(np.array(ring_order(chips)))
    device = np.arange(peers)
    behind = (spot[device // 2][:, None] - spot[None, :]) % chips
    place_of = behind[:, device // 2] + chips * (device[:, None] % 2 != device[None, :] % 2)
    if chips > 8:
        place_of = np.broadcast_to(device, (peers, peers))
    return np.concatenate([place_of, behind, device[:, None]], axis=1).astype(np.int32)


def ring_step(x, peers, step):
    order = ring_order(peers // 2)
    pairs = [
        (2 * order[i] + core, 2 * order[(i + step) % len(order)] + core)
        for i in range(len(order))
        for core in range(2)
    ]
    return lax.ppermute(x, "morton", pairs)


def swap_cores(x, peers):
    return lax.ppermute(x, "morton", [(m, m ^ 1) for m in range(peers)])


def gather_ring(x, peers, step, after):
    chips = peers // 2
    if chips > 8:
        got = lax.all_gather(x[None], "morton", axis=0, tiled=True)
        return [got], ([got] * 4, [got] * 4)
    got = {0: x}
    hops = []
    for way, count, gate in ((step, chips // 2, after[0]), (-step, (chips - 1) // 2, after[1])):
        held = x if gate is None else lax.optimization_barrier((x, gate))[0]
        hops.append([])
        for hop in range(1, count + 1):
            held = ring_step(held, peers, way)
            hops[-1].append(held)
            got[(way * hop) % chips] = held
    mine = [got[k] for k in range(chips)]
    return [t[None] for t in mine + [swap_cores(t, peers) for t in mine]], hops


def scatter_ring(keep, give, peers):
    chips = peers // 2
    other = swap_cores(give, peers)

    def term(k):
        return keep[k] + other[k].astype(F32)

    ups, downs = chips // 2, (chips - 1) // 2
    total = term(0)
    for count, step in ((ups, 1), (downs, -1)):
        held = None
        for hop in range(count, 0, -1):
            part = term((-step * hop) % chips)
            if held is not None:
                part = part + held.astype(F32)
            held = ring_step(part.astype(BF16), peers, step)
        if held is not None:
            total = total + held.astype(F32)
    return total


def call(body, out_shape, in_specs, scratch=(), flops=0, nbytes=0, name=None, out_specs=None):
    return pl.pallas_call(
        body,
        out_shape=out_shape,
        in_specs=in_specs,
        out_specs=out_specs or jax.tree.map(lambda _: VMEM, out_shape),
        scratch_shapes=list(scratch),
        compiler_params=pltpu.CompilerParams(vmem_limit_bytes=VMEM_LIMIT),
        cost_estimate=pl.CostEstimate(flops=flops, bytes_accessed=nbytes, transcendentals=0),
        name=name,
    )


def put_boundary(rows, brick, a, out_ref, stage):
    wide = rows.astype(F32)
    base = brick * ROWS

    def put(at, value, lanes=slice(None)):
        out_ref[pl.ds(pl.multiple_of(base + at, 16), value.shape[0]), lanes] = value

    for edge, at in ((0, 0), (7, 64)):

        @pl.when(a == edge)
        def _():
            put(at, rows)

    @pl.when((a > 0) & (a < 7))
    def _():
        for half in range(2):
            lanes = slice(half * 128, half * 128 + 128)
            stage[half] = wide[:, lanes]
            first = stage[half, pl.ds(0, 8, stride=8), :]
            last = stage[half, pl.ds(7, 8, stride=8), :]
            put(C_LINES - 16 + 16 * a, jnp.concatenate([first, last], axis=0).astype(BF16), lanes)
        pair = jnp.concatenate([wide[:8], wide[56:]], axis=0).astype(BF16)
        put(B_LINES - 16 + 16 * a, pair)


def norm_body(recv, send, x_ref, gain_ref, hidden_ref, out_ref, stage):
    bricks, directions = recv.shape
    gain = gain_ref[...]
    row = lax.broadcasted_iota(jnp.int32, (NOTES, C), 0)
    lane = lax.broadcasted_iota(jnp.int32, (NOTES, C), 1)
    notes = jnp.zeros((NOTES, C), jnp.int32)
    for k in range(send.shape[1]):
        notes = jnp.where((row == 0) & (lane == k), send[0, k], notes)
    for brick in range(bricks):
        for number in range(directions):
            serves = (row == 1) & (lane == recv[brick, number])
            notes = jnp.where(serves, brick * directions + number + 1, notes)
    out_ref[bricks * ROWS :, :] = notes.astype(F32).astype(BF16)

    def step(k, _):
        at = pl.ds(pl.multiple_of(k * 64, 64), 64)
        x = x_ref[at, :].astype(F32)
        inverse = lax.rsqrt(jnp.mean(x * x, axis=-1, keepdims=True) + 1e-6)
        v = x * inverse * gain
        rows = (v / (1.0 + jnp.exp(-v))).astype(BF16)
        hidden_ref[at, :] = rows
        put_boundary(rows, k // 8, k % 8, out_ref, stage)
        return 0

    lax.fori_loop(0, bricks * 8, step, 0)


def extract_body(x_ref, out_ref, stage):
    def step(k, _):
        at = pl.ds(pl.multiple_of(k * 64, 64), 64)
        put_boundary(x_ref[at, :], k // 8, k % 8, out_ref, stage)
        return 0

    lax.fori_loop(0, x_ref.shape[0] // 64, step, 0)


def start_padded(own_ref, cells, halo, bricks):
    zero = jnp.zeros((8, C), F32)

    def clear(k, _):
        for b in range(10):
            cells[k * 10 + b] = zero
        for side in range(2):
            for part in range(HB // 8):
                halo[side, k, part * 8 : part * 8 + 8, :] = zero
        return 0

    lax.fori_loop(0, bricks * 10, clear, 0)

    def fill(k, _):
        plane = (k // 8) * 10 + k % 8 + 1
        rows = own_ref[pl.ds(pl.multiple_of(k * 64, 64), 64), :].astype(F32)
        for b in range(8):
            cells[plane * 10 + b + 1] = rows[b * 8 : b * 8 + 8]
        return 0

    lax.fori_loop(0, bricks * 8, fill, 0)


def add_line(ref, index, line):
    ref[index] = ref[index] + line


def pick(flag, yes, no):
    if isinstance(flag, bool):
        return yes if flag else no
    return jnp.where(flag, yes, no)


def place(kind, e, keep, place_at, source_brick, brick, share, cells, halo):
    flags = [t == -1 for t in e]
    pads = [pick(f, 0, 9) for f in flags]
    facing = pick(flags[0], 64, 0)
    start = source_brick * ROWS

    def rows(at, size):
        got = share[place_at, pl.ds(pl.multiple_of(start + at, 16), size), :].astype(F32)
        return got if keep is None else jnp.where(keep, got, 0.0)

    def half(pair, axis):
        return pick(flags[axis], pair[8:], pair[:8])

    def line_b(at):
        plane = rows(at, 64)
        return pick(flags[1], plane[56:], plane[:8])

    def line_c(at):
        plane = rows(at, 64)
        ends = [
            pick(flags[2], plane[8 * b + 7 : 8 * b + 8], plane[8 * b : 8 * b + 1]) for b in range(8)
        ]
        return jnp.concatenate(ends, axis=0)

    def cell(at):
        line = line_b(at)
        return pick(flags[2], line[7:8], line[0:1])

    side = pick(flags[2], 0, 1)
    base = brick * 10

    def add_halo(at, line):
        halo[side, base + at, 8:16, :] = halo[side, base + at, 8:16, :] + line

    def add_cell(at, value):
        spot = pl.ds(pick(flags[1], 7, 16), 1)
        halo[side, base + at, spot, :] = halo[side, base + at, spot, :] + value

    if kind == (1, 0, 0):
        got = rows(facing, 64)
        first = (base + pads[0]) * 10 + 1
        for b in range(8):
            add_line(cells, first + b, got[b * 8 : b * 8 + 8])
    elif kind == (0, 1, 0):
        for a in range(8):
            if a in (0, 7):
                line = line_b(0 if a == 0 else 64)
            else:
                line = half(rows(B_LINES - 16 + 16 * a, 16), 1)
            add_line(cells, (base + a + 1) * 10 + pads[1], line)
    elif kind == (0, 0, 1):
        for a in range(8):
            if a in (0, 7):
                line = line_c(0 if a == 0 else 64)
            else:
                line = half(rows(C_LINES - 16 + 16 * a, 16), 2)
            add_halo(a + 1, line)
    elif kind == (1, 1, 0):
        add_line(cells, (base + pads[0]) * 10 + pads[1], line_b(facing))
    elif kind == (1, 0, 1):
        add_halo(pads[0], line_c(facing))
    elif kind == (0, 1, 1):
        for a in range(8):
            if a in (0, 7):
                value = cell(0 if a == 0 else 64)
            else:
                line = half(rows(C_LINES - 16 + 16 * a, 16), 2)
                value = pick(flags[1], line[7:8], line[0:1])
            add_cell(a + 1, value)
    else:
        add_cell(pads[0], cell(facing))


def windows(cells, halo, cols, bricks):
    row = lax.broadcasted_iota(jnp.int32, (8, C), 0)

    def step(k, _):
        shifted = [[], [], []]
        for b in range(10):
            x = cells[k * 10 + b]
            before = halo[0, k, pl.ds(b + 7, 1), :]
            after = halo[1, k, pl.ds(b + 7, 1), :]
            shifted[0].append(jnp.where(row == 0, before, pltpu.roll(x, 1, 0)))
            shifted[1].append(x)
            shifted[2].append(jnp.where(row == 7, after, pltpu.roll(x, 7, 0)))
        for j in range(3):
            for l in range(3):
                block = jnp.concatenate(shifted[l][j : j + 8], axis=0).astype(BF16)
                at = (3 * j + l) * C
                cols[k, :, at : at + C] = block
        return 0

    lax.fori_loop(0, bricks * 10, step, 0)


def fetch(parts, share, sems):
    size = parts[0].shape[0]
    copies = [
        pltpu.make_async_copy(part, share.at[pl.ds(k * size, size)], sems.at[k])
        for k, part in enumerate(parts)
    ]
    for copy in copies:
        copy.start()
    return copies


def pad_body(slots, peers, count, *refs):
    recv, table, own_ref = refs[:3]
    parts = refs[3 : 3 + count]
    cols, codes_ref, served_ref = refs[-9:-6]
    cells, halo, share, codes, sems, codes_sem = refs[-6:]
    bricks = own_ref.shape[0] // 512
    me = table[peers + peers // 2]
    copies = fetch(parts, share, sems)
    start_padded(own_ref, cells, halo, bricks)
    for copy in copies:
        copy.wait()
    for k in range(peers):
        notes = share[k, bricks * ROWS :, :].astype(F32).astype(jnp.int32)
        codes_ref[k : k + 1, :] = notes[0:1]
        served_ref[k : k + 1, :] = notes[1:2]
    codes_copy = pltpu.make_async_copy(codes_ref, codes, codes_sem.at[0])
    codes_copy.start()
    codes_copy.wait()
    for brick in range(bricks):
        for number, e in enumerate(DIRECTIONS):
            slot = recv[brick, number]
            safe = jnp.maximum(slot, 0)
            sender = safe // slots
            at = table[sender]
            code = codes[at, me * slots + safe - sender * slots]
            kind = tuple(abs(t) for t in e)
            place(kind, e, slot >= 0, at, code // 6, brick, share, cells, halo)
    windows(cells, halo, cols, bricks)


def weight_grad_body(factor, peers, *refs):
    table, cols, cot_ref = refs[:3]
    keep_ref, give_ref, sums, turned, sem = refs[-5:]
    bricks = cot_ref.shape[0] // 512
    rows = 27 * C // peers
    mine = table[peers + peers // 2] % 2
    for part in range(bricks * 2):
        at = slice(part * 256, part * 256 + 256)
        turned[:, at] = cot_ref[at, :].astype(F32).T.astype(BF16)
    for tap in range(27):
        i, jl = divmod(tap, 9)
        total = None
        for brick in range(bricks):
            right = cols[brick * 10 + i : brick * 10 + i + 8, :, jl * C : jl * C + C].reshape(512, C)
            left = turned[:, brick * 512 : brick * 512 + 512]
            term = jnp.dot(left, right, preferred_element_type=F32)
            total = term if total is None else total + term
        total = (total * factor).T
        start = tap * C
        while start < (tap + 1) * C:
            owner = start // rows
            stop = min((tap + 1) * C, (owner + 1) * rows)
            piece = total[start - tap * C : stop - tap * C]
            bucket = jnp.bitwise_xor(mine, owner % 2)
            where = slice(start - owner * rows, stop - owner * rows)
            sums[bucket, table[peers + owner // 2], where, :] = piece
            start = stop
    keep_copy = pltpu.make_async_copy(sums.at[0], keep_ref, sem.at[0])
    keep_copy.start()

    def narrow(k, _):
        give_ref[k] = sums[1, k].astype(BF16)
        return 0

    lax.fori_loop(0, sums.shape[1], narrow, 0)
    keep_copy.wait()


def tap_sum(cols, weight_ref, brick):
    total = None
    for i in range(3):
        left = cols[brick * 10 + i : brick * 10 + i + 8].reshape(512, 9 * C)
        right = weight_ref[i * 9 * C : (i + 1) * 9 * C, :]
        term = jnp.dot(left, right, preferred_element_type=F32)
        total = term if total is None else total + term
    return total


def mix_body(cols, weight_ref, x_ref, out_ref):
    for brick in range(x_ref.shape[0] // 512):
        at = slice(brick * 512, brick * 512 + 512)
        out_ref[at, :] = (x_ref[at, :].astype(F32) + tap_sum(cols, weight_ref, brick)).astype(BF16)


def input_grad_body(slots, peers, here, count, *refs):
    served, send, table, cot_ref, weight_ref, x_ref, gain_ref = refs[:7]
    parts = refs[7 : 7 + count]
    out_ref, cells, halo, cols, share, sems = refs[7 + count :]
    me = table[peers + peers // 2]
    copies = fetch(parts, share, sems)
    start_padded(cot_ref, cells, halo, 1)
    for copy in copies:
        copy.wait()

    def one(k, _):
        receiver = k // slots
        at = table[receiver]
        info = served[at, me * slots + k - receiver * slots]

        @pl.when((info > 0) & (send[0, k] // 6 == here))
        def _():
            entry = info - 1
            number = 25 - entry % 26
            tap = jnp.where(number >= 13, number + 1, number)
            e = (tap // 9 - 1, (tap // 3) % 3 - 1, tap % 3 - 1)
            on = [t != 0 for t in e]
            for kind in ((1, 0, 0), (0, 1, 0), (0, 0, 1), (1, 1, 0), (1, 0, 1), (0, 1, 1), (1, 1, 1)):
                match = functools.reduce(
                    jnp.logical_and, [f if w else jnp.logical_not(f) for f, w in zip(on, kind)]
                )

                @pl.when(match)
                def _():
                    place(kind, e, None, at, entry // 26, 0, share, cells, halo)

        return 0

    lax.fori_loop(0, send.shape[1], one, 0)
    windows(cells, halo, cols, 1)
    grad = tap_sum(cols, weight_ref, 0)
    x = x_ref[...].astype(F32)
    gain = gain_ref[...]
    inverse = lax.rsqrt(jnp.mean(x * x, axis=-1, keepdims=True) + 1e-6)
    unit = x * inverse
    v = unit * gain
    gate = 1.0 / (1.0 + jnp.exp(-v))
    grad = grad * (gate * (1.0 + v * (1.0 - gate))) * gain
    grad = inverse * (grad - unit * jnp.mean(grad * unit, axis=-1, keepdims=True))
    out_ref[...] = (cot_ref[...].astype(F32) + grad).astype(BF16)


def local(features, norm_gain, conv_weight, recv_slot, send_face, cotangent):
    channels = features.shape[1]
    per_device = features.shape[0]
    bricks = per_device // 512
    peers = lax.axis_size("morton")
    slots = send_face.shape[1] // peers
    factor = 1.0 / math.sqrt(peers * per_device)
    gain = norm_gain.reshape(1, channels)
    sds = jax.ShapeDtypeStruct
    stage = pltpu.VMEM((2, 64, 128), F32)

    def padded(n):
        return [
            pltpu.VMEM((n * 100, 8, channels), F32),
            pltpu.VMEM((2, n * 10, HB, channels), F32),
        ]

    def cols_shape(n):
        return (n * 10, 64, 9 * channels)

    conv_flops = 2 * per_device * 27 * channels * channels

    table = jnp.asarray(ring_tables(peers))[lax.axis_index("morton")]

    hidden, share = call(
        norm_body,
        (sds((per_device, channels), BF16), sds((bricks * ROWS + NOTES, channels), BF16)),
        [SMEM, SMEM, VMEM, VMEM],
        [stage],
        name="norm",
    )(recv_slot, send_face, features, gain)
    hidden_parts, hidden_hops = gather_ring(share, peers, 1, (None, None))

    cot_share = call(
        extract_body,
        sds((bricks * ROWS, channels), BF16),
        [VMEM],
        [stage],
        name="extract",
    )(cotangent)
    gates = (hidden_hops[1][-1], hidden_hops[0][-1])
    cot_parts, (far, near) = gather_ring(cot_share, peers, -1, gates)
    turned = conv_weight.reshape(27, channels, channels)[::-1].transpose(0, 2, 1)
    turned = turned.reshape(27 * channels, channels)
    hidden, turned = lax.optimization_barrier((hidden, turned))

    count = len(hidden_parts)
    rows = 27 * channels // peers
    cols, _, served = call(
        functools.partial(pad_body, slots, peers, count),
        (
            sds(cols_shape(bricks), BF16),
            sds((peers, channels), jnp.int32),
            sds((peers, channels), jnp.int32),
        ),
        [SMEM] * 2 + [VMEM] + [ANY] * (count + 1),
        padded(bricks)
        + [
            pltpu.VMEM((peers, bricks * ROWS + NOTES, channels), BF16),
            pltpu.SMEM((peers, channels), jnp.int32),
            pltpu.SemaphoreType.DMA((count,)),
            pltpu.SemaphoreType.DMA((1,)),
        ],
        flops=conv_flops,
        nbytes=2**24,
        name="pad",
    )(recv_slot, table, hidden, *hidden_parts, far[0])
    keep, give = call(
        functools.partial(weight_grad_body, factor, peers),
        (
            sds((peers // 2, rows, channels), F32),
            sds((peers // 2, rows, channels), BF16),
        ),
        [SMEM] + [VMEM] * 2,
        [
            pltpu.VMEM((2, peers // 2, rows, channels), F32),
            pltpu.VMEM((channels, per_device), BF16),
            pltpu.SemaphoreType.DMA((1,)),
        ],
        flops=conv_flops,
        nbytes=2**24,
        name="weight_grad",
        out_specs=(ANY, VMEM),
    )(table, cols, cotangent)
    give = lax.optimization_barrier((give, far[2], near[1]))[0]
    grad_weight = scatter_ring(keep, give, peers)

    mixed = call(
        mix_body,
        sds((per_device, channels), BF16),
        [VMEM, VMEM, VMEM],
        flops=conv_flops,
        nbytes=2**23,
        name="mix",
    )(cols, conv_weight, features)

    grads = []
    for brick in range(bricks):
        at = slice(brick * 512, brick * 512 + 512)
        grads.append(
            call(
                functools.partial(input_grad_body, slots, peers, brick, count),
                sds((512, channels), BF16),
                [SMEM] * 3 + [VMEM] * 4 + [ANY] * count,
                padded(1)
                + [
                    pltpu.VMEM(cols_shape(1), BF16),
                    pltpu.VMEM((peers, bricks * ROWS, channels), BF16),
                    pltpu.SemaphoreType.DMA((count,)),
                ],
                flops=conv_flops // bricks,
                nbytes=2**24,
                name="input_grad_" + str(brick),
            )(served, send_face, table, cotangent[at], turned, features[at], gain, *cot_parts)
        )
    return (mixed, jnp.concatenate(grads, axis=0), grad_weight)


def solution(mesh):
    rows = P(("groups", "morton"), None)
    return jax.shard_map(
        local,
        mesh=mesh,
        in_specs=(rows, P(), P(), rows, rows, rows),
        out_specs=(rows, rows, rows),
        check_vma=False,
    )
```

time: 168 us -> 156 us (0.929)
  local copies, waits for them, and re-layouts: 13 us -> 38.3 us
  blocking collectives: 21.2 us -> 0 us
  waiting for transfers between devices: 56.7 us -> 48 us
  Pallas kernels: 43.7 us -> 36.8 us
  other arithmetic: 10.1 us -> 4.13 us
  starting transfers between devices: 22.1 us -> 26.7 us
    unnamed x40 -> x74, local copies, waits for them, and re-layouts: 1.77 us -> 29.5 us
    all_gather x1 -> x0, blocking collectives: 21.2 us -> none  [local(): notes = lax.all_gather(notes, 'morton', axis=0, tiled=False)]
    ppermute x21, waiting for transfers between devices: 55.3 us -> 44.2 us  [ring_step(): return lax.ppermute(x, 'morton', pairs)]
    convert_element_type x5, other arithmetic: 7.35 us -> 1.48 us  [scatter_ring(): held = ring_step(part.astype(BF16), peers, step)]
    ppermute x21, starting transfers between devices: 18.9 us -> 24.1 us  [ring_step(): return lax.ppermute(x, 'morton', pairs)]
    pallas_call x1, Pallas kernels: 8.43 us -> 4.61 us  [local(): call(mix_body, sds((per_device, channels), BF16), [VMEM, VMEM, VMEM], flo...]
    pallas_call x4 -> x6, Pallas kernels: 35.3 us -> 32.2 us  [the longest x2 17.1 us: local(): call(functools.partial(input_grad_body, slots, peers, brick, count), sds(...]
    ppermute x17, waiting for transfers between devices: 1.39 us -> 3.72 us  [swap_cores(): return lax.ppermute(x, 'morton', [(m, m ^ 1) for m in range(peers)])]
  transfers between devices with their start and end apart: 38 -> 38, of which waited for: 12 -> 11; matrix products, arithmetic and copies ran while one was open for 12% -> 7% of each run, Pallas kernels for 15% -> 22%
where the time goes in v2:
time: 156 us; the launch traced here: 155 us
  waiting for transfers between devices  48 us (31%)
  local copies, waits for them, and re-layouts  38.3 us (25%)
  Pallas kernels  36.8 us (24%)
  starting transfers between devices  26.7 us (17%)
  other arithmetic  4.13 us (3%)
    ppermute x21, waiting for transfers between devices, ring_step(): return lax.ppermute(x, 'morton', pairs)  44.2 us
    unnamed x74, local copies, waits for them, and re-layouts  29.5 us
    ppermute x21, starting transfers between devices, ring_step(): return lax.ppermute(x, 'morton', pairs)  24.1 us
    pallas_call x2, Pallas kernels, local(): call(functools.partial(input_grad_body, slots, peers, brick, count), sds(...  17.1 us
    pallas_call x1, Pallas kernels, local(): call(functools.partial(pad_body, slots, peers, count), (sds(cols_shape(br...  5.77 us
    reshape x1, local copies, waits for them, and re-layouts, local(): conv_weight.reshape(27, channels, channels)[::-1].transpose(0, 2, 1)  5.75 us
    pallas_call x1, Pallas kernels, local(): call(functools.partial(weight_grad_body, factor, peers), (sds((peers // 2...  5.24 us
    pallas_call x1, Pallas kernels, local(): call(mix_body, sds((per_device, channels), BF16), [VMEM, VMEM, VMEM], flo...  4.61 us
  transfers between devices with their start and end apart: 38, of which 11 were waited for; matrix products, arithmetic and copies ran while one was open for 7% of the time, Pallas kernels for 22%

profile of v2, /device:TPU:0, one launch (start us, length us, event | category | flops | bytes accessed | tf_op | source)
XLA Modules:
  0.0 154.8 jit_solution(18238458090469216292)
XLA Ops:
  3.7 2.9 %norm.1 = (bf16[1024,256]{1,0:T(8,128)(2,1)S(1)}, bf16[656,256]{1,0:T(8,128)(2,1)S(1)}) custom-call(s32[2,26]{1,0:T(2,128)S(1)} %copy-done.9, s32[1,64]{1,0:T(1,128)S(1)} %copy-done.7, bf16[1024,256]{1,0:T(8,128)(2,1)S(1)} %copy-done.3, f32[1,256]{1,0:T(1,128)S(1)} %bitcast.94), custom_call_target="tpu_custom_call" | custom-call | tf_op jit(solution)/shard_map/norm/pallas_call | solution.py:472
  7.4 3.0 %collective-permute-start = (bf16[656,256]{1,0:T(8,128)(2,1)S(1)}, bf16[656,256]{1,0:T(8,128)(2,1)S(1)}, u32[]{:S(2)}, u32[]{:S(2)}) collective-permute-start(bf16[656,256]{1,0:T(8,128)(2,1)S(1)} %get-tuple-element.16), channel_id=1, source_target_pairs={{0,4},{1,5},{4,8},{5,9},{8,12},{9,13},{12,14},{13,15},{14,10},{15,... | collective-permute-start | bytes 1007624 | tf_op jit(solution)/shard_map/ppermute | solution.py:58
  10.4 7.8 %collective-permute-done = bf16[656,256]{1,0:T(8,128)(2,1)S(1)} collective-permute-done((bf16[656,256]{1,0:T(8,128)(2,1)S(1)}, bf16[656,256]{1,0:T(8,128)(2,1)S(1)}, u32[]{:S(2)}, u32[]{:S(2)}) %collective-permute-start) | collective-permute-done | bytes 335904 | tf_op jit(solution)/shard_map/ppermute | solution.py:58
  18.2 1.8 %collective-permute-start.1 = (bf16[656,256]{1,0:T(8,128)(2,1)S(1)}, bf16[656,256]{1,0:T(8,128)(2,1)S(1)}, u32[]{:S(2)}, u32[]{:S(2)}) collective-permute-start(bf16[656,256]{1,0:T(8,128)(2,1)S(1)} %collective-permute-done), channel_id=1, source_target_pairs={{0,4},{1,5},{4,8},{5,9},{8,12},{9,13},{12,14},{13,15},{14,10},{15,... | collective-permute-start | bytes 1007624 | tf_op jit(solution)/shard_map/ppermute | solution.py:58
  20.3 7.0 %collective-permute-done.1 = bf16[656,256]{1,0:T(8,128)(2,1)S(1)} collective-permute-done((bf16[656,256]{1,0:T(8,128)(2,1)S(1)}, bf16[656,256]{1,0:T(8,128)(2,1)S(1)}, u32[]{:S(2)}, u32[]{:S(2)}) %collective-permute-start.1) | collective-permute-done | bytes 335904 | tf_op jit(solution)/shard_map/ppermute | solution.py:58
  32.0 3.5 %collective-permute-done.2 = bf16[656,256]{1,0:T(8,128)(2,1)} collective-permute-done((bf16[656,256]{1,0:T(8,128)(2,1)S(1)}, bf16[656,256]{1,0:T(8,128)(2,1)}, u32[]{:S(2)}, u32[]{:S(2)}) %collective-permute-start.2) | collective-permute-done | bytes 335904 | tf_op jit(solution)/shard_map/ppermute | solution.py:58
  43.6 7.3 %collective-permute-done.15.refs_19_ = bf16[640,256]{1,0:T(8,128)(2,1)} collective-permute-done((bf16[640,256]{1,0:T(8,128)(2,1)}, bf16[640,256]{1,0:T(8,128)(2,1)}, u32[]{:S(2)}, u32[]{:S(2)}) %collective-permute-start.15) | collective-permute-done | bytes 327712 | tf_op jit(solution)/shard_map/ppermute | solution.py:58
  53.7 5.7 %copy.10 = bf16[27,256,256]{1,2,0:T(8,128)(2,1)} copy(bf16[27,256,256]{2,1,0:T(8,128)(2,1)} %bitcast.69) | data formatting | bytes 7077888 | tf_op jit(solution)/shard_map/reshape | solution.py:490
  59.5 2.2 %rev.3 = bf16[27,256,256]{1,2,0:T(8,128)(2,1)S(1)} reverse(bf16[27,256,256]{1,2,0:T(8,128)(2,1)} %copy.10), dimensions={0} | reverse | bytes 7077888 | tf_op jit(solution)/shard_map/rev | solution.py:490
  75.3 5.8 %pad.5 = (bf16[20,64,2304]{2,1,0:T(8,128)(2,1)S(1)}, s32[16,256]{1,0:T(8,128)}, s32[16,256]{1,0:T(8,128)S(1)}) custom-call(s32[2,26]{1,0:T(2,128)S(1)} %copy-done.10, s32[25]{0:T(128)S(1)} %dynamic-slice_bitcast_fusion.refs_1_.refs_2_.refs_0_, bf16[1024,256]{1,0:T(8,128)(2,1)S(1)} %copy-done.12, bf16[1,656,256]{2,1,0:T(8,128)(2,1)S(1)} %bitcast.97, ...), custom_call_target="tpu_custom_call" | custom-call | flops 3623878656 | bytes 16777216 | tf_op jit(solution)/shard_map/pad/pallas_call | solution.py:496
  81.1 2.6 %copy-done.33 = bf16[20,64,2304]{2,1,0:T(8,128)(2,1)} copy-done((bf16[20,64,2304]{2,1,0:T(8,128)(2,1)}, bf16[20,64,2304]{2,1,0:T(8,128)(2,1)S(1)}, u32[]{:S(2)}) %copy-start.33) | copy-done | bytes 5898264
  83.6 2.7 %copy-done.34 = bf16[20,64,2304]{2,1,0:T(8,128)(2,1)S(1)} copy-done((bf16[20,64,2304]{2,1,0:T(8,128)(2,1)S(1)}, bf16[20,64,2304]{2,1,0:T(8,128)(2,1)}, u32[]{:S(2)}) %copy-start.34) | copy-done | bytes 5898264
  86.3 5.2 %weight_grad.1 = (f32[8,432,256]{2,1,0:T(8,128)S(1)}, bf16[8,432,256]{2,1,0:T(8,128)(2,1)S(1)}) custom-call(s32[25]{0:T(128)S(1)} %dynamic-slice_bitcast_fusion.refs_1_.refs_2_.refs_0_, bf16[20,64,2304]{2,1,0:T(8,128)(2,1)S(1)} %copy-done.34, bf16[1024,256]{1,0:T(8,128)(2,1)S(1)} %copy-done.2), custom_call_target="tpu_custom_call" | custom-call | flops 3623878656 | bytes 16777216 | tf_op jit(solution)/shard_map/weight_grad/pallas_call | solution.py:515
  91.7 3.7 %collective-permute-done.30 = bf16[8,432,256]{2,1,0:T(8,128)(2,1)S(1)} collective-permute-done((bf16[8,432,256]{2,1,0:T(8,128)(2,1)S(1)}, bf16[8,432,256]{2,1,0:T(8,128)(2,1)S(1)}, u32[]{:S(2)}, u32[]{:S(2)}) %collective-permute-start.30) | collective-permute-done | bytes 1769504 | tf_op jit(solution)/shard_map/ppermute | solution.py:62
  97.1 5.9 %collective-permute-done.31 = bf16[432,256]{1,0:T(8,128)(2,1)S(1)} collective-permute-done((bf16[432,256]{1,0:T(8,128)(2,1)S(1)}, bf16[432,256]{1,0:T(8,128)(2,1)S(1)}, u32[]{:S(2)}, u32[]{:S(2)}) %collective-permute-start.31) | collective-permute-done | bytes 221216 | tf_op jit(solution)/shard_map/ppermute | solution.py:58
  105.2 4.6 %collective-permute-done.32 = bf16[432,256]{1,0:T(8,128)(2,1)S(1)} collective-permute-done((bf16[432,256]{1,0:T(8,128)(2,1)S(1)}, bf16[432,256]{1,0:T(8,128)(2,1)S(1)}, u32[]{:S(2)}, u32[]{:S(2)}) %collective-permute-start.32) | collective-permute-done | bytes 221216 | tf_op jit(solution)/shard_map/ppermute | solution.py:58
  113.0 2.9 %collective-permute-done.33 = bf16[432,256]{1,0:T(8,128)(2,1)S(1)} collective-permute-done((bf16[432,256]{1,0:T(8,128)(2,1)S(1)}, bf16[432,256]{1,0:T(8,128)(2,1)S(1)}, u32[]{:S(2)}, u32[]{:S(2)}) %collective-permute-start.33) | collective-permute-done | bytes 221216 | tf_op jit(solution)/shard_map/ppermute | solution.py:58
  118.3 3.9 %collective-permute-done.21 = bf16[640,256]{1,0:T(8,128)(2,1)S(1)} collective-permute-done((bf16[640,256]{1,0:T(8,128)(2,1)S(1)}, bf16[640,256]{1,0:T(8,128)(2,1)S(1)}, u32[]{:S(2)}, u32[]{:S(2)}) %collective-permute-start.21) | collective-permute-done | bytes 327712 | tf_op jit(solution)/shard_map/ppermute | solution.py:58
  124.2 2.7 %copy-done.35 = bf16[20,64,2304]{2,1,0:T(8,128)(2,1)S(1)} copy-done((bf16[20,64,2304]{2,1,0:T(8,128)(2,1)S(1)}, bf16[20,64,2304]{2,1,0:T(8,128)(2,1)}, u32[]{:S(2)}) %copy-start.35) | copy-done | bytes 5898264
  126.8 4.6 %mix.1 = bf16[1024,256]{1,0:T(8,128)(2,1)} custom-call(bf16[20,64,2304]{2,1,0:T(8,128)(2,1)S(1)} %copy-done.35, bf16[6912,256]{1,0:T(8,128)(2,1)S(1)} %copy-done, bf16[1024,256]{1,0:T(8,128)(2,1)S(1)} %copy-done.4), custom_call_target="tpu_custom_call" | custom-call | flops 3623878656 | bytes 8388608 | tf_op jit(solution)/shard_map/mix/pallas_call | solution.py:535
  131.5 8.3 %input_grad_1.1 = bf16[512,256]{1,0:T(8,128)(2,1)S(1)} custom-call(s32[16,256]{1,0:T(8,128)S(1)} %get-tuple-element.19.refs_0_, s32[1,64]{1,0:T(1,128)S(1)} %copy-done.8, s32[25]{0:T(128)S(1)} %dynamic-slice_bitcast_fusion.refs_1_.refs_2_.refs_0_, bf16[512,256]{1,0:T(8,128)(2,1)S(1)} %get-tuple-element.32.refs_3_, bf16[6912,256]{1,0:T(8,128)(2,1)S(1)} %bitcast.67, ...), custom_call_target="tpu_custom_call" | custom-call | flops 1811939328 | bytes 16777216 | tf_op jit(solution)/shard_map/input_grad_1/pallas_call | solution.py:548
  139.8 2.5 %collective-permute-start.34 = (bf16[432,256]{1,0:T(8,128)(2,1)S(1)}, bf16[432,256]{1,0:T(8,128)(2,1)S(1)}, u32[]{:S(2)}, u32[]{:S(2)}) collective-permute-start(bf16[432,256]{1,0:T(8,128)(2,1)S(1)} %get-tuple-element.25), channel_id=1, source_target_pairs={{0,4},{1,5},{4,8},{5,9},{8,12},{9,13},{12,14},{13,15},{14,10},{15,... | collective-permute-start | bytes 663560 | tf_op jit(solution)/shard_map/ppermute | solution.py:58
  143.3 8.8 %input_grad_0.1 = bf16[512,256]{1,0:T(8,128)(2,1)S(1)} custom-call(s32[16,256]{1,0:T(8,128)S(1)} %get-tuple-element.19.refs_0_, s32[1,64]{1,0:T(1,128)S(1)} %copy-done.8, s32[25]{0:T(128)S(1)} %dynamic-slice_bitcast_fusion.refs_1_.refs_2_.refs_0_, bf16[512,256]{1,0:T(8,128)(2,1)S(1)} %get-tuple-element.31.refs_3_, bf16[6912,256]{1,0:T(8,128)(2,1)S(1)} %bitcast.68, ...), custom_call_target="tpu_custom_call" | custom-call | flops 1811939328 | bytes 16777216 | tf_op jit(solution)/shard_map/input_grad_0/pallas_call | solution.py:548
  153.0 1.8 %fusion.5 = f32[432,256]{1,0:T(8,128)} fusion(bf16[432,256]{1,0:T(8,128)(2,1)S(1)} %collective-permute-done.37, bf16[432,256]{1,0:T(8,128)(2,1)S(1)} %collective-permute-done.34, f32[8,432,256]{2,1,0:T(8,128)S(1)} %get-tuple-element.22, bf16[8,432,256]{2,1,0:T(8,128)(2,1)} %copy-done.36), kind=kLoop, calls=%fused_computation.12 | loop fusion | flops 663552 | bytes 1548288 | tf_op jit(solution)/shard_map/add | solution.py:100
  (145 shorter events, 46.5 us)
Async XLA Ops:
  7.4 10.8 %collective-permute-start = (bf16[656,256]{1,0:T(8,128)(2,1)S(1)}, bf16[656,256]{1,0:T(8,128)(2,1)S(1)}, u32[]{:S(2)}, u32[]{:S(2)}) collective-permute-start(bf16[656,256]{1,0:T(8,128)(2,1)S(1)} %get-tuple-element.16), channel_id=1, source_target_pairs={{0,4},{1,5},{4,8},{5,9},{8,12},{9,13},{12,14},{13,15},{14,10},{15,... | collective-permute-start | bytes 1007624 | tf_op jit(solution)/shard_map/ppermute | solution.py:58
  10.4 9.6 %collective-permute-start.4 = (bf16[656,256]{1,0:T(8,128)(2,1)S(1)}, bf16[656,256]{1,0:T(8,128)(2,1)S(1)}, u32[]{:S(2)}, u32[]{:S(2)}) collective-permute-start(bf16[656,256]{1,0:T(8,128)(2,1)S(1)} %get-tuple-element.16), channel_id=1, source_target_pairs={{0,2},{1,3},{4,0},{5,1},{8,4},{9,5},{12,8},{13,9},{14,12},{15,13},... | collective-permute-start | bytes 1007624 | tf_op jit(solution)/shard_map/ppermute | solution.py:58
  18.2 9.1 %collective-permute-start.1 = (bf16[656,256]{1,0:T(8,128)(2,1)S(1)}, bf16[656,256]{1,0:T(8,128)(2,1)S(1)}, u32[]{:S(2)}, u32[]{:S(2)}) collective-permute-start(bf16[656,256]{1,0:T(8,128)(2,1)S(1)} %collective-permute-done), channel_id=1, source_target_pairs={{0,4},{1,5},{4,8},{5,9},{8,12},{9,13},{12,14},{13,15},{14,10},{15,... | collective-permute-start | bytes 1007624 | tf_op jit(solution)/shard_map/ppermute | solution.py:58
  20.3 10.3 %collective-permute-start.7 = (bf16[656,256]{1,0:T(8,128)(2,1)S(1)}, bf16[656,256]{1,0:T(8,128)(2,1)S(1)}, u32[]{:S(2)}, u32[]{:S(2)}) collective-permute-start(bf16[656,256]{1,0:T(8,128)(2,1)S(1)} %get-tuple-element.16), channel_id=1, source_target_pairs={{0,1},{1,0},{2,3},{3,2},{4,5},{5,4},{6,7},{7,6},{8,9},{9,8},{10,11... | collective-permute-start | bytes 1007624 | tf_op jit(solution)/shard_map/ppermute | solution.py:62
  29.3 10.4 %collective-permute-start.8 = (bf16[656,256]{1,0:T(8,128)(2,1)S(1)}, bf16[656,256]{1,0:T(8,128)(2,1)S(1)}, u32[]{:S(2)}, u32[]{:S(2)}) collective-permute-start(bf16[656,256]{1,0:T(8,128)(2,1)S(1)} %collective-permute-done), channel_id=1, source_target_pairs={{0,1},{1,0},{2,3},{3,2},{4,5},{5,4},{6,7},{7,6},{8,9},{9,8},{10,11... | collective-permute-start | bytes 1007624 | tf_op jit(solution)/shard_map/ppermute | solution.py:62
  29.3 12.0 %collective-permute-start.14 = (bf16[656,256]{1,0:T(8,128)(2,1)S(1)}, bf16[656,256]{1,0:T(8,128)(2,1)S(1)}, u32[]{:S(2)}, u32[]{:S(2)}) collective-permute-start(bf16[656,256]{1,0:T(8,128)(2,1)S(1)} %collective-permute-done.4), channel_id=1, source_target_pairs={{0,1},{1,0},{2,3},{3,2},{4,5},{5,4},{6,7},{7,6},{8,9},{9,8},{10,11... | collective-permute-start | bytes 1007624 | tf_op jit(solution)/shard_map/ppermute | solution.py:62
  31.3 11.0 %collective-permute-start.9 = (bf16[656,256]{1,0:T(8,128)(2,1)S(1)}, bf16[656,256]{1,0:T(8,128)(2,1)S(1)}, u32[]{:S(2)}, u32[]{:S(2)}) collective-permute-start(bf16[656,256]{1,0:T(8,128)(2,1)S(1)} %collective-permute-done.1), channel_id=1, source_target_pairs={{0,1},{1,0},{2,3},{3,2},{4,5},{5,4},{6,7},{7,6},{8,9},{9,8},{10,11... | collective-permute-start | bytes 1007624 | tf_op jit(solution)/shard_map/ppermute | solution.py:62
  36.7 15.1 %collective-permute-start.13 = (bf16[656,256]{1,0:T(8,128)(2,1)S(1)}, bf16[656,256]{1,0:T(8,128)(2,1)S(1)}, u32[]{:S(2)}, u32[]{:S(2)}) collective-permute-start(bf16[656,256]{1,0:T(8,128)(2,1)S(1)} %collective-permute-done.5), channel_id=1, source_target_pairs={{0,1},{1,0},{2,3},{3,2},{4,5},{5,4},{6,7},{7,6},{8,9},{9,8},{10,11... | collective-permute-start | bytes 1007624 | tf_op jit(solution)/shard_map/ppermute | solution.py:62
  40.5 10.4 %collective-permute-start.15 = (bf16[640,256]{1,0:T(8,128)(2,1)}, bf16[640,256]{1,0:T(8,128)(2,1)}, u32[]{:S(2)}, u32[]{:S(2)}) collective-permute-start(bf16[640,256]{1,0:T(8,128)(2,1)} %extract.1), channel_id=1, source_target_pairs={{0,2},{1,3},{4,0},{5,1},{8,4},{9,5},{12,8},{13,9},{14,12},{15,13},... | collective-permute-start | bytes 983048 | tf_op jit(solution)/shard_map/ppermute | solution.py:58
  42.1 22.3 %collective-permute-start.10 = (bf16[656,256]{1,0:T(8,128)(2,1)}, bf16[656,256]{1,0:T(8,128)(2,1)}, u32[]{:S(2)}, u32[]{:S(2)}) collective-permute-start(bf16[656,256]{1,0:T(8,128)(2,1)} %collective-permute-done.2), channel_id=1, source_target_pairs={{0,1},{1,0},{2,3},{3,2},{4,5},{5,4},{6,7},{7,6},{8,9},{9,8},{10,11... | collective-permute-start | bytes 1007624 | tf_op jit(solution)/shard_map/ppermute | solution.py:62
  43.1 21.4 %collective-permute-start.12 = (bf16[656,256]{1,0:T(8,128)(2,1)}, bf16[656,256]{1,0:T(8,128)(2,1)}, u32[]{:S(2)}, u32[]{:S(2)}) collective-permute-start(bf16[656,256]{1,0:T(8,128)(2,1)} %collective-permute-done.6), channel_id=1, source_target_pairs={{0,1},{1,0},{2,3},{3,2},{4,5},{5,4},{6,7},{7,6},{8,9},{9,8},{10,11... | collective-permute-start | bytes 1007624 | tf_op jit(solution)/shard_map/ppermute | solution.py:62
  43.4 21.1 %collective-permute-start.11 = (bf16[656,256]{1,0:T(8,128)(2,1)}, bf16[656,256]{1,0:T(8,128)(2,1)}, u32[]{:S(2)}, u32[]{:S(2)}) collective-permute-start(bf16[656,256]{1,0:T(8,128)(2,1)} %collective-permute-done.3), channel_id=1, source_target_pairs={{0,1},{1,0},{2,3},{3,2},{4,5},{5,4},{6,7},{7,6},{8,9},{9,8},{10,11... | collective-permute-start | bytes 1007624 | tf_op jit(solution)/shard_map/ppermute | solution.py:62
  50.9 11.5 %collective-permute-start.19 = (bf16[640,256]{1,0:T(8,128)(2,1)}, bf16[640,256]{1,0:T(8,128)(2,1)}, u32[]{:S(2)}, u32[]{:S(2)}) collective-permute-start(bf16[640,256]{1,0:T(8,128)(2,1)} %collective-permute-done.15.refs_19_), channel_id=1, source_target_pairs={{0,2},{1,3},{4,0},{5,1},{8,4},{9,5},{12,8},{13,9},{14,12},{15,13},... | collective-permute-start | bytes 983048 | tf_op jit(solution)/shard_map/ppermute | solution.py:58
  52.6 10.7 %collective-permute-start.16 = (bf16[640,256]{1,0:T(8,128)(2,1)}, bf16[640,256]{1,0:T(8,128)(2,1)}, u32[]{:S(2)}, u32[]{:S(2)}) collective-permute-start(bf16[640,256]{1,0:T(8,128)(2,1)} %extract.1), channel_id=1, source_target_pairs={{0,4},{1,5},{4,8},{5,9},{8,12},{9,13},{12,14},{13,15},{14,10},{15,... | collective-permute-start | bytes 983048 | tf_op jit(solution)/shard_map/ppermute | solution.py:58
  62.4 29.2 %collective-permute-start.20 = (bf16[640,256]{1,0:T(8,128)(2,1)}, bf16[640,256]{1,0:T(8,128)(2,1)S(1)}, u32[]{:S(2)}, u32[]{:S(2)}) collective-permute-start(bf16[640,256]{1,0:T(8,128)(2,1)} %collective-permute-done.19), channel_id=1, source_target_pairs={{0,2},{1,3},{4,0},{5,1},{8,4},{9,5},{12,8},{13,9},{14,12},{15,13},... | collective-permute-start | bytes 983048 | tf_op jit(solution)/shard_map/ppermute | solution.py:58
  63.3 28.3 %collective-permute-start.17 = (bf16[640,256]{1,0:T(8,128)(2,1)}, bf16[640,256]{1,0:T(8,128)(2,1)S(1)}, u32[]{:S(2)}, u32[]{:S(2)}) collective-permute-start(bf16[640,256]{1,0:T(8,128)(2,1)} %collective-permute-done.16), channel_id=1, source_target_pairs={{0,4},{1,5},{4,8},{5,9},{8,12},{9,13},{12,14},{13,15},{14,10},{15,... | collective-permute-start | bytes 983048 | tf_op jit(solution)/shard_map/ppermute | solution.py:58
  112.1 10.9 %collective-permute-start.23 = (bf16[640,256]{1,0:T(8,128)(2,1)}, bf16[640,256]{1,0:T(8,128)(2,1)S(1)}, u32[]{:S(2)}, u32[]{:S(2)}) collective-permute-start(bf16[640,256]{1,0:T(8,128)(2,1)} %collective-permute-done.16), channel_id=1, source_target_pairs={{0,1},{1,0},{2,3},{3,2},{4,5},{5,4},{6,7},{7,6},{8,9},{9,8},{10,11... | collective-permute-start | bytes 983048 | tf_op jit(solution)/shard_map/ppermute | solution.py:62
  112.6 9.7 %collective-permute-start.21 = (bf16[640,256]{1,0:T(8,128)(2,1)S(1)}, bf16[640,256]{1,0:T(8,128)(2,1)S(1)}, u32[]{:S(2)}, u32[]{:S(2)}) collective-permute-start(bf16[640,256]{1,0:T(8,128)(2,1)S(1)} %collective-permute-done.20), channel_id=1, source_target_pairs={{0,2},{1,3},{4,0},{5,1},{8,4},{9,5},{12,8},{13,9},{14,12},{15,13},... | collective-permute-start | bytes 983048 | tf_op jit(solution)/shard_map/ppermute | solution.py:58
  117.8 13.7 %collective-permute-start.27 = (bf16[640,256]{1,0:T(8,128)(2,1)S(1)}, bf16[640,256]{1,0:T(8,128)(2,1)S(1)}, u32[]{:S(2)}, u32[]{:S(2)}) collective-permute-start(bf16[640,256]{1,0:T(8,128)(2,1)S(1)} %collective-permute-done.20), channel_id=1, source_target_pairs={{0,1},{1,0},{2,3},{3,2},{4,5},{5,4},{6,7},{7,6},{8,9},{9,8},{10,11... | collective-permute-start | bytes 983048 | tf_op jit(solution)/shard_map/ppermute | solution.py:62
  117.9 13.6 %collective-permute-start.24 = (bf16[640,256]{1,0:T(8,128)(2,1)S(1)}, bf16[640,256]{1,0:T(8,128)(2,1)S(1)}, u32[]{:S(2)}, u32[]{:S(2)}) collective-permute-start(bf16[640,256]{1,0:T(8,128)(2,1)S(1)} %collective-permute-done.17), channel_id=1, source_target_pairs={{0,1},{1,0},{2,3},{3,2},{4,5},{5,4},{6,7},{7,6},{8,9},{9,8},{10,11... | collective-permute-start | bytes 983048 | tf_op jit(solution)/shard_map/ppermute | solution.py:62
  122.3 9.2 %collective-permute-start.26 = (bf16[640,256]{1,0:T(8,128)(2,1)S(1)}, bf16[640,256]{1,0:T(8,128)(2,1)S(1)}, u32[]{:S(2)}, u32[]{:S(2)}) collective-permute-start(bf16[640,256]{1,0:T(8,128)(2,1)S(1)} %collective-permute-done.21), channel_id=1, source_target_pairs={{0,1},{1,0},{2,3},{3,2},{4,5},{5,4},{6,7},{7,6},{8,9},{9,8},{10,11... | collective-permute-start | bytes 983048 | tf_op jit(solution)/shard_map/ppermute | solution.py:62
  123.1 19.2 %collective-permute-start.36 = (bf16[432,256]{1,0:T(8,128)(2,1)S(1)}, bf16[432,256]{1,0:T(8,128)(2,1)S(1)}, u32[]{:S(2)}, u32[]{:S(2)}) collective-permute-start(bf16[432,256]{1,0:T(8,128)(2,1)S(1)} %get-tuple-element.26), channel_id=1, source_target_pairs={{0,2},{1,3},{4,0},{5,1},{8,4},{9,5},{12,8},{13,9},{14,12},{15,13},... | collective-permute-start | bytes 663560 | tf_op jit(solution)/shard_map/ppermute | solution.py:58
  139.8 13.2 %collective-permute-start.34 = (bf16[432,256]{1,0:T(8,128)(2,1)S(1)}, bf16[432,256]{1,0:T(8,128)(2,1)S(1)}, u32[]{:S(2)}, u32[]{:S(2)}) collective-permute-start(bf16[432,256]{1,0:T(8,128)(2,1)S(1)} %get-tuple-element.25), channel_id=1, source_target_pairs={{0,4},{1,5},{4,8},{5,9},{8,12},{9,13},{12,14},{13,15},{14,10},{15,... | collective-permute-start | bytes 663560 | tf_op jit(solution)/shard_map/ppermute | solution.py:58
  143.3 9.7 %collective-permute-start.37 = (bf16[432,256]{1,0:T(8,128)(2,1)S(1)}, bf16[432,256]{1,0:T(8,128)(2,1)S(1)}, u32[]{:S(2)}, u32[]{:S(2)}) collective-permute-start(bf16[432,256]{1,0:T(8,128)(2,1)S(1)} %fusion.1), channel_id=1, source_target_pairs={{0,2},{1,3},{4,0},{5,1},{8,4},{9,5},{12,8},{13,9},{14,12},{15,13},... | collective-permute-start | bytes 663560 | tf_op jit(solution)/shard_map/ppermute | solution.py:58
  (51 other events, 290.7 us)

commit v3 on v2

--- a/solution.py
+++ b/solution.py
@@ -17,7 +17,7 @@
 ROWS = 320
 NOTES = 16
 HB = 24
-VMEM_LIMIT = 40 * 1024 * 1024
+VMEM_LIMIT = 56 * 1024 * 1024
 DIRECTIONS = [
     (i, j, l)
     for i in (-1, 0, 1)
@@ -29,6 +29,7 @@
 VMEM = pl.BlockSpec(memory_space=pltpu.VMEM)
 SMEM = pl.BlockSpec(memory_space=pltpu.SMEM)
 ANY = pl.BlockSpec(memory_space=pl.ANY)
+HBM = pl.BlockSpec(memory_space=pltpu.HBM)
 
 
 def ring_order(chips):
@@ -62,22 +63,40 @@
     return lax.ppermute(x, "morton", [(m, m ^ 1) for m in range(peers)])
 
 
-def gather_ring(x, peers, step, after):
-    chips = peers // 2
-    if chips > 8:
-        got = lax.all_gather(x[None], "morton", axis=0, tiled=True)
-        return [got], ([got] * 4, [got] * 4)
-    got = {0: x}
-    hops = []
-    for way, count, gate in ((step, chips // 2, after[0]), (-step, (chips - 1) // 2, after[1])):
-        held = x if gate is None else lax.optimization_barrier((x, gate))[0]
-        hops.append([])
-        for hop in range(1, count + 1):
-            held = ring_step(held, peers, way)
-            hops[-1].append(held)
-            got[(way * hop) % chips] = held
-    mine = [got[k] for k in range(chips)]
-    return [t[None] for t in mine + [swap_cores(t, peers) for t in mine]], hops
+class RingGather:
+    def __init__(self, x, peers, step):
+        self.x, self.peers, self.chips = x, peers, peers // 2
+        self.whole = None
+        if self.chips > 8:
+            self.whole = lax.all_gather(x[None], "morton", axis=0, tiled=True)
+        self.steps = (step, -step)
+        self.counts = (self.chips // 2, (self.chips - 1) // 2)
+        self.hops = ([], [])
+
+    def go(self, way, gate=None):
+        hops = self.hops[way]
+        if self.whole is not None or len(hops) == self.counts[way]:
+            return
+        held = hops[-1] if hops else self.x
+        if gate is not None:
+            held = lax.optimization_barrier((held, gate))[0]
+        hops.append(ring_step(held, self.peers, self.steps[way]))
+
+    def last(self, way):
+        return self.x if self.whole is not None else self.hops[way][-1]
+
+    def places(self, gate=None):
+        if self.whole is not None:
+            return [self.whole]
+        got = {0: self.x}
+        for hops, step in zip(self.hops, self.steps):
+            for number, held in enumerate(hops):
+                got[(step * (number + 1)) % self.chips] = held
+        mine = [got[k] for k in range(self.chips)]
+        held = mine
+        if gate is not None:
+            held = [lax.optimization_barrier((t, gate))[0] for t in mine]
+        return [t[None] for t in mine + [swap_cores(t, self.peers) for t in held]]
 
 
 def scatter_ring(keep, give, peers):
@@ -101,7 +120,7 @@
     return total
 
 
-def call(body, out_shape, in_specs, scratch=(), flops=0, nbytes=0, name=None, out_specs=None):
+def call(body, out_shape, in_specs, scratch=(), cost=2, name=None, out_specs=None):
     return pl.pallas_call(
         body,
         out_shape=out_shape,
@@ -109,7 +128,7 @@
         out_specs=out_specs or jax.tree.map(lambda _: VMEM, out_shape),
         scratch_shapes=list(scratch),
         compiler_params=pltpu.CompilerParams(vmem_limit_bytes=VMEM_LIMIT),
-        cost_estimate=pl.CostEstimate(flops=flops, bytes_accessed=nbytes, transcendentals=0),
+        cost_estimate=pl.CostEstimate(flops=cost * 10**9, bytes_accessed=0, transcendentals=0),
         name=name,
     )
 
@@ -465,7 +484,6 @@
     def cols_shape(n):
         return (n * 10, 64, 9 * channels)
 
-    conv_flops = 2 * per_device * 27 * channels * channels
 
     table = jnp.asarray(ring_tables(peers))[lax.axis_index("morton")]
 
@@ -476,7 +494,10 @@
         [stage],
         name="norm",
     )(recv_slot, send_face, features, gain)
-    hidden_parts, hidden_hops = gather_ring(share, peers, 1, (None, None))
+    hidden_ring = RingGather(share, peers, 1)
+    for way in (0, 0, 0, 0, 1, 1, 1):
+        hidden_ring.go(way)
+    hidden_parts = hidden_ring.places()
 
     cot_share = call(
         extract_body,
@@ -485,11 +506,14 @@
         [stage],
         name="extract",
     )(cotangent)
-    gates = (hidden_hops[1][-1], hidden_hops[0][-1])
-    cot_parts, (far, near) = gather_ring(cot_share, peers, -1, gates)
     turned = conv_weight.reshape(27, channels, channels)[::-1].transpose(0, 2, 1)
     turned = turned.reshape(27 * channels, channels)
-    hidden, turned = lax.optimization_barrier((hidden, turned))
+    cot_share, turned = lax.optimization_barrier((cot_share, turned))
+    cot_ring = RingGather(cot_share, peers, -1)
+    cot_ring.go(0, hidden_ring.last(1))
+    first = cot_ring.last(0)
+    cot_ring.go(1, hidden_ring.last(0))
+    cot_ring.go(0)
 
     count = len(hidden_parts)
     rows = 27 * channels // peers
@@ -500,7 +524,7 @@
             sds((peers, channels), jnp.int32),
             sds((peers, channels), jnp.int32),
         ),
-        [SMEM] * 2 + [VMEM] + [ANY] * (count + 1),
+        [SMEM] * 2 + [VMEM] + [HBM] * (count + 1),
         padded(bricks)
         + [
             pltpu.VMEM((peers, bricks * ROWS + NOTES, channels), BF16),
@@ -508,10 +532,11 @@
             pltpu.SemaphoreType.DMA((count,)),
             pltpu.SemaphoreType.DMA((1,)),
         ],
-        flops=conv_flops,
-        nbytes=2**24,
+        cost=6,
         name="pad",
-    )(recv_slot, table, hidden, *hidden_parts, far[0])
+    )(recv_slot, table, hidden, *hidden_parts, first)
+    cot_ring.go(1, cols)
+    cot_ring.go(0, cols)
     keep, give = call(
         functools.partial(weight_grad_body, factor, peers),
         (
@@ -524,22 +549,23 @@
             pltpu.VMEM((channels, per_device), BF16),
             pltpu.SemaphoreType.DMA((1,)),
         ],
-        flops=conv_flops,
-        nbytes=2**24,
+        cost=6,
         name="weight_grad",
         out_specs=(ANY, VMEM),
     )(table, cols, cotangent)
-    give = lax.optimization_barrier((give, far[2], near[1]))[0]
-    grad_weight = scatter_ring(keep, give, peers)
-
     mixed = call(
         mix_body,
         sds((per_device, channels), BF16),
         [VMEM, VMEM, VMEM],
-        flops=conv_flops,
-        nbytes=2**23,
+        cost=5,
         name="mix",
     )(cols, conv_weight, features)
+
+    cot_ring.go(1, give)
+    cot_ring.go(0, give)
+    cot_parts = cot_ring.places(cols)
+    give = lax.optimization_barrier((give, mixed, *cot_parts))[0]
+    grad_weight = scatter_ring(keep, give, peers)
 
     grads = []
     for brick in range(bricks):
@@ -548,15 +574,14 @@
             call(
                 functools.partial(input_grad_body, slots, peers, brick, count),
                 sds((512, channels), BF16),
-                [SMEM] * 3 + [VMEM] * 4 + [ANY] * count,
+                [SMEM] * 3 + [VMEM] * 4 + [HBM] * count,
                 padded(1)
                 + [
                     pltpu.VMEM(cols_shape(1), BF16),
                     pltpu.VMEM((peers, bricks * ROWS, channels), BF16),
                     pltpu.SemaphoreType.DMA((count,)),
                 ],
-                flops=conv_flops // bricks,
-                nbytes=2**24,
+                cost=8,
                 name="input_grad_" + str(brick),
             )(served, send_face, table, cotangent[at], turned, features[at], gain, *cot_parts)
         )

time: 156 us -> 159 us (1.019)
  local copies, waits for them, and re-layouts: 38.3 us -> 12 us
  Pallas kernels: 36.8 us -> 55.3 us
  waiting for transfers between devices: 48 us -> 59.3 us
    unnamed x74 -> x48, local copies, waits for them, and re-layouts: 29.5 us -> 2.46 us
    ppermute x21, waiting for transfers between devices: 44.2 us -> 55.9 us  [ring_step(): return lax.ppermute(x, 'morton', pairs)]
    pallas_call x2, Pallas kernels: 17.1 us -> 21.9 us  [local(): call(functools.partial(input_grad_body, slots, peers, brick, count), sds(...]
    pallas_call x1, Pallas kernels: 5.24 us -> 9.9 us  [local(): call(functools.partial(weight_grad_body, factor, peers), (sds((peers // 2...]
    pallas_call x1, Pallas kernels: 4.61 us -> 8.38 us  [local(): call(mix_body, sds((per_device, channels), BF16), [VMEM, VMEM, VMEM], cos...]
    pallas_call x1, Pallas kernels: 5.77 us -> 8.53 us  [local(): call(functools.partial(pad_body, slots, peers, count), (sds(cols_shape(br...]
  transfers between devices with their start and end apart: 38 -> 38, of which waited for: 11 -> 12; matrix products, arithmetic and copies ran while one was open for 7% -> 7% of each run, Pallas kernels for 22% -> 32%
where the time goes in v3:
time: 159 us; the launch traced here: 158 us
  waiting for transfers between devices  59.3 us (37%)
  Pallas kernels  55.3 us (35%)
  starting transfers between devices  26.9 us (17%)
  local copies, waits for them, and re-layouts  12 us (8%)
  other arithmetic  3.16 us (2%)
    ppermute x21, waiting for transfers between devices, ring_step(): return lax.ppermute(x, 'morton', pairs)  55.9 us
    ppermute x21, starting transfers between devices, ring_step(): return lax.ppermute(x, 'morton', pairs)  24.2 us
    pallas_call x2, Pallas kernels, local(): call(functools.partial(input_grad_body, slots, peers, brick, count), sds(...  21.9 us
    pallas_call x1, Pallas kernels, local(): call(functools.partial(weight_grad_body, factor, peers), (sds((peers // 2...  9.9 us
    pallas_call x1, Pallas kernels, local(): call(functools.partial(pad_body, slots, peers, count), (sds(cols_shape(br...  8.53 us
    pallas_call x1, Pallas kernels, local(): call(mix_body, sds((per_device, channels), BF16), [VMEM, VMEM, VMEM], cos...  8.38 us
    reshape x1, local copies, waits for them, and re-layouts, local(): conv_weight.reshape(27, channels, channels)[::-1].transpose(0, 2, 1)  4.44 us
    pallas_call x1, Pallas kernels, local(): call(norm_body, (sds((per_device, channels), BF16), sds((bricks * ROWS +...  4.26 us
  transfers between devices with their start and end apart: 38, of which 12 were waited for; matrix products, arithmetic and copies ran while one was open for 7% of the time, Pallas kernels for 32%

profile of v3, /device:TPU:0, one launch (start us, length us, event | category | flops | bytes accessed | tf_op | source)
XLA Modules:
  0.0 157.5 jit_solution(10361732048078852077)
XLA Ops:
  0.6 4.3 %norm.1 = (bf16[1024,256]{1,0:T(8,128)(2,1)}, bf16[656,256]{1,0:T(8,128)(2,1)}) custom-call(s32[2,26]{1,0:T(2,128)} %refs_0_.1, s32[1,64]{1,0:T(1,128)} %refs_1_.3, bf16[1024,256]{1,0:T(8,128)(2,1)} %x_ref.5, f32[1,256]{1,0:T(1,128)} %bitcast.102), custom_call_target="tpu_custom_call" | custom-call | flops 2000000000 | tf_op jit(solution)/shard_map/norm/pallas_call | solution.py:490
  4.9 3.0 %collective-permute-start = (bf16[656,256]{1,0:T(8,128)(2,1)}, bf16[656,256]{1,0:T(8,128)(2,1)S(1)}, u32[]{:S(2)}, u32[]{:S(2)}) collective-permute-start(bf16[656,256]{1,0:T(8,128)(2,1)} %get-tuple-element.25), channel_id=1, source_target_pairs={{0,4},{1,5},{4,8},{5,9},{8,12},{9,13},{12,14},{13,15},{14,10},{15,... | collective-permute-start | bytes 1007624 | tf_op jit(solution)/shard_map/ppermute | solution.py:59
  7.9 8.0 %collective-permute-done = bf16[656,256]{1,0:T(8,128)(2,1)S(1)} collective-permute-done((bf16[656,256]{1,0:T(8,128)(2,1)}, bf16[656,256]{1,0:T(8,128)(2,1)S(1)}, u32[]{:S(2)}, u32[]{:S(2)}) %collective-permute-start) | collective-permute-done | bytes 335904 | tf_op jit(solution)/shard_map/ppermute | solution.py:59
  16.0 1.8 %collective-permute-start.1 = (bf16[656,256]{1,0:T(8,128)(2,1)S(1)}, bf16[656,256]{1,0:T(8,128)(2,1)}, u32[]{:S(2)}, u32[]{:S(2)}) collective-permute-start(bf16[656,256]{1,0:T(8,128)(2,1)S(1)} %collective-permute-done), channel_id=1, source_target_pairs={{0,4},{1,5},{4,8},{5,9},{8,12},{9,13},{12,14},{13,15},{14,10},{15,... | collective-permute-start | bytes 1007624 | tf_op jit(solution)/shard_map/ppermute | solution.py:59
  18.0 7.1 %collective-permute-done.1 = bf16[656,256]{1,0:T(8,128)(2,1)} collective-permute-done((bf16[656,256]{1,0:T(8,128)(2,1)S(1)}, bf16[656,256]{1,0:T(8,128)(2,1)}, u32[]{:S(2)}, u32[]{:S(2)}) %collective-permute-start.1) | collective-permute-done | bytes 335904 | tf_op jit(solution)/shard_map/ppermute | solution.py:59
  27.7 5.9 %collective-permute-done.2 = bf16[656,256]{1,0:T(8,128)(2,1)} collective-permute-done((bf16[656,256]{1,0:T(8,128)(2,1)}, bf16[656,256]{1,0:T(8,128)(2,1)}, u32[]{:S(2)}, u32[]{:S(2)}) %collective-permute-start.2) | collective-permute-done | bytes 335904 | tf_op jit(solution)/shard_map/ppermute | solution.py:59
  35.6 2.1 %collective-permute-done.6 = bf16[656,256]{1,0:T(8,128)(2,1)} collective-permute-done((bf16[656,256]{1,0:T(8,128)(2,1)}, bf16[656,256]{1,0:T(8,128)(2,1)}, u32[]{:S(2)}, u32[]{:S(2)}) %collective-permute-start.6) | collective-permute-done | bytes 335904 | tf_op jit(solution)/shard_map/ppermute | solution.py:59
  37.8 3.4 %collective-permute-done.3 = bf16[656,256]{1,0:T(8,128)(2,1)} collective-permute-done((bf16[656,256]{1,0:T(8,128)(2,1)}, bf16[656,256]{1,0:T(8,128)(2,1)}, u32[]{:S(2)}, u32[]{:S(2)}) %collective-permute-start.3) | collective-permute-done | bytes 335904 | tf_op jit(solution)/shard_map/ppermute | solution.py:59
  41.1 2.2 %extract.1 = bf16[640,256]{1,0:T(8,128)(2,1)} custom-call(bf16[1024,256]{1,0:T(8,128)(2,1)} %refs_2_.1), custom_call_target="tpu_custom_call" | custom-call | flops 2000000000 | tf_op jit(solution)/shard_map/extract/pallas_call | solution.py:502
  43.4 4.4 %copy.10 = bf16[27,256,256]{1,2,0:T(8,128)(2,1)S(1)} copy(bf16[27,256,256]{2,1,0:T(8,128)(2,1)} %bitcast.67) | data formatting | bytes 7077888 | tf_op jit(solution)/shard_map/reshape | solution.py:509
  47.8 2.1 %rev.3 = bf16[27,256,256]{1,2,0:T(8,128)(2,1)} reverse(bf16[27,256,256]{1,2,0:T(8,128)(2,1)S(1)} %copy.10), dimensions={0} | reverse | bytes 7077888 | tf_op jit(solution)/shard_map/rev | solution.py:509
  52.2 8.0 %collective-permute-done.15.refs_19_ = bf16[640,256]{1,0:T(8,128)(2,1)S(1)} collective-permute-done((bf16[640,256]{1,0:T(8,128)(2,1)}, bf16[640,256]{1,0:T(8,128)(2,1)S(1)}, u32[]{:S(2)}, u32[]{:S(2)}) %collective-permute-start.15) | collective-permute-done | bytes 327712 | tf_op jit(solution)/shard_map/ppermute | solution.py:59
  62.3 8.5 %pad.5 = (bf16[20,64,2304]{2,1,0:T(8,128)(2,1)}, s32[16,256]{1,0:T(8,128)}, s32[16,256]{1,0:T(8,128)}) custom-call(s32[2,26]{1,0:T(2,128)} %refs_0_.1, s32[25]{0:T(128)} %dynamic-slice_bitcast_fusion.refs_1_.refs_0_.refs_2_, bf16[1024,256]{1,0:T(8,128)(2,1)} %get-tuple-element.24.refs_2_, bf16[1,656,256]{2,1,0:T(8,128)(2,1)} %bitcast.70, ...), custom_call_target="tpu_custom_call" | custom-call | flops 6000000000 | tf_op jit(solution)/shard_map/pad/pallas_call | solution.py:520
  72.9 9.9 %weight_grad.1 = (f32[8,432,256]{2,1,0:T(8,128)}, bf16[8,432,256]{2,1,0:T(8,128)(2,1)}) custom-call(s32[25]{0:T(128)} %dynamic-slice_bitcast_fusion.refs_1_.refs_0_.refs_2_, bf16[20,64,2304]{2,1,0:T(8,128)(2,1)} %get-tuple-element.28.cols.refs_1_, bf16[1024,256]{1,0:T(8,128)(2,1)} %refs_2_.1), custom_call_target="tpu_custom_call" | custom-call | flops 6000000000 | tf_op jit(solution)/shard_map/weight_grad/pallas_call | solution.py:540
  85.6 5.6 %collective-permute-done.21 = bf16[640,256]{1,0:T(8,128)(2,1)S(1)} collective-permute-done((bf16[640,256]{1,0:T(8,128)(2,1)S(1)}, bf16[640,256]{1,0:T(8,128)(2,1)S(1)}, u32[]{:S(2)}, u32[]{:S(2)}) %collective-permute-start.21) | collective-permute-done | bytes 327712 | tf_op jit(solution)/shard_map/ppermute | solution.py:59
  94.1 8.4 %mix.1 = bf16[1024,256]{1,0:T(8,128)(2,1)} custom-call(bf16[20,64,2304]{2,1,0:T(8,128)(2,1)} %get-tuple-element.28.cols.refs_1_, bf16[6912,256]{1,0:T(8,128)(2,1)} %weight_ref.1, bf16[1024,256]{1,0:T(8,128)(2,1)} %x_ref.5), custom_call_target="tpu_custom_call" | custom-call | flops 5000000000 | tf_op jit(solution)/shard_map/mix/pallas_call | solution.py:556
  103.7 3.3 %collective-permute-done.30 = bf16[8,432,256]{2,1,0:T(8,128)(2,1)S(1)} collective-permute-done((bf16[8,432,256]{2,1,0:T(8,128)(2,1)S(1)}, bf16[8,432,256]{2,1,0:T(8,128)(2,1)S(1)}, u32[]{:S(2)}, u32[]{:S(2)}) %collective-permute-start.30) | collective-permute-done | bytes 1769504 | tf_op jit(solution)/shard_map/ppermute | solution.py:63
  108.2 6.7 %collective-permute-done.31 = bf16[432,256]{1,0:T(8,128)(2,1)S(1)} collective-permute-done((bf16[432,256]{1,0:T(8,128)(2,1)S(1)}, bf16[432,256]{1,0:T(8,128)(2,1)S(1)}, u32[]{:S(2)}, u32[]{:S(2)}) %collective-permute-start.31) | collective-permute-done | bytes 221216 | tf_op jit(solution)/shard_map/ppermute | solution.py:59
  117.9 4.0 %collective-permute-done.32 = bf16[432,256]{1,0:T(8,128)(2,1)S(1)} collective-permute-done((bf16[432,256]{1,0:T(8,128)(2,1)S(1)}, bf16[432,256]{1,0:T(8,128)(2,1)S(1)}, u32[]{:S(2)}, u32[]{:S(2)}) %collective-permute-start.32) | collective-permute-done | bytes 221216 | tf_op jit(solution)/shard_map/ppermute | solution.py:59
  124.0 4.1 %collective-permute-done.33 = bf16[432,256]{1,0:T(8,128)(2,1)S(1)} collective-permute-done((bf16[432,256]{1,0:T(8,128)(2,1)S(1)}, bf16[432,256]{1,0:T(8,128)(2,1)S(1)}, u32[]{:S(2)}, u32[]{:S(2)}) %collective-permute-start.33) | collective-permute-done | bytes 221216 | tf_op jit(solution)/shard_map/ppermute | solution.py:59
  128.2 1.8 %collective-permute-start.36 = (bf16[432,256]{1,0:T(8,128)(2,1)S(1)}, bf16[432,256]{1,0:T(8,128)(2,1)S(1)}, u32[]{:S(2)}, u32[]{:S(2)}) collective-permute-start(bf16[432,256]{1,0:T(8,128)(2,1)S(1)} %get-tuple-element.46), channel_id=1, source_target_pairs={{0,2},{1,3},{4,0},{5,1},{8,4},{9,5},{12,8},{13,9},{14,12},{15,13},... | collective-permute-start | bytes 663560 | tf_op jit(solution)/shard_map/ppermute | solution.py:59
  130.1 11.0 %input_grad_0.1 = bf16[512,256]{1,0:T(8,128)(2,1)} custom-call(s32[16,256]{1,0:T(8,128)} %get-tuple-element.29.refs_0_, s32[1,64]{1,0:T(1,128)} %refs_1_.3, s32[25]{0:T(128)} %dynamic-slice_bitcast_fusion.refs_1_.refs_0_.refs_2_, bf16[512,256]{1,0:T(8,128)(2,1)} %get-tuple-element.51.refs_3_, bf16[6912,256]{1,0:T(8,128)(2,1)} %bitcast.68, ...), custom_call_target="tpu_custom_call" | custom-call | flops 8000000000 | tf_op jit(solution)/shard_map/input_grad_0/pallas_call | solution.py:574
  143.9 10.9 %input_grad_1.1 = bf16[512,256]{1,0:T(8,128)(2,1)} custom-call(s32[16,256]{1,0:T(8,128)} %get-tuple-element.29.refs_0_, s32[1,64]{1,0:T(1,128)} %refs_1_.3, s32[25]{0:T(128)} %dynamic-slice_bitcast_fusion.refs_1_.refs_0_.refs_2_, bf16[512,256]{1,0:T(8,128)(2,1)} %get-tuple-element.52.refs_3_, bf16[6912,256]{1,0:T(8,128)(2,1)} %bitcast.69, ...), custom_call_target="tpu_custom_call" | custom-call | flops 8000000000 | tf_op jit(solution)/shard_map/input_grad_1/pallas_call | solution.py:574
  154.9 1.8 %pad_maximum_fusion = bf16[1024,256]{1,0:T(8,128)(2,1)} fusion(bf16[512,256]{1,0:T(8,128)(2,1)} %input_grad_1.1, bf16[512,256]{1,0:T(8,128)(2,1)S(1)} %copy-done.3), kind=kLoop, calls=%fused_computation | loop fusion | flops 1048576 | bytes 1048576 | tf_op jit(solution)/shard_map/concatenate | solution.py:588
  (119 shorter events, 28.1 us)
Async XLA Ops:
  4.9 11.1 %collective-permute-start = (bf16[656,256]{1,0:T(8,128)(2,1)}, bf16[656,256]{1,0:T(8,128)(2,1)S(1)}, u32[]{:S(2)}, u32[]{:S(2)}) collective-permute-start(bf16[656,256]{1,0:T(8,128)(2,1)} %get-tuple-element.25), channel_id=1, source_target_pairs={{0,4},{1,5},{4,8},{5,9},{8,12},{9,13},{12,14},{13,15},{14,10},{15,... | collective-permute-start | bytes 1007624 | tf_op jit(solution)/shard_map/ppermute | solution.py:59
  7.9 9.8 %collective-permute-start.4 = (bf16[656,256]{1,0:T(8,128)(2,1)}, bf16[656,256]{1,0:T(8,128)(2,1)S(1)}, u32[]{:S(2)}, u32[]{:S(2)}) collective-permute-start(bf16[656,256]{1,0:T(8,128)(2,1)} %get-tuple-element.25), channel_id=1, source_target_pairs={{0,2},{1,3},{4,0},{5,1},{8,4},{9,5},{12,8},{13,9},{14,12},{15,13},... | collective-permute-start | bytes 1007624 | tf_op jit(solution)/shard_map/ppermute | solution.py:59
  16.0 9.2 %collective-permute-start.1 = (bf16[656,256]{1,0:T(8,128)(2,1)S(1)}, bf16[656,256]{1,0:T(8,128)(2,1)}, u32[]{:S(2)}, u32[]{:S(2)}) collective-permute-start(bf16[656,256]{1,0:T(8,128)(2,1)S(1)} %collective-permute-done), channel_id=1, source_target_pairs={{0,4},{1,5},{4,8},{5,9},{8,12},{9,13},{12,14},{13,15},{14,10},{15,... | collective-permute-start | bytes 1007624 | tf_op jit(solution)/shard_map/ppermute | solution.py:59
  17.8 9.4 %collective-permute-start.5 = (bf16[656,256]{1,0:T(8,128)(2,1)S(1)}, bf16[656,256]{1,0:T(8,128)(2,1)}, u32[]{:S(2)}, u32[]{:S(2)}) collective-permute-start(bf16[656,256]{1,0:T(8,128)(2,1)S(1)} %collective-permute-done.4), channel_id=1, source_target_pairs={{0,2},{1,3},{4,0},{5,1},{8,4},{9,5},{12,8},{13,9},{14,12},{15,13},... | collective-permute-start | bytes 1007624 | tf_op jit(solution)/shard_map/ppermute | solution.py:59
  25.1 8.5 %collective-permute-start.2 = (bf16[656,256]{1,0:T(8,128)(2,1)}, bf16[656,256]{1,0:T(8,128)(2,1)}, u32[]{:S(2)}, u32[]{:S(2)}) collective-permute-start(bf16[656,256]{1,0:T(8,128)(2,1)} %collective-permute-done.1), channel_id=1, source_target_pairs={{0,4},{1,5},{4,8},{5,9},{8,12},{9,13},{12,14},{13,15},{14,10},{15,... | collective-permute-start | bytes 1007624 | tf_op jit(solution)/shard_map/ppermute | solution.py:59
  27.1 10.6 %collective-permute-start.6 = (bf16[656,256]{1,0:T(8,128)(2,1)}, bf16[656,256]{1,0:T(8,128)(2,1)}, u32[]{:S(2)}, u32[]{:S(2)}) collective-permute-start(bf16[656,256]{1,0:T(8,128)(2,1)} %collective-permute-done.5), channel_id=1, source_target_pairs={{0,2},{1,3},{4,0},{5,1},{8,4},{9,5},{12,8},{13,9},{14,12},{15,13},... | collective-permute-start | bytes 1007624 | tf_op jit(solution)/shard_map/ppermute | solution.py:59
  34.8 15.1 %collective-permute-start.9 = (bf16[656,256]{1,0:T(8,128)(2,1)}, bf16[656,256]{1,0:T(8,128)(2,1)}, u32[]{:S(2)}, u32[]{:S(2)}) collective-permute-start(bf16[656,256]{1,0:T(8,128)(2,1)} %collective-permute-done.1), channel_id=1, source_target_pairs={{0,1},{1,0},{2,3},{3,2},{4,5},{5,4},{6,7},{7,6},{8,9},{9,8},{10,11... | collective-permute-start | bytes 1007624 | tf_op jit(solution)/shard_map/ppermute | solution.py:63
  34.8 26.5 %collective-permute-start.13 = (bf16[656,256]{1,0:T(8,128)(2,1)}, bf16[656,256]{1,0:T(8,128)(2,1)}, u32[]{:S(2)}, u32[]{:S(2)}) collective-permute-start(bf16[656,256]{1,0:T(8,128)(2,1)} %collective-permute-done.5), channel_id=1, source_target_pairs={{0,1},{1,0},{2,3},{3,2},{4,5},{5,4},{6,7},{7,6},{8,9},{9,8},{10,11... | collective-permute-start | bytes 1007624 | tf_op jit(solution)/shard_map/ppermute | solution.py:63
  35.5 26.7 %collective-permute-start.10 = (bf16[656,256]{1,0:T(8,128)(2,1)}, bf16[656,256]{1,0:T(8,128)(2,1)}, u32[]{:S(2)}, u32[]{:S(2)}) collective-permute-start(bf16[656,256]{1,0:T(8,128)(2,1)} %collective-permute-done.2), channel_id=1, source_target_pairs={{0,1},{1,0},{2,3},{3,2},{4,5},{5,4},{6,7},{7,6},{8,9},{9,8},{10,11... | collective-permute-start | bytes 1007624 | tf_op jit(solution)/shard_map/ppermute | solution.py:63
  37.8 24.5 %collective-permute-start.12 = (bf16[656,256]{1,0:T(8,128)(2,1)}, bf16[656,256]{1,0:T(8,128)(2,1)}, u32[]{:S(2)}, u32[]{:S(2)}) collective-permute-start(bf16[656,256]{1,0:T(8,128)(2,1)} %collective-permute-done.6), channel_id=1, source_target_pairs={{0,1},{1,0},{2,3},{3,2},{4,5},{5,4},{6,7},{7,6},{8,9},{9,8},{10,11... | collective-permute-start | bytes 1007624 | tf_op jit(solution)/shard_map/ppermute | solution.py:63
  41.1 21.1 %collective-permute-start.11 = (bf16[656,256]{1,0:T(8,128)(2,1)}, bf16[656,256]{1,0:T(8,128)(2,1)}, u32[]{:S(2)}, u32[]{:S(2)}) collective-permute-start(bf16[656,256]{1,0:T(8,128)(2,1)} %collective-permute-done.3), channel_id=1, source_target_pairs={{0,1},{1,0},{2,3},{3,2},{4,5},{5,4},{6,7},{7,6},{8,9},{9,8},{10,11... | collective-permute-start | bytes 1007624 | tf_op jit(solution)/shard_map/ppermute | solution.py:63
  49.9 10.3 %collective-permute-start.15 = (bf16[640,256]{1,0:T(8,128)(2,1)}, bf16[640,256]{1,0:T(8,128)(2,1)S(1)}, u32[]{:S(2)}, u32[]{:S(2)}) collective-permute-start(bf16[640,256]{1,0:T(8,128)(2,1)} %extract.1), channel_id=1, source_target_pairs={{0,2},{1,3},{4,0},{5,1},{8,4},{9,5},{12,8},{13,9},{14,12},{15,13},... | collective-permute-start | bytes 983048 | tf_op jit(solution)/shard_map/ppermute | solution.py:59
  60.2 10.6 %collective-permute-start.19 = (bf16[640,256]{1,0:T(8,128)(2,1)S(1)}, bf16[640,256]{1,0:T(8,128)(2,1)S(1)}, u32[]{:S(2)}, u32[]{:S(2)}) collective-permute-start(bf16[640,256]{1,0:T(8,128)(2,1)S(1)} %collective-permute-done.15.refs_19_), channel_id=1, source_target_pairs={{0,2},{1,3},{4,0},{5,1},{8,4},{9,5},{12,8},{13,9},{14,12},{15,13},... | collective-permute-start | bytes 983048 | tf_op jit(solution)/shard_map/ppermute | solution.py:59
  61.3 10.7 %collective-permute-start.16 = (bf16[640,256]{1,0:T(8,128)(2,1)}, bf16[640,256]{1,0:T(8,128)(2,1)S(1)}, u32[]{:S(2)}, u32[]{:S(2)}) collective-permute-start(bf16[640,256]{1,0:T(8,128)(2,1)} %extract.1), channel_id=1, source_target_pairs={{0,4},{1,5},{4,8},{5,9},{8,12},{9,13},{12,14},{13,15},{14,10},{15,... | collective-permute-start | bytes 983048 | tf_op jit(solution)/shard_map/ppermute | solution.py:59
  70.8 12.0 %collective-permute-start.20 = (bf16[640,256]{1,0:T(8,128)(2,1)S(1)}, bf16[640,256]{1,0:T(8,128)(2,1)S(1)}, u32[]{:S(2)}, u32[]{:S(2)}) collective-permute-start(bf16[640,256]{1,0:T(8,128)(2,1)S(1)} %collective-permute-done.19), channel_id=1, source_target_pairs={{0,2},{1,3},{4,0},{5,1},{8,4},{9,5},{12,8},{13,9},{14,12},{15,13},... | collective-permute-start | bytes 983048 | tf_op jit(solution)/shard_map/ppermute | solution.py:59
  71.9 12.0 %collective-permute-start.17 = (bf16[640,256]{1,0:T(8,128)(2,1)S(1)}, bf16[640,256]{1,0:T(8,128)(2,1)S(1)}, u32[]{:S(2)}, u32[]{:S(2)}) collective-permute-start(bf16[640,256]{1,0:T(8,128)(2,1)S(1)} %collective-permute-done.16), channel_id=1, source_target_pairs={{0,4},{1,5},{4,8},{5,9},{8,12},{9,13},{12,14},{13,15},{14,10},{15,... | collective-permute-start | bytes 983048 | tf_op jit(solution)/shard_map/ppermute | solution.py:59
  91.2 11.4 %collective-permute-start.23 = (bf16[640,256]{1,0:T(8,128)(2,1)S(1)}, bf16[640,256]{1,0:T(8,128)(2,1)}, u32[]{:S(2)}, u32[]{:S(2)}) collective-permute-start(bf16[640,256]{1,0:T(8,128)(2,1)S(1)} %collective-permute-done.16), channel_id=1, source_target_pairs={{0,1},{1,0},{2,3},{3,2},{4,5},{5,4},{6,7},{7,6},{8,9},{9,8},{10,11... | collective-permute-start | bytes 983048 | tf_op jit(solution)/shard_map/ppermute | solution.py:63
  92.0 10.5 %collective-permute-start.27 = (bf16[640,256]{1,0:T(8,128)(2,1)S(1)}, bf16[640,256]{1,0:T(8,128)(2,1)}, u32[]{:S(2)}, u32[]{:S(2)}) collective-permute-start(bf16[640,256]{1,0:T(8,128)(2,1)S(1)} %collective-permute-done.20), channel_id=1, source_target_pairs={{0,1},{1,0},{2,3},{3,2},{4,5},{5,4},{6,7},{7,6},{8,9},{9,8},{10,11... | collective-permute-start | bytes 983048 | tf_op jit(solution)/shard_map/ppermute | solution.py:63
  92.0 10.5 %collective-permute-start.24 = (bf16[640,256]{1,0:T(8,128)(2,1)S(1)}, bf16[640,256]{1,0:T(8,128)(2,1)S(1)}, u32[]{:S(2)}, u32[]{:S(2)}) collective-permute-start(bf16[640,256]{1,0:T(8,128)(2,1)S(1)} %collective-permute-done.17), channel_id=1, source_target_pairs={{0,1},{1,0},{2,3},{3,2},{4,5},{5,4},{6,7},{7,6},{8,9},{9,8},{10,11... | collective-permute-start | bytes 983048 | tf_op jit(solution)/shard_map/ppermute | solution.py:63
  92.6 10.0 %collective-permute-start.26 = (bf16[640,256]{1,0:T(8,128)(2,1)S(1)}, bf16[640,256]{1,0:T(8,128)(2,1)S(1)}, u32[]{:S(2)}, u32[]{:S(2)}) collective-permute-start(bf16[640,256]{1,0:T(8,128)(2,1)S(1)} %collective-permute-done.21), channel_id=1, source_target_pairs={{0,1},{1,0},{2,3},{3,2},{4,5},{5,4},{6,7},{7,6},{8,9},{9,8},{10,11... | collective-permute-start | bytes 983048 | tf_op jit(solution)/shard_map/ppermute | solution.py:63
  94.0 8.6 %collective-permute-start.25 = (bf16[640,256]{1,0:T(8,128)(2,1)}, bf16[640,256]{1,0:T(8,128)(2,1)S(1)}, u32[]{:S(2)}, u32[]{:S(2)}) collective-permute-start(bf16[640,256]{1,0:T(8,128)(2,1)} %collective-permute-done.18), channel_id=1, source_target_pairs={{0,1},{1,0},{2,3},{3,2},{4,5},{5,4},{6,7},{7,6},{8,9},{9,8},{10,11... | collective-permute-start | bytes 983048 | tf_op jit(solution)/shard_map/ppermute | solution.py:63
  128.2 14.5 %collective-permute-start.36 = (bf16[432,256]{1,0:T(8,128)(2,1)S(1)}, bf16[432,256]{1,0:T(8,128)(2,1)S(1)}, u32[]{:S(2)}, u32[]{:S(2)}) collective-permute-start(bf16[432,256]{1,0:T(8,128)(2,1)S(1)} %get-tuple-element.46), channel_id=1, source_target_pairs={{0,2},{1,3},{4,0},{5,1},{8,4},{9,5},{12,8},{13,9},{14,12},{15,13},... | collective-permute-start | bytes 663560 | tf_op jit(solution)/shard_map/ppermute | solution.py:59
  141.1 15.6 %collective-permute-start.34 = (bf16[432,256]{1,0:T(8,128)(2,1)S(1)}, bf16[432,256]{1,0:T(8,128)(2,1)S(1)}, u32[]{:S(2)}, u32[]{:S(2)}) collective-permute-start(bf16[432,256]{1,0:T(8,128)(2,1)S(1)} %get-tuple-element.45), channel_id=1, source_target_pairs={{0,4},{1,5},{4,8},{5,9},{8,12},{9,13},{12,14},{13,15},{14,10},{15,... | collective-permute-start | bytes 663560 | tf_op jit(solution)/shard_map/ppermute | solution.py:59
  142.9 13.8 %collective-permute-start.37 = (bf16[432,256]{1,0:T(8,128)(2,1)S(1)}, bf16[432,256]{1,0:T(8,128)(2,1)S(1)}, u32[]{:S(2)}, u32[]{:S(2)}) collective-permute-start(bf16[432,256]{1,0:T(8,128)(2,1)S(1)} %fusion.1), channel_id=1, source_target_pairs={{0,2},{1,3},{4,0},{5,1},{8,4},{9,5},{12,8},{13,9},{14,12},{15,13},... | collective-permute-start | bytes 663560 | tf_op jit(solution)/shard_map/ppermute | solution.py:59
  (38 other events, 410.6 us)

commit v4 on v3

--- a/solution.py
+++ b/solution.py
@@ -46,7 +46,9 @@
     place_of = behind[:, device // 2] + chips * (device[:, None] % 2 != device[None, :] % 2)
     if chips > 8:
         place_of = np.broadcast_to(device, (peers, peers))
-    return np.concatenate([place_of, behind, device[:, None]], axis=1).astype(np.int32)
+    half = chips // 2
+    turn = np.where(behind >= half, 2 * (behind - half), 2 * (half - 1 - behind) + 1)
+    return np.concatenate([place_of, behind, turn, device[:, None]], axis=1).astype(np.int32)
 
 
 def ring_step(x, peers, step):
@@ -99,12 +101,14 @@
         return [t[None] for t in mine + [swap_cores(t, self.peers) for t in held]]
 
 
-def scatter_ring(keep, give, peers):
+def scatter_ring(keep, give, peers, gates):
     chips = peers // 2
-    other = swap_cores(give, peers)
+    half = chips // 2
+    other = [swap_cores(t, peers) for t in give]
 
     def term(k):
-        return keep[k] + other[k].astype(F32)
+        pair = other[k - half][0] if k >= half else other[half - 1 - k][1]
+        return keep[k] + pair.astype(F32)
 
     ups, downs = chips // 2, (chips - 1) // 2
     total = term(0)
@@ -114,19 +118,23 @@
             part = term((-step * hop) % chips)
             if held is not None:
                 part = part + held.astype(F32)
-            held = ring_step(part.astype(BF16), peers, step)
+            part = part.astype(BF16)
+            if count - hop < len(gates) and gates[count - hop] is not None:
+                part = lax.optimization_barrier((part, gates[count - hop]))[0]
+            held = ring_step(part, peers, step)
         if held is not None:
             total = total + held.astype(F32)
     return total
 
 
-def call(body, out_shape, in_specs, scratch=(), cost=2, name=None, out_specs=None):
+def call(body, out_shape, in_specs, scratch=(), cost=2, name=None, out_specs=None, aliases=None):
     return pl.pallas_call(
         body,
         out_shape=out_shape,
         in_specs=in_specs,
         out_specs=out_specs or jax.tree.map(lambda _: VMEM, out_shape),
         scratch_shapes=list(scratch),
+        input_output_aliases=aliases or {},
         compiler_params=pltpu.CompilerParams(vmem_limit_bytes=VMEM_LIMIT),
         cost_estimate=pl.CostEstimate(flops=cost * 10**9, bytes_accessed=0, transcendentals=0),
         name=name,
@@ -300,7 +308,7 @@
         add_cell(pads[0], cell(facing))
 
 
-def windows(cells, halo, cols, bricks):
+def windows(cells, halo, cols, out, sems, bricks):
     row = lax.broadcasted_iota(jnp.int32, (8, C), 0)
 
     def step(k, _):
@@ -317,6 +325,15 @@
                 block = jnp.concatenate(shifted[l][j : j + 8], axis=0).astype(BF16)
                 at = (3 * j + l) * C
                 cols[k, :, at : at + C] = block
+        pltpu.make_async_copy(cols.at[k], out.at[k], sems.at[k]).start()
+        return 0
+
+    lax.fori_loop(0, bricks * 10, step, 0)
+
+
+def wait_windows(cols, out, sems, bricks):
+    def step(k, _):
+        pltpu.make_async_copy(cols.at[k], out.at[k], sems.at[k]).wait()
         return 0
 
     lax.fori_loop(0, bricks * 10, step, 0)
@@ -333,15 +350,21 @@
     return copies
 
 
-def pad_body(slots, peers, count, *refs):
-    recv, table, own_ref = refs[:3]
-    parts = refs[3 : 3 + count]
-    cols, codes_ref, served_ref = refs[-9:-6]
-    cells, halo, share, codes, sems, codes_sem = refs[-6:]
+def weight_grad_body(slots, factor, peers, count, *refs):
+    recv, table, own_ref, cot_ref = refs[:4]
+    parts = refs[4 : 4 + count]
+    keep_ref = refs[5 + count]
+    give_refs = refs[6 + count : 6 + count + peers // 4]
+    out_cols, codes_ref, served_ref = refs[-15:-12]
+    cells, halo, share, cols, sums, narrow, turned, codes = refs[-12:-4]
+    sems, cols_sems, codes_sem, out_sems = refs[-4:]
     bricks = own_ref.shape[0] // 512
-    me = table[peers + peers // 2]
+    me = table[2 * peers]
     copies = fetch(parts, share, sems)
     start_padded(own_ref, cells, halo, bricks)
+    for part in range(bricks * 2):
+        at = slice(part * 256, part * 256 + 256)
+        turned[:, at] = cot_ref[at, :].astype(F32).T.astype(BF16)
     for copy in copies:
         copy.wait()
     for k in range(peers):
@@ -360,18 +383,9 @@
             code = codes[at, me * slots + safe - sender * slots]
             kind = tuple(abs(t) for t in e)
             place(kind, e, slot >= 0, at, code // 6, brick, share, cells, halo)
-    windows(cells, halo, cols, bricks)
-
-
-def weight_grad_body(factor, peers, *refs):
-    table, cols, cot_ref = refs[:3]
-    keep_ref, give_ref, sums, turned, sem = refs[-5:]
-    bricks = cot_ref.shape[0] // 512
+    windows(cells, halo, cols, out_cols, cols_sems, bricks)
+
     rows = 27 * C // peers
-    mine = table[peers + peers // 2] % 2
-    for part in range(bricks * 2):
-        at = slice(part * 256, part * 256 + 256)
-        turned[:, at] = cot_ref[at, :].astype(F32).T.astype(BF16)
     for tap in range(27):
         i, jl = divmod(tap, 9)
         total = None
@@ -386,44 +400,89 @@
             owner = start // rows
             stop = min((tap + 1) * C, (owner + 1) * rows)
             piece = total[start - tap * C : stop - tap * C]
-            bucket = jnp.bitwise_xor(mine, owner % 2)
+            bucket = jnp.bitwise_xor(me % 2, owner % 2)
+            behind = table[peers + owner // 2]
             where = slice(start - owner * rows, stop - owner * rows)
-            sums[bucket, table[peers + owner // 2], where, :] = piece
+            sums[bucket, behind, where, :] = piece
+            narrow[bucket, behind, where, :] = piece.astype(BF16)
             start = stop
-    keep_copy = pltpu.make_async_copy(sums.at[0], keep_ref, sem.at[0])
-    keep_copy.start()
-
-    def narrow(k, _):
-        give_ref[k] = sums[1, k].astype(BF16)
-        return 0
-
-    lax.fori_loop(0, sums.shape[1], narrow, 0)
-    keep_copy.wait()
-
-
-def tap_sum(cols, weight_ref, brick):
-    total = None
-    for i in range(3):
-        left = cols[brick * 10 + i : brick * 10 + i + 8].reshape(512, 9 * C)
-        right = weight_ref[i * 9 * C : (i + 1) * 9 * C, :]
-        term = jnp.dot(left, right, preferred_element_type=F32)
-        total = term if total is None else total + term
-    return total
-
-
-def mix_body(cols, weight_ref, x_ref, out_ref):
-    for brick in range(x_ref.shape[0] // 512):
+            if stop == (owner + 1) * rows:
+
+                @pl.when(bucket == 0)
+                def _():
+                    pltpu.make_async_copy(
+                        sums.at[0, behind], keep_ref.at[behind], out_sems.at[0, behind]
+                    ).start()
+
+                turn = table[peers + peers // 2 + owner // 2]
+                for hop, give_ref in enumerate(give_refs):
+
+                    @pl.when((bucket == 1) & (turn // 2 == hop))
+                    def _():
+                        pltpu.make_async_copy(
+                            narrow.at[1, behind], give_ref.at[turn % 2], out_sems.at[1, turn]
+                        ).start()
+
+    for k in range(peers // 2):
+        pltpu.make_async_copy(sums.at[0, k], keep_ref.at[k], out_sems.at[0, k]).wait()
+        pltpu.make_async_copy(narrow.at[1, k], give_refs[k // 2].at[k % 2], out_sems.at[1, k]).wait()
+    wait_windows(cols, out_cols, cols_sems, bricks)
+
+
+GROUP = 3 * C
+
+
+def start_stream(cols_ref, first, cols, weight_ref, weight, sems):
+    copies = []
+    planes = cols.shape[0]
+    for g in range(3):
+        lanes = pl.ds(g * GROUP, GROUP)
+        group = [
+            pltpu.make_async_copy(
+                cols_ref.at[pl.ds(first, planes), :, lanes], cols.at[:, :, lanes], sems.at[g, 3]
+            )
+        ]
+        for i in range(3):
+            at = pl.ds((i * 3 + g) * GROUP, GROUP)
+            group.append(pltpu.make_async_copy(weight_ref.at[at], weight.at[at], sems.at[g, i]))
+        copies.append(group)
+    for group in copies:
+        for copy in group:
+            copy.start()
+    return copies
+
+
+def tap_sum(copies, cols, weight):
+    bricks = cols.shape[0] // 10
+    totals = [None] * bricks
+    for g in range(3):
+        for copy in copies[g]:
+            copy.wait()
+        for brick in range(bricks):
+            for i in range(3):
+                at = brick * 10 + i
+                left = cols[at : at + 8, :, g * GROUP : g * GROUP + GROUP].reshape(512, GROUP)
+                right = weight[(i * 3 + g) * GROUP : (i * 3 + g + 1) * GROUP, :]
+                term = jnp.dot(left, right, preferred_element_type=F32)
+                totals[brick] = term if totals[brick] is None else totals[brick] + term
+    return totals
+
+
+def mix_body(cols_ref, weight_ref, x_ref, out_ref, cols, weight, sems):
+    copies = start_stream(cols_ref, 0, cols, weight_ref, weight, sems)
+    for brick, total in enumerate(tap_sum(copies, cols, weight)):
         at = slice(brick * 512, brick * 512 + 512)
-        out_ref[at, :] = (x_ref[at, :].astype(F32) + tap_sum(cols, weight_ref, brick)).astype(BF16)
-
-
-def input_grad_body(slots, peers, here, count, *refs):
-    served, send, table, cot_ref, weight_ref, x_ref, gain_ref = refs[:7]
-    parts = refs[7 : 7 + count]
-    out_ref, cells, halo, cols, share, sems = refs[7 + count :]
-    me = table[peers + peers // 2]
+        out_ref[at, :] = (x_ref[at, :].astype(F32) + total).astype(BF16)
+
+
+def cot_pad_body(slots, peers, count, *refs):
+    served, send, table, cot_ref = refs[:4]
+    parts = refs[4 : 4 + count]
+    out_cols, cells, halo, cols, share, sems, cols_sems = refs[4 + count :]
+    bricks = cot_ref.shape[0] // 512
+    me = table[2 * peers]
     copies = fetch(parts, share, sems)
-    start_padded(cot_ref, cells, halo, 1)
+    start_padded(cot_ref, cells, halo, bricks)
     for copy in copies:
         copy.wait()
 
@@ -432,9 +491,10 @@
         at = table[receiver]
         info = served[at, me * slots + k - receiver * slots]
 
-        @pl.when((info > 0) & (send[0, k] // 6 == here))
+        @pl.when(info > 0)
         def _():
             entry = info - 1
+            brick = send[0, k] // 6
             number = 25 - entry % 26
             tap = jnp.where(number >= 13, number + 1, number)
             e = (tap // 9 - 1, (tap // 3) % 3 - 1, tap % 3 - 1)
@@ -446,22 +506,33 @@
 
                 @pl.when(match)
                 def _():
-                    place(kind, e, None, at, entry // 26, 0, share, cells, halo)
+                    place(kind, e, None, at, entry // 26, brick, share, cells, halo)
 
         return 0
 
     lax.fori_loop(0, send.shape[1], one, 0)
-    windows(cells, halo, cols, 1)
-    grad = tap_sum(cols, weight_ref, 0)
-    x = x_ref[...].astype(F32)
+    windows(cells, halo, cols, out_cols, cols_sems, bricks)
+    wait_windows(cols, out_cols, cols_sems, bricks)
+
+
+def input_grad_body(here, *refs):
+    cols_ref, weight_ref, cot_ref, x_ref, gain_ref = refs[:5]
+    out_ref, cols, weight, rows, sems, row_sem = refs[-6:]
+    copies = start_stream(cols_ref, here * 10, cols, weight_ref, weight, sems)
+    at = slice(here * 512, here * 512 + 512)
+    x = x_ref[at, :].astype(F32)
     gain = gain_ref[...]
     inverse = lax.rsqrt(jnp.mean(x * x, axis=-1, keepdims=True) + 1e-6)
+    (grad,) = tap_sum(copies, cols, weight)
     unit = x * inverse
     v = unit * gain
     gate = 1.0 / (1.0 + jnp.exp(-v))
     grad = grad * (gate * (1.0 + v * (1.0 - gate))) * gain
     grad = inverse * (grad - unit * jnp.mean(grad * unit, axis=-1, keepdims=True))
-    out_ref[...] = (cot_ref[...].astype(F32) + grad).astype(BF16)
+    rows[...] = (cot_ref[at, :].astype(F32) + grad).astype(BF16)
+    copy = pltpu.make_async_copy(rows, out_ref.at[pl.ds(here * 512, 512)], row_sem.at[0])
+    copy.start()
+    copy.wait()
 
 
 def local(features, norm_gain, conv_weight, recv_slot, send_face, cotangent):
@@ -494,11 +565,6 @@
         [stage],
         name="norm",
     )(recv_slot, send_face, features, gain)
-    hidden_ring = RingGather(share, peers, 1)
-    for way in (0, 0, 0, 0, 1, 1, 1):
-        hidden_ring.go(way)
-    hidden_parts = hidden_ring.places()
-
     cot_share = call(
         extract_body,
         sds((bricks * ROWS, channels), BF16),
@@ -508,7 +574,16 @@
     )(cotangent)
     turned = conv_weight.reshape(27, channels, channels)[::-1].transpose(0, 2, 1)
     turned = turned.reshape(27 * channels, channels)
-    cot_share, turned = lax.optimization_barrier((cot_share, turned))
+
+    hidden_ring = RingGather(share, peers, 1)
+    hidden_ring.go(0)
+    hidden_ring.go(1)
+    hidden_ring.go(0, (cot_share, turned))
+    hidden_ring.go(1, (cot_share, turned))
+    for way in (0, 1, 0):
+        hidden_ring.go(way)
+    hidden_parts = hidden_ring.places()
+
     cot_ring = RingGather(cot_share, peers, -1)
     cot_ring.go(0, hidden_ring.last(1))
     first = cot_ring.last(0)
@@ -517,75 +592,93 @@
 
     count = len(hidden_parts)
     rows = 27 * channels // peers
-    cols, _, served = call(
-        functools.partial(pad_body, slots, peers, count),
+    chips = peers // 2
+    keep, *give, cols, _, served = call(
+        functools.partial(weight_grad_body, slots, factor, peers, count),
         (
+            sds((chips, rows, channels), F32),
+            *[sds((2, rows, channels), BF16)] * (chips // 2),
             sds(cols_shape(bricks), BF16),
             sds((peers, channels), jnp.int32),
             sds((peers, channels), jnp.int32),
         ),
-        [SMEM] * 2 + [VMEM] + [HBM] * (count + 1),
+        [SMEM] * 2 + [VMEM] * 2 + [HBM] * (count + 1),
         padded(bricks)
         + [
             pltpu.VMEM((peers, bricks * ROWS + NOTES, channels), BF16),
+            pltpu.VMEM(cols_shape(bricks), BF16),
+            pltpu.VMEM((2, chips, rows, channels), F32),
+            pltpu.VMEM((2, chips, rows, channels), BF16),
+            pltpu.VMEM((channels, per_device), BF16),
             pltpu.SMEM((peers, channels), jnp.int32),
             pltpu.SemaphoreType.DMA((count,)),
+            pltpu.SemaphoreType.DMA((bricks * 10,)),
             pltpu.SemaphoreType.DMA((1,)),
+            pltpu.SemaphoreType.DMA((2, chips)),
         ],
-        cost=6,
-        name="pad",
-    )(recv_slot, table, hidden, *hidden_parts, first)
+        cost=9,
+        name="weight_grad",
+        out_specs=(*[HBM] * (2 + chips // 2), VMEM, VMEM),
+    )(recv_slot, table, hidden, cotangent, *hidden_parts, first)
+
     cot_ring.go(1, cols)
     cot_ring.go(0, cols)
-    keep, give = call(
-        functools.partial(weight_grad_body, factor, peers),
-        (
-            sds((peers // 2, rows, channels), F32),
-            sds((peers // 2, rows, channels), BF16),
-        ),
-        [SMEM] + [VMEM] * 2,
-        [
-            pltpu.VMEM((2, peers // 2, rows, channels), F32),
-            pltpu.VMEM((channels, per_device), BF16),
-            pltpu.SemaphoreType.DMA((1,)),
-        ],
-        cost=6,
-        name="weight_grad",
-        out_specs=(ANY, VMEM),
-    )(table, cols, cotangent)
+    third = (cot_ring.last(0), cot_ring.last(1))
+    weight_scratch = [
+        pltpu.VMEM((27 * channels, channels), BF16),
+        pltpu.SemaphoreType.DMA((3, 4)),
+    ]
     mixed = call(
         mix_body,
         sds((per_device, channels), BF16),
-        [VMEM, VMEM, VMEM],
-        cost=5,
+        [HBM, HBM, VMEM],
+        [pltpu.VMEM(cols_shape(bricks), BF16)] + weight_scratch,
+        cost=6,
         name="mix",
     )(cols, conv_weight, features)
-
-    cot_ring.go(1, give)
-    cot_ring.go(0, give)
+    cot_ring.go(1)
+    cot_ring.go(0)
+    fourth = (cot_ring.last(0), cot_ring.last(1))
     cot_parts = cot_ring.places(cols)
-    give = lax.optimization_barrier((give, mixed, *cot_parts))[0]
-    grad_weight = scatter_ring(keep, give, peers)
+
+    cot_cols = call(
+        functools.partial(cot_pad_body, slots, peers, count),
+        sds(cols_shape(bricks), BF16),
+        [SMEM] * 3 + [VMEM] + [HBM] * count,
+        padded(bricks)
+        + [
+            pltpu.VMEM(cols_shape(bricks), BF16),
+            pltpu.VMEM((peers, bricks * ROWS, channels), BF16),
+            pltpu.SemaphoreType.DMA((count,)),
+            pltpu.SemaphoreType.DMA((bricks * 10,)),
+        ],
+        cost=7,
+        name="cot_pad",
+        out_specs=HBM,
+    )(served, send_face, table, cotangent, *cot_parts)
 
     grads = []
     for brick in range(bricks):
-        at = slice(brick * 512, brick * 512 + 512)
         grads.append(
             call(
-                functools.partial(input_grad_body, slots, peers, brick, count),
-                sds((512, channels), BF16),
-                [SMEM] * 3 + [VMEM] * 4 + [HBM] * count,
-                padded(1)
-                + [
-                    pltpu.VMEM(cols_shape(1), BF16),
-                    pltpu.VMEM((peers, bricks * ROWS, channels), BF16),
-                    pltpu.SemaphoreType.DMA((count,)),
-                ],
-                cost=8,
+                functools.partial(input_grad_body, brick),
+                sds((per_device, channels), BF16),
+                [HBM, HBM, VMEM, VMEM, VMEM] + [HBM] * len(grads[-1:]),
+                [pltpu.VMEM(cols_shape(1), BF16)]
+                + weight_scratch[:1]
+                + [pltpu.VMEM((512, channels), BF16)]
+                + weight_scratch[1:]
+                + [pltpu.SemaphoreType.DMA((1,))],
+                cost=5,
                 name="input_grad_" + str(brick),
-            )(served, send_face, table, cotangent[at], turned, features[at], gain, *cot_parts)
+                out_specs=HBM,
+                aliases={5: 0} if grads else None,
+            )(cot_cols, turned, cotangent, features, gain, *grads[-1:])
         )
-    return (mixed, jnp.concatenate(grads, axis=0), grad_weight)
+    gates = (None, fourth, cot_cols, grads[0])
+    give = [lax.optimization_barrier((t, third, mixed))[0] for t in give]
+    grad_weight = scatter_ring(keep, give, peers, gates)
+    return (mixed, grads[-1], grad_weight)
 
 
 def solution(mesh):

time: 159 us -> 132 us (0.83)
  waiting for transfers between devices: 59.3 us -> 38.3 us
  local copies, waits for them, and re-layouts: 12 us -> 8.69 us
  starting transfers between devices: 26.9 us -> 29.8 us
  Pallas kernels: 55.3 us -> 52.7 us
  other arithmetic: 3.16 us -> 1.38 us
    ppermute x21, waiting for transfers between devices: 55.9 us -> 38.2 us  [ring_step(): return lax.ppermute(x, 'morton', pairs)]
    ppermute x17 -> x20, waiting for transfers between devices: 3.36 us -> 0.05 us  [swap_cores(): return lax.ppermute(x, 'morton', [(m, m ^ 1) for m in range(peers)])]
    pallas_call x5, Pallas kernels: 48.8 us -> 46.2 us  [the longest x2 14.2 us: local(): call(functools.partial(input_grad_body, brick), sds((per_device, channels...]
    ppermute x21, starting transfers between devices: 24.2 us -> 26.3 us  [ring_step(): return lax.ppermute(x, 'morton', pairs)]
    concatenate x1 -> x0, other arithmetic: 1.78 us -> none  [local(): return (mixed, jnp.concatenate(grads, axis=0), grad_weight)]
    slice x2 -> x0, local copies, waits for them, and re-layouts: 1.74 us -> none  [the longest x1 0.88 us: local(): cotangent[at]]
    unnamed x48 -> x62, local copies, waits for them, and re-layouts: 2.46 us -> 0.82 us
    ppermute x17 -> x20, starting transfers between devices: 2.75 us -> 3.5 us  [swap_cores(): return lax.ppermute(x, 'morton', [(m, m ^ 1) for m in range(peers)])]
  transfers between devices with their start and end apart: 38 -> 41, of which waited for: 12 -> 10; matrix products, arithmetic and copies ran while one was open for 7% -> 6% of each run, Pallas kernels for 32% -> 37%
where the time goes in v4:
time: 132 us
  Pallas kernels  52.7 us (40%)
  waiting for transfers between devices  38.3 us (29%)
  starting transfers between devices  29.8 us (23%)
  local copies, waits for them, and re-layouts  8.69 us (7%)
  other arithmetic  1.38 us (1%)
    ppermute x21, waiting for transfers between devices, ring_step(): return lax.ppermute(x, 'morton', pairs)  38.2 us
    ppermute x21, starting transfers between devices, ring_step(): return lax.ppermute(x, 'morton', pairs)  26.3 us
    pallas_call x2, Pallas kernels, local(): call(functools.partial(input_grad_body, brick), sds((per_device, channels...  14.2 us
    pallas_call x1, Pallas kernels, local(): call(functools.partial(weight_grad_body, slots, factor, peers, count), (s...  12.7 us
    pallas_call x1, Pallas kernels, local(): call(functools.partial(cot_pad_body, slots, peers, count), sds(cols_shape...  11.6 us
    pallas_call x1, Pallas kernels, local(): call(mix_body, sds((per_device, channels), BF16), [HBM, HBM, VMEM], [pltp...  7.69 us
    reshape x1, local copies, waits for them, and re-layouts, local(): conv_weight.reshape(27, channels, channels)[::-1].transpose(0, 2, 1)  4.44 us
    pallas_call x1, Pallas kernels, local(): call(norm_body, (sds((per_device, channels), BF16), sds((bricks * ROWS +...  4.26 us
  transfers between devices with their start and end apart: 41, of which 10 were waited for; matrix products, arithmetic and copies ran while one was open for 6% of the time, Pallas kernels for 37%

profile of v4, /device:TPU:0, one launch (start us, length us, event | category | flops | bytes accessed | tf_op | source)
XLA Modules:
  0.0 132.0 jit_solution(1505271913752006202)
XLA Ops:
  0.6 4.3 %norm.1 = (bf16[1024,256]{1,0:T(8,128)(2,1)}, bf16[656,256]{1,0:T(8,128)(2,1)}) custom-call(s32[2,26]{1,0:T(2,128)} %refs_0_.1, s32[1,64]{1,0:T(1,128)} %refs_1_.1, bf16[1024,256]{1,0:T(8,128)(2,1)} %refs_3_.7, f32[1,256]{1,0:T(1,128)} %bitcast.96), custom_call_target="tpu_custom_call" | custom-call | flops 2000000000 | tf_op jit(solution)/shard_map/norm/pallas_call | solution.py:561
  4.9 3.0 %collective-permute-start = (bf16[656,256]{1,0:T(8,128)(2,1)}, bf16[656,256]{1,0:T(8,128)(2,1)}, u32[]{:S(2)}, u32[]{:S(2)}) collective-permute-start(bf16[656,256]{1,0:T(8,128)(2,1)} %get-tuple-element.34), channel_id=1, source_target_pairs={{0,4},{1,5},{4,8},{5,9},{8,12},{9,13},{12,14},{13,15},{14,10},{15,... | collective-permute-start | bytes 1007624 | tf_op jit(solution)/shard_map/ppermute | solution.py:61
  7.9 4.4 %copy.11 = bf16[27,256,256]{1,2,0:T(8,128)(2,1)S(1)} copy(bf16[27,256,256]{2,1,0:T(8,128)(2,1)} %bitcast.67) | data formatting | bytes 7077888 | tf_op jit(solution)/shard_map/reshape | solution.py:575
  12.4 2.2 %rev.3 = bf16[27,256,256]{1,2,0:T(8,128)(2,1)} reverse(bf16[27,256,256]{1,2,0:T(8,128)(2,1)S(1)} %copy.11), dimensions={0} | reverse | bytes 7077888 | tf_op jit(solution)/shard_map/rev | solution.py:575
  14.6 2.3 %extract.1 = bf16[640,256]{1,0:T(8,128)(2,1)} custom-call(bf16[1024,256]{1,0:T(8,128)(2,1)} %refs_2_.3), custom_call_target="tpu_custom_call" | custom-call | flops 2000000000 | tf_op jit(solution)/shard_map/extract/pallas_call | solution.py:568
  16.9 2.0 %collective-permute-start.1 = (bf16[656,256]{1,0:T(8,128)(2,1)}, bf16[656,256]{1,0:T(8,128)(2,1)S(1)}, u32[]{:S(2)}, u32[]{:S(2)}) collective-permute-start(bf16[656,256]{1,0:T(8,128)(2,1)} %collective-permute-done), channel_id=1, source_target_pairs={{0,4},{1,5},{4,8},{5,9},{8,12},{9,13},{12,14},{13,15},{14,10},{15,... | collective-permute-start | bytes 1007624 | tf_op jit(solution)/shard_map/ppermute | solution.py:61
  18.9 7.5 %collective-permute-done.1 = bf16[656,256]{1,0:T(8,128)(2,1)S(1)} collective-permute-done((bf16[656,256]{1,0:T(8,128)(2,1)}, bf16[656,256]{1,0:T(8,128)(2,1)S(1)}, u32[]{:S(2)}, u32[]{:S(2)}) %collective-permute-start.1) | collective-permute-done | bytes 335904 | tf_op jit(solution)/shard_map/ppermute | solution.py:61
  26.4 1.7 %collective-permute-start.2 = (bf16[656,256]{1,0:T(8,128)(2,1)S(1)}, bf16[656,256]{1,0:T(8,128)(2,1)S(1)}, u32[]{:S(2)}, u32[]{:S(2)}) collective-permute-start(bf16[656,256]{1,0:T(8,128)(2,1)S(1)} %collective-permute-done.1), channel_id=1, source_target_pairs={{0,4},{1,5},{4,8},{5,9},{8,12},{9,13},{12,14},{13,15},{14,10},{15,... | collective-permute-start | bytes 1007624 | tf_op jit(solution)/shard_map/ppermute | solution.py:61
  29.0 5.8 %collective-permute-done.2 = bf16[656,256]{1,0:T(8,128)(2,1)S(1)} collective-permute-done((bf16[656,256]{1,0:T(8,128)(2,1)S(1)}, bf16[656,256]{1,0:T(8,128)(2,1)S(1)}, u32[]{:S(2)}, u32[]{:S(2)}) %collective-permute-start.2) | collective-permute-done | bytes 335904 | tf_op jit(solution)/shard_map/ppermute | solution.py:61
  34.9 1.4 %collective-permute-start.3 = (bf16[656,256]{1,0:T(8,128)(2,1)S(1)}, bf16[656,256]{1,0:T(8,128)(2,1)S(1)}, u32[]{:S(2)}, u32[]{:S(2)}) collective-permute-start(bf16[656,256]{1,0:T(8,128)(2,1)S(1)} %collective-permute-done.2), channel_id=1, source_target_pairs={{0,4},{1,5},{4,8},{5,9},{8,12},{9,13},{12,14},{13,15},{14,10},{15,... | collective-permute-start | bytes 1007624 | tf_op jit(solution)/shard_map/ppermute | solution.py:61
  36.9 2.1 %collective-permute-done.6 = bf16[656,256]{1,0:T(8,128)(2,1)S(1)} collective-permute-done((bf16[656,256]{1,0:T(8,128)(2,1)S(1)}, bf16[656,256]{1,0:T(8,128)(2,1)S(1)}, u32[]{:S(2)}, u32[]{:S(2)}) %collective-permute-start.6) | collective-permute-done | bytes 335904 | tf_op jit(solution)/shard_map/ppermute | solution.py:61
  39.0 3.4 %collective-permute-done.3 = bf16[656,256]{1,0:T(8,128)(2,1)S(1)} collective-permute-done((bf16[656,256]{1,0:T(8,128)(2,1)S(1)}, bf16[656,256]{1,0:T(8,128)(2,1)S(1)}, u32[]{:S(2)}, u32[]{:S(2)}) %collective-permute-start.3) | collective-permute-done | bytes 335904 | tf_op jit(solution)/shard_map/ppermute | solution.py:61
  44.8 8.1 %collective-permute-done.15.refs_20_ = bf16[640,256]{1,0:T(8,128)(2,1)} collective-permute-done((bf16[640,256]{1,0:T(8,128)(2,1)}, bf16[640,256]{1,0:T(8,128)(2,1)}, u32[]{:S(2)}, u32[]{:S(2)}) %collective-permute-start.15) | collective-permute-done | bytes 327712 | tf_op jit(solution)/shard_map/ppermute | solution.py:61
  55.0 12.7 %weight_grad.1 = (f32[8,432,256]{2,1,0:T(8,128)}, bf16[2,432,256]{2,1,0:T(8,128)(2,1)}, bf16[2,432,256]{2,1,0:T(8,128)(2,1)}, bf16[2,432,256]{2,1,0:T(8,128)(2,1...) custom-call(s32[2,26]{1,0:T(2,128)} %refs_0_.1, ...), custom_call_target="tpu_custom_call" | custom-call | flops 8999999488 | tf_op jit(solution)/shard_map/weight_grad/pallas_call | solution.py:596
  69.8 7.7 %mix.1 = bf16[1024,256]{1,0:T(8,128)(2,1)} custom-call(bf16[20,64,2304]{2,1,0:T(8,128)(2,1)} %get-tuple-element.38.cols_ref, bf16[6912,256]{1,0:T(8,128)(2,1)} %weight_ref.1, bf16[1024,256]{1,0:T(8,128)(2,1)} %refs_3_.7), custom_call_target="tpu_custom_call" | custom-call | flops 6000000000 | tf_op jit(solution)/shard_map/mix/pallas_call | solution.py:631
  78.2 1.6 %collective-permute-start.21 = (bf16[640,256]{1,0:T(8,128)(2,1)S(1)}, bf16[640,256]{1,0:T(8,128)(2,1)S(1)}, u32[]{:S(2)}, u32[]{:S(2)}) collective-permute-start(bf16[640,256]{1,0:T(8,128)(2,1)S(1)} %collective-permute-done.20), channel_id=1, source_target_pairs={{0,2},{1,3},{4,0},{5,1},{8,4},{9,5},{12,8},{13,9},{14,12},{15,13},... | collective-permute-start | bytes 983048 | tf_op jit(solution)/shard_map/ppermute | solution.py:61
  81.0 6.9 %collective-permute-done.21 = bf16[640,256]{1,0:T(8,128)(2,1)S(1)} collective-permute-done((bf16[640,256]{1,0:T(8,128)(2,1)S(1)}, bf16[640,256]{1,0:T(8,128)(2,1)S(1)}, u32[]{:S(2)}, u32[]{:S(2)}) %collective-permute-start.21) | collective-permute-done | bytes 327712 | tf_op jit(solution)/shard_map/ppermute | solution.py:61
  89.2 1.6 %collective-permute-start.38 = (bf16[432,256]{1,0:T(8,128)(2,1)S(1)}, bf16[432,256]{1,0:T(8,128)(2,1)S(1)}, u32[]{:S(2)}, u32[]{:S(2)}) collective-permute-start(bf16[432,256]{1,0:T(8,128)(2,1)S(1)} %get-tuple-element.68), channel_id=1, source_target_pairs={{0,2},{1,3},{4,0},{5,1},{8,4},{9,5},{12,8},{13,9},{14,12},{15,13},... | collective-permute-start | bytes 663560 | tf_op jit(solution)/shard_map/ppermute | solution.py:61
  91.4 3.0 %collective-permute-done.34 = bf16[432,256]{1,0:T(8,128)(2,1)S(1)} collective-permute-done((bf16[432,256]{1,0:T(8,128)(2,1)S(1)}, bf16[432,256]{1,0:T(8,128)(2,1)S(1)}, u32[]{:S(2)}, u32[]{:S(2)}) %collective-permute-start.34) | collective-permute-done | bytes 221216 | tf_op jit(solution)/shard_map/ppermute | solution.py:61
  99.2 11.6 %cot_pad.1.refs_0_ = bf16[20,64,2304]{2,1,0:T(8,128)(2,1)} custom-call(s32[16,256]{1,0:T(8,128)} %get-tuple-element.39.refs_0_, s32[1,64]{1,0:T(1,128)} %refs_1_.1, s32[33]{0:T(128)} %dynamic-slice_bitcast_fusion.refs_1_.refs_2_, bf16[1024,256]{1,0:T(8,128)(2,1)} %refs_2_.3, bf16[1,640,256]{2,1,0:T(8,128)(2,1)} %bitcast.81, bf16[1,640,256]{2,1,0:T(8,128)(2,1)} %bitcast.83, ...), custom_call_target="tpu_custom_call" | custom-call | flops 7000000000 | tf_op jit(solution)/shard_map/cot_pad/pallas_call | solution.py:644
  111.0 3.6 %collective-permute-start.36 = (bf16[432,256]{1,0:T(8,128)(2,1)S(1)}, bf16[432,256]{1,0:T(8,128)(2,1)S(1)}, u32[]{:S(2)}, u32[]{:S(2)}) collective-permute-start(bf16[432,256]{1,0:T(8,128)(2,1)S(1)} %get-tuple-element.59), channel_id=1, source_target_pairs={{0,4},{1,5},{4,8},{5,9},{8,12},{9,13},{12,14},{13,15},{14,10},{15,... | collective-permute-start | bytes 663560 | tf_op jit(solution)/shard_map/ppermute | solution.py:61
  114.6 7.1 %input_grad_0.1.refs_5_ = bf16[1024,256]{1,0:T(8,128)(2,1)} custom-call(bf16[20,64,2304]{2,1,0:T(8,128)(2,1)} %cot_pad.1.refs_0_, bf16[6912,256]{1,0:T(8,128)(2,1)} %bitcast.68, bf16[1024,256]{1,0:T(8,128)(2,1)} %refs_2_.3, bf16[1024,256]{1,0:T(8,128)(2,1)} %refs_3_.7, f32[1,256]{1,0:T(1,128)} %bitcast.97), custom_call_target="tpu_custom_call" | custom-call | flops 5000000000 | tf_op jit(solution)/shard_map/input_grad_0/pallas_call | solution.py:663
  121.9 2.0 %collective-permute-start.37 = (bf16[432,256]{1,0:T(8,128)(2,1)S(1)}, bf16[432,256]{1,0:T(8,128)(2,1)S(1)}, u32[]{:S(2)}, u32[]{:S(2)}) collective-permute-start(bf16[432,256]{1,0:T(8,128)(2,1)S(1)} %fusion.4), channel_id=1, source_target_pairs={{0,4},{1,5},{4,8},{5,9},{8,12},{9,13},{12,14},{13,15},{14,10},{15,... | collective-permute-start | bytes 663560 | tf_op jit(solution)/shard_map/ppermute | solution.py:61
  124.0 7.1 %input_grad_1.1 = bf16[1024,256]{1,0:T(8,128)(2,1)} custom-call(bf16[20,64,2304]{2,1,0:T(8,128)(2,1)} %cot_pad.1.refs_0_, bf16[6912,256]{1,0:T(8,128)(2,1)} %bitcast.69, bf16[1024,256]{1,0:T(8,128)(2,1)} %refs_2_.3, bf16[1024,256]{1,0:T(8,128)(2,1)} %refs_3_.7, f32[1,256]{1,0:T(1,128)} %bitcast.98, ...), custom_call_target="tpu_custom_call", output_to_operand_aliasing={{}: (5, {})} | custom-call | flops 5000000000 | tf_op jit(solution)/shard_map/input_grad_1/pallas_call | solution.py:663
  (135 shorter events, 17.6 us)
Async XLA Ops:
  4.9 12.0 %collective-permute-start = (bf16[656,256]{1,0:T(8,128)(2,1)}, bf16[656,256]{1,0:T(8,128)(2,1)}, u32[]{:S(2)}, u32[]{:S(2)}) collective-permute-start(bf16[656,256]{1,0:T(8,128)(2,1)} %get-tuple-element.34), channel_id=1, source_target_pairs={{0,4},{1,5},{4,8},{5,9},{8,12},{9,13},{12,14},{13,15},{14,10},{15,... | collective-permute-start | bytes 1007624 | tf_op jit(solution)/shard_map/ppermute | solution.py:61
  7.9 11.0 %collective-permute-start.4 = (bf16[656,256]{1,0:T(8,128)(2,1)}, bf16[656,256]{1,0:T(8,128)(2,1)}, u32[]{:S(2)}, u32[]{:S(2)}) collective-permute-start(bf16[656,256]{1,0:T(8,128)(2,1)} %get-tuple-element.34), channel_id=1, source_target_pairs={{0,2},{1,3},{4,0},{5,1},{8,4},{9,5},{12,8},{13,9},{14,12},{15,13},... | collective-permute-start | bytes 1007624 | tf_op jit(solution)/shard_map/ppermute | solution.py:61
  16.9 9.6 %collective-permute-start.1 = (bf16[656,256]{1,0:T(8,128)(2,1)}, bf16[656,256]{1,0:T(8,128)(2,1)S(1)}, u32[]{:S(2)}, u32[]{:S(2)}) collective-permute-start(bf16[656,256]{1,0:T(8,128)(2,1)} %collective-permute-done), channel_id=1, source_target_pairs={{0,4},{1,5},{4,8},{5,9},{8,12},{9,13},{12,14},{13,15},{14,10},{15,... | collective-permute-start | bytes 1007624 | tf_op jit(solution)/shard_map/ppermute | solution.py:61
  18.9 9.8 %collective-permute-start.5 = (bf16[656,256]{1,0:T(8,128)(2,1)}, bf16[656,256]{1,0:T(8,128)(2,1)S(1)}, u32[]{:S(2)}, u32[]{:S(2)}) collective-permute-start(bf16[656,256]{1,0:T(8,128)(2,1)} %collective-permute-done.4), channel_id=1, source_target_pairs={{0,2},{1,3},{4,0},{5,1},{8,4},{9,5},{12,8},{13,9},{14,12},{15,13},... | collective-permute-start | bytes 1007624 | tf_op jit(solution)/shard_map/ppermute | solution.py:61
  28.7 10.3 %collective-permute-start.6 = (bf16[656,256]{1,0:T(8,128)(2,1)S(1)}, bf16[656,256]{1,0:T(8,128)(2,1)S(1)}, u32[]{:S(2)}, u32[]{:S(2)}) collective-permute-start(bf16[656,256]{1,0:T(8,128)(2,1)S(1)} %collective-permute-done.5), channel_id=1, source_target_pairs={{0,2},{1,3},{4,0},{5,1},{8,4},{9,5},{12,8},{13,9},{14,12},{15,13},... | collective-permute-start | bytes 1007624 | tf_op jit(solution)/shard_map/ppermute | solution.py:61
  36.3 17.6 %collective-permute-start.13 = (bf16[656,256]{1,0:T(8,128)(2,1)S(1)}, bf16[656,256]{1,0:T(8,128)(2,1)S(1)}, u32[]{:S(2)}, u32[]{:S(2)}) collective-permute-start(bf16[656,256]{1,0:T(8,128)(2,1)S(1)} %collective-permute-done.5), channel_id=1, source_target_pairs={{0,1},{1,0},{2,3},{3,2},{4,5},{5,4},{6,7},{7,6},{8,9},{9,8},{10,11... | collective-permute-start | bytes 1007624 | tf_op jit(solution)/shard_map/ppermute | solution.py:65
  36.8 18.0 %collective-permute-start.10 = (bf16[656,256]{1,0:T(8,128)(2,1)S(1)}, bf16[656,256]{1,0:T(8,128)(2,1)}, u32[]{:S(2)}, u32[]{:S(2)}) collective-permute-start(bf16[656,256]{1,0:T(8,128)(2,1)S(1)} %collective-permute-done.2), channel_id=1, source_target_pairs={{0,1},{1,0},{2,3},{3,2},{4,5},{5,4},{6,7},{7,6},{8,9},{9,8},{10,11... | collective-permute-start | bytes 1007624 | tf_op jit(solution)/shard_map/ppermute | solution.py:65
  39.0 15.9 %collective-permute-start.12 = (bf16[656,256]{1,0:T(8,128)(2,1)S(1)}, bf16[656,256]{1,0:T(8,128)(2,1)}, u32[]{:S(2)}, u32[]{:S(2)}) collective-permute-start(bf16[656,256]{1,0:T(8,128)(2,1)S(1)} %collective-permute-done.6), channel_id=1, source_target_pairs={{0,1},{1,0},{2,3},{3,2},{4,5},{5,4},{6,7},{7,6},{8,9},{9,8},{10,11... | collective-permute-start | bytes 1007624 | tf_op jit(solution)/shard_map/ppermute | solution.py:65
  42.4 12.5 %collective-permute-start.11 = (bf16[656,256]{1,0:T(8,128)(2,1)S(1)}, bf16[656,256]{1,0:T(8,128)(2,1)}, u32[]{:S(2)}, u32[]{:S(2)}) collective-permute-start(bf16[656,256]{1,0:T(8,128)(2,1)S(1)} %collective-permute-done.3), channel_id=1, source_target_pairs={{0,1},{1,0},{2,3},{3,2},{4,5},{5,4},{6,7},{7,6},{8,9},{9,8},{10,11... | collective-permute-start | bytes 1007624 | tf_op jit(solution)/shard_map/ppermute | solution.py:65
  42.4 10.4 %collective-permute-start.15 = (bf16[640,256]{1,0:T(8,128)(2,1)}, bf16[640,256]{1,0:T(8,128)(2,1)}, u32[]{:S(2)}, u32[]{:S(2)}) collective-permute-start(bf16[640,256]{1,0:T(8,128)(2,1)} %extract.1), channel_id=1, source_target_pairs={{0,2},{1,3},{4,0},{5,1},{8,4},{9,5},{12,8},{13,9},{14,12},{15,13},... | collective-permute-start | bytes 983048 | tf_op jit(solution)/shard_map/ppermute | solution.py:61
  52.8 14.8 %collective-permute-start.19 = (bf16[640,256]{1,0:T(8,128)(2,1)}, bf16[640,256]{1,0:T(8,128)(2,1)S(1)}, u32[]{:S(2)}, u32[]{:S(2)}) collective-permute-start(bf16[640,256]{1,0:T(8,128)(2,1)} %collective-permute-done.15.refs_20_), channel_id=1, source_target_pairs={{0,2},{1,3},{4,0},{5,1},{8,4},{9,5},{12,8},{13,9},{14,12},{15,13},... | collective-permute-start | bytes 983048 | tf_op jit(solution)/shard_map/ppermute | solution.py:61
  53.9 15.1 %collective-permute-start.16 = (bf16[640,256]{1,0:T(8,128)(2,1)}, bf16[640,256]{1,0:T(8,128)(2,1)S(1)}, u32[]{:S(2)}, u32[]{:S(2)}) collective-permute-start(bf16[640,256]{1,0:T(8,128)(2,1)} %extract.1), channel_id=1, source_target_pairs={{0,4},{1,5},{4,8},{5,9},{8,12},{9,13},{12,14},{13,15},{14,10},{15,... | collective-permute-start | bytes 983048 | tf_op jit(solution)/shard_map/ppermute | solution.py:61
  67.7 9.8 %collective-permute-start.20 = (bf16[640,256]{1,0:T(8,128)(2,1)S(1)}, bf16[640,256]{1,0:T(8,128)(2,1)S(1)}, u32[]{:S(2)}, u32[]{:S(2)}) collective-permute-start(bf16[640,256]{1,0:T(8,128)(2,1)S(1)} %collective-permute-done.19), channel_id=1, source_target_pairs={{0,2},{1,3},{4,0},{5,1},{8,4},{9,5},{12,8},{13,9},{14,12},{15,13},... | collective-permute-start | bytes 983048 | tf_op jit(solution)/shard_map/ppermute | solution.py:61
  78.2 9.7 %collective-permute-start.21 = (bf16[640,256]{1,0:T(8,128)(2,1)S(1)}, bf16[640,256]{1,0:T(8,128)(2,1)S(1)}, u32[]{:S(2)}, u32[]{:S(2)}) collective-permute-start(bf16[640,256]{1,0:T(8,128)(2,1)S(1)} %collective-permute-done.20), channel_id=1, source_target_pairs={{0,2},{1,3},{4,0},{5,1},{8,4},{9,5},{12,8},{13,9},{14,12},{15,13},... | collective-permute-start | bytes 983048 | tf_op jit(solution)/shard_map/ppermute | solution.py:61
  79.8 9.4 %collective-permute-start.18 = (bf16[640,256]{1,0:T(8,128)(2,1)S(1)}, bf16[640,256]{1,0:T(8,128)(2,1)S(1)}, u32[]{:S(2)}, u32[]{:S(2)}) collective-permute-start(bf16[640,256]{1,0:T(8,128)(2,1)S(1)} %collective-permute-done.17), channel_id=1, source_target_pairs={{0,4},{1,5},{4,8},{5,9},{8,12},{9,13},{12,14},{13,15},{14,10},{15,... | collective-permute-start | bytes 983048 | tf_op jit(solution)/shard_map/ppermute | solution.py:61
  80.2 10.6 %collective-permute-start.23 = (bf16[640,256]{1,0:T(8,128)(2,1)S(1)}, bf16[640,256]{1,0:T(8,128)(2,1)S(1)}, u32[]{:S(2)}, u32[]{:S(2)}) collective-permute-start(bf16[640,256]{1,0:T(8,128)(2,1)S(1)} %collective-permute-done.16), channel_id=1, source_target_pairs={{0,1},{1,0},{2,3},{3,2},{4,5},{5,4},{6,7},{7,6},{8,9},{9,8},{10,11... | collective-permute-start | bytes 983048 | tf_op jit(solution)/shard_map/ppermute | solution.py:65
  80.3 10.6 %collective-permute-start.28 = (bf16[640,256]{1,0:T(8,128)(2,1)S(1)}, bf16[640,256]{1,0:T(8,128)(2,1)S(1)}, u32[]{:S(2)}, u32[]{:S(2)}) collective-permute-start(bf16[640,256]{1,0:T(8,128)(2,1)S(1)} %collective-permute-done.19), channel_id=1, source_target_pairs={{0,1},{1,0},{2,3},{3,2},{4,5},{5,4},{6,7},{7,6},{8,9},{9,8},{10,11... | collective-permute-start | bytes 983048 | tf_op jit(solution)/shard_map/ppermute | solution.py:65
  80.8 10.5 %collective-permute-start.32 = (bf16[2,432,256]{2,1,0:T(8,128)(2,1)S(1)}, bf16[2,432,256]{2,1,0:T(8,128)(2,1)S(1)}, u32[]{:S(2)}, u32[]{:S(2)}) collective-permute-start(bf16[2,432,256]{2,1,0:T(8,128)(2,1)S(1)} %copy-done.3), channel_id=1, source_target_pairs={{0,1},{1,0},{2,3},{3,2},{4,5},{5,4},{6,7},{7,6},{8,9},{9,8},{10,11... | collective-permute-start | bytes 1327112 | tf_op jit(solution)/shard_map/ppermute | solution.py:65
  95.7 15.1 %collective-permute-start.31 = (bf16[2,432,256]{2,1,0:T(8,128)(2,1)S(1)}, bf16[2,432,256]{2,1,0:T(8,128)(2,1)S(1)}, u32[]{:S(2)}, u32[]{:S(2)}) collective-permute-start(bf16[2,432,256]{2,1,0:T(8,128)(2,1)S(1)} %copy-done.2), channel_id=1, source_target_pairs={{0,1},{1,0},{2,3},{3,2},{4,5},{5,4},{6,7},{7,6},{8,9},{9,8},{10,11... | collective-permute-start | bytes 1327112 | tf_op jit(solution)/shard_map/ppermute | solution.py:65
  96.3 25.6 %collective-permute-start.30 = (bf16[2,432,256]{2,1,0:T(8,128)(2,1)S(1)}, bf16[2,432,256]{2,1,0:T(8,128)(2,1)S(1)}, u32[]{:S(2)}, u32[]{:S(2)}) collective-permute-start(bf16[2,432,256]{2,1,0:T(8,128)(2,1)S(1)} %copy-done.1), channel_id=1, source_target_pairs={{0,1},{1,0},{2,3},{3,2},{4,5},{5,4},{6,7},{7,6},{8,9},{9,8},{10,11... | collective-permute-start | bytes 1327112 | tf_op jit(solution)/shard_map/ppermute | solution.py:65
  96.4 14.5 %collective-permute-start.35 = (bf16[432,256]{1,0:T(8,128)(2,1)S(1)}, bf16[432,256]{1,0:T(8,128)(2,1)S(1)}, u32[]{:S(2)}, u32[]{:S(2)}) collective-permute-start(bf16[432,256]{1,0:T(8,128)(2,1)S(1)} %get-tuple-element.58), channel_id=1, source_target_pairs={{0,4},{1,5},{4,8},{5,9},{8,12},{9,13},{12,14},{13,15},{14,10},{15,... | collective-permute-start | bytes 663560 | tf_op jit(solution)/shard_map/ppermute | solution.py:61
  97.8 13.1 %collective-permute-start.39 = (bf16[432,256]{1,0:T(8,128)(2,1)S(1)}, bf16[432,256]{1,0:T(8,128)(2,1)S(1)}, u32[]{:S(2)}, u32[]{:S(2)}) collective-permute-start(bf16[432,256]{1,0:T(8,128)(2,1)S(1)} %get-tuple-element.61), channel_id=1, source_target_pairs={{0,2},{1,3},{4,0},{5,1},{8,4},{9,5},{12,8},{13,9},{14,12},{15,13},... | collective-permute-start | bytes 663560 | tf_op jit(solution)/shard_map/ppermute | solution.py:61
  111.0 10.8 %collective-permute-start.36 = (bf16[432,256]{1,0:T(8,128)(2,1)S(1)}, bf16[432,256]{1,0:T(8,128)(2,1)S(1)}, u32[]{:S(2)}, u32[]{:S(2)}) collective-permute-start(bf16[432,256]{1,0:T(8,128)(2,1)S(1)} %get-tuple-element.59), channel_id=1, source_target_pairs={{0,4},{1,5},{4,8},{5,9},{8,12},{9,13},{12,14},{13,15},{14,10},{15,... | collective-permute-start | bytes 663560 | tf_op jit(solution)/shard_map/ppermute | solution.py:61
  121.8 9.3 %collective-permute-start.40 = (bf16[432,256]{1,0:T(8,128)(2,1)S(1)}, bf16[432,256]{1,0:T(8,128)(2,1)S(1)}, u32[]{:S(2)}, u32[]{:S(2)}) collective-permute-start(bf16[432,256]{1,0:T(8,128)(2,1)S(1)} %get-tuple-element.62), channel_id=1, source_target_pairs={{0,2},{1,3},{4,0},{5,1},{8,4},{9,5},{12,8},{13,9},{14,12},{15,13},... | collective-permute-start | bytes 663560 | tf_op jit(solution)/shard_map/ppermute | solution.py:61
  (48 other events, 505.0 us)

commit v5 on v4

--- a/solution.py
+++ b/solution.py
@@ -43,18 +43,29 @@
     spot = np.argsort(np.array(ring_order(chips)))
     device = np.arange(peers)
     behind = (spot[device // 2][:, None] - spot[None, :]) % chips
-    place_of = behind[:, device // 2] + chips * (device[:, None] % 2 != device[None, :] % 2)
-    if chips > 8:
-        place_of = np.broadcast_to(device, (peers, peers))
     half = chips // 2
     turn = np.where(behind >= half, 2 * (behind - half), 2 * (half - 1 - behind) + 1)
+    place_of = np.broadcast_to(device, (peers, peers)).copy()
+    if chips <= 8:
+        for me in range(peers):
+            for other in range(peers):
+                away = behind[me, other // 2] if me % 2 == 0 else -behind[me, other // 2] % chips
+                same = me % 2 == other % 2
+                if away == 0:
+                    place = 0 if same else 1
+                elif away < half or (away == half and same):
+                    place = 1 + away if same else 1 + half + away
+                else:
+                    away = chips - away
+                    place = half + (away if not same else half + away) + half
+                place_of[me, other] = place
     return np.concatenate([place_of, behind, turn, device[:, None]], axis=1).astype(np.int32)
 
 
 def ring_step(x, peers, step):
     order = ring_order(peers // 2)
     pairs = [
-        (2 * order[i] + core, 2 * order[(i + step) % len(order)] + core)
+        (2 * order[i] + core, 2 * order[(i + (step or 1 - 2 * core)) % len(order)] + core)
         for i in range(len(order))
         for core in range(2)
     ]
@@ -66,39 +77,36 @@
 
 
 class RingGather:
-    def __init__(self, x, peers, step):
+    def __init__(self, x, peers, gate=None):
         self.x, self.peers, self.chips = x, peers, peers // 2
         self.whole = None
         if self.chips > 8:
             self.whole = lax.all_gather(x[None], "morton", axis=0, tiled=True)
-        self.steps = (step, -step)
-        self.counts = (self.chips // 2, (self.chips - 1) // 2)
-        self.hops = ([], [])
-
-    def go(self, way, gate=None):
-        hops = self.hops[way]
-        if self.whole is not None or len(hops) == self.counts[way]:
             return
-        held = hops[-1] if hops else self.x
+        if gate is not None:
+            x = lax.optimization_barrier((x, gate))[0]
+        self.chains = ([x], [swap_cores(x, peers)])
+
+    def go(self, chain, gate=None):
+        if self.whole is not None or len(self.chains[chain]) > self.chips // 2 - chain:
+            return
+        held = self.chains[chain][-1]
         if gate is not None:
             held = lax.optimization_barrier((held, gate))[0]
-        hops.append(ring_step(held, self.peers, self.steps[way]))
-
-    def last(self, way):
-        return self.x if self.whole is not None else self.hops[way][-1]
+        self.chains[chain].append(ring_step(held, self.peers, 0))
+
+    def last(self, chain):
+        return self.x if self.whole is not None else self.chains[chain][-1]
 
     def places(self, gate=None):
         if self.whole is not None:
             return [self.whole]
-        got = {0: self.x}
-        for hops, step in zip(self.hops, self.steps):
-            for number, held in enumerate(hops):
-                got[(step * (number + 1)) % self.chips] = held
-        mine = [got[k] for k in range(self.chips)]
+        mine = self.chains[0][1:] + self.chains[1][1:]
         held = mine
         if gate is not None:
             held = [lax.optimization_barrier((t, gate))[0] for t in mine]
-        return [t[None] for t in mine + [swap_cores(t, self.peers) for t in held]]
+        others = [swap_cores(t, self.peers) for t in held]
+        return [t[None] for t in [self.x, self.chains[1][0]] + mine + others]
 
 
 def scatter_ring(keep, give, peers, gates):
@@ -308,7 +316,7 @@
         add_cell(pads[0], cell(facing))
 
 
-def windows(cells, halo, cols, out, sems, bricks):
+def windows(cells, halo, cols, bricks, out=None, sems=None):
     row = lax.broadcasted_iota(jnp.int32, (8, C), 0)
 
     def step(k, _):
@@ -325,7 +333,8 @@
                 block = jnp.concatenate(shifted[l][j : j + 8], axis=0).astype(BF16)
                 at = (3 * j + l) * C
                 cols[k, :, at : at + C] = block
-        pltpu.make_async_copy(cols.at[k], out.at[k], sems.at[k]).start()
+        if out is not None:
+            pltpu.make_async_copy(cols.at[k], out.at[k], sems.at[k]).start()
         return 0
 
     lax.fori_loop(0, bricks * 10, step, 0)
@@ -353,8 +362,8 @@
 def weight_grad_body(slots, factor, peers, count, *refs):
     recv, table, own_ref, cot_ref = refs[:4]
     parts = refs[4 : 4 + count]
-    keep_ref = refs[5 + count]
-    give_refs = refs[6 + count : 6 + count + peers // 4]
+    keep_ref = refs[4 + count]
+    give_refs = refs[5 + count : 5 + count + peers // 4]
     out_cols, codes_ref, served_ref = refs[-15:-12]
     cells, halo, share, cols, sums, narrow, turned, codes = refs[-12:-4]
     sems, cols_sems, codes_sem, out_sems = refs[-4:]
@@ -383,7 +392,7 @@
             code = codes[at, me * slots + safe - sender * slots]
             kind = tuple(abs(t) for t in e)
             place(kind, e, slot >= 0, at, code // 6, brick, share, cells, halo)
-    windows(cells, halo, cols, out_cols, cols_sems, bricks)
+    windows(cells, halo, cols, bricks, out_cols, cols_sems)
 
     rows = 27 * C // peers
     for tap in range(27):
@@ -475,64 +484,94 @@
         out_ref[at, :] = (x_ref[at, :].astype(F32) + total).astype(BF16)
 
 
-def cot_pad_body(slots, peers, count, *refs):
-    served, send, table, cot_ref = refs[:4]
-    parts = refs[4 : 4 + count]
-    out_cols, cells, halo, cols, share, sems, cols_sems = refs[4 + count :]
+def input_grad_body(slots, peers, count, *refs):
+    served, send, table, cot_ref, x_ref, gain_ref, weight_ref = refs[:7]
+    parts = refs[7 : 7 + count]
+    out_ref, cells, halo, cols, share, weight, heads, more, sems, weight_sem = refs[7 + count :]
     bricks = cot_ref.shape[0] // 512
     me = table[2 * peers]
     copies = fetch(parts, share, sems)
+    weight_copy = pltpu.make_async_copy(weight_ref, weight, weight_sem.at[0])
+    weight_copy.start()
+
+    def no_head(k, _):
+        heads[k] = -1
+        return 0
+
+    lax.fori_loop(0, bricks * 26, no_head, 0)
+
+    def source_of(k):
+        receiver = k // slots
+        at = table[receiver]
+        return at, served[at, me * slots + k - receiver * slots] - 1
+
+    def sort(k, found):
+        _, entry = source_of(k)
+        asked = entry >= 0
+        key = send[0, k] // 6 * 26 + 25 - jnp.maximum(entry, 0) % 26
+        first = asked & (heads[key] < 0)
+        extra = asked & jnp.logical_not(first)
+
+        @pl.when(first)
+        def _():
+            heads[key] = k
+
+        @pl.when(extra)
+        def _():
+            more[found] = k
+
+        return found + jnp.where(extra, 1, 0)
+
+    found = lax.fori_loop(0, send.shape[1], sort, 0)
     start_padded(cot_ref, cells, halo, bricks)
     for copy in copies:
         copy.wait()
-
-    def one(k, _):
-        receiver = k // slots
-        at = table[receiver]
-        info = served[at, me * slots + k - receiver * slots]
-
-        @pl.when(info > 0)
-        def _():
-            entry = info - 1
-            brick = send[0, k] // 6
-            number = 25 - entry % 26
-            tap = jnp.where(number >= 13, number + 1, number)
-            e = (tap // 9 - 1, (tap // 3) % 3 - 1, tap % 3 - 1)
-            on = [t != 0 for t in e]
-            for kind in ((1, 0, 0), (0, 1, 0), (0, 0, 1), (1, 1, 0), (1, 0, 1), (0, 1, 1), (1, 1, 1)):
-                match = functools.reduce(
-                    jnp.logical_and, [f if w else jnp.logical_not(f) for f, w in zip(on, kind)]
-                )
-
-                @pl.when(match)
-                def _():
-                    place(kind, e, None, at, entry // 26, brick, share, cells, halo)
+    for brick in range(bricks):
+        for number, e in enumerate(DIRECTIONS):
+            head = heads[brick * 26 + number]
+            at, entry = source_of(jnp.maximum(head, 0))
+            kind = tuple(abs(t) for t in e)
+            source = jnp.maximum(entry, 0) // 26
+            place(kind, e, head >= 0, at, source, brick, share, cells, halo)
+
+    def one(n, _):
+        k = more[n]
+        at, entry = source_of(k)
+        number = 25 - entry % 26
+        tap = jnp.where(number >= 13, number + 1, number)
+        e = (tap // 9 - 1, (tap // 3) % 3 - 1, tap % 3 - 1)
+        on = [t != 0 for t in e]
+        for kind in ((1, 0, 0), (0, 1, 0), (0, 0, 1), (1, 1, 0), (1, 0, 1), (0, 1, 1), (1, 1, 1)):
+            match = functools.reduce(
+                jnp.logical_and, [f if w else jnp.logical_not(f) for f, w in zip(on, kind)]
+            )
+
+            @pl.when(match)
+            def _():
+                place(kind, e, None, at, entry // 26, send[0, k] // 6, share, cells, halo)
 
         return 0
 
-    lax.fori_loop(0, send.shape[1], one, 0)
-    windows(cells, halo, cols, out_cols, cols_sems, bricks)
-    wait_windows(cols, out_cols, cols_sems, bricks)
-
-
-def input_grad_body(here, *refs):
-    cols_ref, weight_ref, cot_ref, x_ref, gain_ref = refs[:5]
-    out_ref, cols, weight, rows, sems, row_sem = refs[-6:]
-    copies = start_stream(cols_ref, here * 10, cols, weight_ref, weight, sems)
-    at = slice(here * 512, here * 512 + 512)
-    x = x_ref[at, :].astype(F32)
+    lax.fori_loop(0, found, one, 0)
+    windows(cells, halo, cols, bricks)
+    weight_copy.wait()
     gain = gain_ref[...]
-    inverse = lax.rsqrt(jnp.mean(x * x, axis=-1, keepdims=True) + 1e-6)
-    (grad,) = tap_sum(copies, cols, weight)
-    unit = x * inverse
-    v = unit * gain
-    gate = 1.0 / (1.0 + jnp.exp(-v))
-    grad = grad * (gate * (1.0 + v * (1.0 - gate))) * gain
-    grad = inverse * (grad - unit * jnp.mean(grad * unit, axis=-1, keepdims=True))
-    rows[...] = (cot_ref[at, :].astype(F32) + grad).astype(BF16)
-    copy = pltpu.make_async_copy(rows, out_ref.at[pl.ds(here * 512, 512)], row_sem.at[0])
-    copy.start()
-    copy.wait()
+    for brick in range(bricks):
+        rows = slice(brick * 512, brick * 512 + 512)
+        grad = None
+        for i in range(3):
+            left = cols[brick * 10 + i : brick * 10 + i + 8].reshape(512, 9 * C)
+            right = weight[i * 9 * C : (i + 1) * 9 * C, :]
+            term = jnp.dot(left, right, preferred_element_type=F32)
+            grad = term if grad is None else grad + term
+        x = x_ref[rows, :].astype(F32)
+        inverse = lax.rsqrt(jnp.mean(x * x, axis=-1, keepdims=True) + 1e-6)
+        unit = x * inverse
+        v = unit * gain
+        gate = 1.0 / (1.0 + jnp.exp(-v))
+        grad = grad * (gate * (1.0 + v * (1.0 - gate))) * gain
+        grad = inverse * (grad - unit * jnp.mean(grad * unit, axis=-1, keepdims=True))
+        out_ref[rows, :] = (cot_ref[rows, :].astype(F32) + grad).astype(BF16)
 
 
 def local(features, norm_gain, conv_weight, recv_slot, send_face, cotangent):
@@ -575,20 +614,19 @@
     turned = conv_weight.reshape(27, channels, channels)[::-1].transpose(0, 2, 1)
     turned = turned.reshape(27 * channels, channels)
 
-    hidden_ring = RingGather(share, peers, 1)
+    hidden_ring = RingGather(share, peers)
     hidden_ring.go(0)
     hidden_ring.go(1)
-    hidden_ring.go(0, (cot_share, turned))
-    hidden_ring.go(1, (cot_share, turned))
-    for way in (0, 1, 0):
-        hidden_ring.go(way)
+    hidden_ring.go(0, cot_share)
+    hidden_ring.go(1)
+    hidden_ring.go(0, turned)
+    hidden_ring.go(1)
+    hidden_ring.go(0)
     hidden_parts = hidden_ring.places()
 
-    cot_ring = RingGather(cot_share, peers, -1)
-    cot_ring.go(0, hidden_ring.last(1))
-    first = cot_ring.last(0)
+    cot_ring = RingGather(cot_share, peers, hidden_ring.last(1))
+    cot_ring.go(0, hidden_ring.last(0))
     cot_ring.go(1, hidden_ring.last(0))
-    cot_ring.go(0)
 
     count = len(hidden_parts)
     rows = 27 * channels // peers
@@ -602,7 +640,7 @@
             sds((peers, channels), jnp.int32),
             sds((peers, channels), jnp.int32),
         ),
-        [SMEM] * 2 + [VMEM] * 2 + [HBM] * (count + 1),
+        [SMEM] * 2 + [VMEM] * 2 + [HBM] * count,
         padded(bricks)
         + [
             pltpu.VMEM((peers, bricks * ROWS + NOTES, channels), BF16),
@@ -619,11 +657,10 @@
         cost=9,
         name="weight_grad",
         out_specs=(*[HBM] * (2 + chips // 2), VMEM, VMEM),
-    )(recv_slot, table, hidden, cotangent, *hidden_parts, first)
-
+    )(recv_slot, table, hidden, cotangent, *hidden_parts)
+
+    cot_ring.go(0, cols)
     cot_ring.go(1, cols)
-    cot_ring.go(0, cols)
-    third = (cot_ring.last(0), cot_ring.last(1))
     weight_scratch = [
         pltpu.VMEM((27 * channels, channels), BF16),
         pltpu.SemaphoreType.DMA((3, 4)),
@@ -636,49 +673,33 @@
         cost=6,
         name="mix",
     )(cols, conv_weight, features)
+    cot_ring.go(0)
     cot_ring.go(1)
+    third = (cot_ring.last(0), cot_ring.last(1))
     cot_ring.go(0)
-    fourth = (cot_ring.last(0), cot_ring.last(1))
+    fourth = cot_ring.last(0)
     cot_parts = cot_ring.places(cols)
 
-    cot_cols = call(
-        functools.partial(cot_pad_body, slots, peers, count),
-        sds(cols_shape(bricks), BF16),
-        [SMEM] * 3 + [VMEM] + [HBM] * count,
+    grad_features = call(
+        functools.partial(input_grad_body, slots, peers, count),
+        sds((per_device, channels), BF16),
+        [SMEM] * 3 + [VMEM] * 3 + [HBM] * (1 + count),
         padded(bricks)
         + [
             pltpu.VMEM(cols_shape(bricks), BF16),
             pltpu.VMEM((peers, bricks * ROWS, channels), BF16),
+            weight_scratch[0],
+            pltpu.SMEM((bricks * 26,), jnp.int32),
+            pltpu.SMEM((peers * slots,), jnp.int32),
             pltpu.SemaphoreType.DMA((count,)),
-            pltpu.SemaphoreType.DMA((bricks * 10,)),
+            pltpu.SemaphoreType.DMA((1,)),
         ],
-        cost=7,
-        name="cot_pad",
-        out_specs=HBM,
-    )(served, send_face, table, cotangent, *cot_parts)
-
-    grads = []
-    for brick in range(bricks):
-        grads.append(
-            call(
-                functools.partial(input_grad_body, brick),
-                sds((per_device, channels), BF16),
-                [HBM, HBM, VMEM, VMEM, VMEM] + [HBM] * len(grads[-1:]),
-                [pltpu.VMEM(cols_shape(1), BF16)]
-                + weight_scratch[:1]
-                + [pltpu.VMEM((512, channels), BF16)]
-                + weight_scratch[1:]
-                + [pltpu.SemaphoreType.DMA((1,))],
-                cost=5,
-                name="input_grad_" + str(brick),
-                out_specs=HBM,
-                aliases={5: 0} if grads else None,
-            )(cot_cols, turned, cotangent, features, gain, *grads[-1:])
-        )
-    gates = (None, fourth, cot_cols, grads[0])
-    give = [lax.optimization_barrier((t, third, mixed))[0] for t in give]
+        cost=13,
+        name="input_grad",
+    )(served, send_face, table, cotangent, features, gain, turned, *cot_parts)
+    gates = (mixed, third, fourth)
     grad_weight = scatter_ring(keep, give, peers, gates)
-    return (mixed, grads[-1], grad_weight)
+    return (mixed, grad_features, grad_weight)
 
 
 def solution(mesh):

time: 132 us -> 122 us (0.924)
  Pallas kernels: 52.7 us -> 39.3 us
  starting transfers between devices: 29.8 us -> 32.8 us
  local copies, waits for them, and re-layouts: 8.69 us -> 11 us
  waiting for transfers between devices: 38.3 us -> 36.5 us
    pallas_call x3 -> x1, Pallas kernels: 25.8 us -> 12.5 us  [local(): call(functools.partial(input_grad_body, slots, peers, count), sds((per_de...]
    unnamed x62 -> x56, local copies, waits for them, and re-layouts: 0.82 us -> 3.17 us
    ppermute x21, starting transfers between devices: 26.3 us -> 28.2 us  [ring_step(): return lax.ppermute(x, 'morton', pairs)]
    ppermute x21, waiting for transfers between devices: 38.2 us -> 36.4 us  [ring_step(): return lax.ppermute(x, 'morton', pairs)]
  transfers between devices with their start and end apart: 41 -> 41, of which waited for: 10 -> 12; matrix products, arithmetic and copies ran while one was open for 6% -> 7% of each run, Pallas kernels for 37% -> 29%
where the time goes in v5:
time: 122 us
  Pallas kernels  39.3 us (32%)
  waiting for transfers between devices  36.5 us (30%)
  starting transfers between devices  32.8 us (27%)
  local copies, waits for them, and re-layouts  11 us (9%)
  other arithmetic  1.39 us (1%)
    ppermute x21, waiting for transfers between devices, ring_step(): return lax.ppermute(x, 'morton', pairs)  36.4 us
    ppermute x21, starting transfers between devices, ring_step(): return lax.ppermute(x, 'morton', pairs)  28.2 us
    pallas_call x1, Pallas kernels, local(): call(functools.partial(weight_grad_body, slots, factor, peers, count), (s...  12.6 us
    pallas_call x1, Pallas kernels, local(): call(functools.partial(input_grad_body, slots, peers, count), sds((per_de...  12.5 us
    pallas_call x1, Pallas kernels, local(): call(mix_body, sds((per_device, channels), BF16), [HBM, HBM, VMEM], [pltp...  7.69 us
    ppermute x20, starting transfers between devices, swap_cores(): return lax.ppermute(x, 'morton', [(m, m ^ 1) for m in range(peers)])  4.59 us
    reshape x1, local copies, waits for them, and re-layouts, local(): conv_weight.reshape(27, channels, channels)[::-1].transpose(0, 2, 1)  4.44 us
    pallas_call x1, Pallas kernels, local(): call(norm_body, (sds((per_device, channels), BF16), sds((bricks * ROWS +...  4.26 us
  transfers between devices with their start and end apart: 41, of which 12 were waited for; matrix products, arithmetic and copies ran while one was open for 7% of the time, Pallas kernels for 29%

profile of v5, /device:TPU:0, one launch (start us, length us, event | category | flops | bytes accessed | tf_op | source)
XLA Modules:
  0.0 121.8 jit_solution(9646536211351306031)
XLA Ops:
  0.6 4.3 %norm.1 = (bf16[1024,256]{1,0:T(8,128)(2,1)}, bf16[656,256]{1,0:T(8,128)(2,1)}) custom-call(s32[2,26]{1,0:T(2,128)} %refs_0_.1, s32[1,64]{1,0:T(1,128)} %refs_1_.1, bf16[1024,256]{1,0:T(8,128)(2,1)} %refs_4_.1, f32[1,256]{1,0:T(1,128)} %bitcast.95), custom_call_target="tpu_custom_call" | custom-call | flops 2000000000 | tf_op jit(solution)/shard_map/norm/pallas_call | solution.py:600
  5.3 2.6 %collective-permute-start.1 = (bf16[656,256]{1,0:T(8,128)(2,1)}, bf16[656,256]{1,0:T(8,128)(2,1)}, u32[]{:S(2)}, u32[]{:S(2)}) collective-permute-start(bf16[656,256]{1,0:T(8,128)(2,1)} %get-tuple-element.31), channel_id=1, source_target_pairs={{0,4},{1,3},{4,8},{5,1},{8,12},{9,5},{12,14},{13,9},{14,10},{15,13... | collective-permute-start | bytes 1007624 | tf_op jit(solution)/shard_map/ppermute | solution.py:72
  7.9 1.8 %collective-permute-start.5 = (bf16[656,256]{1,0:T(8,128)(2,1)S(1)}, bf16[656,256]{1,0:T(8,128)(2,1)}, u32[]{:S(2)}, u32[]{:S(2)}) collective-permute-start(bf16[656,256]{1,0:T(8,128)(2,1)S(1)} %collective-permute-done), channel_id=1, source_target_pairs={{0,4},{1,3},{4,8},{5,1},{8,12},{9,5},{12,14},{13,9},{14,10},{15,13... | collective-permute-start | bytes 1007624 | tf_op jit(solution)/shard_map/ppermute | solution.py:72
  9.8 2.2 %extract.1 = bf16[640,256]{1,0:T(8,128)(2,1)} custom-call(bf16[1024,256]{1,0:T(8,128)(2,1)} %refs_3_.3), custom_call_target="tpu_custom_call" | custom-call | flops 2000000000 | tf_op jit(solution)/shard_map/extract/pallas_call | solution.py:607
  13.3 2.1 %collective-permute-start.2 = (bf16[656,256]{1,0:T(8,128)(2,1)}, bf16[656,256]{1,0:T(8,128)(2,1)}, u32[]{:S(2)}, u32[]{:S(2)}) collective-permute-start(bf16[656,256]{1,0:T(8,128)(2,1)} %collective-permute-done.1), channel_id=1, source_target_pairs={{0,4},{1,3},{4,8},{5,1},{8,12},{9,5},{12,14},{13,9},{14,10},{15,13... | collective-permute-start | bytes 1007624 | tf_op jit(solution)/shard_map/ppermute | solution.py:72
  16.9 2.1 %collective-permute-start.6 = (bf16[656,256]{1,0:T(8,128)(2,1)}, bf16[656,256]{1,0:T(8,128)(2,1)}, u32[]{:S(2)}, u32[]{:S(2)}) collective-permute-start(bf16[656,256]{1,0:T(8,128)(2,1)} %collective-permute-done.5), channel_id=1, source_target_pairs={{0,4},{1,3},{4,8},{5,1},{8,12},{9,5},{12,14},{13,9},{14,10},{15,13... | collective-permute-start | bytes 1007624 | tf_op jit(solution)/shard_map/ppermute | solution.py:72
  19.0 4.4 %copy.10 = bf16[27,256,256]{1,2,0:T(8,128)(2,1)S(1)} copy(bf16[27,256,256]{2,1,0:T(8,128)(2,1)} %bitcast.67) | data formatting | bytes 7077888 | tf_op jit(solution)/shard_map/reshape | solution.py:614
  23.4 2.1 %rev.3 = bf16[27,256,256]{1,2,0:T(8,128)(2,1)} reverse(bf16[27,256,256]{1,2,0:T(8,128)(2,1)S(1)} %copy.10), dimensions={0} | reverse | bytes 7077888 | tf_op jit(solution)/shard_map/rev | solution.py:614
  25.5 1.6 %collective-permute-start.3 = (bf16[656,256]{1,0:T(8,128)(2,1)}, bf16[656,256]{1,0:T(8,128)(2,1)S(1)}, u32[]{:S(2)}, u32[]{:S(2)}) collective-permute-start(bf16[656,256]{1,0:T(8,128)(2,1)} %collective-permute-done.2), channel_id=1, source_target_pairs={{0,4},{1,3},{4,8},{5,1},{8,12},{9,5},{12,14},{13,9},{14,10},{15,13... | collective-permute-start | bytes 1007624 | tf_op jit(solution)/shard_map/ppermute | solution.py:72
  27.1 1.6 %collective-permute-start.7 = (bf16[656,256]{1,0:T(8,128)(2,1)}, bf16[656,256]{1,0:T(8,128)(2,1)S(1)}, u32[]{:S(2)}, u32[]{:S(2)}) collective-permute-start(bf16[656,256]{1,0:T(8,128)(2,1)} %collective-permute-done.6), channel_id=1, source_target_pairs={{0,4},{1,3},{4,8},{5,1},{8,12},{9,5},{12,14},{13,9},{14,10},{15,13... | collective-permute-start | bytes 1007624 | tf_op jit(solution)/shard_map/ppermute | solution.py:72
  29.2 3.7 %collective-permute-done.3 = bf16[656,256]{1,0:T(8,128)(2,1)S(1)} collective-permute-done((bf16[656,256]{1,0:T(8,128)(2,1)}, bf16[656,256]{1,0:T(8,128)(2,1)S(1)}, u32[]{:S(2)}, u32[]{:S(2)}) %collective-permute-start.3) | collective-permute-done | bytes 335904 | tf_op jit(solution)/shard_map/ppermute | solution.py:72
  34.5 2.0 %collective-permute-done.7 = bf16[656,256]{1,0:T(8,128)(2,1)S(1)} collective-permute-done((bf16[656,256]{1,0:T(8,128)(2,1)}, bf16[656,256]{1,0:T(8,128)(2,1)S(1)}, u32[]{:S(2)}, u32[]{:S(2)}) %collective-permute-start.7) | collective-permute-done | bytes 335904 | tf_op jit(solution)/shard_map/ppermute | solution.py:72
  37.5 2.6 %collective-permute-done.4 = bf16[656,256]{1,0:T(8,128)(2,1)S(1)} collective-permute-done((bf16[656,256]{1,0:T(8,128)(2,1)S(1)}, bf16[656,256]{1,0:T(8,128)(2,1)S(1)}, u32[]{:S(2)}, u32[]{:S(2)}) %collective-permute-start.4) | collective-permute-done | bytes 335904 | tf_op jit(solution)/shard_map/ppermute | solution.py:72
  41.9 1.6 %collective-permute-start.16 = (bf16[640,256]{1,0:T(8,128)(2,1)}, bf16[640,256]{1,0:T(8,128)(2,1)S(1)}, u32[]{:S(2)}, u32[]{:S(2)}) collective-permute-start(bf16[640,256]{1,0:T(8,128)(2,1)} %extract.1), channel_id=1, source_target_pairs={{0,4},{1,3},{4,8},{5,1},{8,12},{9,5},{12,14},{13,9},{14,10},{15,13... | collective-permute-start | bytes 983048 | tf_op jit(solution)/shard_map/ppermute | solution.py:72
  43.5 1.6 %collective-permute-start.20 = (bf16[640,256]{1,0:T(8,128)(2,1)}, bf16[640,256]{1,0:T(8,128)(2,1)}, u32[]{:S(2)}, u32[]{:S(2)}) collective-permute-start(bf16[640,256]{1,0:T(8,128)(2,1)} %collective-permute-done.15), channel_id=1, source_target_pairs={{0,4},{1,3},{4,8},{5,1},{8,12},{9,5},{12,14},{13,9},{14,10},{15,13... | collective-permute-start | bytes 983048 | tf_op jit(solution)/shard_map/ppermute | solution.py:72
  46.0 12.6 %weight_grad.1 = (f32[8,432,256]{2,1,0:T(8,128)}, bf16[2,432,256]{2,1,0:T(8,128)(2,1)}, bf16[2,432,256]{2,1,0:T(8,128)(2,1)}, bf16[2,432,256]{2,1,0:T(8,128)(2,1...) custom-call(s32[2,26]{1,0:T(2,128)} %refs_0_.1, ...), custom_call_target="tpu_custom_call" | custom-call | flops 8999999488 | tf_op jit(solution)/shard_map/weight_grad/pallas_call | solution.py:634
  61.5 7.7 %mix.1 = bf16[1024,256]{1,0:T(8,128)(2,1)} custom-call(bf16[20,64,2304]{2,1,0:T(8,128)(2,1)} %get-tuple-element.34.cols_ref, bf16[6912,256]{1,0:T(8,128)(2,1)} %weight_ref.1, bf16[1024,256]{1,0:T(8,128)(2,1)} %refs_4_.1), custom_call_target="tpu_custom_call" | custom-call | flops 6000000000 | tf_op jit(solution)/shard_map/mix/pallas_call | solution.py:668
  72.5 6.1 %collective-permute-done.21 = bf16[640,256]{1,0:T(8,128)(2,1)S(1)} collective-permute-done((bf16[640,256]{1,0:T(8,128)(2,1)}, bf16[640,256]{1,0:T(8,128)(2,1)S(1)}, u32[]{:S(2)}, u32[]{:S(2)}) %collective-permute-start.21) | collective-permute-done | bytes 327712 | tf_op jit(solution)/shard_map/ppermute | solution.py:72
  79.4 1.6 %collective-permute-done.34 = bf16[432,256]{1,0:T(8,128)(2,1)S(1)} collective-permute-done((bf16[432,256]{1,0:T(8,128)(2,1)S(1)}, bf16[432,256]{1,0:T(8,128)(2,1)S(1)}, u32[]{:S(2)}, u32[]{:S(2)}) %collective-permute-start.34) | collective-permute-done | bytes 221216 | tf_op jit(solution)/shard_map/ppermute | solution.py:72
  81.2 3.3 %collective-permute-done.18 = bf16[640,256]{1,0:T(8,128)(2,1)S(1)} collective-permute-done((bf16[640,256]{1,0:T(8,128)(2,1)S(1)}, bf16[640,256]{1,0:T(8,128)(2,1)S(1)}, u32[]{:S(2)}, u32[]{:S(2)}) %collective-permute-start.18) | collective-permute-done | bytes 327712 | tf_op jit(solution)/shard_map/ppermute | solution.py:72
  84.5 3.5 %collective-permute-done.22 = bf16[640,256]{1,0:T(8,128)(2,1)S(1)} collective-permute-done((bf16[640,256]{1,0:T(8,128)(2,1)S(1)}, bf16[640,256]{1,0:T(8,128)(2,1)S(1)}, u32[]{:S(2)}, u32[]{:S(2)}) %collective-permute-start.22) | collective-permute-done | bytes 327712 | tf_op jit(solution)/shard_map/ppermute | solution.py:72
  91.4 5.1 %collective-permute-done.39 = bf16[432,256]{1,0:T(8,128)(2,1)S(1)} collective-permute-done((bf16[432,256]{1,0:T(8,128)(2,1)S(1)}, bf16[432,256]{1,0:T(8,128)(2,1)S(1)}, u32[]{:S(2)}, u32[]{:S(2)}) %collective-permute-start.39) | collective-permute-done | bytes 221216 | tf_op jit(solution)/shard_map/ppermute | solution.py:72
  100.6 4.1 %collective-permute-done.36 = bf16[432,256]{1,0:T(8,128)(2,1)S(1)} collective-permute-done((bf16[432,256]{1,0:T(8,128)(2,1)S(1)}, bf16[432,256]{1,0:T(8,128)(2,1)S(1)}, u32[]{:S(2)}, u32[]{:S(2)}) %collective-permute-start.36) | collective-permute-done | bytes 221216 | tf_op jit(solution)/shard_map/ppermute | solution.py:72
  108.5 12.5 %input_grad.1 = bf16[1024,256]{1,0:T(8,128)(2,1)} custom-call(s32[16,256]{1,0:T(8,128)} %get-tuple-element.35.refs_0_, s32[1,64]{1,0:T(1,128)} %refs_1_.1, s32[33]{0:T(128)} %dynamic-slice_bitcast_fusion.refs_1_.refs_2_, bf16[1024,256]{1,0:T(8,128)(2,1)} %refs_3_.3, bf16[1024,256]{1,0:T(8,128)(2,1)} %refs_4_.1, f32[1,256]{1,0:T(1,128)} %bitcast.96, ...), custom_call_target="tpu_custom_call" | custom-call | flops 12999999488 | tf_op jit(solution)/shard_map/input_grad/pallas_call | solution.py:683
  (127 shorter events, 28.2 us)
Async XLA Ops:
  5.3 8.0 %collective-permute-start.1 = (bf16[656,256]{1,0:T(8,128)(2,1)}, bf16[656,256]{1,0:T(8,128)(2,1)}, u32[]{:S(2)}, u32[]{:S(2)}) collective-permute-start(bf16[656,256]{1,0:T(8,128)(2,1)} %get-tuple-element.31), channel_id=1, source_target_pairs={{0,4},{1,3},{4,8},{5,1},{8,12},{9,5},{12,14},{13,9},{14,10},{15,13... | collective-permute-start | bytes 1007624 | tf_op jit(solution)/shard_map/ppermute | solution.py:72
  7.9 9.0 %collective-permute-start.5 = (bf16[656,256]{1,0:T(8,128)(2,1)S(1)}, bf16[656,256]{1,0:T(8,128)(2,1)}, u32[]{:S(2)}, u32[]{:S(2)}) collective-permute-start(bf16[656,256]{1,0:T(8,128)(2,1)S(1)} %collective-permute-done), channel_id=1, source_target_pairs={{0,4},{1,3},{4,8},{5,1},{8,12},{9,5},{12,14},{13,9},{14,10},{15,13... | collective-permute-start | bytes 1007624 | tf_op jit(solution)/shard_map/ppermute | solution.py:72
  13.3 12.2 %collective-permute-start.2 = (bf16[656,256]{1,0:T(8,128)(2,1)}, bf16[656,256]{1,0:T(8,128)(2,1)}, u32[]{:S(2)}, u32[]{:S(2)}) collective-permute-start(bf16[656,256]{1,0:T(8,128)(2,1)} %collective-permute-done.1), channel_id=1, source_target_pairs={{0,4},{1,3},{4,8},{5,1},{8,12},{9,5},{12,14},{13,9},{14,10},{15,13... | collective-permute-start | bytes 1007624 | tf_op jit(solution)/shard_map/ppermute | solution.py:72
  16.9 10.2 %collective-permute-start.6 = (bf16[656,256]{1,0:T(8,128)(2,1)}, bf16[656,256]{1,0:T(8,128)(2,1)}, u32[]{:S(2)}, u32[]{:S(2)}) collective-permute-start(bf16[656,256]{1,0:T(8,128)(2,1)} %collective-permute-done.5), channel_id=1, source_target_pairs={{0,4},{1,3},{4,8},{5,1},{8,12},{9,5},{12,14},{13,9},{14,10},{15,13... | collective-permute-start | bytes 1007624 | tf_op jit(solution)/shard_map/ppermute | solution.py:72
  27.1 9.4 %collective-permute-start.7 = (bf16[656,256]{1,0:T(8,128)(2,1)}, bf16[656,256]{1,0:T(8,128)(2,1)S(1)}, u32[]{:S(2)}, u32[]{:S(2)}) collective-permute-start(bf16[656,256]{1,0:T(8,128)(2,1)} %collective-permute-done.6), channel_id=1, source_target_pairs={{0,4},{1,3},{4,8},{5,1},{8,12},{9,5},{12,14},{13,9},{14,10},{15,13... | collective-permute-start | bytes 1007624 | tf_op jit(solution)/shard_map/ppermute | solution.py:72
  28.7 8.3 %collective-permute-start.8 = (bf16[656,256]{1,0:T(8,128)(2,1)}, bf16[656,256]{1,0:T(8,128)(2,1)S(1)}, u32[]{:S(2)}, u32[]{:S(2)}) collective-permute-start(bf16[656,256]{1,0:T(8,128)(2,1)} %collective-permute-done.1), channel_id=1, source_target_pairs={{0,1},{1,0},{2,3},{3,2},{4,5},{5,4},{6,7},{7,6},{8,9},{9,8},{10,11... | collective-permute-start | bytes 1007624 | tf_op jit(solution)/shard_map/ppermute | solution.py:76
  28.7 8.4 %collective-permute-start.9 = (bf16[656,256]{1,0:T(8,128)(2,1)}, bf16[656,256]{1,0:T(8,128)(2,1)S(1)}, u32[]{:S(2)}, u32[]{:S(2)}) collective-permute-start(bf16[656,256]{1,0:T(8,128)(2,1)} %collective-permute-done.2), channel_id=1, source_target_pairs={{0,1},{1,0},{2,3},{3,2},{4,5},{5,4},{6,7},{7,6},{8,9},{9,8},{10,11... | collective-permute-start | bytes 1007624 | tf_op jit(solution)/shard_map/ppermute | solution.py:76
  41.9 17.3 %collective-permute-start.16 = (bf16[640,256]{1,0:T(8,128)(2,1)}, bf16[640,256]{1,0:T(8,128)(2,1)S(1)}, u32[]{:S(2)}, u32[]{:S(2)}) collective-permute-start(bf16[640,256]{1,0:T(8,128)(2,1)} %extract.1), channel_id=1, source_target_pairs={{0,4},{1,3},{4,8},{5,1},{8,12},{9,5},{12,14},{13,9},{14,10},{15,13... | collective-permute-start | bytes 983048 | tf_op jit(solution)/shard_map/ppermute | solution.py:72
  43.5 25.8 %collective-permute-start.20 = (bf16[640,256]{1,0:T(8,128)(2,1)}, bf16[640,256]{1,0:T(8,128)(2,1)}, u32[]{:S(2)}, u32[]{:S(2)}) collective-permute-start(bf16[640,256]{1,0:T(8,128)(2,1)} %collective-permute-done.15), channel_id=1, source_target_pairs={{0,4},{1,3},{4,8},{5,1},{8,12},{9,5},{12,14},{13,9},{14,10},{15,13... | collective-permute-start | bytes 983048 | tf_op jit(solution)/shard_map/ppermute | solution.py:72
  58.6 11.3 %collective-permute-start.33 = (bf16[2,432,256]{2,1,0:T(8,128)(2,1)}, bf16[2,432,256]{2,1,0:T(8,128)(2,1)S(1)}, u32[]{:S(2)}, u32[]{:S(2)}) collective-permute-start(bf16[2,432,256]{2,1,0:T(8,128)(2,1)} %get-tuple-element.50), channel_id=1, source_target_pairs={{0,1},{1,0},{2,3},{3,2},{4,5},{5,4},{6,7},{7,6},{8,9},{9,8},{10,11... | collective-permute-start | bytes 1327112 | tf_op jit(solution)/shard_map/ppermute | solution.py:76
  58.7 20.7 %collective-permute-start.32 = (bf16[2,432,256]{2,1,0:T(8,128)(2,1)}, bf16[2,432,256]{2,1,0:T(8,128)(2,1)S(1)}, u32[]{:S(2)}, u32[]{:S(2)}) collective-permute-start(bf16[2,432,256]{2,1,0:T(8,128)(2,1)} %get-tuple-element.49), channel_id=1, source_target_pairs={{0,1},{1,0},{2,3},{3,2},{4,5},{5,4},{6,7},{7,6},{8,9},{9,8},{10,11... | collective-permute-start | bytes 1327112 | tf_op jit(solution)/shard_map/ppermute | solution.py:76
  60.0 12.2 %collective-permute-start.17 = (bf16[640,256]{1,0:T(8,128)(2,1)}, bf16[640,256]{1,0:T(8,128)(2,1)S(1)}, u32[]{:S(2)}, u32[]{:S(2)}) collective-permute-start(bf16[640,256]{1,0:T(8,128)(2,1)} %copy-done.14), channel_id=1, source_target_pairs={{0,4},{1,3},{4,8},{5,1},{8,12},{9,5},{12,14},{13,9},{14,10},{15,13... | collective-permute-start | bytes 983048 | tf_op jit(solution)/shard_map/ppermute | solution.py:72
  69.2 9.4 %collective-permute-start.21 = (bf16[640,256]{1,0:T(8,128)(2,1)}, bf16[640,256]{1,0:T(8,128)(2,1)S(1)}, u32[]{:S(2)}, u32[]{:S(2)}) collective-permute-start(bf16[640,256]{1,0:T(8,128)(2,1)} %collective-permute-done.20), channel_id=1, source_target_pairs={{0,4},{1,3},{4,8},{5,1},{8,12},{9,5},{12,14},{13,9},{14,10},{15,13... | collective-permute-start | bytes 983048 | tf_op jit(solution)/shard_map/ppermute | solution.py:72
  70.0 9.4 %collective-permute-start.38 = (bf16[432,256]{1,0:T(8,128)(2,1)S(1)}, bf16[432,256]{1,0:T(8,128)(2,1)S(1)}, u32[]{:S(2)}, u32[]{:S(2)}) collective-permute-start(bf16[432,256]{1,0:T(8,128)(2,1)S(1)} %get-tuple-element.54), channel_id=1, source_target_pairs={{0,2},{1,3},{4,0},{5,1},{8,4},{9,5},{12,8},{13,9},{14,12},{15,13},... | collective-permute-start | bytes 663560 | tf_op jit(solution)/shard_map/ppermute | solution.py:72
  71.5 9.6 %collective-permute-start.34 = (bf16[432,256]{1,0:T(8,128)(2,1)S(1)}, bf16[432,256]{1,0:T(8,128)(2,1)S(1)}, u32[]{:S(2)}, u32[]{:S(2)}) collective-permute-start(bf16[432,256]{1,0:T(8,128)(2,1)S(1)} %get-tuple-element.51), channel_id=1, source_target_pairs={{0,4},{1,5},{4,8},{5,9},{8,12},{9,13},{12,14},{13,15},{14,10},{15,... | collective-permute-start | bytes 663560 | tf_op jit(solution)/shard_map/ppermute | solution.py:72
  72.1 12.4 %collective-permute-start.18 = (bf16[640,256]{1,0:T(8,128)(2,1)S(1)}, bf16[640,256]{1,0:T(8,128)(2,1)S(1)}, u32[]{:S(2)}, u32[]{:S(2)}) collective-permute-start(bf16[640,256]{1,0:T(8,128)(2,1)S(1)} %collective-permute-done.17), channel_id=1, source_target_pairs={{0,4},{1,3},{4,8},{5,1},{8,12},{9,5},{12,14},{13,9},{14,10},{15,13... | collective-permute-start | bytes 983048 | tf_op jit(solution)/shard_map/ppermute | solution.py:72
  78.7 9.4 %collective-permute-start.22 = (bf16[640,256]{1,0:T(8,128)(2,1)S(1)}, bf16[640,256]{1,0:T(8,128)(2,1)S(1)}, u32[]{:S(2)}, u32[]{:S(2)}) collective-permute-start(bf16[640,256]{1,0:T(8,128)(2,1)S(1)} %collective-permute-done.21), channel_id=1, source_target_pairs={{0,4},{1,3},{4,8},{5,1},{8,12},{9,5},{12,14},{13,9},{14,10},{15,13... | collective-permute-start | bytes 983048 | tf_op jit(solution)/shard_map/ppermute | solution.py:72
  79.4 11.4 %collective-permute-start.31 = (bf16[2,432,256]{2,1,0:T(8,128)(2,1)S(1)}, bf16[2,432,256]{2,1,0:T(8,128)(2,1)S(1)}, u32[]{:S(2)}, u32[]{:S(2)}) collective-permute-start(bf16[2,432,256]{2,1,0:T(8,128)(2,1)S(1)} %copy-done.2), channel_id=1, source_target_pairs={{0,1},{1,0},{2,3},{3,2},{4,5},{5,4},{6,7},{7,6},{8,9},{9,8},{10,11... | collective-permute-start | bytes 1327112 | tf_op jit(solution)/shard_map/ppermute | solution.py:76
  88.0 8.4 %collective-permute-start.39 = (bf16[432,256]{1,0:T(8,128)(2,1)S(1)}, bf16[432,256]{1,0:T(8,128)(2,1)S(1)}, u32[]{:S(2)}, u32[]{:S(2)}) collective-permute-start(bf16[432,256]{1,0:T(8,128)(2,1)S(1)} %get-tuple-element.55), channel_id=1, source_target_pairs={{0,2},{1,3},{4,0},{5,1},{8,4},{9,5},{12,8},{13,9},{14,12},{15,13},... | collective-permute-start | bytes 663560 | tf_op jit(solution)/shard_map/ppermute | solution.py:72
  90.1 8.1 %collective-permute-start.19 = (bf16[640,256]{1,0:T(8,128)(2,1)S(1)}, bf16[640,256]{1,0:T(8,128)(2,1)S(1)}, u32[]{:S(2)}, u32[]{:S(2)}) collective-permute-start(bf16[640,256]{1,0:T(8,128)(2,1)S(1)} %collective-permute-done.18), channel_id=1, source_target_pairs={{0,4},{1,3},{4,8},{5,1},{8,12},{9,5},{12,14},{13,9},{14,10},{15,13... | collective-permute-start | bytes 983048 | tf_op jit(solution)/shard_map/ppermute | solution.py:72
  90.8 8.7 %collective-permute-start.23 = (bf16[640,256]{1,0:T(8,128)(2,1)S(1)}, bf16[640,256]{1,0:T(8,128)(2,1)S(1)}, u32[]{:S(2)}, u32[]{:S(2)}) collective-permute-start(bf16[640,256]{1,0:T(8,128)(2,1)S(1)} %copy-done.15), channel_id=1, source_target_pairs={{0,1},{1,0},{2,3},{3,2},{4,5},{5,4},{6,7},{7,6},{8,9},{9,8},{10,11... | collective-permute-start | bytes 983048 | tf_op jit(solution)/shard_map/ppermute | solution.py:76
  90.9 9.2 %collective-permute-start.30 = (bf16[2,432,256]{2,1,0:T(8,128)(2,1)S(1)}, bf16[2,432,256]{2,1,0:T(8,128)(2,1)S(1)}, u32[]{:S(2)}, u32[]{:S(2)}) collective-permute-start(bf16[2,432,256]{2,1,0:T(8,128)(2,1)S(1)} %copy-done.1), channel_id=1, source_target_pairs={{0,1},{1,0},{2,3},{3,2},{4,5},{5,4},{6,7},{7,6},{8,9},{9,8},{10,11... | collective-permute-start | bytes 1327112 | tf_op jit(solution)/shard_map/ppermute | solution.py:76
  104.8 16.2 %collective-permute-start.40 = (bf16[432,256]{1,0:T(8,128)(2,1)S(1)}, bf16[432,256]{1,0:T(8,128)(2,1)S(1)}, u32[]{:S(2)}, u32[]{:S(2)}) collective-permute-start(bf16[432,256]{1,0:T(8,128)(2,1)S(1)} %get-tuple-element.56), channel_id=1, source_target_pairs={{0,2},{1,3},{4,0},{5,1},{8,4},{9,5},{12,8},{13,9},{14,12},{15,13},... | collective-permute-start | bytes 663560 | tf_op jit(solution)/shard_map/ppermute | solution.py:72
  106.0 15.0 %collective-permute-start.37 = (bf16[432,256]{1,0:T(8,128)(2,1)S(1)}, bf16[432,256]{1,0:T(8,128)(2,1)S(1)}, u32[]{:S(2)}, u32[]{:S(2)}) collective-permute-start(bf16[432,256]{1,0:T(8,128)(2,1)S(1)} %fusion.4), channel_id=1, source_target_pairs={{0,4},{1,5},{4,8},{5,9},{8,12},{9,13},{12,14},{13,15},{14,10},{15,... | collective-permute-start | bytes 663560 | tf_op jit(solution)/shard_map/ppermute | solution.py:72
  (45 other events, 370.4 us)

commit v6 on v5

--- a/solution.py
+++ b/solution.py
@@ -62,10 +62,10 @@
     return np.concatenate([place_of, behind, turn, device[:, None]], axis=1).astype(np.int32)
 
 
-def ring_step(x, peers, step):
+def ring_step(x, peers, step, cross=0):
     order = ring_order(peers // 2)
     pairs = [
-        (2 * order[i] + core, 2 * order[(i + (step or 1 - 2 * core)) % len(order)] + core)
+        (2 * order[i] + (core ^ cross), 2 * order[(i + (step or 1 - 2 * core)) % len(order)] + core)
         for i in range(len(order))
         for core in range(2)
     ]
@@ -77,15 +77,13 @@
 
 
 class RingGather:
-    def __init__(self, x, peers, gate=None):
+    def __init__(self, x, peers):
         self.x, self.peers, self.chips = x, peers, peers // 2
         self.whole = None
         if self.chips > 8:
             self.whole = lax.all_gather(x[None], "morton", axis=0, tiled=True)
             return
-        if gate is not None:
-            x = lax.optimization_barrier((x, gate))[0]
-        self.chains = ([x], [swap_cores(x, peers)])
+        self.chains = ([x], [x])
 
     def go(self, chain, gate=None):
         if self.whole is not None or len(self.chains[chain]) > self.chips // 2 - chain:
@@ -93,7 +91,8 @@
         held = self.chains[chain][-1]
         if gate is not None:
             held = lax.optimization_barrier((held, gate))[0]
-        self.chains[chain].append(ring_step(held, self.peers, 0))
+        cross = int(chain == 1 and len(self.chains[chain]) == 1)
+        self.chains[chain].append(ring_step(held, self.peers, 0, cross))
 
     def last(self, chain):
         return self.x if self.whole is not None else self.chains[chain][-1]
@@ -105,34 +104,41 @@
         held = mine
         if gate is not None:
             held = [lax.optimization_barrier((t, gate))[0] for t in mine]
-        others = [swap_cores(t, self.peers) for t in held]
-        return [t[None] for t in [self.x, self.chains[1][0]] + mine + others]
-
-
-def scatter_ring(keep, give, peers, gates):
-    chips = peers // 2
-    half = chips // 2
-    other = [swap_cores(t, peers) for t in give]
-
-    def term(k):
-        pair = other[k - half][0] if k >= half else other[half - 1 - k][1]
-        return keep[k] + pair.astype(F32)
-
-    ups, downs = chips // 2, (chips - 1) // 2
-    total = term(0)
-    for count, step in ((ups, 1), (downs, -1)):
-        held = None
-        for hop in range(count, 0, -1):
-            part = term((-step * hop) % chips)
-            if held is not None:
-                part = part + held.astype(F32)
+        others = [swap_cores(t, self.peers) for t in [self.x] + held]
+        return [t[None] for t in [self.x] + others[:1] + mine + others[1:]]
+
+
+class RingScatter:
+    def __init__(self, keep, give, peers):
+        self.keep, self.peers, self.chips = keep, peers, peers // 2
+        self.other = [swap_cores(t, peers) for t in give]
+        self.held = [None, None]
+        self.hop = 0
+
+    def term(self, k):
+        half = self.chips // 2
+        pair = self.other[k - half][0] if k >= half else self.other[half - 1 - k][1]
+        return self.keep[k] + pair.astype(F32)
+
+    def go(self, gate=None):
+        sent = []
+        for way, step, count in ((0, 1, self.chips // 2), (1, -1, (self.chips - 1) // 2)):
+            left = count - self.hop
+            if left <= 0:
+                continue
+            part = self.term((-step * left) % self.chips)
+            if self.held[way] is not None:
+                part = part + self.held[way].astype(F32)
             part = part.astype(BF16)
-            if count - hop < len(gates) and gates[count - hop] is not None:
-                part = lax.optimization_barrier((part, gates[count - hop]))[0]
-            held = ring_step(part, peers, step)
-        if held is not None:
-            total = total + held.astype(F32)
-    return total
+            if gate is not None:
+                part = lax.optimization_barrier((part, gate))[0]
+            sent.append(part)
+            self.held[way] = ring_step(part, self.peers, step)
+        self.hop += 1
+        return sent
+
+    def total(self):
+        return sum((t.astype(F32) for t in self.held if t is not None), self.term(0))
 
 
 def call(body, out_shape, in_specs, scratch=(), cost=2, name=None, out_specs=None, aliases=None):
@@ -177,15 +183,16 @@
 def norm_body(recv, send, x_ref, gain_ref, hidden_ref, out_ref, stage):
     bricks, directions = recv.shape
     gain = gain_ref[...]
-    row = lax.broadcasted_iota(jnp.int32, (NOTES, C), 0)
-    lane = lax.broadcasted_iota(jnp.int32, (NOTES, C), 1)
-    notes = jnp.zeros((NOTES, C), jnp.int32)
+    lane = lax.broadcasted_iota(jnp.int32, (1, C), 1)
+    codes = jnp.zeros((1, C), jnp.int32)
     for k in range(send.shape[1]):
-        notes = jnp.where((row == 0) & (lane == k), send[0, k], notes)
+        codes = jnp.where(lane == k, send[0, k], codes)
+    served = jnp.zeros((1, C), jnp.int32)
     for brick in range(bricks):
         for number in range(directions):
-            serves = (row == 1) & (lane == recv[brick, number])
-            notes = jnp.where(serves, brick * directions + number + 1, notes)
+            served = jnp.where(lane == recv[brick, number], brick * directions + number + 1, served)
+    row = lax.broadcasted_iota(jnp.int32, (NOTES, C), 0)
+    notes = jnp.where(row == 0, codes, jnp.where(row == 1, served, 0))
     out_ref[bricks * ROWS :, :] = notes.astype(F32).astype(BF16)
 
     def step(k, _):
@@ -604,6 +611,7 @@
         [stage],
         name="norm",
     )(recv_slot, send_face, features, gain)
+    hidden_ring = RingGather(share, peers)
     cot_share = call(
         extract_body,
         sds((bricks * ROWS, channels), BF16),
@@ -611,21 +619,17 @@
         [stage],
         name="extract",
     )(cotangent)
-    turned = conv_weight.reshape(27, channels, channels)[::-1].transpose(0, 2, 1)
-    turned = turned.reshape(27 * channels, channels)
-
-    hidden_ring = RingGather(share, peers)
     hidden_ring.go(0)
     hidden_ring.go(1)
     hidden_ring.go(0, cot_share)
     hidden_ring.go(1)
-    hidden_ring.go(0, turned)
+    hidden_ring.go(0, table)
     hidden_ring.go(1)
     hidden_ring.go(0)
     hidden_parts = hidden_ring.places()
 
-    cot_ring = RingGather(cot_share, peers, hidden_ring.last(1))
-    cot_ring.go(0, hidden_ring.last(0))
+    cot_ring = RingGather(cot_share, peers)
+    cot_ring.go(0, hidden_ring.last(1))
     cot_ring.go(1, hidden_ring.last(0))
 
     count = len(hidden_parts)
@@ -659,8 +663,14 @@
         out_specs=(*[HBM] * (2 + chips // 2), VMEM, VMEM),
     )(recv_slot, table, hidden, cotangent, *hidden_parts)
 
+    first = (cot_ring.last(0), cot_ring.last(1))
+    give = [lax.optimization_barrier((t, first))[0] for t in give]
+    sums_ring = RingScatter(keep, give, peers)
+    sent = sums_ring.go()
     cot_ring.go(0, cols)
     cot_ring.go(1, cols)
+    second = (cot_ring.last(0), cot_ring.last(1))
+    mix_cols = lax.optimization_barrier((cols, sent))[0]
     weight_scratch = [
         pltpu.VMEM((27 * channels, channels), BF16),
         pltpu.SemaphoreType.DMA((3, 4)),
@@ -672,13 +682,19 @@
         [pltpu.VMEM(cols_shape(bricks), BF16)] + weight_scratch,
         cost=6,
         name="mix",
-    )(cols, conv_weight, features)
+    )(mix_cols, conv_weight, features)
+    sent = sums_ring.go((second, mixed))
     cot_ring.go(0)
     cot_ring.go(1)
     third = (cot_ring.last(0), cot_ring.last(1))
+    turned = lax.optimization_barrier((conv_weight, sent))[0]
+    turned = turned.reshape(27, channels, channels)[::-1].transpose(0, 2, 1)
+    turned = turned.reshape(27 * channels, channels)
+    sums_ring.go((third, turned))
     cot_ring.go(0)
-    fourth = cot_ring.last(0)
+    sent = sums_ring.go(cot_ring.last(0))
     cot_parts = cot_ring.places(cols)
+    turned = lax.optimization_barrier((turned, sent))[0]
 
     grad_features = call(
         functools.partial(input_grad_body, slots, peers, count),
@@ -697,9 +713,9 @@
         cost=13,
         name="input_grad",
     )(served, send_face, table, cotangent, features, gain, turned, *cot_parts)
-    gates = (mixed, third, fourth)
-    grad_weight = scatter_ring(keep, give, peers, gates)
-    return (mixed, grad_features, grad_weight)
+    for _ in range(chips // 2 - 4):
+        sums_ring.go()
+    return (mixed, grad_features, sums_ring.total())
 
 
 def solution(mesh):

time: 122 us -> 115 us (0.943)
  waiting for transfers between devices: 36.5 us -> 27.2 us
  other arithmetic: 1.39 us -> 7.89 us
  starting transfers between devices: 32.8 us -> 29.7 us
  local copies, waits for them, and re-layouts: 11 us -> 9.45 us
    ppermute x21, waiting for transfers between devices: 36.4 us -> 27.1 us  [ring_step(): return lax.ppermute(x, 'morton', pairs)]
    convert_element_type x4, other arithmetic: 0.51 us -> 6 us  [go(): part = part.astype(BF16)]
    ppermute x21, starting transfers between devices: 28.2 us -> 26.4 us  [ring_step(): return lax.ppermute(x, 'morton', pairs)]
    unnamed x56 -> x54, local copies, waits for them, and re-layouts: 3.17 us -> 1.79 us
    ppermute x20, starting transfers between devices: 4.59 us -> 3.27 us  [swap_cores(): return lax.ppermute(x, 'morton', [(m, m ^ 1) for m in range(peers)])]
  transfers between devices with their start and end apart: 41 -> 41, of which waited for: 12 -> 10; matrix products, arithmetic and copies ran while one was open for 7% -> 12% of each run, Pallas kernels for 29% -> 31%
where the time goes in v6:
time: 115 us
  Pallas kernels  39.8 us (35%)
  starting transfers between devices  29.7 us (26%)
  waiting for transfers between devices  27.2 us (24%)
  local copies, waits for them, and re-layouts  9.45 us (8%)
  other arithmetic  7.89 us (7%)
    ppermute x21, waiting for transfers between devices, ring_step(): return lax.ppermute(x, 'morton', pairs)  27.1 us
    ppermute x21, starting transfers between devices, ring_step(): return lax.ppermute(x, 'morton', pairs)  26.4 us
    pallas_call x1, Pallas kernels, local(): call(functools.partial(input_grad_body, slots, peers, count), sds((per_de...  13 us
    pallas_call x1, Pallas kernels, local(): call(functools.partial(weight_grad_body, slots, factor, peers, count), (s...  12.6 us
    pallas_call x1, Pallas kernels, local(): call(mix_body, sds((per_device, channels), BF16), [HBM, HBM, VMEM], [pltp...  7.69 us
    convert_element_type x4, other arithmetic, go(): part = part.astype(BF16)  6 us
    reshape x1, local copies, waits for them, and re-layouts, local(): turned = turned.reshape(27, channels, channels)[::-1].transpose(0, 2, 1)  4.44 us
    pallas_call x1, Pallas kernels, local(): call(norm_body, (sds((per_device, channels), BF16), sds((bricks * ROWS +...  4.2 us
  transfers between devices with their start and end apart: 41, of which 10 were waited for; matrix products, arithmetic and copies ran while one was open for 12% of the time, Pallas kernels for 31%

profile of v6, /device:TPU:0, one launch (start us, length us, event | category | flops | bytes accessed | tf_op | source)
XLA Modules:
  0.0 115.1 jit_solution(7484287070204264088)
XLA Ops:
  0.6 4.2 %norm.1 = (bf16[1024,256]{1,0:T(8,128)(2,1)}, bf16[656,256]{1,0:T(8,128)(2,1)}) custom-call(s32[2,26]{1,0:T(2,128)} %refs_0_.1, s32[1,64]{1,0:T(1,128)} %refs_1_.1, bf16[1024,256]{1,0:T(8,128)(2,1)} %refs_4_.1, f32[1,256]{1,0:T(1,128)} %bitcast.97), custom_call_target="tpu_custom_call" | custom-call | flops 2000000000 | tf_op jit(solution)/shard_map/norm/pallas_call | solution.py:607
  4.8 3.0 %collective-permute-start.1 = (bf16[656,256]{1,0:T(8,128)(2,1)}, bf16[656,256]{1,0:T(8,128)(2,1)S(1)}, u32[]{:S(2)}, u32[]{:S(2)}) collective-permute-start(bf16[656,256]{1,0:T(8,128)(2,1)} %get-tuple-element.36), channel_id=1, source_target_pairs={{0,4},{1,3},{4,8},{5,1},{8,12},{9,5},{12,14},{13,9},{14,10},{15,13... | collective-permute-start | bytes 1007624 | tf_op jit(solution)/shard_map/ppermute | solution.py:72
  8.5 2.2 %extract.1 = bf16[640,256]{1,0:T(8,128)(2,1)} custom-call(bf16[1024,256]{1,0:T(8,128)(2,1)} %refs_3_.3), custom_call_target="tpu_custom_call" | custom-call | flops 2000000000 | tf_op jit(solution)/shard_map/extract/pallas_call | solution.py:615
  10.8 4.7 %collective-permute-done.1 = bf16[656,256]{1,0:T(8,128)(2,1)S(1)} collective-permute-done((bf16[656,256]{1,0:T(8,128)(2,1)}, bf16[656,256]{1,0:T(8,128)(2,1)S(1)}, u32[]{:S(2)}, u32[]{:S(2)}) %collective-permute-start.1) | collective-permute-done | bytes 335904 | tf_op jit(solution)/shard_map/ppermute | solution.py:72
  15.4 2.4 %collective-permute-start.2 = (bf16[656,256]{1,0:T(8,128)(2,1)S(1)}, bf16[656,256]{1,0:T(8,128)(2,1)S(1)}, u32[]{:S(2)}, u32[]{:S(2)}) collective-permute-start(bf16[656,256]{1,0:T(8,128)(2,1)S(1)} %collective-permute-done.1), channel_id=1, source_target_pairs={{0,4},{1,3},{4,8},{5,1},{8,12},{9,5},{12,14},{13,9},{14,10},{15,13... | collective-permute-start | bytes 1007624 | tf_op jit(solution)/shard_map/ppermute | solution.py:72
  19.1 1.6 %collective-permute-start.6 = (bf16[656,256]{1,0:T(8,128)(2,1)S(1)}, bf16[656,256]{1,0:T(8,128)(2,1)S(1)}, u32[]{:S(2)}, u32[]{:S(2)}) collective-permute-start(bf16[656,256]{1,0:T(8,128)(2,1)S(1)} %collective-permute-done.5), channel_id=1, source_target_pairs={{0,4},{1,3},{4,8},{5,1},{8,12},{9,5},{12,14},{13,9},{14,10},{15,13... | collective-permute-start | bytes 1007624 | tf_op jit(solution)/shard_map/ppermute | solution.py:72
  20.6 3.2 %collective-permute-done.2 = bf16[656,256]{1,0:T(8,128)(2,1)S(1)} collective-permute-done((bf16[656,256]{1,0:T(8,128)(2,1)S(1)}, bf16[656,256]{1,0:T(8,128)(2,1)S(1)}, u32[]{:S(2)}, u32[]{:S(2)}) %collective-permute-start.2) | collective-permute-done | bytes 335904 | tf_op jit(solution)/shard_map/ppermute | solution.py:72
  25.5 2.0 %collective-permute-done.6 = bf16[656,256]{1,0:T(8,128)(2,1)S(1)} collective-permute-done((bf16[656,256]{1,0:T(8,128)(2,1)S(1)}, bf16[656,256]{1,0:T(8,128)(2,1)S(1)}, u32[]{:S(2)}, u32[]{:S(2)}) %collective-permute-start.6) | collective-permute-done | bytes 335904 | tf_op jit(solution)/shard_map/ppermute | solution.py:72
  28.6 2.5 %collective-permute-done.3 = bf16[656,256]{1,0:T(8,128)(2,1)S(1)} collective-permute-done((bf16[656,256]{1,0:T(8,128)(2,1)S(1)}, bf16[656,256]{1,0:T(8,128)(2,1)S(1)}, u32[]{:S(2)}, u32[]{:S(2)}) %collective-permute-start.3) | collective-permute-done | bytes 335904 | tf_op jit(solution)/shard_map/ppermute | solution.py:72
  32.8 1.9 %collective-permute-done.7 = bf16[656,256]{1,0:T(8,128)(2,1)S(1)} collective-permute-done((bf16[656,256]{1,0:T(8,128)(2,1)S(1)}, bf16[656,256]{1,0:T(8,128)(2,1)S(1)}, u32[]{:S(2)}, u32[]{:S(2)}) %collective-permute-start.7) | collective-permute-done | bytes 335904 | tf_op jit(solution)/shard_map/ppermute | solution.py:72
  34.7 3.6 %collective-permute-done.4 = bf16[656,256]{1,0:T(8,128)(2,1)S(1)} collective-permute-done((bf16[656,256]{1,0:T(8,128)(2,1)S(1)}, bf16[656,256]{1,0:T(8,128)(2,1)S(1)}, u32[]{:S(2)}, u32[]{:S(2)}) %collective-permute-start.4) | collective-permute-done | bytes 335904 | tf_op jit(solution)/shard_map/ppermute | solution.py:72
  39.5 2.3 %collective-permute-start.16 = (bf16[640,256]{1,0:T(8,128)(2,1)}, bf16[640,256]{1,0:T(8,128)(2,1)S(1)}, u32[]{:S(2)}, u32[]{:S(2)}) collective-permute-start(bf16[640,256]{1,0:T(8,128)(2,1)} %extract.1), channel_id=1, source_target_pairs={{1,4},{0,3},{5,8},{4,1},{9,12},{8,5},{13,14},{12,9},{15,10},{14,13... | collective-permute-start | bytes 983048 | tf_op jit(solution)/shard_map/ppermute | solution.py:72
  42.7 12.6 %weight_grad.1 = (f32[8,432,256]{2,1,0:T(8,128)}, bf16[2,432,256]{2,1,0:T(8,128)(2,1)}, bf16[2,432,256]{2,1,0:T(8,128)(2,1)}, bf16[2,432,256]{2,1,0:T(8,128)(2,1...) custom-call(s32[2,26]{1,0:T(2,128)} %refs_0_.1, ...), custom_call_target="tpu_custom_call" | custom-call | flops 8999999488 | tf_op jit(solution)/shard_map/weight_grad/pallas_call | solution.py:638
  56.5 2.3 %collective-permute-start.21 = (bf16[640,256]{1,0:T(8,128)(2,1)S(1)}, bf16[640,256]{1,0:T(8,128)(2,1)}, u32[]{:S(2)}, u32[]{:S(2)}) collective-permute-start(bf16[640,256]{1,0:T(8,128)(2,1)S(1)} %collective-permute-done.16), channel_id=1, source_target_pairs={{0,4},{1,3},{4,8},{5,1},{8,12},{9,5},{12,14},{13,9},{14,10},{15,13... | collective-permute-start | bytes 983048 | tf_op jit(solution)/shard_map/ppermute | solution.py:72
  60.2 2.0 %collective-permute-start.19 = (bf16[432,256]{1,0:T(8,128)(2,1)S(1)}, bf16[432,256]{1,0:T(8,128)(2,1)S(1)}, u32[]{:S(2)}, u32[]{:S(2)}) collective-permute-start(bf16[432,256]{1,0:T(8,128)(2,1)S(1)} %get-tuple-element.72), channel_id=1, source_target_pairs={{0,4},{1,5},{4,8},{5,9},{8,12},{9,13},{12,14},{13,15},{14,10},{15,... | collective-permute-start | bytes 663560 | tf_op jit(solution)/shard_map/ppermute | solution.py:72
  62.2 7.7 %mix.1 = bf16[1024,256]{1,0:T(8,128)(2,1)} custom-call(bf16[20,64,2304]{2,1,0:T(8,128)(2,1)} %get-tuple-element.45.cols_ref, bf16[6912,256]{1,0:T(8,128)(2,1)} %weight_ref.1, bf16[1024,256]{1,0:T(8,128)(2,1)} %refs_4_.1), custom_call_target="tpu_custom_call" | custom-call | flops 6000000000 | tf_op jit(solution)/shard_map/mix/pallas_call | solution.py:678
  71.9 2.1 %fusion.4 = (bf16[432,256]{1,0:T(8,128)(2,1)}, bf16[432,256]{1,0:T(8,128)(2,1)}) fusion(bf16[432,256]{1,0:T(8,128)(2,1)S(1)} %collective-permute-done.22, f32[8,432,256]{2,1,0:T(8,128)} %get-tuple-element.40, bf16[2,432,256]{2,1,0:T(8,128)(2,1)S(1)} %collective-permute-done.18, bf16[432,256]{1,0:T(8,128)(2,1)S(1)} %collective-permute-done.19), kind=kLoop, calls=%fused_computation.9 | loop fusion | flops 1105920 | bytes 2211840 | tf_op jit(solution)/shard_map/convert_element_type | solution.py:132
  74.4 1.6 %collective-permute-start.39 = (bf16[432,256]{1,0:T(8,128)(2,1)}, bf16[432,256]{1,0:T(8,128)(2,1)}, u32[]{:S(2)}, u32[]{:S(2)}) collective-permute-start(bf16[432,256]{1,0:T(8,128)(2,1)} %get-tuple-element.52), channel_id=1, source_target_pairs={{0,2},{1,3},{4,0},{5,1},{8,4},{9,5},{12,8},{13,9},{14,12},{15,13},... | collective-permute-start | bytes 663560 | tf_op jit(solution)/shard_map/ppermute | solution.py:72
  76.0 1.8 %collective-permute-done.26 = bf16[640,256]{1,0:T(8,128)(2,1)} collective-permute-done((bf16[640,256]{1,0:T(8,128)(2,1)S(1)}, bf16[640,256]{1,0:T(8,128)(2,1)}, u32[]{:S(2)}, u32[]{:S(2)}) %collective-permute-start.26) | collective-permute-done | bytes 327712 | tf_op jit(solution)/shard_map/ppermute | solution.py:72
  78.0 4.4 %copy.10 = bf16[27,256,256]{1,2,0:T(8,128)(2,1)S(1)} copy(bf16[27,256,256]{2,1,0:T(8,128)(2,1)} %bitcast.67) | data formatting | bytes 7077888 | tf_op jit(solution)/shard_map/reshape | solution.py:691
  82.4 2.0 %rev.3 = bf16[27,256,256]{1,2,0:T(8,128)(2,1)} reverse(bf16[27,256,256]{1,2,0:T(8,128)(2,1)S(1)} %copy.10), dimensions={0} | reverse | bytes 7077888 | tf_op jit(solution)/shard_map/rev | solution.py:691
  90.5 5.4 %collective-permute-done.28 = bf16[432,256]{1,0:T(8,128)(2,1)S(1)} collective-permute-done((bf16[432,256]{1,0:T(8,128)(2,1)S(1)}, bf16[432,256]{1,0:T(8,128)(2,1)S(1)}, u32[]{:S(2)}, u32[]{:S(2)}) %collective-permute-start.28) | collective-permute-done | bytes 221216 | tf_op jit(solution)/shard_map/ppermute | solution.py:72
  100.1 13.0 %input_grad.1 = bf16[1024,256]{1,0:T(8,128)(2,1)} custom-call(s32[16,256]{1,0:T(8,128)} %get-tuple-element.46.refs_0_, s32[1,64]{1,0:T(1,128)} %refs_1_.1, s32[33]{0:T(128)} %dynamic-slice_bitcast_fusion.refs_1_.refs_2_, bf16[1024,256]{1,0:T(8,128)(2,1)} %refs_3_.3, bf16[1024,256]{1,0:T(8,128)(2,1)} %refs_4_.1, f32[1,256]{1,0:T(1,128)} %bitcast.98, ...), custom_call_target="tpu_custom_call" | custom-call | flops 12999999488 | tf_op jit(solution)/shard_map/input_grad/pallas_call | solution.py:699
  113.2 1.9 %fusion.1 = f32[432,256]{1,0:T(8,128)} fusion(bf16[432,256]{1,0:T(8,128)(2,1)S(1)} %collective-permute-done.40, bf16[432,256]{1,0:T(8,128)(2,1)S(1)} %collective-permute-done.38, f32[8,432,256]{2,1,0:T(8,128)} %get-tuple-element.40, bf16[2,432,256]{2,1,0:T(8,128)(2,1)S(1)} %collective-permute-done.23), kind=kLoop, calls=%fused_computation.3 | loop fusion | flops 663552 | bytes 1548288 | tf_op jit(solution)/shard_map/add | solution.py:141
  (125 shorter events, 23.6 us)
Async XLA Ops:
  4.8 10.6 %collective-permute-start.1 = (bf16[656,256]{1,0:T(8,128)(2,1)}, bf16[656,256]{1,0:T(8,128)(2,1)S(1)}, u32[]{:S(2)}, u32[]{:S(2)}) collective-permute-start(bf16[656,256]{1,0:T(8,128)(2,1)} %get-tuple-element.36), channel_id=1, source_target_pairs={{0,4},{1,3},{4,8},{5,1},{8,12},{9,5},{12,14},{13,9},{14,10},{15,13... | collective-permute-start | bytes 1007624 | tf_op jit(solution)/shard_map/ppermute | solution.py:72
  7.9 11.2 %collective-permute-start.5 = (bf16[656,256]{1,0:T(8,128)(2,1)}, bf16[656,256]{1,0:T(8,128)(2,1)S(1)}, u32[]{:S(2)}, u32[]{:S(2)}) collective-permute-start(bf16[656,256]{1,0:T(8,128)(2,1)} %get-tuple-element.36), channel_id=1, source_target_pairs={{1,4},{0,3},{5,8},{4,1},{9,12},{8,5},{13,14},{12,9},{15,10},{14,13... | collective-permute-start | bytes 1007624 | tf_op jit(solution)/shard_map/ppermute | solution.py:72
  15.4 8.4 %collective-permute-start.2 = (bf16[656,256]{1,0:T(8,128)(2,1)S(1)}, bf16[656,256]{1,0:T(8,128)(2,1)S(1)}, u32[]{:S(2)}, u32[]{:S(2)}) collective-permute-start(bf16[656,256]{1,0:T(8,128)(2,1)S(1)} %collective-permute-done.1), channel_id=1, source_target_pairs={{0,4},{1,3},{4,8},{5,1},{8,12},{9,5},{12,14},{13,9},{14,10},{15,13... | collective-permute-start | bytes 1007624 | tf_op jit(solution)/shard_map/ppermute | solution.py:72
  19.1 8.4 %collective-permute-start.6 = (bf16[656,256]{1,0:T(8,128)(2,1)S(1)}, bf16[656,256]{1,0:T(8,128)(2,1)S(1)}, u32[]{:S(2)}, u32[]{:S(2)}) collective-permute-start(bf16[656,256]{1,0:T(8,128)(2,1)S(1)} %collective-permute-done.5), channel_id=1, source_target_pairs={{0,4},{1,3},{4,8},{5,1},{8,12},{9,5},{12,14},{13,9},{14,10},{15,13... | collective-permute-start | bytes 1007624 | tf_op jit(solution)/shard_map/ppermute | solution.py:72
  32.7 9.0 %collective-permute-start.10 = (bf16[656,256]{1,0:T(8,128)(2,1)S(1)}, bf16[656,256]{1,0:T(8,128)(2,1)S(1)}, u32[]{:S(2)}, u32[]{:S(2)}) collective-permute-start(bf16[656,256]{1,0:T(8,128)(2,1)S(1)} %collective-permute-done.3), channel_id=1, source_target_pairs={{0,1},{1,0},{2,3},{3,2},{4,5},{5,4},{6,7},{7,6},{8,9},{9,8},{10,11... | collective-permute-start | bytes 1007624 | tf_op jit(solution)/shard_map/ppermute | solution.py:76
  38.3 17.0 %collective-permute-start.15 = (bf16[640,256]{1,0:T(8,128)(2,1)}, bf16[640,256]{1,0:T(8,128)(2,1)S(1)}, u32[]{:S(2)}, u32[]{:S(2)}) collective-permute-start(bf16[640,256]{1,0:T(8,128)(2,1)} %extract.1), channel_id=1, source_target_pairs={{0,4},{1,3},{4,8},{5,1},{8,12},{9,5},{12,14},{13,9},{14,10},{15,13... | collective-permute-start | bytes 983048 | tf_op jit(solution)/shard_map/ppermute | solution.py:72
  39.5 15.9 %collective-permute-start.16 = (bf16[640,256]{1,0:T(8,128)(2,1)}, bf16[640,256]{1,0:T(8,128)(2,1)S(1)}, u32[]{:S(2)}, u32[]{:S(2)}) collective-permute-start(bf16[640,256]{1,0:T(8,128)(2,1)} %extract.1), channel_id=1, source_target_pairs={{1,4},{0,3},{5,8},{4,1},{9,12},{8,5},{13,14},{12,9},{15,10},{14,13... | collective-permute-start | bytes 983048 | tf_op jit(solution)/shard_map/ppermute | solution.py:72
  55.4 14.5 %collective-permute-start.20 = (bf16[640,256]{1,0:T(8,128)(2,1)S(1)}, bf16[640,256]{1,0:T(8,128)(2,1)S(1)}, u32[]{:S(2)}, u32[]{:S(2)}) collective-permute-start(bf16[640,256]{1,0:T(8,128)(2,1)S(1)} %collective-permute-done.15), channel_id=1, source_target_pairs={{0,4},{1,3},{4,8},{5,1},{8,12},{9,5},{12,14},{13,9},{14,10},{15,13... | collective-permute-start | bytes 983048 | tf_op jit(solution)/shard_map/ppermute | solution.py:72
  56.5 13.5 %collective-permute-start.21 = (bf16[640,256]{1,0:T(8,128)(2,1)S(1)}, bf16[640,256]{1,0:T(8,128)(2,1)}, u32[]{:S(2)}, u32[]{:S(2)}) collective-permute-start(bf16[640,256]{1,0:T(8,128)(2,1)S(1)} %collective-permute-done.16), channel_id=1, source_target_pairs={{0,4},{1,3},{4,8},{5,1},{8,12},{9,5},{12,14},{13,9},{14,10},{15,13... | collective-permute-start | bytes 983048 | tf_op jit(solution)/shard_map/ppermute | solution.py:72
  58.8 11.6 %collective-permute-start.18 = (bf16[2,432,256]{2,1,0:T(8,128)(2,1)}, bf16[2,432,256]{2,1,0:T(8,128)(2,1)S(1)}, u32[]{:S(2)}, u32[]{:S(2)}) collective-permute-start(bf16[2,432,256]{2,1,0:T(8,128)(2,1)} %get-tuple-element.48), channel_id=1, source_target_pairs={{0,1},{1,0},{2,3},{3,2},{4,5},{5,4},{6,7},{7,6},{8,9},{9,8},{10,11... | collective-permute-start | bytes 1327112 | tf_op jit(solution)/shard_map/ppermute | solution.py:76
  60.1 11.8 %collective-permute-start.22 = (bf16[432,256]{1,0:T(8,128)(2,1)S(1)}, bf16[432,256]{1,0:T(8,128)(2,1)S(1)}, u32[]{:S(2)}, u32[]{:S(2)}) collective-permute-start(bf16[432,256]{1,0:T(8,128)(2,1)S(1)} %get-tuple-element.71), channel_id=1, source_target_pairs={{0,2},{1,3},{4,0},{5,1},{8,4},{9,5},{12,8},{13,9},{14,12},{15,13},... | collective-permute-start | bytes 663560 | tf_op jit(solution)/shard_map/ppermute | solution.py:72
  60.2 11.7 %collective-permute-start.19 = (bf16[432,256]{1,0:T(8,128)(2,1)S(1)}, bf16[432,256]{1,0:T(8,128)(2,1)S(1)}, u32[]{:S(2)}, u32[]{:S(2)}) collective-permute-start(bf16[432,256]{1,0:T(8,128)(2,1)S(1)} %get-tuple-element.72), channel_id=1, source_target_pairs={{0,4},{1,5},{4,8},{5,9},{8,12},{9,13},{12,14},{13,15},{14,10},{15,... | collective-permute-start | bytes 663560 | tf_op jit(solution)/shard_map/ppermute | solution.py:72
  69.9 14.5 %collective-permute-start.24 = (bf16[2,432,256]{2,1,0:T(8,128)(2,1)}, bf16[2,432,256]{2,1,0:T(8,128)(2,1)}, u32[]{:S(2)}, u32[]{:S(2)}) collective-permute-start(bf16[2,432,256]{2,1,0:T(8,128)(2,1)} %get-tuple-element.57), channel_id=1, source_target_pairs={{0,1},{1,0},{2,3},{3,2},{4,5},{5,4},{6,7},{7,6},{8,9},{9,8},{10,11... | collective-permute-start | bytes 1327112 | tf_op jit(solution)/shard_map/ppermute | solution.py:76
  70.0 7.8 %collective-permute-start.26 = (bf16[640,256]{1,0:T(8,128)(2,1)S(1)}, bf16[640,256]{1,0:T(8,128)(2,1)}, u32[]{:S(2)}, u32[]{:S(2)}) collective-permute-start(bf16[640,256]{1,0:T(8,128)(2,1)S(1)} %collective-permute-done.20), channel_id=1, source_target_pairs={{0,4},{1,3},{4,8},{5,1},{8,12},{9,5},{12,14},{13,9},{14,10},{15,13... | collective-permute-start | bytes 983048 | tf_op jit(solution)/shard_map/ppermute | solution.py:72
  70.5 13.9 %collective-permute-start.27 = (bf16[640,256]{1,0:T(8,128)(2,1)}, bf16[640,256]{1,0:T(8,128)(2,1)}, u32[]{:S(2)}, u32[]{:S(2)}) collective-permute-start(bf16[640,256]{1,0:T(8,128)(2,1)} %collective-permute-done.21), channel_id=1, source_target_pairs={{0,4},{1,3},{4,8},{5,1},{8,12},{9,5},{12,14},{13,9},{14,10},{15,13... | collective-permute-start | bytes 983048 | tf_op jit(solution)/shard_map/ppermute | solution.py:72
  74.0 11.5 %collective-permute-start.25 = (bf16[432,256]{1,0:T(8,128)(2,1)}, bf16[432,256]{1,0:T(8,128)(2,1)}, u32[]{:S(2)}, u32[]{:S(2)}) collective-permute-start(bf16[432,256]{1,0:T(8,128)(2,1)} %get-tuple-element.51), channel_id=1, source_target_pairs={{0,4},{1,5},{4,8},{5,9},{8,12},{9,13},{12,14},{13,15},{14,10},{15,... | collective-permute-start | bytes 663560 | tf_op jit(solution)/shard_map/ppermute | solution.py:72
  74.4 11.1 %collective-permute-start.39 = (bf16[432,256]{1,0:T(8,128)(2,1)}, bf16[432,256]{1,0:T(8,128)(2,1)}, u32[]{:S(2)}, u32[]{:S(2)}) collective-permute-start(bf16[432,256]{1,0:T(8,128)(2,1)} %get-tuple-element.52), channel_id=1, source_target_pairs={{0,2},{1,3},{4,0},{5,1},{8,4},{9,5},{12,8},{13,9},{14,12},{15,13},... | collective-permute-start | bytes 663560 | tf_op jit(solution)/shard_map/ppermute | solution.py:72
  77.8 11.2 %collective-permute-start.29 = (bf16[640,256]{1,0:T(8,128)(2,1)}, bf16[640,256]{1,0:T(8,128)(2,1)}, u32[]{:S(2)}, u32[]{:S(2)}) collective-permute-start(bf16[640,256]{1,0:T(8,128)(2,1)} %collective-permute-done.26), channel_id=1, source_target_pairs={{0,4},{1,3},{4,8},{5,1},{8,12},{9,5},{12,14},{13,9},{14,10},{15,13... | collective-permute-start | bytes 983048 | tf_op jit(solution)/shard_map/ppermute | solution.py:72
  89.4 7.6 %collective-permute-start.32 = (bf16[640,256]{1,0:T(8,128)(2,1)}, bf16[640,256]{1,0:T(8,128)(2,1)S(1)}, u32[]{:S(2)}, u32[]{:S(2)}) collective-permute-start(bf16[640,256]{1,0:T(8,128)(2,1)} %copy-done.18), channel_id=1, source_target_pairs={{0,1},{1,0},{2,3},{3,2},{4,5},{5,4},{6,7},{7,6},{8,9},{9,8},{10,11... | collective-permute-start | bytes 983048 | tf_op jit(solution)/shard_map/ppermute | solution.py:76
  89.5 8.3 %collective-permute-start.36 = (bf16[640,256]{1,0:T(8,128)(2,1)}, bf16[640,256]{1,0:T(8,128)(2,1)S(1)}, u32[]{:S(2)}, u32[]{:S(2)}) collective-permute-start(bf16[640,256]{1,0:T(8,128)(2,1)} %collective-permute-done.21), channel_id=1, source_target_pairs={{0,1},{1,0},{2,3},{3,2},{4,5},{5,4},{6,7},{7,6},{8,9},{9,8},{10,11... | collective-permute-start | bytes 983048 | tf_op jit(solution)/shard_map/ppermute | solution.py:76
  90.0 9.2 %collective-permute-start.33 = (bf16[640,256]{1,0:T(8,128)(2,1)}, bf16[640,256]{1,0:T(8,128)(2,1)S(1)}, u32[]{:S(2)}, u32[]{:S(2)}) collective-permute-start(bf16[640,256]{1,0:T(8,128)(2,1)} %collective-permute-done.26), channel_id=1, source_target_pairs={{0,1},{1,0},{2,3},{3,2},{4,5},{5,4},{6,7},{7,6},{8,9},{9,8},{10,11... | collective-permute-start | bytes 983048 | tf_op jit(solution)/shard_map/ppermute | solution.py:76
  90.0 9.1 %collective-permute-start.37 = (bf16[640,256]{1,0:T(8,128)(2,1)}, bf16[640,256]{1,0:T(8,128)(2,1)S(1)}, u32[]{:S(2)}, u32[]{:S(2)}) collective-permute-start(bf16[640,256]{1,0:T(8,128)(2,1)} %collective-permute-done.27), channel_id=1, source_target_pairs={{0,1},{1,0},{2,3},{3,2},{4,5},{5,4},{6,7},{7,6},{8,9},{9,8},{10,11... | collective-permute-start | bytes 983048 | tf_op jit(solution)/shard_map/ppermute | solution.py:76
  97.0 16.1 %collective-permute-start.40 = (bf16[432,256]{1,0:T(8,128)(2,1)S(1)}, bf16[432,256]{1,0:T(8,128)(2,1)S(1)}, u32[]{:S(2)}, u32[]{:S(2)}) collective-permute-start(bf16[432,256]{1,0:T(8,128)(2,1)S(1)} %get-tuple-element.66), channel_id=1, source_target_pairs={{0,2},{1,3},{4,0},{5,1},{8,4},{9,5},{12,8},{13,9},{14,12},{15,13},... | collective-permute-start | bytes 663560 | tf_op jit(solution)/shard_map/ppermute | solution.py:72
  97.7 15.4 %collective-permute-start.38 = (bf16[432,256]{1,0:T(8,128)(2,1)S(1)}, bf16[432,256]{1,0:T(8,128)(2,1)S(1)}, u32[]{:S(2)}, u32[]{:S(2)}) collective-permute-start(bf16[432,256]{1,0:T(8,128)(2,1)S(1)} %fusion.3), channel_id=1, source_target_pairs={{0,4},{1,5},{4,8},{5,9},{8,12},{9,13},{12,14},{13,15},{14,10},{15,... | collective-permute-start | bytes 663560 | tf_op jit(solution)/shard_map/ppermute | solution.py:72
  (44 other events, 331.6 us)

commit v7 on v6

--- a/solution.py
+++ b/solution.py
@@ -623,12 +623,13 @@
     hidden_ring.go(1)
     hidden_ring.go(0, cot_share)
     hidden_ring.go(1)
+    cot_ring = RingGather(cot_share, peers)
+    cot_ring.go(0, hidden_ring.last(0))
+    cot_ring.go(1, hidden_ring.last(1))
     hidden_ring.go(0, table)
     hidden_ring.go(1)
     hidden_ring.go(0)
     hidden_parts = hidden_ring.places()
-
-    cot_ring = RingGather(cot_share, peers)
     cot_ring.go(0, hidden_ring.last(1))
     cot_ring.go(1, hidden_ring.last(0))
 
@@ -671,29 +672,23 @@
     cot_ring.go(1, cols)
     second = (cot_ring.last(0), cot_ring.last(1))
     mix_cols = lax.optimization_barrier((cols, sent))[0]
-    weight_scratch = [
-        pltpu.VMEM((27 * channels, channels), BF16),
-        pltpu.SemaphoreType.DMA((3, 4)),
-    ]
+    weight_scratch = pltpu.VMEM((27 * channels, channels), BF16)
     mixed = call(
         mix_body,
         sds((per_device, channels), BF16),
         [HBM, HBM, VMEM],
-        [pltpu.VMEM(cols_shape(bricks), BF16)] + weight_scratch,
+        [pltpu.VMEM(cols_shape(bricks), BF16), weight_scratch, pltpu.SemaphoreType.DMA((3, 4))],
         cost=6,
         name="mix",
     )(mix_cols, conv_weight, features)
     sent = sums_ring.go((second, mixed))
     cot_ring.go(0)
-    cot_ring.go(1)
-    third = (cot_ring.last(0), cot_ring.last(1))
     turned = lax.optimization_barrier((conv_weight, sent))[0]
     turned = turned.reshape(27, channels, channels)[::-1].transpose(0, 2, 1)
     turned = turned.reshape(27 * channels, channels)
-    sums_ring.go((third, turned))
-    cot_ring.go(0)
-    sent = sums_ring.go(cot_ring.last(0))
+    sums_ring.go((cot_ring.last(0), turned))
     cot_parts = cot_ring.places(cols)
+    sent = sums_ring.go()
     turned = lax.optimization_barrier((turned, sent))[0]
 
     grad_features = call(
@@ -704,7 +699,7 @@
         + [
             pltpu.VMEM(cols_shape(bricks), BF16),
             pltpu.VMEM((peers, bricks * ROWS, channels), BF16),
-            weight_scratch[0],
+            weight_scratch,
             pltpu.SMEM((bricks * 26,), jnp.int32),
             pltpu.SMEM((peers * slots,), jnp.int32),
             pltpu.SemaphoreType.DMA((count,)),

time: 115 us -> 121 us (1.052); the launches traced: 115 us -> 119 us
  starting transfers between devices: 29.7 us -> 32.5 us
  waiting for transfers between devices: 27.2 us -> 29 us
    ppermute x21, waiting for transfers between devices: 27.1 us -> 28.9 us  [ring_step(): return lax.ppermute(x, 'morton', pairs)]
    ppermute x21, starting transfers between devices: 26.4 us -> 28.2 us  [ring_step(): return lax.ppermute(x, 'morton', pairs)]
  transfers between devices with their start and end apart: 41 -> 41, of which waited for: 10 -> 8; matrix products, arithmetic and copies ran while one was open for 12% -> 11% of each run, Pallas kernels for 31% -> 29%
where the time goes in v7:
time: 121 us; the launch traced here: 119 us
  Pallas kernels  39.4 us (33%)
  starting transfers between devices  32.5 us (27%)
  waiting for transfers between devices  29 us (24%)
  local copies, waits for them, and re-layouts  9.52 us (8%)
  other arithmetic  7.91 us (7%)
    ppermute x21, waiting for transfers between devices, ring_step(): return lax.ppermute(x, 'morton', pairs)  28.9 us
    ppermute x21, starting transfers between devices, ring_step(): return lax.ppermute(x, 'morton', pairs)  28.2 us
    pallas_call x1, Pallas kernels, local(): call(functools.partial(input_grad_body, slots, peers, count), sds((per_de...  12.6 us
    pallas_call x1, Pallas kernels, local(): call(functools.partial(weight_grad_body, slots, factor, peers, count), (s...  12.6 us
    pallas_call x1, Pallas kernels, local(): call(mix_body, sds((per_device, channels), BF16), [HBM, HBM, VMEM], [pltp...  7.69 us
    convert_element_type x4, other arithmetic, go(): part = part.astype(BF16)  6.02 us
    reshape x1, local copies, waits for them, and re-layouts, local(): turned = turned.reshape(27, channels, channels)[::-1].transpose(0, 2, 1)  4.44 us
    ppermute x20, starting transfers between devices, swap_cores(): return lax.ppermute(x, 'morton', [(m, m ^ 1) for m in range(peers)])  4.34 us
  transfers between devices with their start and end apart: 41, of which 8 were waited for; matrix products, arithmetic and copies ran while one was open for 11% of the time, Pallas kernels for 29%

profile of v7, /device:TPU:0, one launch (start us, length us, event | category | flops | bytes accessed | tf_op | source)
XLA Modules:
  0.0 119.4 jit_solution(10216825655941924875)
XLA Ops:
  0.6 4.2 %norm.1 = (bf16[1024,256]{1,0:T(8,128)(2,1)}, bf16[656,256]{1,0:T(8,128)(2,1)}) custom-call(s32[2,26]{1,0:T(2,128)} %refs_0_.1, s32[1,64]{1,0:T(1,128)} %refs_1_.1, bf16[1024,256]{1,0:T(8,128)(2,1)} %refs_4_.1, f32[1,256]{1,0:T(1,128)} %bitcast.97), custom_call_target="tpu_custom_call" | custom-call | flops 2000000000 | tf_op jit(solution)/shard_map/norm/pallas_call | solution.py:607
  4.8 3.0 %collective-permute-start.1 = (bf16[656,256]{1,0:T(8,128)(2,1)}, bf16[656,256]{1,0:T(8,128)(2,1)S(1)}, u32[]{:S(2)}, u32[]{:S(2)}) collective-permute-start(bf16[656,256]{1,0:T(8,128)(2,1)} %get-tuple-element.37), channel_id=1, source_target_pairs={{0,4},{1,3},{4,8},{5,1},{8,12},{9,5},{12,14},{13,9},{14,10},{15,13... | collective-permute-start | bytes 1007624 | tf_op jit(solution)/shard_map/ppermute | solution.py:72
  8.5 2.2 %extract.1 = bf16[640,256]{1,0:T(8,128)(2,1)} custom-call(bf16[1024,256]{1,0:T(8,128)(2,1)} %refs_3_.3), custom_call_target="tpu_custom_call" | custom-call | flops 2000000000 | tf_op jit(solution)/shard_map/extract/pallas_call | solution.py:615
  10.8 4.7 %collective-permute-done.1 = bf16[656,256]{1,0:T(8,128)(2,1)S(1)} collective-permute-done((bf16[656,256]{1,0:T(8,128)(2,1)}, bf16[656,256]{1,0:T(8,128)(2,1)S(1)}, u32[]{:S(2)}, u32[]{:S(2)}) %collective-permute-start.1) | collective-permute-done | bytes 335904 | tf_op jit(solution)/shard_map/ppermute | solution.py:72
  15.4 2.4 %collective-permute-start.2 = (bf16[656,256]{1,0:T(8,128)(2,1)S(1)}, bf16[656,256]{1,0:T(8,128)(2,1)S(1)}, u32[]{:S(2)}, u32[]{:S(2)}) collective-permute-start(bf16[656,256]{1,0:T(8,128)(2,1)S(1)} %collective-permute-done.1), channel_id=1, source_target_pairs={{0,4},{1,3},{4,8},{5,1},{8,12},{9,5},{12,14},{13,9},{14,10},{15,13... | collective-permute-start | bytes 1007624 | tf_op jit(solution)/shard_map/ppermute | solution.py:72
  19.1 1.6 %collective-permute-start.6 = (bf16[656,256]{1,0:T(8,128)(2,1)S(1)}, bf16[656,256]{1,0:T(8,128)(2,1)S(1)}, u32[]{:S(2)}, u32[]{:S(2)}) collective-permute-start(bf16[656,256]{1,0:T(8,128)(2,1)S(1)} %collective-permute-done.5), channel_id=1, source_target_pairs={{0,4},{1,3},{4,8},{5,1},{8,12},{9,5},{12,14},{13,9},{14,10},{15,13... | collective-permute-start | bytes 1007624 | tf_op jit(solution)/shard_map/ppermute | solution.py:72
  20.7 3.2 %collective-permute-done.2 = bf16[656,256]{1,0:T(8,128)(2,1)S(1)} collective-permute-done((bf16[656,256]{1,0:T(8,128)(2,1)S(1)}, bf16[656,256]{1,0:T(8,128)(2,1)S(1)}, u32[]{:S(2)}, u32[]{:S(2)}) %collective-permute-start.2) | collective-permute-done | bytes 335904 | tf_op jit(solution)/shard_map/ppermute | solution.py:72
  25.5 2.0 %collective-permute-done.6 = bf16[656,256]{1,0:T(8,128)(2,1)S(1)} collective-permute-done((bf16[656,256]{1,0:T(8,128)(2,1)S(1)}, bf16[656,256]{1,0:T(8,128)(2,1)S(1)}, u32[]{:S(2)}, u32[]{:S(2)}) %collective-permute-start.6) | collective-permute-done | bytes 335904 | tf_op jit(solution)/shard_map/ppermute | solution.py:72
  28.6 2.5 %collective-permute-done.3 = bf16[656,256]{1,0:T(8,128)(2,1)S(1)} collective-permute-done((bf16[656,256]{1,0:T(8,128)(2,1)S(1)}, bf16[656,256]{1,0:T(8,128)(2,1)S(1)}, u32[]{:S(2)}, u32[]{:S(2)}) %collective-permute-start.3) | collective-permute-done | bytes 335904 | tf_op jit(solution)/shard_map/ppermute | solution.py:72
  32.2 1.6 %collective-permute-start.15 = (bf16[640,256]{1,0:T(8,128)(2,1)}, bf16[640,256]{1,0:T(8,128)(2,1)S(1)}, u32[]{:S(2)}, u32[]{:S(2)}) collective-permute-start(bf16[640,256]{1,0:T(8,128)(2,1)} %extract.1), channel_id=1, source_target_pairs={{0,4},{1,3},{4,8},{5,1},{8,12},{9,5},{12,14},{13,9},{14,10},{15,13... | collective-permute-start | bytes 983048 | tf_op jit(solution)/shard_map/ppermute | solution.py:72
  34.1 8.4 %collective-permute-done.17 = bf16[640,256]{1,0:T(8,128)(2,1)S(1)} collective-permute-done((bf16[640,256]{1,0:T(8,128)(2,1)}, bf16[640,256]{1,0:T(8,128)(2,1)S(1)}, u32[]{:S(2)}, u32[]{:S(2)}) %collective-permute-start.17) | collective-permute-done | bytes 327712 | tf_op jit(solution)/shard_map/ppermute | solution.py:72
  42.5 2.8 %collective-permute-done.15 = bf16[640,256]{1,0:T(8,128)(2,1)S(1)} collective-permute-done((bf16[640,256]{1,0:T(8,128)(2,1)}, bf16[640,256]{1,0:T(8,128)(2,1)S(1)}, u32[]{:S(2)}, u32[]{:S(2)}) %collective-permute-start.15) | collective-permute-done | bytes 327712 | tf_op jit(solution)/shard_map/ppermute | solution.py:72
  47.0 1.6 %collective-permute-start.18 = (bf16[640,256]{1,0:T(8,128)(2,1)S(1)}, bf16[640,256]{1,0:T(8,128)(2,1)S(1)}, u32[]{:S(2)}, u32[]{:S(2)}) collective-permute-start(bf16[640,256]{1,0:T(8,128)(2,1)S(1)} %collective-permute-done.17), channel_id=1, source_target_pairs={{0,4},{1,3},{4,8},{5,1},{8,12},{9,5},{12,14},{13,9},{14,10},{15,13... | collective-permute-start | bytes 983048 | tf_op jit(solution)/shard_map/ppermute | solution.py:72
  49.6 12.6 %weight_grad.1 = (f32[8,432,256]{2,1,0:T(8,128)}, bf16[2,432,256]{2,1,0:T(8,128)(2,1)}, bf16[2,432,256]{2,1,0:T(8,128)(2,1)}, bf16[2,432,256]{2,1,0:T(8,128)(2,1...) custom-call(s32[2,26]{1,0:T(2,128)} %refs_0_.1, ...), custom_call_target="tpu_custom_call" | custom-call | flops 8999999488 | tf_op jit(solution)/shard_map/weight_grad/pallas_call | solution.py:639
  64.0 2.3 %collective-permute-start.23 = (bf16[640,256]{1,0:T(8,128)(2,1)S(1)}, bf16[640,256]{1,0:T(8,128)(2,1)S(1)}, u32[]{:S(2)}, u32[]{:S(2)}) collective-permute-start(bf16[640,256]{1,0:T(8,128)(2,1)S(1)} %collective-permute-done.18), channel_id=1, source_target_pairs={{0,4},{1,3},{4,8},{5,1},{8,12},{9,5},{12,14},{13,9},{14,10},{15,13... | collective-permute-start | bytes 983048 | tf_op jit(solution)/shard_map/ppermute | solution.py:72
  67.7 2.0 %collective-permute-start.21 = (bf16[432,256]{1,0:T(8,128)(2,1)S(1)}, bf16[432,256]{1,0:T(8,128)(2,1)S(1)}, u32[]{:S(2)}, u32[]{:S(2)}) collective-permute-start(bf16[432,256]{1,0:T(8,128)(2,1)S(1)} %get-tuple-element.74), channel_id=1, source_target_pairs={{0,4},{1,5},{4,8},{5,9},{8,12},{9,13},{12,14},{13,15},{14,10},{15,... | collective-permute-start | bytes 663560 | tf_op jit(solution)/shard_map/ppermute | solution.py:72
  69.7 7.7 %mix.1 = bf16[1024,256]{1,0:T(8,128)(2,1)} custom-call(bf16[20,64,2304]{2,1,0:T(8,128)(2,1)} %get-tuple-element.48.cols_ref, bf16[6912,256]{1,0:T(8,128)(2,1)} %weight_ref.1, bf16[1024,256]{1,0:T(8,128)(2,1)} %refs_4_.1), custom_call_target="tpu_custom_call" | custom-call | flops 6000000000 | tf_op jit(solution)/shard_map/mix/pallas_call | solution.py:676
  78.5 2.1 %fusion.4 = (bf16[432,256]{1,0:T(8,128)(2,1)}, bf16[432,256]{1,0:T(8,128)(2,1)}) fusion(bf16[432,256]{1,0:T(8,128)(2,1)S(1)} %collective-permute-done.24, f32[8,432,256]{2,1,0:T(8,128)} %get-tuple-element.41, bf16[2,432,256]{2,1,0:T(8,128)(2,1)S(1)} %collective-permute-done.20, bf16[432,256]{1,0:T(8,128)(2,1)S(1)} %collective-permute-done.21), kind=kLoop, calls=%fused_computation.9 | loop fusion | flops 1105920 | bytes 2211840 | tf_op jit(solution)/shard_map/convert_element_type | solution.py:132
  83.9 4.4 %copy.10 = bf16[27,256,256]{1,2,0:T(8,128)(2,1)S(1)} copy(bf16[27,256,256]{2,1,0:T(8,128)(2,1)} %bitcast.67) | data formatting | bytes 7077888 | tf_op jit(solution)/shard_map/reshape | solution.py:687
  88.3 2.0 %rev.3 = bf16[27,256,256]{1,2,0:T(8,128)(2,1)} reverse(bf16[27,256,256]{1,2,0:T(8,128)(2,1)S(1)} %copy.10), dimensions={0} | reverse | bytes 7077888 | tf_op jit(solution)/shard_map/rev | solution.py:687
  92.9 2.3 %collective-permute-start.29 = (bf16[432,256]{1,0:T(8,128)(2,1)S(1)}, bf16[432,256]{1,0:T(8,128)(2,1)S(1)}, u32[]{:S(2)}, u32[]{:S(2)}) collective-permute-start(bf16[432,256]{1,0:T(8,128)(2,1)S(1)} %get-tuple-element.61), channel_id=1, source_target_pairs={{0,4},{1,5},{4,8},{5,9},{8,12},{9,13},{12,14},{13,15},{14,10},{15,... | collective-permute-start | bytes 663560 | tf_op jit(solution)/shard_map/ppermute | solution.py:72
  96.2 4.3 %collective-permute-done.29 = bf16[432,256]{1,0:T(8,128)(2,1)S(1)} collective-permute-done((bf16[432,256]{1,0:T(8,128)(2,1)S(1)}, bf16[432,256]{1,0:T(8,128)(2,1)S(1)}, u32[]{:S(2)}, u32[]{:S(2)}) %collective-permute-start.29) | collective-permute-done | bytes 221216 | tf_op jit(solution)/shard_map/ppermute | solution.py:72
  104.8 12.6 %input_grad.1 = bf16[1024,256]{1,0:T(8,128)(2,1)} custom-call(s32[16,256]{1,0:T(8,128)} %get-tuple-element.49.refs_0_, s32[1,64]{1,0:T(1,128)} %refs_1_.1, s32[33]{0:T(128)} %dynamic-slice_bitcast_fusion.refs_1_.refs_2_, bf16[1024,256]{1,0:T(8,128)(2,1)} %refs_3_.3, bf16[1024,256]{1,0:T(8,128)(2,1)} %refs_4_.1, f32[1,256]{1,0:T(1,128)} %bitcast.98, ...), custom_call_target="tpu_custom_call" | custom-call | flops 12999999488 | tf_op jit(solution)/shard_map/input_grad/pallas_call | solution.py:694
  117.5 1.9 %fusion.1 = f32[432,256]{1,0:T(8,128)} fusion(bf16[432,256]{1,0:T(8,128)(2,1)S(1)} %collective-permute-done.40, bf16[432,256]{1,0:T(8,128)(2,1)S(1)} %collective-permute-done.38, f32[8,432,256]{2,1,0:T(8,128)} %get-tuple-element.41, bf16[2,432,256]{2,1,0:T(8,128)(2,1)S(1)} %collective-permute-done.25), kind=kLoop, calls=%fused_computation.3 | loop fusion | flops 663552 | bytes 1548288 | tf_op jit(solution)/shard_map/add | solution.py:141
  (127 shorter events, 23.8 us)
Async XLA Ops:
  4.8 10.6 %collective-permute-start.1 = (bf16[656,256]{1,0:T(8,128)(2,1)}, bf16[656,256]{1,0:T(8,128)(2,1)S(1)}, u32[]{:S(2)}, u32[]{:S(2)}) collective-permute-start(bf16[656,256]{1,0:T(8,128)(2,1)} %get-tuple-element.37), channel_id=1, source_target_pairs={{0,4},{1,3},{4,8},{5,1},{8,12},{9,5},{12,14},{13,9},{14,10},{15,13... | collective-permute-start | bytes 1007624 | tf_op jit(solution)/shard_map/ppermute | solution.py:72
  7.9 11.2 %collective-permute-start.5 = (bf16[656,256]{1,0:T(8,128)(2,1)}, bf16[656,256]{1,0:T(8,128)(2,1)S(1)}, u32[]{:S(2)}, u32[]{:S(2)}) collective-permute-start(bf16[656,256]{1,0:T(8,128)(2,1)} %get-tuple-element.37), channel_id=1, source_target_pairs={{1,4},{0,3},{5,8},{4,1},{9,12},{8,5},{13,14},{12,9},{15,10},{14,13... | collective-permute-start | bytes 1007624 | tf_op jit(solution)/shard_map/ppermute | solution.py:72
  15.4 8.4 %collective-permute-start.2 = (bf16[656,256]{1,0:T(8,128)(2,1)S(1)}, bf16[656,256]{1,0:T(8,128)(2,1)S(1)}, u32[]{:S(2)}, u32[]{:S(2)}) collective-permute-start(bf16[656,256]{1,0:T(8,128)(2,1)S(1)} %collective-permute-done.1), channel_id=1, source_target_pairs={{0,4},{1,3},{4,8},{5,1},{8,12},{9,5},{12,14},{13,9},{14,10},{15,13... | collective-permute-start | bytes 1007624 | tf_op jit(solution)/shard_map/ppermute | solution.py:72
  19.1 8.4 %collective-permute-start.6 = (bf16[656,256]{1,0:T(8,128)(2,1)S(1)}, bf16[656,256]{1,0:T(8,128)(2,1)S(1)}, u32[]{:S(2)}, u32[]{:S(2)}) collective-permute-start(bf16[656,256]{1,0:T(8,128)(2,1)S(1)} %collective-permute-done.5), channel_id=1, source_target_pairs={{0,4},{1,3},{4,8},{5,1},{8,12},{9,5},{12,14},{13,9},{14,10},{15,13... | collective-permute-start | bytes 1007624 | tf_op jit(solution)/shard_map/ppermute | solution.py:72
  25.5 8.3 %collective-permute-start.8 = (bf16[656,256]{1,0:T(8,128)(2,1)S(1)}, bf16[656,256]{1,0:T(8,128)(2,1)S(1)}, u32[]{:S(2)}, u32[]{:S(2)}) collective-permute-start(bf16[656,256]{1,0:T(8,128)(2,1)S(1)} %collective-permute-done.1), channel_id=1, source_target_pairs={{0,1},{1,0},{2,3},{3,2},{4,5},{5,4},{6,7},{7,6},{8,9},{9,8},{10,11... | collective-permute-start | bytes 1007624 | tf_op jit(solution)/shard_map/ppermute | solution.py:76
  27.5 17.8 %collective-permute-start.7 = (bf16[656,256]{1,0:T(8,128)(2,1)S(1)}, bf16[656,256]{1,0:T(8,128)(2,1)S(1)}, u32[]{:S(2)}, u32[]{:S(2)}) collective-permute-start(bf16[656,256]{1,0:T(8,128)(2,1)S(1)} %collective-permute-done.6), channel_id=1, source_target_pairs={{0,4},{1,3},{4,8},{5,1},{8,12},{9,5},{12,14},{13,9},{14,10},{15,13... | collective-permute-start | bytes 1007624 | tf_op jit(solution)/shard_map/ppermute | solution.py:72
  31.1 14.7 %collective-permute-start.4 = (bf16[656,256]{1,0:T(8,128)(2,1)S(1)}, bf16[656,256]{1,0:T(8,128)(2,1)S(1)}, u32[]{:S(2)}, u32[]{:S(2)}) collective-permute-start(bf16[656,256]{1,0:T(8,128)(2,1)S(1)} %collective-permute-done.3), channel_id=1, source_target_pairs={{0,4},{1,3},{4,8},{5,1},{8,12},{9,5},{12,14},{13,9},{14,10},{15,13... | collective-permute-start | bytes 1007624 | tf_op jit(solution)/shard_map/ppermute | solution.py:72
  32.2 10.3 %collective-permute-start.17 = (bf16[640,256]{1,0:T(8,128)(2,1)}, bf16[640,256]{1,0:T(8,128)(2,1)S(1)}, u32[]{:S(2)}, u32[]{:S(2)}) collective-permute-start(bf16[640,256]{1,0:T(8,128)(2,1)} %extract.1), channel_id=1, source_target_pairs={{1,4},{0,3},{5,8},{4,1},{9,12},{8,5},{13,14},{12,9},{15,10},{14,13... | collective-permute-start | bytes 983048 | tf_op jit(solution)/shard_map/ppermute | solution.py:72
  32.2 13.1 %collective-permute-start.15 = (bf16[640,256]{1,0:T(8,128)(2,1)}, bf16[640,256]{1,0:T(8,128)(2,1)S(1)}, u32[]{:S(2)}, u32[]{:S(2)}) collective-permute-start(bf16[640,256]{1,0:T(8,128)(2,1)} %extract.1), channel_id=1, source_target_pairs={{0,4},{1,3},{4,8},{5,1},{8,12},{9,5},{12,14},{13,9},{14,10},{15,13... | collective-permute-start | bytes 983048 | tf_op jit(solution)/shard_map/ppermute | solution.py:72
  33.9 12.1 %collective-permute-start.13 = (bf16[656,256]{1,0:T(8,128)(2,1)S(1)}, bf16[656,256]{1,0:T(8,128)(2,1)S(1)}, u32[]{:S(2)}, u32[]{:S(2)}) collective-permute-start(bf16[656,256]{1,0:T(8,128)(2,1)S(1)} %collective-permute-done.6), channel_id=1, source_target_pairs={{0,1},{1,0},{2,3},{3,2},{4,5},{5,4},{6,7},{7,6},{8,9},{9,8},{10,11... | collective-permute-start | bytes 1007624 | tf_op jit(solution)/shard_map/ppermute | solution.py:76
  45.9 16.3 %collective-permute-start.16 = (bf16[640,256]{1,0:T(8,128)(2,1)S(1)}, bf16[640,256]{1,0:T(8,128)(2,1)S(1)}, u32[]{:S(2)}, u32[]{:S(2)}) collective-permute-start(bf16[640,256]{1,0:T(8,128)(2,1)S(1)} %collective-permute-done.15), channel_id=1, source_target_pairs={{0,4},{1,3},{4,8},{5,1},{8,12},{9,5},{12,14},{13,9},{14,10},{15,13... | collective-permute-start | bytes 983048 | tf_op jit(solution)/shard_map/ppermute | solution.py:72
  47.0 15.2 %collective-permute-start.18 = (bf16[640,256]{1,0:T(8,128)(2,1)S(1)}, bf16[640,256]{1,0:T(8,128)(2,1)S(1)}, u32[]{:S(2)}, u32[]{:S(2)}) collective-permute-start(bf16[640,256]{1,0:T(8,128)(2,1)S(1)} %collective-permute-done.17), channel_id=1, source_target_pairs={{0,4},{1,3},{4,8},{5,1},{8,12},{9,5},{12,14},{13,9},{14,10},{15,13... | collective-permute-start | bytes 983048 | tf_op jit(solution)/shard_map/ppermute | solution.py:72
  63.2 17.4 %collective-permute-start.22 = (bf16[640,256]{1,0:T(8,128)(2,1)S(1)}, bf16[640,256]{1,0:T(8,128)(2,1)}, u32[]{:S(2)}, u32[]{:S(2)}) collective-permute-start(bf16[640,256]{1,0:T(8,128)(2,1)S(1)} %collective-permute-done.16), channel_id=1, source_target_pairs={{0,4},{1,3},{4,8},{5,1},{8,12},{9,5},{12,14},{13,9},{14,10},{15,13... | collective-permute-start | bytes 983048 | tf_op jit(solution)/shard_map/ppermute | solution.py:72
  64.0 16.6 %collective-permute-start.23 = (bf16[640,256]{1,0:T(8,128)(2,1)S(1)}, bf16[640,256]{1,0:T(8,128)(2,1)S(1)}, u32[]{:S(2)}, u32[]{:S(2)}) collective-permute-start(bf16[640,256]{1,0:T(8,128)(2,1)S(1)} %collective-permute-done.18), channel_id=1, source_target_pairs={{0,4},{1,3},{4,8},{5,1},{8,12},{9,5},{12,14},{13,9},{14,10},{15,13... | collective-permute-start | bytes 983048 | tf_op jit(solution)/shard_map/ppermute | solution.py:72
  66.4 11.1 %collective-permute-start.20 = (bf16[2,432,256]{2,1,0:T(8,128)(2,1)}, bf16[2,432,256]{2,1,0:T(8,128)(2,1)S(1)}, u32[]{:S(2)}, u32[]{:S(2)}) collective-permute-start(bf16[2,432,256]{2,1,0:T(8,128)(2,1)} %get-tuple-element.51), channel_id=1, source_target_pairs={{0,1},{1,0},{2,3},{3,2},{4,5},{5,4},{6,7},{7,6},{8,9},{9,8},{10,11... | collective-permute-start | bytes 1327112 | tf_op jit(solution)/shard_map/ppermute | solution.py:76
  67.6 9.9 %collective-permute-start.24 = (bf16[432,256]{1,0:T(8,128)(2,1)S(1)}, bf16[432,256]{1,0:T(8,128)(2,1)S(1)}, u32[]{:S(2)}, u32[]{:S(2)}) collective-permute-start(bf16[432,256]{1,0:T(8,128)(2,1)S(1)} %get-tuple-element.73), channel_id=1, source_target_pairs={{0,2},{1,3},{4,0},{5,1},{8,4},{9,5},{12,8},{13,9},{14,12},{15,13},... | collective-permute-start | bytes 663560 | tf_op jit(solution)/shard_map/ppermute | solution.py:72
  67.7 10.8 %collective-permute-start.21 = (bf16[432,256]{1,0:T(8,128)(2,1)S(1)}, bf16[432,256]{1,0:T(8,128)(2,1)S(1)}, u32[]{:S(2)}, u32[]{:S(2)}) collective-permute-start(bf16[432,256]{1,0:T(8,128)(2,1)S(1)} %get-tuple-element.74), channel_id=1, source_target_pairs={{0,4},{1,5},{4,8},{5,9},{8,12},{9,13},{12,14},{13,15},{14,10},{15,... | collective-permute-start | bytes 663560 | tf_op jit(solution)/shard_map/ppermute | solution.py:72
  77.4 12.9 %collective-permute-start.26 = (bf16[2,432,256]{2,1,0:T(8,128)(2,1)}, bf16[2,432,256]{2,1,0:T(8,128)(2,1)}, u32[]{:S(2)}, u32[]{:S(2)}) collective-permute-start(bf16[2,432,256]{2,1,0:T(8,128)(2,1)} %get-tuple-element.60), channel_id=1, source_target_pairs={{0,1},{1,0},{2,3},{3,2},{4,5},{5,4},{6,7},{7,6},{8,9},{9,8},{10,11... | collective-permute-start | bytes 1327112 | tf_op jit(solution)/shard_map/ppermute | solution.py:76
  80.6 10.2 %collective-permute-start.27 = (bf16[432,256]{1,0:T(8,128)(2,1)}, bf16[432,256]{1,0:T(8,128)(2,1)}, u32[]{:S(2)}, u32[]{:S(2)}) collective-permute-start(bf16[432,256]{1,0:T(8,128)(2,1)} %get-tuple-element.54), channel_id=1, source_target_pairs={{0,4},{1,5},{4,8},{5,9},{8,12},{9,13},{12,14},{13,15},{14,10},{15,... | collective-permute-start | bytes 663560 | tf_op jit(solution)/shard_map/ppermute | solution.py:72
  81.5 9.3 %collective-permute-start.39 = (bf16[432,256]{1,0:T(8,128)(2,1)}, bf16[432,256]{1,0:T(8,128)(2,1)}, u32[]{:S(2)}, u32[]{:S(2)}) collective-permute-start(bf16[432,256]{1,0:T(8,128)(2,1)} %get-tuple-element.55), channel_id=1, source_target_pairs={{0,2},{1,3},{4,0},{5,1},{8,4},{9,5},{12,8},{13,9},{14,12},{15,13},... | collective-permute-start | bytes 663560 | tf_op jit(solution)/shard_map/ppermute | solution.py:72
  82.7 10.2 %collective-permute-start.28 = (bf16[640,256]{1,0:T(8,128)(2,1)}, bf16[640,256]{1,0:T(8,128)(2,1)}, u32[]{:S(2)}, u32[]{:S(2)}) collective-permute-start(bf16[640,256]{1,0:T(8,128)(2,1)} %collective-permute-done.22), channel_id=1, source_target_pairs={{0,4},{1,3},{4,8},{5,1},{8,12},{9,5},{12,14},{13,9},{14,10},{15,13... | collective-permute-start | bytes 983048 | tf_op jit(solution)/shard_map/ppermute | solution.py:72
  83.9 11.3 %collective-permute-start.30 = (bf16[640,256]{1,0:T(8,128)(2,1)}, bf16[640,256]{1,0:T(8,128)(2,1)}, u32[]{:S(2)}, u32[]{:S(2)}) collective-permute-start(bf16[640,256]{1,0:T(8,128)(2,1)} %extract.1), channel_id=1, source_target_pairs={{0,1},{1,0},{2,3},{3,2},{4,5},{5,4},{6,7},{7,6},{8,9},{9,8},{10,11... | collective-permute-start | bytes 983048 | tf_op jit(solution)/shard_map/ppermute | solution.py:76
  101.7 15.8 %collective-permute-start.40 = (bf16[432,256]{1,0:T(8,128)(2,1)S(1)}, bf16[432,256]{1,0:T(8,128)(2,1)S(1)}, u32[]{:S(2)}, u32[]{:S(2)}) collective-permute-start(bf16[432,256]{1,0:T(8,128)(2,1)S(1)} %get-tuple-element.68), channel_id=1, source_target_pairs={{0,2},{1,3},{4,0},{5,1},{8,4},{9,5},{12,8},{13,9},{14,12},{15,13},... | collective-permute-start | bytes 663560 | tf_op jit(solution)/shard_map/ppermute | solution.py:72
  102.6 14.9 %collective-permute-start.38 = (bf16[432,256]{1,0:T(8,128)(2,1)S(1)}, bf16[432,256]{1,0:T(8,128)(2,1)S(1)}, u32[]{:S(2)}, u32[]{:S(2)}) collective-permute-start(bf16[432,256]{1,0:T(8,128)(2,1)S(1)} %fusion.3), channel_id=1, source_target_pairs={{0,4},{1,5},{4,8},{5,9},{8,12},{9,13},{12,14},{13,15},{14,10},{15,... | collective-permute-start | bytes 663560 | tf_op jit(solution)/shard_map/ppermute | solution.py:72
  (45 other events, 396.4 us)

commit v8 on v6

--- a/solution.py
+++ b/solution.py
@@ -491,14 +491,14 @@
         out_ref[at, :] = (x_ref[at, :].astype(F32) + total).astype(BF16)
 
 
-def input_grad_body(slots, peers, count, *refs):
-    served, send, table, cot_ref, x_ref, gain_ref, weight_ref = refs[:7]
-    parts = refs[7 : 7 + count]
-    out_ref, cells, halo, cols, share, weight, heads, more, sems, weight_sem = refs[7 + count :]
+def input_grad_body(slots, peers, *refs):
+    served, send, table, cot_ref, x_ref, gain_ref, weight_ref, all_ref = refs[:8]
+    out_ref, cells, halo, cols, share, weight, heads, more, sems = refs[8:]
     bricks = cot_ref.shape[0] // 512
     me = table[2 * peers]
-    copies = fetch(parts, share, sems)
-    weight_copy = pltpu.make_async_copy(weight_ref, weight, weight_sem.at[0])
+    share_copy = pltpu.make_async_copy(all_ref, share, sems.at[0])
+    share_copy.start()
+    weight_copy = pltpu.make_async_copy(weight_ref, weight, sems.at[1])
     weight_copy.start()
 
     def no_head(k, _):
@@ -509,8 +509,7 @@
 
     def source_of(k):
         receiver = k // slots
-        at = table[receiver]
-        return at, served[at, me * slots + k - receiver * slots] - 1
+        return receiver, served[table[receiver], me * slots + k - receiver * slots] - 1
 
     def sort(k, found):
         _, entry = source_of(k)
@@ -531,8 +530,7 @@
 
     found = lax.fori_loop(0, send.shape[1], sort, 0)
     start_padded(cot_ref, cells, halo, bricks)
-    for copy in copies:
-        copy.wait()
+    share_copy.wait()
     for brick in range(bricks):
         for number, e in enumerate(DIRECTIONS):
             head = heads[brick * 26 + number]
@@ -566,10 +564,12 @@
     for brick in range(bricks):
         rows = slice(brick * 512, brick * 512 + 512)
         grad = None
-        for i in range(3):
-            left = cols[brick * 10 + i : brick * 10 + i + 8].reshape(512, 9 * C)
-            right = weight[i * 9 * C : (i + 1) * 9 * C, :]
-            term = jnp.dot(left, right, preferred_element_type=F32)
+        for tap in range(27):
+            i, jl = divmod(tap, 9)
+            first = brick * 10 + i
+            left = cols[first : first + 8, :, jl * C : jl * C + C].reshape(512, C)
+            right = weight[(26 - tap) * C : (27 - tap) * C, :]
+            term = lax.dot_general(left, right, (((1,), (1,)), ((), ())), preferred_element_type=F32)
             grad = term if grad is None else grad + term
         x = x_ref[rows, :].astype(F32)
         inverse = lax.rsqrt(jnp.mean(x * x, axis=-1, keepdims=True) + 1e-6)
@@ -627,10 +627,7 @@
     hidden_ring.go(1)
     hidden_ring.go(0)
     hidden_parts = hidden_ring.places()
-
-    cot_ring = RingGather(cot_share, peers)
-    cot_ring.go(0, hidden_ring.last(1))
-    cot_ring.go(1, hidden_ring.last(0))
+    cot_all = lax.all_gather(cot_share[None], "morton", axis=0, tiled=True)
 
     count = len(hidden_parts)
     rows = 27 * channels // peers
@@ -663,13 +660,8 @@
         out_specs=(*[HBM] * (2 + chips // 2), VMEM, VMEM),
     )(recv_slot, table, hidden, cotangent, *hidden_parts)
 
-    first = (cot_ring.last(0), cot_ring.last(1))
-    give = [lax.optimization_barrier((t, first))[0] for t in give]
     sums_ring = RingScatter(keep, give, peers)
     sent = sums_ring.go()
-    cot_ring.go(0, cols)
-    cot_ring.go(1, cols)
-    second = (cot_ring.last(0), cot_ring.last(1))
     mix_cols = lax.optimization_barrier((cols, sent))[0]
     weight_scratch = [
         pltpu.VMEM((27 * channels, channels), BF16),
@@ -683,23 +675,15 @@
         cost=6,
         name="mix",
     )(mix_cols, conv_weight, features)
-    sent = sums_ring.go((second, mixed))
-    cot_ring.go(0)
-    cot_ring.go(1)
-    third = (cot_ring.last(0), cot_ring.last(1))
-    turned = lax.optimization_barrier((conv_weight, sent))[0]
-    turned = turned.reshape(27, channels, channels)[::-1].transpose(0, 2, 1)
-    turned = turned.reshape(27 * channels, channels)
-    sums_ring.go((third, turned))
-    cot_ring.go(0)
-    sent = sums_ring.go(cot_ring.last(0))
-    cot_parts = cot_ring.places(cols)
-    turned = lax.optimization_barrier((turned, sent))[0]
+    sums_ring.go(mixed)
+    sums_ring.go()
+    sent = sums_ring.go()
+    served = lax.optimization_barrier((served, sent))[0]
 
     grad_features = call(
-        functools.partial(input_grad_body, slots, peers, count),
+        functools.partial(input_grad_body, slots, peers),
         sds((per_device, channels), BF16),
-        [SMEM] * 3 + [VMEM] * 3 + [HBM] * (1 + count),
+        [SMEM] * 3 + [VMEM] * 3 + [HBM] * 2,
         padded(bricks)
         + [
             pltpu.VMEM(cols_shape(bricks), BF16),
@@ -707,12 +691,11 @@
             weight_scratch[0],
             pltpu.SMEM((bricks * 26,), jnp.int32),
             pltpu.SMEM((peers * slots,), jnp.int32),
-            pltpu.SemaphoreType.DMA((count,)),
-            pltpu.SemaphoreType.DMA((1,)),
+            pltpu.SemaphoreType.DMA((2,)),
         ],
         cost=13,
         name="input_grad",
-    )(served, send_face, table, cotangent, features, gain, turned, *cot_parts)
+    )(served, send_face, table, cotangent, features, gain, conv_weight, cot_all)
     for _ in range(chips // 2 - 4):
         sums_ring.go()
     return (mixed, grad_features, sums_ring.total())

time: 115 us -> 146 us (1.27); the launches traced: 115 us -> 144 us
  waiting for transfers between devices: 27.2 us -> 52 us
  between operations: 1.08 us -> 14.3 us
  local copies, waits for them, and re-layouts: 9.45 us -> 1.96 us
  other arithmetic: 7.89 us -> 2.55 us
  starting transfers between devices: 29.7 us -> 34.7 us
    ppermute x21 -> x14, waiting for transfers between devices: 27.1 us -> 49.5 us  [ring_step(): return lax.ppermute(x, 'morton', pairs)]
    reshape x1 -> x0, local copies, waits for them, and re-layouts: 4.44 us -> none  [local(): turned = turned.reshape(27, channels, channels)[::-1].transpose(0, 2, 1)]
    convert_element_type x4, other arithmetic: 6 us -> 1.66 us  [go(): part = part.astype(BF16)]
    ppermute x20 -> x12, starting transfers between devices: 3.27 us -> 7.12 us  [swap_cores(): return lax.ppermute(x, 'morton', [(m, m ^ 1) for m in range(peers)])]
    ppermute x20 -> x12, waiting for transfers between devices: 0.05 us -> 2.54 us  [swap_cores(): return lax.ppermute(x, 'morton', [(m, m ^ 1) for m in range(peers)])]
    rev x1 -> x0, local copies, waits for them, and re-layouts: 1.99 us -> none  [local(): turned = turned.reshape(27, channels, channels)[::-1].transpose(0, 2, 1)]
    pallas_call x1, Pallas kernels: 13 us -> 11.4 us  [local(): call(functools.partial(input_grad_body, slots, peers), sds((per_device, c...]
    ppermute x21 -> x14, starting transfers between devices: 26.4 us -> 27.6 us  [ring_step(): return lax.ppermute(x, 'morton', pairs)]
  transfers between devices with their start and end apart: 41 -> 27, of which waited for: 10 -> 12; matrix products, arithmetic and copies ran while one was open for 12% -> 3% of each run, Pallas kernels for 31% -> 17%
where the time goes in v8:
time: 146 us; the launch traced here: 144 us
  waiting for transfers between devices  52 us (36%)
  Pallas kernels  38.5 us (26%)
  starting transfers between devices  34.7 us (24%)
  between operations  14.3 us (10%)
  other arithmetic  2.55 us (2%)
  local copies, waits for them, and re-layouts  1.96 us (1%)
    ppermute x14, waiting for transfers between devices, ring_step(): return lax.ppermute(x, 'morton', pairs)  49.5 us
    ppermute x14, starting transfers between devices, ring_step(): return lax.ppermute(x, 'morton', pairs)  27.6 us
    pallas_call x1, Pallas kernels, local(): call(functools.partial(weight_grad_body, slots, factor, peers, count), (s...  12.6 us
    pallas_call x1, Pallas kernels, local(): call(functools.partial(input_grad_body, slots, peers), sds((per_device, c...  11.4 us
    pallas_call x1, Pallas kernels, local(): call(mix_body, sds((per_device, channels), BF16), [HBM, HBM, VMEM], [pltp...  8 us
    ppermute x12, starting transfers between devices, swap_cores(): return lax.ppermute(x, 'morton', [(m, m ^ 1) for m in range(peers)])  7.12 us
    pallas_call x1, Pallas kernels, local(): call(norm_body, (sds((per_device, channels), BF16), sds((bricks * ROWS +...  4.2 us
  transfers between devices with their start and end apart: 27, of which 12 were waited for; matrix products, arithmetic and copies ran while one was open for 3% of the time, Pallas kernels for 17%

profile of v8, /device:TPU:0, one launch (start us, length us, event | category | flops | bytes accessed | tf_op | source)
XLA Modules:
  0.0 144.1 jit_solution(5786864954878924481)
XLA Ops:
  7.2 2.2 %extract.1 = bf16[640,256]{1,0:T(8,128)(2,1)} custom-call(bf16[1024,256]{1,0:T(8,128)(2,1)} %refs_3_.3), custom_call_target="tpu_custom_call" | custom-call | flops 2000000000 | tf_op jit(solution)/shard_map/extract/pallas_call | solution.py:615
  9.5 4.2 %norm.1 = (bf16[1024,256]{1,0:T(8,128)(2,1)}, bf16[656,256]{1,0:T(8,128)(2,1)}) custom-call(s32[2,26]{1,0:T(2,128)} %refs_0_.1, s32[1,64]{1,0:T(1,128)} %refs_1_.1, bf16[1024,256]{1,0:T(8,128)(2,1)} %refs_4_.1, f32[1,256]{1,0:T(1,128)} %bitcast.65), custom_call_target="tpu_custom_call" | custom-call | flops 2000000000 | tf_op jit(solution)/shard_map/norm/pallas_call | solution.py:607
  13.7 3.0 %collective-permute-start.1 = (bf16[656,256]{1,0:T(8,128)(2,1)}, bf16[656,256]{1,0:T(8,128)(2,1)S(1)}, u32[]{:S(2)}, u32[]{:S(2)}) collective-permute-start(bf16[656,256]{1,0:T(8,128)(2,1)} %get-tuple-element.19), channel_id=1, source_target_pairs={{0,4},{1,3},{4,8},{5,1},{8,12},{9,5},{12,14},{13,9},{14,10},{15,13... | collective-permute-start | bytes 1007624 | tf_op jit(solution)/shard_map/ppermute | solution.py:72
  17.4 9.2 %collective-permute-done.1 = bf16[656,256]{1,0:T(8,128)(2,1)S(1)} collective-permute-done((bf16[656,256]{1,0:T(8,128)(2,1)}, bf16[656,256]{1,0:T(8,128)(2,1)S(1)}, u32[]{:S(2)}, u32[]{:S(2)}) %collective-permute-start.1) | collective-permute-done | bytes 335904 | tf_op jit(solution)/shard_map/ppermute | solution.py:72
  26.6 2.4 %collective-permute-start.2 = (bf16[656,256]{1,0:T(8,128)(2,1)S(1)}, bf16[656,256]{1,0:T(8,128)(2,1)S(1)}, u32[]{:S(2)}, u32[]{:S(2)}) collective-permute-start(bf16[656,256]{1,0:T(8,128)(2,1)S(1)} %collective-permute-done.1), channel_id=1, source_target_pairs={{0,4},{1,3},{4,8},{5,1},{8,12},{9,5},{12,14},{13,9},{14,10},{15,13... | collective-permute-start | bytes 1007624 | tf_op jit(solution)/shard_map/ppermute | solution.py:72
  30.3 3.1 %collective-permute-start.6 = (bf16[656,256]{1,0:T(8,128)(2,1)S(1)}, bf16[656,256]{1,0:T(8,128)(2,1)S(1)}, u32[]{:S(2)}, u32[]{:S(2)}) collective-permute-start(bf16[656,256]{1,0:T(8,128)(2,1)S(1)} %collective-permute-done.5), channel_id=1, source_target_pairs={{0,4},{1,3},{4,8},{5,1},{8,12},{9,5},{12,14},{13,9},{14,10},{15,13... | collective-permute-start | bytes 1007624 | tf_op jit(solution)/shard_map/ppermute | solution.py:72
  33.4 5.9 %collective-permute-done.2 = bf16[656,256]{1,0:T(8,128)(2,1)S(1)} collective-permute-done((bf16[656,256]{1,0:T(8,128)(2,1)S(1)}, bf16[656,256]{1,0:T(8,128)(2,1)S(1)}, u32[]{:S(2)}, u32[]{:S(2)}) %collective-permute-start.2) | collective-permute-done | bytes 335904 | tf_op jit(solution)/shard_map/ppermute | solution.py:72
  39.3 2.5 %collective-permute-start.3 = (bf16[656,256]{1,0:T(8,128)(2,1)S(1)}, bf16[656,256]{1,0:T(8,128)(2,1)S(1)}, u32[]{:S(2)}, u32[]{:S(2)}) collective-permute-start(bf16[656,256]{1,0:T(8,128)(2,1)S(1)} %collective-permute-done.2), channel_id=1, source_target_pairs={{0,4},{1,3},{4,8},{5,1},{8,12},{9,5},{12,14},{13,9},{14,10},{15,13... | collective-permute-start | bytes 1007624 | tf_op jit(solution)/shard_map/ppermute | solution.py:72
  42.9 2.5 %collective-permute-start.7 = (bf16[656,256]{1,0:T(8,128)(2,1)S(1)}, bf16[656,256]{1,0:T(8,128)(2,1)S(1)}, u32[]{:S(2)}, u32[]{:S(2)}) collective-permute-start(bf16[656,256]{1,0:T(8,128)(2,1)S(1)} %collective-permute-done.6), channel_id=1, source_target_pairs={{0,4},{1,3},{4,8},{5,1},{8,12},{9,5},{12,14},{13,9},{14,10},{15,13... | collective-permute-start | bytes 1007624 | tf_op jit(solution)/shard_map/ppermute | solution.py:72
  45.4 4.0 %collective-permute-done.3 = bf16[656,256]{1,0:T(8,128)(2,1)S(1)} collective-permute-done((bf16[656,256]{1,0:T(8,128)(2,1)S(1)}, bf16[656,256]{1,0:T(8,128)(2,1)S(1)}, u32[]{:S(2)}, u32[]{:S(2)}) %collective-permute-start.3) | collective-permute-done | bytes 335904 | tf_op jit(solution)/shard_map/ppermute | solution.py:72
  49.4 3.4 %collective-permute-start.4 = (bf16[656,256]{1,0:T(8,128)(2,1)S(1)}, bf16[656,256]{1,0:T(8,128)(2,1)S(1)}, u32[]{:S(2)}, u32[]{:S(2)}) collective-permute-start(bf16[656,256]{1,0:T(8,128)(2,1)S(1)} %collective-permute-done.3), channel_id=1, source_target_pairs={{0,4},{1,3},{4,8},{5,1},{8,12},{9,5},{12,14},{13,9},{14,10},{15,13... | collective-permute-start | bytes 1007624 | tf_op jit(solution)/shard_map/ppermute | solution.py:72
  53.4 6.8 %collective-permute-done.7 = bf16[656,256]{1,0:T(8,128)(2,1)S(1)} collective-permute-done((bf16[656,256]{1,0:T(8,128)(2,1)S(1)}, bf16[656,256]{1,0:T(8,128)(2,1)S(1)}, u32[]{:S(2)}, u32[]{:S(2)}) %collective-permute-start.7) | collective-permute-done | bytes 335904 | tf_op jit(solution)/shard_map/ppermute | solution.py:72
  60.2 8.9 %collective-permute-done.4 = bf16[656,256]{1,0:T(8,128)(2,1)S(1)} collective-permute-done((bf16[656,256]{1,0:T(8,128)(2,1)S(1)}, bf16[656,256]{1,0:T(8,128)(2,1)S(1)}, u32[]{:S(2)}, u32[]{:S(2)}) %collective-permute-start.4) | collective-permute-done | bytes 335904 | tf_op jit(solution)/shard_map/ppermute | solution.py:72
  69.2 5.1 %collective-permute-start.11 = (bf16[656,256]{1,0:T(8,128)(2,1)S(1)}, bf16[656,256]{1,0:T(8,128)(2,1)S(1)}, u32[]{:S(2)}, u32[]{:S(2)}) collective-permute-start(bf16[656,256]{1,0:T(8,128)(2,1)S(1)} %collective-permute-done.4), channel_id=1, source_target_pairs={{0,1},{1,0},{2,3},{3,2},{4,5},{5,4},{6,7},{7,6},{8,9},{9,8},{10,11... | collective-permute-start | bytes 1007624 | tf_op jit(solution)/shard_map/ppermute | solution.py:76
  76.4 12.6 %weight_grad.1 = (f32[8,432,256]{2,1,0:T(8,128)}, bf16[2,432,256]{2,1,0:T(8,128)(2,1)}, bf16[2,432,256]{2,1,0:T(8,128)(2,1)}, bf16[2,432,256]{2,1,0:T(8,128)(2,1...) custom-call(s32[2,26]{1,0:T(2,128)} %refs_0_.1, ...), custom_call_target="tpu_custom_call" | custom-call | flops 8999999488 | tf_op jit(solution)/shard_map/weight_grad/pallas_call | solution.py:635
  92.3 1.5 %collective-permute-start.19 = (bf16[432,256]{1,0:T(8,128)(2,1)S(1)}, bf16[432,256]{1,0:T(8,128)(2,1)S(1)}, u32[]{:S(2)}, u32[]{:S(2)}) collective-permute-start(bf16[432,256]{1,0:T(8,128)(2,1)S(1)} %get-tuple-element.38), channel_id=1, source_target_pairs={{0,4},{1,5},{4,8},{5,9},{8,12},{9,13},{12,14},{13,15},{14,10},{15,... | collective-permute-start | bytes 663560 | tf_op jit(solution)/shard_map/ppermute | solution.py:72
  93.9 2.8 %collective-permute-start.23 = (bf16[432,256]{1,0:T(8,128)(2,1)S(1)}, bf16[432,256]{1,0:T(8,128)(2,1)S(1)}, u32[]{:S(2)}, u32[]{:S(2)}) collective-permute-start(bf16[432,256]{1,0:T(8,128)(2,1)S(1)} %get-tuple-element.37), channel_id=1, source_target_pairs={{0,2},{1,3},{4,0},{5,1},{8,4},{9,5},{12,8},{13,9},{14,12},{15,13},... | collective-permute-start | bytes 663560 | tf_op jit(solution)/shard_map/ppermute | solution.py:72
  96.7 8.0 %mix.1 = bf16[1024,256]{1,0:T(8,128)(2,1)} custom-call(bf16[20,64,2304]{2,1,0:T(8,128)(2,1)} %get-tuple-element.25.cols_ref, bf16[6912,256]{1,0:T(8,128)(2,1)} %refs_6_.1, bf16[1024,256]{1,0:T(8,128)(2,1)} %refs_4_.1), custom_call_target="tpu_custom_call" | custom-call | flops 6000000000 | tf_op jit(solution)/shard_map/mix/pallas_call | solution.py:670
  105.0 2.0 %collective-permute-start.24 = (bf16[432,256]{1,0:T(8,128)(2,1)S(1)}, bf16[432,256]{1,0:T(8,128)(2,1)S(1)}, u32[]{:S(2)}, u32[]{:S(2)}) collective-permute-start(bf16[432,256]{1,0:T(8,128)(2,1)S(1)} %get-tuple-element.32), channel_id=1, source_target_pairs={{0,2},{1,3},{4,0},{5,1},{8,4},{9,5},{12,8},{13,9},{14,12},{15,13},... | collective-permute-start | bytes 663560 | tf_op jit(solution)/shard_map/ppermute | solution.py:72
  107.0 5.2 %collective-permute-done.20 = bf16[432,256]{1,0:T(8,128)(2,1)S(1)} collective-permute-done((bf16[432,256]{1,0:T(8,128)(2,1)S(1)}, bf16[432,256]{1,0:T(8,128)(2,1)S(1)}, u32[]{:S(2)}, u32[]{:S(2)}) %collective-permute-start.20) | collective-permute-done | bytes 221216 | tf_op jit(solution)/shard_map/ppermute | solution.py:72
  112.4 1.8 %collective-permute-start.21 = (bf16[432,256]{1,0:T(8,128)(2,1)S(1)}, bf16[432,256]{1,0:T(8,128)(2,1)S(1)}, u32[]{:S(2)}, u32[]{:S(2)}) collective-permute-start(bf16[432,256]{1,0:T(8,128)(2,1)S(1)} %get-tuple-element.34), channel_id=1, source_target_pairs={{0,4},{1,5},{4,8},{5,9},{8,12},{9,13},{12,14},{13,15},{14,10},{15,... | collective-permute-start | bytes 663560 | tf_op jit(solution)/shard_map/ppermute | solution.py:72
  114.5 4.3 %collective-permute-done.21 = bf16[432,256]{1,0:T(8,128)(2,1)S(1)} collective-permute-done((bf16[432,256]{1,0:T(8,128)(2,1)S(1)}, bf16[432,256]{1,0:T(8,128)(2,1)S(1)}, u32[]{:S(2)}, u32[]{:S(2)}) %collective-permute-start.21) | collective-permute-done | bytes 221216 | tf_op jit(solution)/shard_map/ppermute | solution.py:72
  120.4 4.5 %collective-permute-done.22 = bf16[432,256]{1,0:T(8,128)(2,1)S(1)} collective-permute-done((bf16[432,256]{1,0:T(8,128)(2,1)S(1)}, bf16[432,256]{1,0:T(8,128)(2,1)S(1)}, u32[]{:S(2)}, u32[]{:S(2)}) %collective-permute-start.22) | collective-permute-done | bytes 221216 | tf_op jit(solution)/shard_map/ppermute | solution.py:72
  125.8 11.4 %input_grad.1 = bf16[1024,256]{1,0:T(8,128)(2,1)} custom-call(s32[16,256]{1,0:T(8,128)} %get-tuple-element.31.refs_0_, s32[1,64]{1,0:T(1,128)} %refs_1_.1, s32[33]{0:T(128)} %dynamic-slice_bitcast_fusion.refs_1_.refs_2_, bf16[1024,256]{1,0:T(8,128)(2,1)} %refs_3_.3, bf16[1024,256]{1,0:T(8,128)(2,1)} %refs_4_.1, f32[1,256]{1,0:T(1,128)} %bitcast.66, ...), custom_call_target="tpu_custom_call" | custom-call | flops 12999999488 | tf_op jit(solution)/shard_map/input_grad/pallas_call | solution.py:683
  (76 shorter events, 12.4 us)
Async XLA Ops:
  7.2 118.6 %all-gather.3.cloned.1.call-start = ((), (), s32[]{:S(2)}) async-start(), calls=%async_computation | async-start | bytes 5570560 | tf_op jit(solution)/shard_map/all_gather | solution.py:630
  13.7 12.9 %collective-permute-start.1 = (bf16[656,256]{1,0:T(8,128)(2,1)}, bf16[656,256]{1,0:T(8,128)(2,1)S(1)}, u32[]{:S(2)}, u32[]{:S(2)}) collective-permute-start(bf16[656,256]{1,0:T(8,128)(2,1)} %get-tuple-element.19), channel_id=1, source_target_pairs={{0,4},{1,3},{4,8},{5,1},{8,12},{9,5},{12,14},{13,9},{14,10},{15,13... | collective-permute-start | bytes 1007624 | tf_op jit(solution)/shard_map/ppermute | solution.py:72
  16.7 13.6 %collective-permute-start.5 = (bf16[656,256]{1,0:T(8,128)(2,1)}, bf16[656,256]{1,0:T(8,128)(2,1)S(1)}, u32[]{:S(2)}, u32[]{:S(2)}) collective-permute-start(bf16[656,256]{1,0:T(8,128)(2,1)} %get-tuple-element.19), channel_id=1, source_target_pairs={{1,4},{0,3},{5,8},{4,1},{9,12},{8,5},{13,14},{12,9},{15,10},{14,13... | collective-permute-start | bytes 1007624 | tf_op jit(solution)/shard_map/ppermute | solution.py:72
  26.6 12.7 %collective-permute-start.2 = (bf16[656,256]{1,0:T(8,128)(2,1)S(1)}, bf16[656,256]{1,0:T(8,128)(2,1)S(1)}, u32[]{:S(2)}, u32[]{:S(2)}) collective-permute-start(bf16[656,256]{1,0:T(8,128)(2,1)S(1)} %collective-permute-done.1), channel_id=1, source_target_pairs={{0,4},{1,3},{4,8},{5,1},{8,12},{9,5},{12,14},{13,9},{14,10},{15,13... | collective-permute-start | bytes 1007624 | tf_op jit(solution)/shard_map/ppermute | solution.py:72
  30.3 12.7 %collective-permute-start.6 = (bf16[656,256]{1,0:T(8,128)(2,1)S(1)}, bf16[656,256]{1,0:T(8,128)(2,1)S(1)}, u32[]{:S(2)}, u32[]{:S(2)}) collective-permute-start(bf16[656,256]{1,0:T(8,128)(2,1)S(1)} %collective-permute-done.5), channel_id=1, source_target_pairs={{0,4},{1,3},{4,8},{5,1},{8,12},{9,5},{12,14},{13,9},{14,10},{15,13... | collective-permute-start | bytes 1007624 | tf_op jit(solution)/shard_map/ppermute | solution.py:72
  39.3 10.1 %collective-permute-start.3 = (bf16[656,256]{1,0:T(8,128)(2,1)S(1)}, bf16[656,256]{1,0:T(8,128)(2,1)S(1)}, u32[]{:S(2)}, u32[]{:S(2)}) collective-permute-start(bf16[656,256]{1,0:T(8,128)(2,1)S(1)} %collective-permute-done.2), channel_id=1, source_target_pairs={{0,4},{1,3},{4,8},{5,1},{8,12},{9,5},{12,14},{13,9},{14,10},{15,13... | collective-permute-start | bytes 1007624 | tf_op jit(solution)/shard_map/ppermute | solution.py:72
  41.8 11.0 %collective-permute-start = (bf16[656,256]{1,0:T(8,128)(2,1)}, bf16[656,256]{1,0:T(8,128)(2,1)S(1)}, u32[]{:S(2)}, u32[]{:S(2)}) collective-permute-start(bf16[656,256]{1,0:T(8,128)(2,1)} %get-tuple-element.19), channel_id=1, source_target_pairs={{0,1},{1,0},{2,3},{3,2},{4,5},{5,4},{6,7},{7,6},{8,9},{9,8},{10,11... | collective-permute-start | bytes 1007624 | tf_op jit(solution)/shard_map/ppermute | solution.py:76
  41.8 11.0 %collective-permute-start.8 = (bf16[656,256]{1,0:T(8,128)(2,1)S(1)}, bf16[656,256]{1,0:T(8,128)(2,1)S(1)}, u32[]{:S(2)}, u32[]{:S(2)}) collective-permute-start(bf16[656,256]{1,0:T(8,128)(2,1)S(1)} %collective-permute-done.1), channel_id=1, source_target_pairs={{0,1},{1,0},{2,3},{3,2},{4,5},{5,4},{6,7},{7,6},{8,9},{9,8},{10,11... | collective-permute-start | bytes 1007624 | tf_op jit(solution)/shard_map/ppermute | solution.py:76
  42.3 11.0 %collective-permute-start.12 = (bf16[656,256]{1,0:T(8,128)(2,1)S(1)}, bf16[656,256]{1,0:T(8,128)(2,1)S(1)}, u32[]{:S(2)}, u32[]{:S(2)}) collective-permute-start(bf16[656,256]{1,0:T(8,128)(2,1)S(1)} %collective-permute-done.5), channel_id=1, source_target_pairs={{0,1},{1,0},{2,3},{3,2},{4,5},{5,4},{6,7},{7,6},{8,9},{9,8},{10,11... | collective-permute-start | bytes 1007624 | tf_op jit(solution)/shard_map/ppermute | solution.py:76
  42.9 17.3 %collective-permute-start.7 = (bf16[656,256]{1,0:T(8,128)(2,1)S(1)}, bf16[656,256]{1,0:T(8,128)(2,1)S(1)}, u32[]{:S(2)}, u32[]{:S(2)}) collective-permute-start(bf16[656,256]{1,0:T(8,128)(2,1)S(1)} %collective-permute-done.6), channel_id=1, source_target_pairs={{0,4},{1,3},{4,8},{5,1},{8,12},{9,5},{12,14},{13,9},{14,10},{15,13... | collective-permute-start | bytes 1007624 | tf_op jit(solution)/shard_map/ppermute | solution.py:72
  49.4 19.8 %collective-permute-start.4 = (bf16[656,256]{1,0:T(8,128)(2,1)S(1)}, bf16[656,256]{1,0:T(8,128)(2,1)S(1)}, u32[]{:S(2)}, u32[]{:S(2)}) collective-permute-start(bf16[656,256]{1,0:T(8,128)(2,1)S(1)} %collective-permute-done.3), channel_id=1, source_target_pairs={{0,4},{1,3},{4,8},{5,1},{8,12},{9,5},{12,14},{13,9},{14,10},{15,13... | collective-permute-start | bytes 1007624 | tf_op jit(solution)/shard_map/ppermute | solution.py:72
  52.8 21.4 %collective-permute-start.9 = (bf16[656,256]{1,0:T(8,128)(2,1)S(1)}, bf16[656,256]{1,0:T(8,128)(2,1)S(1)}, u32[]{:S(2)}, u32[]{:S(2)}) collective-permute-start(bf16[656,256]{1,0:T(8,128)(2,1)S(1)} %collective-permute-done.2), channel_id=1, source_target_pairs={{0,1},{1,0},{2,3},{3,2},{4,5},{5,4},{6,7},{7,6},{8,9},{9,8},{10,11... | collective-permute-start | bytes 1007624 | tf_op jit(solution)/shard_map/ppermute | solution.py:76
  52.8 21.4 %collective-permute-start.13 = (bf16[656,256]{1,0:T(8,128)(2,1)S(1)}, bf16[656,256]{1,0:T(8,128)(2,1)S(1)}, u32[]{:S(2)}, u32[]{:S(2)}) collective-permute-start(bf16[656,256]{1,0:T(8,128)(2,1)S(1)} %collective-permute-done.6), channel_id=1, source_target_pairs={{0,1},{1,0},{2,3},{3,2},{4,5},{5,4},{6,7},{7,6},{8,9},{9,8},{10,11... | collective-permute-start | bytes 1007624 | tf_op jit(solution)/shard_map/ppermute | solution.py:76
  53.3 20.9 %collective-permute-start.10 = (bf16[656,256]{1,0:T(8,128)(2,1)S(1)}, bf16[656,256]{1,0:T(8,128)(2,1)S(1)}, u32[]{:S(2)}, u32[]{:S(2)}) collective-permute-start(bf16[656,256]{1,0:T(8,128)(2,1)S(1)} %collective-permute-done.3), channel_id=1, source_target_pairs={{0,1},{1,0},{2,3},{3,2},{4,5},{5,4},{6,7},{7,6},{8,9},{9,8},{10,11... | collective-permute-start | bytes 1007624 | tf_op jit(solution)/shard_map/ppermute | solution.py:76
  60.2 14.1 %collective-permute-start.14 = (bf16[656,256]{1,0:T(8,128)(2,1)S(1)}, bf16[656,256]{1,0:T(8,128)(2,1)S(1)}, u32[]{:S(2)}, u32[]{:S(2)}) collective-permute-start(bf16[656,256]{1,0:T(8,128)(2,1)S(1)} %collective-permute-done.7), channel_id=1, source_target_pairs={{0,1},{1,0},{2,3},{3,2},{4,5},{5,4},{6,7},{7,6},{8,9},{9,8},{10,11... | collective-permute-start | bytes 1007624 | tf_op jit(solution)/shard_map/ppermute | solution.py:76
  69.2 6.5 %collective-permute-start.11 = (bf16[656,256]{1,0:T(8,128)(2,1)S(1)}, bf16[656,256]{1,0:T(8,128)(2,1)S(1)}, u32[]{:S(2)}, u32[]{:S(2)}) collective-permute-start(bf16[656,256]{1,0:T(8,128)(2,1)S(1)} %collective-permute-done.4), channel_id=1, source_target_pairs={{0,1},{1,0},{2,3},{3,2},{4,5},{5,4},{6,7},{7,6},{8,9},{9,8},{10,11... | collective-permute-start | bytes 1007624 | tf_op jit(solution)/shard_map/ppermute | solution.py:76
  89.4 15.3 %collective-permute-start.18 = (bf16[2,432,256]{2,1,0:T(8,128)(2,1)}, bf16[2,432,256]{2,1,0:T(8,128)(2,1)S(1)}, u32[]{:S(2)}, u32[]{:S(2)}) collective-permute-start(bf16[2,432,256]{2,1,0:T(8,128)(2,1)} %get-tuple-element.29), channel_id=1, source_target_pairs={{0,1},{1,0},{2,3},{3,2},{4,5},{5,4},{6,7},{7,6},{8,9},{9,8},{10,11... | collective-permute-start | bytes 1327112 | tf_op jit(solution)/shard_map/ppermute | solution.py:76
  89.6 17.4 %collective-permute-start.17 = (bf16[2,432,256]{2,1,0:T(8,128)(2,1)}, bf16[2,432,256]{2,1,0:T(8,128)(2,1)S(1)}, u32[]{:S(2)}, u32[]{:S(2)}) collective-permute-start(bf16[2,432,256]{2,1,0:T(8,128)(2,1)} %get-tuple-element.28), channel_id=1, source_target_pairs={{0,1},{1,0},{2,3},{3,2},{4,5},{5,4},{6,7},{7,6},{8,9},{9,8},{10,11... | collective-permute-start | bytes 1327112 | tf_op jit(solution)/shard_map/ppermute | solution.py:76
  92.3 12.4 %collective-permute-start.19 = (bf16[432,256]{1,0:T(8,128)(2,1)S(1)}, bf16[432,256]{1,0:T(8,128)(2,1)S(1)}, u32[]{:S(2)}, u32[]{:S(2)}) collective-permute-start(bf16[432,256]{1,0:T(8,128)(2,1)S(1)} %get-tuple-element.38), channel_id=1, source_target_pairs={{0,4},{1,5},{4,8},{5,9},{8,12},{9,13},{12,14},{13,15},{14,10},{15,... | collective-permute-start | bytes 663560 | tf_op jit(solution)/shard_map/ppermute | solution.py:72
  93.9 10.9 %collective-permute-start.23 = (bf16[432,256]{1,0:T(8,128)(2,1)S(1)}, bf16[432,256]{1,0:T(8,128)(2,1)S(1)}, u32[]{:S(2)}, u32[]{:S(2)}) collective-permute-start(bf16[432,256]{1,0:T(8,128)(2,1)S(1)} %get-tuple-element.37), channel_id=1, source_target_pairs={{0,2},{1,3},{4,0},{5,1},{8,4},{9,5},{12,8},{13,9},{14,12},{15,13},... | collective-permute-start | bytes 663560 | tf_op jit(solution)/shard_map/ppermute | solution.py:72
  104.9 7.3 %collective-permute-start.20 = (bf16[432,256]{1,0:T(8,128)(2,1)S(1)}, bf16[432,256]{1,0:T(8,128)(2,1)S(1)}, u32[]{:S(2)}, u32[]{:S(2)}) collective-permute-start(bf16[432,256]{1,0:T(8,128)(2,1)S(1)} %get-tuple-element.30), channel_id=1, source_target_pairs={{0,4},{1,5},{4,8},{5,9},{8,12},{9,13},{12,14},{13,15},{14,10},{15,... | collective-permute-start | bytes 663560 | tf_op jit(solution)/shard_map/ppermute | solution.py:72
  105.0 7.3 %collective-permute-start.24 = (bf16[432,256]{1,0:T(8,128)(2,1)S(1)}, bf16[432,256]{1,0:T(8,128)(2,1)S(1)}, u32[]{:S(2)}, u32[]{:S(2)}) collective-permute-start(bf16[432,256]{1,0:T(8,128)(2,1)S(1)} %get-tuple-element.32), channel_id=1, source_target_pairs={{0,2},{1,3},{4,0},{5,1},{8,4},{9,5},{12,8},{13,9},{14,12},{15,13},... | collective-permute-start | bytes 663560 | tf_op jit(solution)/shard_map/ppermute | solution.py:72
  107.0 7.5 %collective-permute-start.16 = (bf16[2,432,256]{2,1,0:T(8,128)(2,1)S(1)}, bf16[2,432,256]{2,1,0:T(8,128)(2,1)S(1)}, u32[]{:S(2)}, u32[]{:S(2)}) collective-permute-start(bf16[2,432,256]{2,1,0:T(8,128)(2,1)S(1)} %copy-done.1), channel_id=1, source_target_pairs={{0,1},{1,0},{2,3},{3,2},{4,5},{5,4},{6,7},{7,6},{8,9},{9,8},{10,11... | collective-permute-start | bytes 1327112 | tf_op jit(solution)/shard_map/ppermute | solution.py:76
  112.4 6.4 %collective-permute-start.21 = (bf16[432,256]{1,0:T(8,128)(2,1)S(1)}, bf16[432,256]{1,0:T(8,128)(2,1)S(1)}, u32[]{:S(2)}, u32[]{:S(2)}) collective-permute-start(bf16[432,256]{1,0:T(8,128)(2,1)S(1)} %get-tuple-element.34), channel_id=1, source_target_pairs={{0,4},{1,5},{4,8},{5,9},{8,12},{9,13},{12,14},{13,15},{14,10},{15,... | collective-permute-start | bytes 663560 | tf_op jit(solution)/shard_map/ppermute | solution.py:72
  (20 other events, 319.2 us)
Sparse Core Ops, SparseCore 0:
  10.3 66.0 all-gather.2

commit v9 on v6

--- a/solution.py
+++ b/solution.py
@@ -155,29 +155,39 @@
     )
 
 
-def put_boundary(rows, brick, a, out_ref, stage):
+PLANES = 4
+
+
+def put_boundary(rows, base, a, out_ref, stage):
     wide = rows.astype(F32)
-    base = brick * ROWS
 
     def put(at, value, lanes=slice(None)):
         out_ref[pl.ds(pl.multiple_of(base + at, 16), value.shape[0]), lanes] = value
 
-    for edge, at in ((0, 0), (7, 64)):
-
-        @pl.when(a == edge)
-        def _():
-            put(at, rows)
-
-    @pl.when((a > 0) & (a < 7))
-    def _():
-        for half in range(2):
-            lanes = slice(half * 128, half * 128 + 128)
-            stage[half] = wide[:, lanes]
-            first = stage[half, pl.ds(0, 8, stride=8), :]
-            last = stage[half, pl.ds(7, 8, stride=8), :]
-            put(C_LINES - 16 + 16 * a, jnp.concatenate([first, last], axis=0).astype(BF16), lanes)
-        pair = jnp.concatenate([wide[:8], wide[56:]], axis=0).astype(BF16)
-        put(B_LINES - 16 + 16 * a, pair)
+    if a in (0, 7):
+        put(0 if a == 0 else 64, rows)
+        return
+    for half in range(2):
+        lanes = slice(half * 128, half * 128 + 128)
+        stage[half] = wide[:, lanes]
+        first = stage[half, pl.ds(0, 8, stride=8), :]
+        last = stage[half, pl.ds(7, 8, stride=8), :]
+        put(C_LINES - 16 + 16 * a, jnp.concatenate([first, last], axis=0).astype(BF16), lanes)
+    pair = jnp.concatenate([wide[:8], wide[56:]], axis=0).astype(BF16)
+    put(B_LINES - 16 + 16 * a, pair)
+
+
+def each_brick(rows_of, bricks, out_ref, stage):
+    def step(brick, _):
+        for first in range(0, 8, PLANES):
+            at = pl.multiple_of(brick * 512 + first * 64, 64)
+            rows = rows_of(pl.ds(at, PLANES * 64))
+            for t in range(PLANES):
+                plane = rows[t * 64 : t * 64 + 64]
+                put_boundary(plane, brick * ROWS, first + t, out_ref, stage.at[first + t])
+        return 0
+
+    lax.fori_loop(0, bricks, step, 0)
 
 
 def norm_body(recv, send, x_ref, gain_ref, hidden_ref, out_ref, stage):
@@ -195,26 +205,19 @@
     notes = jnp.where(row == 0, codes, jnp.where(row == 1, served, 0))
     out_ref[bricks * ROWS :, :] = notes.astype(F32).astype(BF16)
 
-    def step(k, _):
-        at = pl.ds(pl.multiple_of(k * 64, 64), 64)
+    def rows_of(at):
         x = x_ref[at, :].astype(F32)
         inverse = lax.rsqrt(jnp.mean(x * x, axis=-1, keepdims=True) + 1e-6)
         v = x * inverse * gain
         rows = (v / (1.0 + jnp.exp(-v))).astype(BF16)
         hidden_ref[at, :] = rows
-        put_boundary(rows, k // 8, k % 8, out_ref, stage)
-        return 0
-
-    lax.fori_loop(0, bricks * 8, step, 0)
+        return rows
+
+    each_brick(rows_of, bricks, out_ref, stage)
 
 
 def extract_body(x_ref, out_ref, stage):
-    def step(k, _):
-        at = pl.ds(pl.multiple_of(k * 64, 64), 64)
-        put_boundary(x_ref[at, :], k // 8, k % 8, out_ref, stage)
-        return 0
-
-    lax.fori_loop(0, x_ref.shape[0] // 64, step, 0)
+    each_brick(lambda at: x_ref[at, :], x_ref.shape[0] // 512, out_ref, stage)
 
 
 def start_padded(own_ref, cells, halo, bricks):
@@ -355,10 +358,11 @@
     lax.fori_loop(0, bricks * 10, step, 0)
 
 
-def fetch(parts, share, sems):
+def fetch(parts, share, sems, first=0, rows=None):
     size = parts[0].shape[0]
+    lines = pl.ds(first, rows or parts[0].shape[1])
     copies = [
-        pltpu.make_async_copy(part, share.at[pl.ds(k * size, size)], sems.at[k])
+        pltpu.make_async_copy(part.at[:, lines], share.at[pl.ds(k * size, size), lines], sems.at[k])
         for k, part in enumerate(parts)
     ]
     for copy in copies:
@@ -371,17 +375,17 @@
     parts = refs[4 : 4 + count]
     keep_ref = refs[4 + count]
     give_refs = refs[5 + count : 5 + count + peers // 4]
-    out_cols, codes_ref, served_ref = refs[-15:-12]
-    cells, halo, share, cols, sums, narrow, turned, codes = refs[-12:-4]
-    sems, cols_sems, codes_sem, out_sems = refs[-4:]
+    out_cols, codes_ref, served_ref = refs[-16:-13]
+    cells, halo, share, cols, sums, narrow, turned, codes = refs[-13:-5]
+    sems, cols_sems, codes_sem, out_sems, notes_sems = refs[-5:]
     bricks = own_ref.shape[0] // 512
     me = table[2 * peers]
-    copies = fetch(parts, share, sems)
-    start_padded(own_ref, cells, halo, bricks)
+    notes_copies = fetch(parts, share, notes_sems, bricks * ROWS, NOTES)
+    copies = fetch(parts, share, sems, 0, bricks * ROWS)
     for part in range(bricks * 2):
         at = slice(part * 256, part * 256 + 256)
         turned[:, at] = cot_ref[at, :].astype(F32).T.astype(BF16)
-    for copy in copies:
+    for copy in notes_copies:
         copy.wait()
     for k in range(peers):
         notes = share[k, bricks * ROWS :, :].astype(F32).astype(jnp.int32)
@@ -389,7 +393,10 @@
         served_ref[k : k + 1, :] = notes[1:2]
     codes_copy = pltpu.make_async_copy(codes_ref, codes, codes_sem.at[0])
     codes_copy.start()
+    start_padded(own_ref, cells, halo, bricks)
     codes_copy.wait()
+    for copy in copies:
+        copy.wait()
     for brick in range(bricks):
         for number, e in enumerate(DIRECTIONS):
             slot = recv[brick, number]
@@ -566,10 +573,12 @@
     for brick in range(bricks):
         rows = slice(brick * 512, brick * 512 + 512)
         grad = None
-        for i in range(3):
-            left = cols[brick * 10 + i : brick * 10 + i + 8].reshape(512, 9 * C)
-            right = weight[i * 9 * C : (i + 1) * 9 * C, :]
-            term = jnp.dot(left, right, preferred_element_type=F32)
+        for tap in range(27):
+            i, jl = divmod(tap, 9)
+            first = brick * 10 + i
+            left = cols[first : first + 8, :, jl * C : jl * C + C].reshape(512, C)
+            right = weight[(26 - tap) * C : (27 - tap) * C, :]
+            term = lax.dot_general(left, right, (((1,), (1,)), ((), ())), preferred_element_type=F32)
             grad = term if grad is None else grad + term
         x = x_ref[rows, :].astype(F32)
         inverse = lax.rsqrt(jnp.mean(x * x, axis=-1, keepdims=True) + 1e-6)
@@ -590,7 +599,7 @@
     factor = 1.0 / math.sqrt(peers * per_device)
     gain = norm_gain.reshape(1, channels)
     sds = jax.ShapeDtypeStruct
-    stage = pltpu.VMEM((2, 64, 128), F32)
+    stage = pltpu.VMEM((8, 2, 64, 128), F32)
 
     def padded(n):
         return [
@@ -657,6 +666,7 @@
             pltpu.SemaphoreType.DMA((bricks * 10,)),
             pltpu.SemaphoreType.DMA((1,)),
             pltpu.SemaphoreType.DMA((2, chips)),
+            pltpu.SemaphoreType.DMA((count,)),
         ],
         cost=9,
         name="weight_grad",
@@ -687,14 +697,11 @@
     cot_ring.go(0)
     cot_ring.go(1)
     third = (cot_ring.last(0), cot_ring.last(1))
-    turned = lax.optimization_barrier((conv_weight, sent))[0]
-    turned = turned.reshape(27, channels, channels)[::-1].transpose(0, 2, 1)
-    turned = turned.reshape(27 * channels, channels)
-    sums_ring.go((third, turned))
+    sums_ring.go(third)
     cot_ring.go(0)
     sent = sums_ring.go(cot_ring.last(0))
     cot_parts = cot_ring.places(cols)
-    turned = lax.optimization_barrier((turned, sent))[0]
+    served = lax.optimization_barrier((served, sent))[0]
 
     grad_features = call(
         functools.partial(input_grad_body, slots, peers, count),
@@ -712,7 +719,7 @@
         ],
         cost=13,
         name="input_grad",
-    )(served, send_face, table, cotangent, features, gain, turned, *cot_parts)
+    )(served, send_face, table, cotangent, features, gain, conv_weight, *cot_parts)
     for _ in range(chips // 2 - 4):
         sums_ring.go()
     return (mixed, grad_features, sums_ring.total())

time: 115 us -> 111 us (0.965)
  waiting for transfers between devices: 27.2 us -> 36.3 us
  local copies, waits for them, and re-layouts: 9.45 us -> 3.01 us
  other arithmetic: 7.89 us -> 2.53 us
  Pallas kernels: 39.8 us -> 36.5 us
  starting transfers between devices: 29.7 us -> 30.9 us
    ppermute x21, waiting for transfers between devices: 27.1 us -> 36.2 us  [ring_step(): return lax.ppermute(x, 'morton', pairs)]
    reshape x1 -> x0, local copies, waits for them, and re-layouts: 4.44 us -> none  [local(): turned = turned.reshape(27, channels, channels)[::-1].transpose(0, 2, 1)]
    convert_element_type x4, other arithmetic: 6 us -> 1.65 us  [go(): part = part.astype(BF16)]
    rev x1 -> x0, local copies, waits for them, and re-layouts: 1.99 us -> none  [local(): turned = turned.reshape(27, channels, channels)[::-1].transpose(0, 2, 1)]
    pallas_call x1, Pallas kernels: 4.2 us -> 2.68 us  [local(): call(norm_body, (sds((per_device, channels), BF16), sds((bricks * ROWS +...]
  transfers between devices with their start and end apart: 41 -> 41, of which waited for: 10 -> 10; matrix products, arithmetic and copies ran while one was open for 12% -> 3% of each run, Pallas kernels for 31% -> 31%
where the time goes in v9:
time: 111 us; the launch traced here: 110 us
  Pallas kernels  36.5 us (33%)
  waiting for transfers between devices  36.3 us (33%)
  starting transfers between devices  30.9 us (28%)
  local copies, waits for them, and re-layouts  3.01 us (3%)
  other arithmetic  2.53 us (2%)
  between operations  1.14 us (1%)
    ppermute x21, waiting for transfers between devices, ring_step(): return lax.ppermute(x, 'morton', pairs)  36.2 us
    ppermute x21, starting transfers between devices, ring_step(): return lax.ppermute(x, 'morton', pairs)  26.9 us
    pallas_call x1, Pallas kernels, local(): call(functools.partial(input_grad_body, slots, peers, count), sds((per_de...  12.3 us
    pallas_call x1, Pallas kernels, local(): call(functools.partial(weight_grad_body, slots, factor, peers, count), (s...  12 us
    pallas_call x1, Pallas kernels, local(): call(mix_body, sds((per_device, channels), BF16), [HBM, HBM, VMEM], [pltp...  7.69 us
    ppermute x20, starting transfers between devices, swap_cores(): return lax.ppermute(x, 'morton', [(m, m ^ 1) for m in range(peers)])  3.98 us
    pallas_call x1, Pallas kernels, local(): call(norm_body, (sds((per_device, channels), BF16), sds((bricks * ROWS +...  2.68 us
  transfers between devices with their start and end apart: 41, of which 10 were waited for; matrix products, arithmetic and copies ran while one was open for 3% of the time, Pallas kernels for 31%

profile of v9, /device:TPU:0, one launch (start us, length us, event | category | flops | bytes accessed | tf_op | source)
XLA Modules:
  0.0 110.4 jit_solution(717725238065585431)
XLA Ops:
  0.6 2.7 %norm.1 = (bf16[1024,256]{1,0:T(8,128)(2,1)}, bf16[656,256]{1,0:T(8,128)(2,1)}) custom-call(s32[2,26]{1,0:T(2,128)} %refs_0_.1, s32[1,64]{1,0:T(1,128)} %refs_1_.1, bf16[1024,256]{1,0:T(8,128)(2,1)} %refs_4_.1, f32[1,256]{1,0:T(1,128)} %bitcast.95), custom_call_target="tpu_custom_call" | custom-call | flops 2000000000 | tf_op jit(solution)/shard_map/norm/pallas_call | solution.py:616
  3.3 3.0 %collective-permute-start.1 = (bf16[656,256]{1,0:T(8,128)(2,1)}, bf16[656,256]{1,0:T(8,128)(2,1)S(1)}, u32[]{:S(2)}, u32[]{:S(2)}) collective-permute-start(bf16[656,256]{1,0:T(8,128)(2,1)} %get-tuple-element.35), channel_id=1, source_target_pairs={{0,4},{1,3},{4,8},{5,1},{8,12},{9,5},{12,14},{13,9},{14,10},{15,13... | collective-permute-start | bytes 1007624 | tf_op jit(solution)/shard_map/ppermute | solution.py:72
  7.0 1.9 %extract.1 = bf16[640,256]{1,0:T(8,128)(2,1)} custom-call(bf16[1024,256]{1,0:T(8,128)(2,1)} %refs_3_.3), custom_call_target="tpu_custom_call" | custom-call | flops 2000000000 | tf_op jit(solution)/shard_map/extract/pallas_call | solution.py:624
  8.9 5.0 %collective-permute-done.1 = bf16[656,256]{1,0:T(8,128)(2,1)S(1)} collective-permute-done((bf16[656,256]{1,0:T(8,128)(2,1)}, bf16[656,256]{1,0:T(8,128)(2,1)S(1)}, u32[]{:S(2)}, u32[]{:S(2)}) %collective-permute-start.1) | collective-permute-done | bytes 335904 | tf_op jit(solution)/shard_map/ppermute | solution.py:72
  13.9 2.4 %collective-permute-start.2 = (bf16[656,256]{1,0:T(8,128)(2,1)S(1)}, bf16[656,256]{1,0:T(8,128)(2,1)S(1)}, u32[]{:S(2)}, u32[]{:S(2)}) collective-permute-start(bf16[656,256]{1,0:T(8,128)(2,1)S(1)} %collective-permute-done.1), channel_id=1, source_target_pairs={{0,4},{1,3},{4,8},{5,1},{8,12},{9,5},{12,14},{13,9},{14,10},{15,13... | collective-permute-start | bytes 1007624 | tf_op jit(solution)/shard_map/ppermute | solution.py:72
  16.3 1.2 %dynamic-slice_bitcast_fusion.refs_1_.refs_2_ = s32[33]{0:T(128)} fusion(s32[16,33]{1,0:T(8,128)} %constant.10.clone, s32[]{:T(128)S(6)} %select_n.3), kind=kLoop, calls=%fused_computation.16 | loop fusion | bytes 268 | tf_op jit(solution)/shard_map/squeeze | solution.py:614
  17.5 1.6 %collective-permute-start.6 = (bf16[656,256]{1,0:T(8,128)(2,1)S(1)}, bf16[656,256]{1,0:T(8,128)(2,1)S(1)}, u32[]{:S(2)}, u32[]{:S(2)}) collective-permute-start(bf16[656,256]{1,0:T(8,128)(2,1)S(1)} %collective-permute-done.5), channel_id=1, source_target_pairs={{0,4},{1,3},{4,8},{5,1},{8,12},{9,5},{12,14},{13,9},{14,10},{15,13... | collective-permute-start | bytes 1007624 | tf_op jit(solution)/shard_map/ppermute | solution.py:72
  19.1 3.3 %collective-permute-done.2 = bf16[656,256]{1,0:T(8,128)(2,1)S(1)} collective-permute-done((bf16[656,256]{1,0:T(8,128)(2,1)S(1)}, bf16[656,256]{1,0:T(8,128)(2,1)S(1)}, u32[]{:S(2)}, u32[]{:S(2)}) %collective-permute-start.2) | collective-permute-done | bytes 335904 | tf_op jit(solution)/shard_map/ppermute | solution.py:72
  24.0 2.0 %collective-permute-done.6 = bf16[656,256]{1,0:T(8,128)(2,1)S(1)} collective-permute-done((bf16[656,256]{1,0:T(8,128)(2,1)S(1)}, bf16[656,256]{1,0:T(8,128)(2,1)S(1)}, u32[]{:S(2)}, u32[]{:S(2)}) %collective-permute-start.6) | collective-permute-done | bytes 335904 | tf_op jit(solution)/shard_map/ppermute | solution.py:72
  27.1 2.5 %collective-permute-done.3 = bf16[656,256]{1,0:T(8,128)(2,1)S(1)} collective-permute-done((bf16[656,256]{1,0:T(8,128)(2,1)S(1)}, bf16[656,256]{1,0:T(8,128)(2,1)S(1)}, u32[]{:S(2)}, u32[]{:S(2)}) %collective-permute-start.3) | collective-permute-done | bytes 335904 | tf_op jit(solution)/shard_map/ppermute | solution.py:72
  31.3 1.9 %collective-permute-done.7 = bf16[656,256]{1,0:T(8,128)(2,1)S(1)} collective-permute-done((bf16[656,256]{1,0:T(8,128)(2,1)S(1)}, bf16[656,256]{1,0:T(8,128)(2,1)S(1)}, u32[]{:S(2)}, u32[]{:S(2)}) %collective-permute-start.7) | collective-permute-done | bytes 335904 | tf_op jit(solution)/shard_map/ppermute | solution.py:72
  33.2 3.6 %collective-permute-done.4 = bf16[656,256]{1,0:T(8,128)(2,1)S(1)} collective-permute-done((bf16[656,256]{1,0:T(8,128)(2,1)S(1)}, bf16[656,256]{1,0:T(8,128)(2,1)S(1)}, u32[]{:S(2)}, u32[]{:S(2)}) %collective-permute-start.4) | collective-permute-done | bytes 335904 | tf_op jit(solution)/shard_map/ppermute | solution.py:72
  37.9 2.3 %collective-permute-start.16 = (bf16[640,256]{1,0:T(8,128)(2,1)}, bf16[640,256]{1,0:T(8,128)(2,1)S(1)}, u32[]{:S(2)}, u32[]{:S(2)}) collective-permute-start(bf16[640,256]{1,0:T(8,128)(2,1)} %extract.1), channel_id=1, source_target_pairs={{1,4},{0,3},{5,8},{4,1},{9,12},{8,5},{13,14},{12,9},{15,10},{14,13... | collective-permute-start | bytes 983048 | tf_op jit(solution)/shard_map/ppermute | solution.py:72
  41.2 12.0 %weight_grad.1 = (f32[8,432,256]{2,1,0:T(8,128)}, bf16[2,432,256]{2,1,0:T(8,128)(2,1)}, bf16[2,432,256]{2,1,0:T(8,128)(2,1)}, bf16[2,432,256]{2,1,0:T(8,128)(2,1...) custom-call(s32[2,26]{1,0:T(2,128)} %refs_0_.1, ...), custom_call_target="tpu_custom_call" | custom-call | flops 8999999488 | tf_op jit(solution)/shard_map/weight_grad/pallas_call | solution.py:647
  55.1 1.6 %collective-permute-start.22 = (bf16[640,256]{1,0:T(8,128)(2,1)S(1)}, bf16[640,256]{1,0:T(8,128)(2,1)S(1)}, u32[]{:S(2)}, u32[]{:S(2)}) collective-permute-start(bf16[640,256]{1,0:T(8,128)(2,1)S(1)} %collective-permute-done.15), channel_id=1, source_target_pairs={{0,4},{1,3},{4,8},{5,1},{8,12},{9,5},{12,14},{13,9},{14,10},{15,13... | collective-permute-start | bytes 983048 | tf_op jit(solution)/shard_map/ppermute | solution.py:72
  56.7 1.2 %fusion.7 = (bf16[432,256]{1,0:T(8,128)(2,1)S(1)}, bf16[432,256]{1,0:T(8,128)(2,1)S(1)}) fusion(f32[8,432,256]{2,1,0:T(8,128)} %get-tuple-element.39, bf16[2,432,256]{2,1,0:T(8,128)(2,1)S(1)} %collective-permute-done.17), kind=kLoop, calls=%fused_computation.15 | loop fusion | flops 663552 | bytes 1769472 | tf_op jit(solution)/shard_map/convert_element_type | solution.py:132
  58.5 1.6 %collective-permute-start.38 = (bf16[432,256]{1,0:T(8,128)(2,1)S(1)}, bf16[432,256]{1,0:T(8,128)(2,1)S(1)}, u32[]{:S(2)}, u32[]{:S(2)}) collective-permute-start(bf16[432,256]{1,0:T(8,128)(2,1)S(1)} %get-tuple-element.69), channel_id=1, source_target_pairs={{0,2},{1,3},{4,0},{5,1},{8,4},{9,5},{12,8},{13,9},{14,12},{15,13},... | collective-permute-start | bytes 663560 | tf_op jit(solution)/shard_map/ppermute | solution.py:72
  60.1 7.7 %mix.1 = bf16[1024,256]{1,0:T(8,128)(2,1)} custom-call(bf16[20,64,2304]{2,1,0:T(8,128)(2,1)} %get-tuple-element.44.cols_ref, bf16[6912,256]{1,0:T(8,128)(2,1)} %refs_6_.1, bf16[1024,256]{1,0:T(8,128)(2,1)} %refs_4_.1), custom_call_target="tpu_custom_call" | custom-call | flops 6000000000 | tf_op jit(solution)/shard_map/mix/pallas_call | solution.py:688
  70.8 1.3 %collective-permute-start.39 = (bf16[432,256]{1,0:T(8,128)(2,1)S(1)}, bf16[432,256]{1,0:T(8,128)(2,1)S(1)}, u32[]{:S(2)}, u32[]{:S(2)}) collective-permute-start(bf16[432,256]{1,0:T(8,128)(2,1)S(1)} %get-tuple-element.63), channel_id=1, source_target_pairs={{0,2},{1,3},{4,0},{5,1},{8,4},{9,5},{12,8},{13,9},{14,12},{15,13},... | collective-permute-start | bytes 663560 | tf_op jit(solution)/shard_map/ppermute | solution.py:72
  72.1 8.9 %collective-permute-done.25 = bf16[640,256]{1,0:T(8,128)(2,1)S(1)} collective-permute-done((bf16[640,256]{1,0:T(8,128)(2,1)S(1)}, bf16[640,256]{1,0:T(8,128)(2,1)S(1)}, u32[]{:S(2)}, u32[]{:S(2)}) %collective-permute-start.25) | collective-permute-done | bytes 327712 | tf_op jit(solution)/shard_map/ppermute | solution.py:72
  84.0 4.0 %collective-permute-done.28 = bf16[640,256]{1,0:T(8,128)(2,1)S(1)} collective-permute-done((bf16[640,256]{1,0:T(8,128)(2,1)S(1)}, bf16[640,256]{1,0:T(8,128)(2,1)S(1)}, u32[]{:S(2)}, u32[]{:S(2)}) %collective-permute-start.28) | collective-permute-done | bytes 327712 | tf_op jit(solution)/shard_map/ppermute | solution.py:72
  89.9 4.1 %collective-permute-done.27 = bf16[432,256]{1,0:T(8,128)(2,1)S(1)} collective-permute-done((bf16[432,256]{1,0:T(8,128)(2,1)S(1)}, bf16[432,256]{1,0:T(8,128)(2,1)S(1)}, u32[]{:S(2)}, u32[]{:S(2)}) %collective-permute-start.27) | collective-permute-done | bytes 221216 | tf_op jit(solution)/shard_map/ppermute | solution.py:72
  94.8 1.4 %collective-permute-start.37 = (bf16[432,256]{1,0:T(8,128)(2,1)S(1)}, bf16[432,256]{1,0:T(8,128)(2,1)S(1)}, u32[]{:S(2)}, u32[]{:S(2)}) collective-permute-start(bf16[432,256]{1,0:T(8,128)(2,1)S(1)} %fusion.5), channel_id=1, source_target_pairs={{0,4},{1,5},{4,8},{5,9},{8,12},{9,13},{12,14},{13,15},{14,10},{15,... | collective-permute-start | bytes 663560 | tf_op jit(solution)/shard_map/ppermute | solution.py:72
  97.2 12.3 %input_grad.1 = bf16[1024,256]{1,0:T(8,128)(2,1)} custom-call(s32[16,256]{1,0:T(8,128)} %get-tuple-element.57.refs_0_, s32[1,64]{1,0:T(1,128)} %refs_1_.1, s32[33]{0:T(128)} %dynamic-slice_bitcast_fusion.refs_1_.refs_2_, bf16[1024,256]{1,0:T(8,128)(2,1)} %refs_3_.3, bf16[1024,256]{1,0:T(8,128)(2,1)} %refs_4_.1, f32[1,256]{1,0:T(1,128)} %bitcast.96, ...), custom_call_target="tpu_custom_call" | custom-call | flops 12999999488 | tf_op jit(solution)/shard_map/input_grad/pallas_call | solution.py:706
  (139 shorter events, 19.8 us)
Async XLA Ops:
  3.3 10.6 %collective-permute-start.1 = (bf16[656,256]{1,0:T(8,128)(2,1)}, bf16[656,256]{1,0:T(8,128)(2,1)S(1)}, u32[]{:S(2)}, u32[]{:S(2)}) collective-permute-start(bf16[656,256]{1,0:T(8,128)(2,1)} %get-tuple-element.35), channel_id=1, source_target_pairs={{0,4},{1,3},{4,8},{5,1},{8,12},{9,5},{12,14},{13,9},{14,10},{15,13... | collective-permute-start | bytes 1007624 | tf_op jit(solution)/shard_map/ppermute | solution.py:72
  6.3 11.2 %collective-permute-start.5 = (bf16[656,256]{1,0:T(8,128)(2,1)}, bf16[656,256]{1,0:T(8,128)(2,1)S(1)}, u32[]{:S(2)}, u32[]{:S(2)}) collective-permute-start(bf16[656,256]{1,0:T(8,128)(2,1)} %get-tuple-element.35), channel_id=1, source_target_pairs={{1,4},{0,3},{5,8},{4,1},{9,12},{8,5},{13,14},{12,9},{15,10},{14,13... | collective-permute-start | bytes 1007624 | tf_op jit(solution)/shard_map/ppermute | solution.py:72
  13.9 8.4 %collective-permute-start.2 = (bf16[656,256]{1,0:T(8,128)(2,1)S(1)}, bf16[656,256]{1,0:T(8,128)(2,1)S(1)}, u32[]{:S(2)}, u32[]{:S(2)}) collective-permute-start(bf16[656,256]{1,0:T(8,128)(2,1)S(1)} %collective-permute-done.1), channel_id=1, source_target_pairs={{0,4},{1,3},{4,8},{5,1},{8,12},{9,5},{12,14},{13,9},{14,10},{15,13... | collective-permute-start | bytes 1007624 | tf_op jit(solution)/shard_map/ppermute | solution.py:72
  17.5 8.4 %collective-permute-start.6 = (bf16[656,256]{1,0:T(8,128)(2,1)S(1)}, bf16[656,256]{1,0:T(8,128)(2,1)S(1)}, u32[]{:S(2)}, u32[]{:S(2)}) collective-permute-start(bf16[656,256]{1,0:T(8,128)(2,1)S(1)} %collective-permute-done.5), channel_id=1, source_target_pairs={{0,4},{1,3},{4,8},{5,1},{8,12},{9,5},{12,14},{13,9},{14,10},{15,13... | collective-permute-start | bytes 1007624 | tf_op jit(solution)/shard_map/ppermute | solution.py:72
  23.5 7.2 %collective-permute-start = (bf16[656,256]{1,0:T(8,128)(2,1)S(1)}, bf16[656,256]{1,0:T(8,128)(2,1)S(1)}, u32[]{:S(2)}, u32[]{:S(2)}) collective-permute-start(bf16[656,256]{1,0:T(8,128)(2,1)S(1)} %copy-done.3), channel_id=1, source_target_pairs={{0,1},{1,0},{2,3},{3,2},{4,5},{5,4},{6,7},{7,6},{8,9},{9,8},{10,11... | collective-permute-start | bytes 1007624 | tf_op jit(solution)/shard_map/ppermute | solution.py:76
  23.5 7.2 %collective-permute-start.8 = (bf16[656,256]{1,0:T(8,128)(2,1)S(1)}, bf16[656,256]{1,0:T(8,128)(2,1)S(1)}, u32[]{:S(2)}, u32[]{:S(2)}) collective-permute-start(bf16[656,256]{1,0:T(8,128)(2,1)S(1)} %collective-permute-done.1), channel_id=1, source_target_pairs={{0,1},{1,0},{2,3},{3,2},{4,5},{5,4},{6,7},{7,6},{8,9},{9,8},{10,11... | collective-permute-start | bytes 1007624 | tf_op jit(solution)/shard_map/ppermute | solution.py:76
  24.0 7.2 %collective-permute-start.12 = (bf16[656,256]{1,0:T(8,128)(2,1)S(1)}, bf16[656,256]{1,0:T(8,128)(2,1)S(1)}, u32[]{:S(2)}, u32[]{:S(2)}) collective-permute-start(bf16[656,256]{1,0:T(8,128)(2,1)S(1)} %collective-permute-done.5), channel_id=1, source_target_pairs={{0,1},{1,0},{2,3},{3,2},{4,5},{5,4},{6,7},{7,6},{8,9},{9,8},{10,11... | collective-permute-start | bytes 1007624 | tf_op jit(solution)/shard_map/ppermute | solution.py:76
  26.0 7.2 %collective-permute-start.7 = (bf16[656,256]{1,0:T(8,128)(2,1)S(1)}, bf16[656,256]{1,0:T(8,128)(2,1)S(1)}, u32[]{:S(2)}, u32[]{:S(2)}) collective-permute-start(bf16[656,256]{1,0:T(8,128)(2,1)S(1)} %collective-permute-done.6), channel_id=1, source_target_pairs={{0,4},{1,3},{4,8},{5,1},{8,12},{9,5},{12,14},{13,9},{14,10},{15,13... | collective-permute-start | bytes 1007624 | tf_op jit(solution)/shard_map/ppermute | solution.py:72
  30.7 7.2 %collective-permute-start.13 = (bf16[656,256]{1,0:T(8,128)(2,1)S(1)}, bf16[656,256]{1,0:T(8,128)(2,1)S(1)}, u32[]{:S(2)}, u32[]{:S(2)}) collective-permute-start(bf16[656,256]{1,0:T(8,128)(2,1)S(1)} %collective-permute-done.6), channel_id=1, source_target_pairs={{0,1},{1,0},{2,3},{3,2},{4,5},{5,4},{6,7},{7,6},{8,9},{9,8},{10,11... | collective-permute-start | bytes 1007624 | tf_op jit(solution)/shard_map/ppermute | solution.py:76
  31.2 9.0 %collective-permute-start.10 = (bf16[656,256]{1,0:T(8,128)(2,1)S(1)}, bf16[656,256]{1,0:T(8,128)(2,1)S(1)}, u32[]{:S(2)}, u32[]{:S(2)}) collective-permute-start(bf16[656,256]{1,0:T(8,128)(2,1)S(1)} %collective-permute-done.3), channel_id=1, source_target_pairs={{0,1},{1,0},{2,3},{3,2},{4,5},{5,4},{6,7},{7,6},{8,9},{9,8},{10,11... | collective-permute-start | bytes 1007624 | tf_op jit(solution)/shard_map/ppermute | solution.py:76
  36.8 16.4 %collective-permute-start.15 = (bf16[640,256]{1,0:T(8,128)(2,1)}, bf16[640,256]{1,0:T(8,128)(2,1)S(1)}, u32[]{:S(2)}, u32[]{:S(2)}) collective-permute-start(bf16[640,256]{1,0:T(8,128)(2,1)} %extract.1), channel_id=1, source_target_pairs={{0,4},{1,3},{4,8},{5,1},{8,12},{9,5},{12,14},{13,9},{14,10},{15,13... | collective-permute-start | bytes 983048 | tf_op jit(solution)/shard_map/ppermute | solution.py:72
  37.9 15.3 %collective-permute-start.16 = (bf16[640,256]{1,0:T(8,128)(2,1)}, bf16[640,256]{1,0:T(8,128)(2,1)S(1)}, u32[]{:S(2)}, u32[]{:S(2)}) collective-permute-start(bf16[640,256]{1,0:T(8,128)(2,1)} %extract.1), channel_id=1, source_target_pairs={{1,4},{0,3},{5,8},{4,1},{9,12},{8,5},{13,14},{12,9},{15,10},{14,13... | collective-permute-start | bytes 983048 | tf_op jit(solution)/shard_map/ppermute | solution.py:72
  53.3 14.5 %collective-permute-start.23 = (bf16[640,256]{1,0:T(8,128)(2,1)S(1)}, bf16[640,256]{1,0:T(8,128)(2,1)S(1)}, u32[]{:S(2)}, u32[]{:S(2)}) collective-permute-start(bf16[640,256]{1,0:T(8,128)(2,1)S(1)} %collective-permute-done.16), channel_id=1, source_target_pairs={{0,4},{1,3},{4,8},{5,1},{8,12},{9,5},{12,14},{13,9},{14,10},{15,13... | collective-permute-start | bytes 983048 | tf_op jit(solution)/shard_map/ppermute | solution.py:72
  54.4 14.5 %collective-permute-start.20 = (bf16[2,432,256]{2,1,0:T(8,128)(2,1)}, bf16[2,432,256]{2,1,0:T(8,128)(2,1)S(1)}, u32[]{:S(2)}, u32[]{:S(2)}) collective-permute-start(bf16[2,432,256]{2,1,0:T(8,128)(2,1)} %get-tuple-element.51), channel_id=1, source_target_pairs={{0,1},{1,0},{2,3},{3,2},{4,5},{5,4},{6,7},{7,6},{8,9},{9,8},{10,11... | collective-permute-start | bytes 1327112 | tf_op jit(solution)/shard_map/ppermute | solution.py:76
  55.1 12.9 %collective-permute-start.22 = (bf16[640,256]{1,0:T(8,128)(2,1)S(1)}, bf16[640,256]{1,0:T(8,128)(2,1)S(1)}, u32[]{:S(2)}, u32[]{:S(2)}) collective-permute-start(bf16[640,256]{1,0:T(8,128)(2,1)S(1)} %collective-permute-done.15), channel_id=1, source_target_pairs={{0,4},{1,3},{4,8},{5,1},{8,12},{9,5},{12,14},{13,9},{14,10},{15,13... | collective-permute-start | bytes 983048 | tf_op jit(solution)/shard_map/ppermute | solution.py:72
  58.0 11.8 %collective-permute-start.21 = (bf16[432,256]{1,0:T(8,128)(2,1)S(1)}, bf16[432,256]{1,0:T(8,128)(2,1)S(1)}, u32[]{:S(2)}, u32[]{:S(2)}) collective-permute-start(bf16[432,256]{1,0:T(8,128)(2,1)S(1)} %get-tuple-element.70), channel_id=1, source_target_pairs={{0,4},{1,5},{4,8},{5,9},{8,12},{9,13},{12,14},{13,15},{14,10},{15,... | collective-permute-start | bytes 663560 | tf_op jit(solution)/shard_map/ppermute | solution.py:72
  58.5 11.3 %collective-permute-start.38 = (bf16[432,256]{1,0:T(8,128)(2,1)S(1)}, bf16[432,256]{1,0:T(8,128)(2,1)S(1)}, u32[]{:S(2)}, u32[]{:S(2)}) collective-permute-start(bf16[432,256]{1,0:T(8,128)(2,1)S(1)} %get-tuple-element.69), channel_id=1, source_target_pairs={{0,2},{1,3},{4,0},{5,1},{8,4},{9,5},{12,8},{13,9},{14,12},{15,13},... | collective-permute-start | bytes 663560 | tf_op jit(solution)/shard_map/ppermute | solution.py:72
  67.8 14.0 %collective-permute-start.19 = (bf16[2,432,256]{2,1,0:T(8,128)(2,1)S(1)}, bf16[2,432,256]{2,1,0:T(8,128)(2,1)S(1)}, u32[]{:S(2)}, u32[]{:S(2)}) collective-permute-start(bf16[2,432,256]{2,1,0:T(8,128)(2,1)S(1)} %copy-done.2), channel_id=1, source_target_pairs={{0,1},{1,0},{2,3},{3,2},{4,5},{5,4},{6,7},{7,6},{8,9},{9,8},{10,11... | collective-permute-start | bytes 1327112 | tf_op jit(solution)/shard_map/ppermute | solution.py:76
  67.9 13.9 %collective-permute-start.26 = (bf16[640,256]{1,0:T(8,128)(2,1)S(1)}, bf16[640,256]{1,0:T(8,128)(2,1)S(1)}, u32[]{:S(2)}, u32[]{:S(2)}) collective-permute-start(bf16[640,256]{1,0:T(8,128)(2,1)S(1)} %collective-permute-done.23), channel_id=1, source_target_pairs={{0,4},{1,3},{4,8},{5,1},{8,12},{9,5},{12,14},{13,9},{14,10},{15,13... | collective-permute-start | bytes 983048 | tf_op jit(solution)/shard_map/ppermute | solution.py:72
  68.9 12.1 %collective-permute-start.25 = (bf16[640,256]{1,0:T(8,128)(2,1)S(1)}, bf16[640,256]{1,0:T(8,128)(2,1)S(1)}, u32[]{:S(2)}, u32[]{:S(2)}) collective-permute-start(bf16[640,256]{1,0:T(8,128)(2,1)S(1)} %collective-permute-done.22), channel_id=1, source_target_pairs={{0,4},{1,3},{4,8},{5,1},{8,12},{9,5},{12,14},{13,9},{14,10},{15,13... | collective-permute-start | bytes 983048 | tf_op jit(solution)/shard_map/ppermute | solution.py:72
  70.0 13.3 %collective-permute-start.24 = (bf16[432,256]{1,0:T(8,128)(2,1)S(1)}, bf16[432,256]{1,0:T(8,128)(2,1)S(1)}, u32[]{:S(2)}, u32[]{:S(2)}) collective-permute-start(bf16[432,256]{1,0:T(8,128)(2,1)S(1)} %get-tuple-element.54), channel_id=1, source_target_pairs={{0,4},{1,5},{4,8},{5,9},{8,12},{9,13},{12,14},{13,15},{14,10},{15,... | collective-permute-start | bytes 663560 | tf_op jit(solution)/shard_map/ppermute | solution.py:72
  70.8 12.5 %collective-permute-start.39 = (bf16[432,256]{1,0:T(8,128)(2,1)S(1)}, bf16[432,256]{1,0:T(8,128)(2,1)S(1)}, u32[]{:S(2)}, u32[]{:S(2)}) collective-permute-start(bf16[432,256]{1,0:T(8,128)(2,1)S(1)} %get-tuple-element.63), channel_id=1, source_target_pairs={{0,2},{1,3},{4,0},{5,1},{8,4},{9,5},{12,8},{13,9},{14,12},{15,13},... | collective-permute-start | bytes 663560 | tf_op jit(solution)/shard_map/ppermute | solution.py:72
  94.2 15.3 %collective-permute-start.40 = (bf16[432,256]{1,0:T(8,128)(2,1)S(1)}, bf16[432,256]{1,0:T(8,128)(2,1)S(1)}, u32[]{:S(2)}, u32[]{:S(2)}) collective-permute-start(bf16[432,256]{1,0:T(8,128)(2,1)S(1)} %get-tuple-element.64), channel_id=1, source_target_pairs={{0,2},{1,3},{4,0},{5,1},{8,4},{9,5},{12,8},{13,9},{14,12},{15,13},... | collective-permute-start | bytes 663560 | tf_op jit(solution)/shard_map/ppermute | solution.py:72
  94.8 14.7 %collective-permute-start.37 = (bf16[432,256]{1,0:T(8,128)(2,1)S(1)}, bf16[432,256]{1,0:T(8,128)(2,1)S(1)}, u32[]{:S(2)}, u32[]{:S(2)}) collective-permute-start(bf16[432,256]{1,0:T(8,128)(2,1)S(1)} %fusion.5), channel_id=1, source_target_pairs={{0,4},{1,5},{4,8},{5,9},{8,12},{9,13},{12,14},{13,15},{14,10},{15,... | collective-permute-start | bytes 663560 | tf_op jit(solution)/shard_map/ppermute | solution.py:72
  (52 other events, 517.2 us)

commit v10 on v9

--- a/solution.py
+++ b/solution.py
@@ -137,8 +137,9 @@
         self.hop += 1
         return sent
 
-    def total(self):
-        return sum((t.astype(F32) for t in self.held if t is not None), self.term(0))
+    def total(self, gate):
+        held = lax.optimization_barrier((*self.held, gate))[:2]
+        return sum((t.astype(F32) for t in held), self.term(0))
 
 
 def call(body, out_shape, in_specs, scratch=(), cost=2, name=None, out_specs=None, aliases=None):
@@ -676,31 +677,28 @@
     first = (cot_ring.last(0), cot_ring.last(1))
     give = [lax.optimization_barrier((t, first))[0] for t in give]
     sums_ring = RingScatter(keep, give, peers)
-    sent = sums_ring.go()
+    sums_ring.go()
     cot_ring.go(0, cols)
     cot_ring.go(1, cols)
     second = (cot_ring.last(0), cot_ring.last(1))
+    sent = sums_ring.go(second)
     mix_cols = lax.optimization_barrier((cols, sent))[0]
-    weight_scratch = [
-        pltpu.VMEM((27 * channels, channels), BF16),
-        pltpu.SemaphoreType.DMA((3, 4)),
-    ]
+    weight_scratch = pltpu.VMEM((27 * channels, channels), BF16)
     mixed = call(
         mix_body,
         sds((per_device, channels), BF16),
         [HBM, HBM, VMEM],
-        [pltpu.VMEM(cols_shape(bricks), BF16)] + weight_scratch,
+        [pltpu.VMEM(cols_shape(bricks), BF16), weight_scratch, pltpu.SemaphoreType.DMA((3, 4))],
         cost=6,
         name="mix",
     )(mix_cols, conv_weight, features)
-    sent = sums_ring.go((second, mixed))
     cot_ring.go(0)
     cot_ring.go(1)
     third = (cot_ring.last(0), cot_ring.last(1))
-    sums_ring.go(third)
-    cot_ring.go(0)
-    sent = sums_ring.go(cot_ring.last(0))
+    sent = sums_ring.go((third, mixed))
+    cot_ring.go(0, sent)
     cot_parts = cot_ring.places(cols)
+    sent = sums_ring.go(tuple(t for k, t in enumerate(cot_parts) if k != peers // 2 + peers // 4))
     served = lax.optimization_barrier((served, sent))[0]
 
     grad_features = call(
@@ -711,7 +709,7 @@
         + [
             pltpu.VMEM(cols_shape(bricks), BF16),
             pltpu.VMEM((peers, bricks * ROWS, channels), BF16),
-            weight_scratch[0],
+            weight_scratch,
             pltpu.SMEM((bricks * 26,), jnp.int32),
             pltpu.SMEM((peers * slots,), jnp.int32),
             pltpu.SemaphoreType.DMA((count,)),
@@ -722,7 +720,7 @@
     )(served, send_face, table, cotangent, features, gain, conv_weight, *cot_parts)
     for _ in range(chips // 2 - 4):
         sums_ring.go()
-    return (mixed, grad_features, sums_ring.total())
+    return (mixed, grad_features, sums_ring.total(grad_features))
 
 
 def solution(mesh):

time: 111 us -> 111 us (level)
  waiting for transfers between devices: 36.3 us -> 32.6 us
  starting transfers between devices: 30.9 us -> 33.7 us
  other arithmetic: 2.53 us -> 3.66 us
    ppermute x21, waiting for transfers between devices: 36.2 us -> 32.5 us  [ring_step(): return lax.ppermute(x, 'morton', pairs)]
    ppermute x21, starting transfers between devices: 26.9 us -> 30.1 us  [ring_step(): return lax.ppermute(x, 'morton', pairs)]
    convert_element_type x4, other arithmetic: 1.65 us -> 2.79 us  [go(): part = part.astype(BF16)]
  transfers between devices with their start and end apart: 41 -> 41, of which waited for: 10 -> 11; matrix products, arithmetic and copies ran while one was open for 3% -> 4% of each run, Pallas kernels for 31% -> 30%
where the time goes in v10:
time: 111 us; the launch traced here: 110 us
  Pallas kernels  36 us (32%)
  starting transfers between devices  33.7 us (30%)
  waiting for transfers between devices  32.6 us (29%)
  other arithmetic  3.66 us (3%)
  local copies, waits for them, and re-layouts  2.86 us (3%)
  between operations  1.12 us (1%)
    ppermute x21, waiting for transfers between devices, ring_step(): return lax.ppermute(x, 'morton', pairs)  32.5 us
    ppermute x21, starting transfers between devices, ring_step(): return lax.ppermute(x, 'morton', pairs)  30.1 us
    pallas_call x1, Pallas kernels, local(): call(functools.partial(weight_grad_body, slots, factor, peers, count), (s...  12 us
    pallas_call x1, Pallas kernels, local(): call(functools.partial(input_grad_body, slots, peers, count), sds((per_de...  11.7 us
    pallas_call x1, Pallas kernels, local(): call(mix_body, sds((per_device, channels), BF16), [HBM, HBM, VMEM], [pltp...  7.69 us
    ppermute x20, starting transfers between devices, swap_cores(): return lax.ppermute(x, 'morton', [(m, m ^ 1) for m in range(peers)])  3.64 us
    convert_element_type x4, other arithmetic, go(): part = part.astype(BF16)  2.79 us
    pallas_call x1, Pallas kernels, local(): call(norm_body, (sds((per_device, channels), BF16), sds((bricks * ROWS +...  2.68 us
  transfers between devices with their start and end apart: 41, of which 11 were waited for; matrix products, arithmetic and copies ran while one was open for 4% of the time, Pallas kernels for 30%

profile of v10, /device:TPU:0, one launch (start us, length us, event | category | flops | bytes accessed | tf_op | source)
XLA Modules:
  0.0 109.9 jit_solution(12758000391240542314)
XLA Ops:
  0.6 2.7 %norm.1 = (bf16[1024,256]{1,0:T(8,128)(2,1)}, bf16[656,256]{1,0:T(8,128)(2,1)}) custom-call(s32[2,26]{1,0:T(2,128)} %refs_0_.1, s32[1,64]{1,0:T(1,128)} %refs_1_.1, bf16[1024,256]{1,0:T(8,128)(2,1)} %refs_4_.1, f32[1,256]{1,0:T(1,128)} %bitcast.95), custom_call_target="tpu_custom_call" | custom-call | flops 2000000000 | tf_op jit(solution)/shard_map/norm/pallas_call | solution.py:617
  3.3 3.0 %collective-permute-start.1 = (bf16[656,256]{1,0:T(8,128)(2,1)}, bf16[656,256]{1,0:T(8,128)(2,1)S(1)}, u32[]{:S(2)}, u32[]{:S(2)}) collective-permute-start(bf16[656,256]{1,0:T(8,128)(2,1)} %get-tuple-element.38), channel_id=1, source_target_pairs={{0,4},{1,3},{4,8},{5,1},{8,12},{9,5},{12,14},{13,9},{14,10},{15,13... | collective-permute-start | bytes 1007624 | tf_op jit(solution)/shard_map/ppermute | solution.py:72
  7.0 1.9 %extract.1 = bf16[640,256]{1,0:T(8,128)(2,1)} custom-call(bf16[1024,256]{1,0:T(8,128)(2,1)} %refs_3_.3), custom_call_target="tpu_custom_call" | custom-call | flops 2000000000 | tf_op jit(solution)/shard_map/extract/pallas_call | solution.py:625
  8.9 5.0 %collective-permute-done.1 = bf16[656,256]{1,0:T(8,128)(2,1)S(1)} collective-permute-done((bf16[656,256]{1,0:T(8,128)(2,1)}, bf16[656,256]{1,0:T(8,128)(2,1)S(1)}, u32[]{:S(2)}, u32[]{:S(2)}) %collective-permute-start.1) | collective-permute-done | bytes 335904 | tf_op jit(solution)/shard_map/ppermute | solution.py:72
  13.9 2.4 %collective-permute-start.2 = (bf16[656,256]{1,0:T(8,128)(2,1)S(1)}, bf16[656,256]{1,0:T(8,128)(2,1)S(1)}, u32[]{:S(2)}, u32[]{:S(2)}) collective-permute-start(bf16[656,256]{1,0:T(8,128)(2,1)S(1)} %collective-permute-done.1), channel_id=1, source_target_pairs={{0,4},{1,3},{4,8},{5,1},{8,12},{9,5},{12,14},{13,9},{14,10},{15,13... | collective-permute-start | bytes 1007624 | tf_op jit(solution)/shard_map/ppermute | solution.py:72
  17.5 1.6 %collective-permute-start.6 = (bf16[656,256]{1,0:T(8,128)(2,1)S(1)}, bf16[656,256]{1,0:T(8,128)(2,1)S(1)}, u32[]{:S(2)}, u32[]{:S(2)}) collective-permute-start(bf16[656,256]{1,0:T(8,128)(2,1)S(1)} %collective-permute-done.5), channel_id=1, source_target_pairs={{0,4},{1,3},{4,8},{5,1},{8,12},{9,5},{12,14},{13,9},{14,10},{15,13... | collective-permute-start | bytes 1007624 | tf_op jit(solution)/shard_map/ppermute | solution.py:72
  19.1 3.3 %collective-permute-done.2 = bf16[656,256]{1,0:T(8,128)(2,1)S(1)} collective-permute-done((bf16[656,256]{1,0:T(8,128)(2,1)S(1)}, bf16[656,256]{1,0:T(8,128)(2,1)S(1)}, u32[]{:S(2)}, u32[]{:S(2)}) %collective-permute-start.2) | collective-permute-done | bytes 335904 | tf_op jit(solution)/shard_map/ppermute | solution.py:72
  24.0 2.0 %collective-permute-done.6 = bf16[656,256]{1,0:T(8,128)(2,1)S(1)} collective-permute-done((bf16[656,256]{1,0:T(8,128)(2,1)S(1)}, bf16[656,256]{1,0:T(8,128)(2,1)S(1)}, u32[]{:S(2)}, u32[]{:S(2)}) %collective-permute-start.6) | collective-permute-done | bytes 335904 | tf_op jit(solution)/shard_map/ppermute | solution.py:72
  27.1 2.5 %collective-permute-done.3 = bf16[656,256]{1,0:T(8,128)(2,1)S(1)} collective-permute-done((bf16[656,256]{1,0:T(8,128)(2,1)S(1)}, bf16[656,256]{1,0:T(8,128)(2,1)S(1)}, u32[]{:S(2)}, u32[]{:S(2)}) %collective-permute-start.3) | collective-permute-done | bytes 335904 | tf_op jit(solution)/shard_map/ppermute | solution.py:72
  31.3 1.9 %collective-permute-done.7 = bf16[656,256]{1,0:T(8,128)(2,1)S(1)} collective-permute-done((bf16[656,256]{1,0:T(8,128)(2,1)S(1)}, bf16[656,256]{1,0:T(8,128)(2,1)S(1)}, u32[]{:S(2)}, u32[]{:S(2)}) %collective-permute-start.7) | collective-permute-done | bytes 335904 | tf_op jit(solution)/shard_map/ppermute | solution.py:72
  33.2 3.6 %collective-permute-done.4 = bf16[656,256]{1,0:T(8,128)(2,1)S(1)} collective-permute-done((bf16[656,256]{1,0:T(8,128)(2,1)S(1)}, bf16[656,256]{1,0:T(8,128)(2,1)S(1)}, u32[]{:S(2)}, u32[]{:S(2)}) %collective-permute-start.4) | collective-permute-done | bytes 335904 | tf_op jit(solution)/shard_map/ppermute | solution.py:72
  37.9 2.3 %collective-permute-start.16 = (bf16[640,256]{1,0:T(8,128)(2,1)}, bf16[640,256]{1,0:T(8,128)(2,1)S(1)}, u32[]{:S(2)}, u32[]{:S(2)}) collective-permute-start(bf16[640,256]{1,0:T(8,128)(2,1)} %extract.1), channel_id=1, source_target_pairs={{1,4},{0,3},{5,8},{4,1},{9,12},{8,5},{13,14},{12,9},{15,10},{14,13... | collective-permute-start | bytes 983048 | tf_op jit(solution)/shard_map/ppermute | solution.py:72
  41.2 12.0 %weight_grad.1 = (f32[8,432,256]{2,1,0:T(8,128)}, bf16[2,432,256]{2,1,0:T(8,128)(2,1)}, bf16[2,432,256]{2,1,0:T(8,128)(2,1)}, bf16[2,432,256]{2,1,0:T(8,128)(2,1...) custom-call(s32[2,26]{1,0:T(2,128)} %refs_0_.1, ...), custom_call_target="tpu_custom_call" | custom-call | flops 8999999488 | tf_op jit(solution)/shard_map/weight_grad/pallas_call | solution.py:648
  55.1 1.7 %collective-permute-start.20 = (bf16[640,256]{1,0:T(8,128)(2,1)S(1)}, bf16[640,256]{1,0:T(8,128)(2,1)S(1)}, u32[]{:S(2)}, u32[]{:S(2)}) collective-permute-start(bf16[640,256]{1,0:T(8,128)(2,1)S(1)} %collective-permute-done.15), channel_id=1, source_target_pairs={{0,4},{1,3},{4,8},{5,1},{8,12},{9,5},{12,14},{13,9},{14,10},{15,13... | collective-permute-start | bytes 983048 | tf_op jit(solution)/shard_map/ppermute | solution.py:72
  58.5 1.6 %collective-permute-start.22 = (bf16[432,256]{1,0:T(8,128)(2,1)S(1)}, bf16[432,256]{1,0:T(8,128)(2,1)S(1)}, u32[]{:S(2)}, u32[]{:S(2)}) collective-permute-start(bf16[432,256]{1,0:T(8,128)(2,1)S(1)} %get-tuple-element.75), channel_id=1, source_target_pairs={{0,2},{1,3},{4,0},{5,1},{8,4},{9,5},{12,8},{13,9},{14,12},{15,13},... | collective-permute-start | bytes 663560 | tf_op jit(solution)/shard_map/ppermute | solution.py:72
  60.6 5.7 %collective-permute-done.20 = bf16[640,256]{1,0:T(8,128)(2,1)S(1)} collective-permute-done((bf16[640,256]{1,0:T(8,128)(2,1)S(1)}, bf16[640,256]{1,0:T(8,128)(2,1)S(1)}, u32[]{:S(2)}, u32[]{:S(2)}) %collective-permute-start.20) | collective-permute-done | bytes 327712 | tf_op jit(solution)/shard_map/ppermute | solution.py:72
  67.4 2.3 %collective-permute-start.26 = (bf16[640,256]{1,0:T(8,128)(2,1)S(1)}, bf16[640,256]{1,0:T(8,128)(2,1)S(1)}, u32[]{:S(2)}, u32[]{:S(2)}) collective-permute-start(bf16[640,256]{1,0:T(8,128)(2,1)S(1)} %collective-permute-done.20), channel_id=1, source_target_pairs={{0,4},{1,3},{4,8},{5,1},{8,12},{9,5},{12,14},{13,9},{14,10},{15,13... | collective-permute-start | bytes 983048 | tf_op jit(solution)/shard_map/ppermute | solution.py:72
  71.6 1.5 %collective-permute-start.25 = (bf16[432,256]{1,0:T(8,128)(2,1)S(1)}, bf16[432,256]{1,0:T(8,128)(2,1)S(1)}, u32[]{:S(2)}, u32[]{:S(2)}) collective-permute-start(bf16[432,256]{1,0:T(8,128)(2,1)S(1)} %get-tuple-element.51), channel_id=1, source_target_pairs={{0,4},{1,5},{4,8},{5,9},{8,12},{9,13},{12,14},{13,15},{14,10},{15,... | collective-permute-start | bytes 663560 | tf_op jit(solution)/shard_map/ppermute | solution.py:72
  73.1 7.7 %mix.1 = bf16[1024,256]{1,0:T(8,128)(2,1)} custom-call(bf16[20,64,2304]{2,1,0:T(8,128)(2,1)} %get-tuple-element.53.cols_ref, bf16[6912,256]{1,0:T(8,128)(2,1)} %refs_6_.1, bf16[1024,256]{1,0:T(8,128)(2,1)} %refs_4_.1), custom_call_target="tpu_custom_call" | custom-call | flops 6000000000 | tf_op jit(solution)/shard_map/mix/pallas_call | solution.py:687
  83.5 2.3 %collective-permute-start.28 = (bf16[432,256]{1,0:T(8,128)(2,1)S(1)}, bf16[432,256]{1,0:T(8,128)(2,1)S(1)}, u32[]{:S(2)}, u32[]{:S(2)}) collective-permute-start(bf16[432,256]{1,0:T(8,128)(2,1)S(1)} %get-tuple-element.59), channel_id=1, source_target_pairs={{0,4},{1,5},{4,8},{5,9},{8,12},{9,13},{12,14},{13,15},{14,10},{15,... | collective-permute-start | bytes 663560 | tf_op jit(solution)/shard_map/ppermute | solution.py:72
  86.5 5.4 %collective-permute-done.31 = bf16[640,256]{1,0:T(8,128)(2,1)S(1)} collective-permute-done((bf16[640,256]{1,0:T(8,128)(2,1)S(1)}, bf16[640,256]{1,0:T(8,128)(2,1)S(1)}, u32[]{:S(2)}, u32[]{:S(2)}) %collective-permute-start.31) | collective-permute-done | bytes 327712 | tf_op jit(solution)/shard_map/ppermute | solution.py:72
  91.9 2.4 %collective-permute-done.28 = bf16[432,256]{1,0:T(8,128)(2,1)S(1)} collective-permute-done((bf16[432,256]{1,0:T(8,128)(2,1)S(1)}, bf16[432,256]{1,0:T(8,128)(2,1)S(1)}, u32[]{:S(2)}, u32[]{:S(2)}) %collective-permute-start.28) | collective-permute-done | bytes 221216 | tf_op jit(solution)/shard_map/ppermute | solution.py:72
  94.4 1.5 %collective-permute-start.40 = (bf16[432,256]{1,0:T(8,128)(2,1)S(1)}, bf16[432,256]{1,0:T(8,128)(2,1)S(1)}, u32[]{:S(2)}, u32[]{:S(2)}) collective-permute-start(bf16[432,256]{1,0:T(8,128)(2,1)S(1)} %get-tuple-element.60), channel_id=1, source_target_pairs={{0,2},{1,3},{4,0},{5,1},{8,4},{9,5},{12,8},{13,9},{14,12},{15,13},... | collective-permute-start | bytes 663560 | tf_op jit(solution)/shard_map/ppermute | solution.py:72
  97.3 11.7 %input_grad.1 = bf16[1024,256]{1,0:T(8,128)(2,1)} custom-call(s32[16,256]{1,0:T(8,128)} %get-tuple-element.67.refs_0_, s32[1,64]{1,0:T(1,128)} %refs_1_.1, s32[33]{0:T(128)} %dynamic-slice_bitcast_fusion.refs_1_.refs_2_, bf16[1024,256]{1,0:T(8,128)(2,1)} %refs_3_.3, bf16[1024,256]{1,0:T(8,128)(2,1)} %refs_4_.1, f32[1,256]{1,0:T(1,128)} %bitcast.96, ...), custom_call_target="tpu_custom_call" | custom-call | flops 12999999488 | tf_op jit(solution)/shard_map/input_grad/pallas_call | solution.py:704
  (137 shorter events, 20.9 us)
Async XLA Ops:
  3.3 10.6 %collective-permute-start.1 = (bf16[656,256]{1,0:T(8,128)(2,1)}, bf16[656,256]{1,0:T(8,128)(2,1)S(1)}, u32[]{:S(2)}, u32[]{:S(2)}) collective-permute-start(bf16[656,256]{1,0:T(8,128)(2,1)} %get-tuple-element.38), channel_id=1, source_target_pairs={{0,4},{1,3},{4,8},{5,1},{8,12},{9,5},{12,14},{13,9},{14,10},{15,13... | collective-permute-start | bytes 1007624 | tf_op jit(solution)/shard_map/ppermute | solution.py:72
  6.3 11.2 %collective-permute-start.5 = (bf16[656,256]{1,0:T(8,128)(2,1)}, bf16[656,256]{1,0:T(8,128)(2,1)S(1)}, u32[]{:S(2)}, u32[]{:S(2)}) collective-permute-start(bf16[656,256]{1,0:T(8,128)(2,1)} %get-tuple-element.38), channel_id=1, source_target_pairs={{1,4},{0,3},{5,8},{4,1},{9,12},{8,5},{13,14},{12,9},{15,10},{14,13... | collective-permute-start | bytes 1007624 | tf_op jit(solution)/shard_map/ppermute | solution.py:72
  13.9 8.4 %collective-permute-start.2 = (bf16[656,256]{1,0:T(8,128)(2,1)S(1)}, bf16[656,256]{1,0:T(8,128)(2,1)S(1)}, u32[]{:S(2)}, u32[]{:S(2)}) collective-permute-start(bf16[656,256]{1,0:T(8,128)(2,1)S(1)} %collective-permute-done.1), channel_id=1, source_target_pairs={{0,4},{1,3},{4,8},{5,1},{8,12},{9,5},{12,14},{13,9},{14,10},{15,13... | collective-permute-start | bytes 1007624 | tf_op jit(solution)/shard_map/ppermute | solution.py:72
  17.5 8.4 %collective-permute-start.6 = (bf16[656,256]{1,0:T(8,128)(2,1)S(1)}, bf16[656,256]{1,0:T(8,128)(2,1)S(1)}, u32[]{:S(2)}, u32[]{:S(2)}) collective-permute-start(bf16[656,256]{1,0:T(8,128)(2,1)S(1)} %collective-permute-done.5), channel_id=1, source_target_pairs={{0,4},{1,3},{4,8},{5,1},{8,12},{9,5},{12,14},{13,9},{14,10},{15,13... | collective-permute-start | bytes 1007624 | tf_op jit(solution)/shard_map/ppermute | solution.py:72
  31.2 9.0 %collective-permute-start.10 = (bf16[656,256]{1,0:T(8,128)(2,1)S(1)}, bf16[656,256]{1,0:T(8,128)(2,1)S(1)}, u32[]{:S(2)}, u32[]{:S(2)}) collective-permute-start(bf16[656,256]{1,0:T(8,128)(2,1)S(1)} %collective-permute-done.3), channel_id=1, source_target_pairs={{0,1},{1,0},{2,3},{3,2},{4,5},{5,4},{6,7},{7,6},{8,9},{9,8},{10,11... | collective-permute-start | bytes 1007624 | tf_op jit(solution)/shard_map/ppermute | solution.py:76
  36.8 16.5 %collective-permute-start.15 = (bf16[640,256]{1,0:T(8,128)(2,1)}, bf16[640,256]{1,0:T(8,128)(2,1)S(1)}, u32[]{:S(2)}, u32[]{:S(2)}) collective-permute-start(bf16[640,256]{1,0:T(8,128)(2,1)} %extract.1), channel_id=1, source_target_pairs={{0,4},{1,3},{4,8},{5,1},{8,12},{9,5},{12,14},{13,9},{14,10},{15,13... | collective-permute-start | bytes 983048 | tf_op jit(solution)/shard_map/ppermute | solution.py:72
  37.9 15.3 %collective-permute-start.16 = (bf16[640,256]{1,0:T(8,128)(2,1)}, bf16[640,256]{1,0:T(8,128)(2,1)S(1)}, u32[]{:S(2)}, u32[]{:S(2)}) collective-permute-start(bf16[640,256]{1,0:T(8,128)(2,1)} %extract.1), channel_id=1, source_target_pairs={{1,4},{0,3},{5,8},{4,1},{9,12},{8,5},{13,14},{12,9},{15,10},{14,13... | collective-permute-start | bytes 983048 | tf_op jit(solution)/shard_map/ppermute | solution.py:72
  53.4 7.3 %collective-permute-start.21 = (bf16[640,256]{1,0:T(8,128)(2,1)S(1)}, bf16[640,256]{1,0:T(8,128)(2,1)S(1)}, u32[]{:S(2)}, u32[]{:S(2)}) collective-permute-start(bf16[640,256]{1,0:T(8,128)(2,1)S(1)} %collective-permute-done.16), channel_id=1, source_target_pairs={{0,4},{1,3},{4,8},{5,1},{8,12},{9,5},{12,14},{13,9},{14,10},{15,13... | collective-permute-start | bytes 983048 | tf_op jit(solution)/shard_map/ppermute | solution.py:72
  54.4 13.0 %collective-permute-start.17 = (bf16[2,432,256]{2,1,0:T(8,128)(2,1)}, bf16[2,432,256]{2,1,0:T(8,128)(2,1)S(1)}, u32[]{:S(2)}, u32[]{:S(2)}) collective-permute-start(bf16[2,432,256]{2,1,0:T(8,128)(2,1)} %get-tuple-element.46), channel_id=1, source_target_pairs={{0,1},{1,0},{2,3},{3,2},{4,5},{5,4},{6,7},{7,6},{8,9},{9,8},{10,11... | collective-permute-start | bytes 1327112 | tf_op jit(solution)/shard_map/ppermute | solution.py:76
  55.1 11.3 %collective-permute-start.20 = (bf16[640,256]{1,0:T(8,128)(2,1)S(1)}, bf16[640,256]{1,0:T(8,128)(2,1)S(1)}, u32[]{:S(2)}, u32[]{:S(2)}) collective-permute-start(bf16[640,256]{1,0:T(8,128)(2,1)S(1)} %collective-permute-done.15), channel_id=1, source_target_pairs={{0,4},{1,3},{4,8},{5,1},{8,12},{9,5},{12,14},{13,9},{14,10},{15,13... | collective-permute-start | bytes 983048 | tf_op jit(solution)/shard_map/ppermute | solution.py:72
  58.0 11.7 %collective-permute-start.19 = (bf16[432,256]{1,0:T(8,128)(2,1)S(1)}, bf16[432,256]{1,0:T(8,128)(2,1)S(1)}, u32[]{:S(2)}, u32[]{:S(2)}) collective-permute-start(bf16[432,256]{1,0:T(8,128)(2,1)S(1)} %get-tuple-element.76), channel_id=1, source_target_pairs={{0,4},{1,5},{4,8},{5,9},{8,12},{9,13},{12,14},{13,15},{14,10},{15,... | collective-permute-start | bytes 663560 | tf_op jit(solution)/shard_map/ppermute | solution.py:72
  58.5 11.2 %collective-permute-start.22 = (bf16[432,256]{1,0:T(8,128)(2,1)S(1)}, bf16[432,256]{1,0:T(8,128)(2,1)S(1)}, u32[]{:S(2)}, u32[]{:S(2)}) collective-permute-start(bf16[432,256]{1,0:T(8,128)(2,1)S(1)} %get-tuple-element.75), channel_id=1, source_target_pairs={{0,2},{1,3},{4,0},{5,1},{8,4},{9,5},{12,8},{13,9},{14,12},{15,13},... | collective-permute-start | bytes 663560 | tf_op jit(solution)/shard_map/ppermute | solution.py:72
  60.6 20.2 %collective-permute-start.24 = (bf16[2,432,256]{2,1,0:T(8,128)(2,1)}, bf16[2,432,256]{2,1,0:T(8,128)(2,1)S(1)}, u32[]{:S(2)}, u32[]{:S(2)}) collective-permute-start(bf16[2,432,256]{2,1,0:T(8,128)(2,1)} %get-tuple-element.58), channel_id=1, source_target_pairs={{0,1},{1,0},{2,3},{3,2},{4,5},{5,4},{6,7},{7,6},{8,9},{9,8},{10,11... | collective-permute-start | bytes 1327112 | tf_op jit(solution)/shard_map/ppermute | solution.py:76
  66.4 15.5 %collective-permute-start.27 = (bf16[640,256]{1,0:T(8,128)(2,1)S(1)}, bf16[640,256]{1,0:T(8,128)(2,1)S(1)}, u32[]{:S(2)}, u32[]{:S(2)}) collective-permute-start(bf16[640,256]{1,0:T(8,128)(2,1)S(1)} %collective-permute-done.21), channel_id=1, source_target_pairs={{0,4},{1,3},{4,8},{5,1},{8,12},{9,5},{12,14},{13,9},{14,10},{15,13... | collective-permute-start | bytes 983048 | tf_op jit(solution)/shard_map/ppermute | solution.py:72
  67.4 15.1 %collective-permute-start.26 = (bf16[640,256]{1,0:T(8,128)(2,1)S(1)}, bf16[640,256]{1,0:T(8,128)(2,1)S(1)}, u32[]{:S(2)}, u32[]{:S(2)}) collective-permute-start(bf16[640,256]{1,0:T(8,128)(2,1)S(1)} %collective-permute-done.20), channel_id=1, source_target_pairs={{0,4},{1,3},{4,8},{5,1},{8,12},{9,5},{12,14},{13,9},{14,10},{15,13... | collective-permute-start | bytes 983048 | tf_op jit(solution)/shard_map/ppermute | solution.py:72
  71.0 9.9 %collective-permute-start.30 = (bf16[432,256]{1,0:T(8,128)(2,1)S(1)}, bf16[432,256]{1,0:T(8,128)(2,1)S(1)}, u32[]{:S(2)}, u32[]{:S(2)}) collective-permute-start(bf16[432,256]{1,0:T(8,128)(2,1)S(1)} %get-tuple-element.52), channel_id=1, source_target_pairs={{0,2},{1,3},{4,0},{5,1},{8,4},{9,5},{12,8},{13,9},{14,12},{15,13},... | collective-permute-start | bytes 663560 | tf_op jit(solution)/shard_map/ppermute | solution.py:72
  71.6 10.1 %collective-permute-start.25 = (bf16[432,256]{1,0:T(8,128)(2,1)S(1)}, bf16[432,256]{1,0:T(8,128)(2,1)S(1)}, u32[]{:S(2)}, u32[]{:S(2)}) collective-permute-start(bf16[432,256]{1,0:T(8,128)(2,1)S(1)} %get-tuple-element.51), channel_id=1, source_target_pairs={{0,4},{1,5},{4,8},{5,9},{8,12},{9,13},{12,14},{13,15},{14,10},{15,... | collective-permute-start | bytes 663560 | tf_op jit(solution)/shard_map/ppermute | solution.py:72
  82.5 9.4 %collective-permute-start.31 = (bf16[640,256]{1,0:T(8,128)(2,1)S(1)}, bf16[640,256]{1,0:T(8,128)(2,1)S(1)}, u32[]{:S(2)}, u32[]{:S(2)}) collective-permute-start(bf16[640,256]{1,0:T(8,128)(2,1)S(1)} %collective-permute-done.26), channel_id=1, source_target_pairs={{0,4},{1,3},{4,8},{5,1},{8,12},{9,5},{12,14},{13,9},{14,10},{15,13... | collective-permute-start | bytes 983048 | tf_op jit(solution)/shard_map/ppermute | solution.py:72
  83.5 10.8 %collective-permute-start.28 = (bf16[432,256]{1,0:T(8,128)(2,1)S(1)}, bf16[432,256]{1,0:T(8,128)(2,1)S(1)}, u32[]{:S(2)}, u32[]{:S(2)}) collective-permute-start(bf16[432,256]{1,0:T(8,128)(2,1)S(1)} %get-tuple-element.59), channel_id=1, source_target_pairs={{0,4},{1,5},{4,8},{5,9},{8,12},{9,13},{12,14},{13,15},{14,10},{15,... | collective-permute-start | bytes 663560 | tf_op jit(solution)/shard_map/ppermute | solution.py:72
  85.8 8.5 %collective-permute-start.36 = (bf16[640,256]{1,0:T(8,128)(2,1)S(1)}, bf16[640,256]{1,0:T(8,128)(2,1)S(1)}, u32[]{:S(2)}, u32[]{:S(2)}) collective-permute-start(bf16[640,256]{1,0:T(8,128)(2,1)S(1)} %collective-permute-done.21), channel_id=1, source_target_pairs={{0,1},{1,0},{2,3},{3,2},{4,5},{5,4},{6,7},{7,6},{8,9},{9,8},{10,11... | collective-permute-start | bytes 983048 | tf_op jit(solution)/shard_map/ppermute | solution.py:76
  85.9 10.0 %collective-permute-start.33 = (bf16[640,256]{1,0:T(8,128)(2,1)S(1)}, bf16[640,256]{1,0:T(8,128)(2,1)S(1)}, u32[]{:S(2)}, u32[]{:S(2)}) collective-permute-start(bf16[640,256]{1,0:T(8,128)(2,1)S(1)} %collective-permute-done.20), channel_id=1, source_target_pairs={{0,1},{1,0},{2,3},{3,2},{4,5},{5,4},{6,7},{7,6},{8,9},{9,8},{10,11... | collective-permute-start | bytes 983048 | tf_op jit(solution)/shard_map/ppermute | solution.py:76
  86.5 9.5 %collective-permute-start.37 = (bf16[640,256]{1,0:T(8,128)(2,1)S(1)}, bf16[640,256]{1,0:T(8,128)(2,1)S(1)}, u32[]{:S(2)}, u32[]{:S(2)}) collective-permute-start(bf16[640,256]{1,0:T(8,128)(2,1)S(1)} %collective-permute-done.27), channel_id=1, source_target_pairs={{0,1},{1,0},{2,3},{3,2},{4,5},{5,4},{6,7},{7,6},{8,9},{9,8},{10,11... | collective-permute-start | bytes 983048 | tf_op jit(solution)/shard_map/ppermute | solution.py:76
  94.4 14.6 %collective-permute-start.40 = (bf16[432,256]{1,0:T(8,128)(2,1)S(1)}, bf16[432,256]{1,0:T(8,128)(2,1)S(1)}, u32[]{:S(2)}, u32[]{:S(2)}) collective-permute-start(bf16[432,256]{1,0:T(8,128)(2,1)S(1)} %get-tuple-element.60), channel_id=1, source_target_pairs={{0,2},{1,3},{4,0},{5,1},{8,4},{9,5},{12,8},{13,9},{14,12},{15,13},... | collective-permute-start | bytes 663560 | tf_op jit(solution)/shard_map/ppermute | solution.py:72
  96.0 13.1 %collective-permute-start.39 = (bf16[432,256]{1,0:T(8,128)(2,1)S(1)}, bf16[432,256]{1,0:T(8,128)(2,1)S(1)}, u32[]{:S(2)}, u32[]{:S(2)}) collective-permute-start(bf16[432,256]{1,0:T(8,128)(2,1)S(1)} %fusion.3), channel_id=1, source_target_pairs={{0,4},{1,5},{4,8},{5,9},{8,12},{9,13},{12,14},{13,15},{14,10},{15,... | collective-permute-start | bytes 663560 | tf_op jit(solution)/shard_map/ppermute | solution.py:72
  (51 other events, 456.9 us)

commit v11 on v10

--- a/solution.py
+++ b/solution.py
@@ -492,11 +492,16 @@
     return totals
 
 
-def mix_body(cols_ref, weight_ref, x_ref, out_ref, cols, weight, sems):
-    copies = start_stream(cols_ref, 0, cols, weight_ref, weight, sems)
-    for brick, total in enumerate(tap_sum(copies, cols, weight)):
-        at = slice(brick * 512, brick * 512 + 512)
-        out_ref[at, :] = (x_ref[at, :].astype(F32) + total).astype(BF16)
+def mix_body(here, *refs):
+    cols_ref, weight_ref, x_ref = refs[:3]
+    out_ref, cols, weight, rows, sems, row_sem = refs[-6:]
+    copies = start_stream(cols_ref, here * 10, cols, weight_ref, weight, sems)
+    (total,) = tap_sum(copies, cols, weight)
+    at = pl.ds(here * 512, 512)
+    rows[...] = (x_ref[at, :].astype(F32) + total).astype(BF16)
+    copy = pltpu.make_async_copy(rows, out_ref.at[at], row_sem.at[0])
+    copy.start()
+    copy.wait()
 
 
 def input_grad_body(slots, peers, count, *refs):
@@ -677,26 +682,36 @@
     first = (cot_ring.last(0), cot_ring.last(1))
     give = [lax.optimization_barrier((t, first))[0] for t in give]
     sums_ring = RingScatter(keep, give, peers)
-    sums_ring.go()
+    sent = sums_ring.go()
     cot_ring.go(0, cols)
     cot_ring.go(1, cols)
-    second = (cot_ring.last(0), cot_ring.last(1))
-    sent = sums_ring.go(second)
-    mix_cols = lax.optimization_barrier((cols, sent))[0]
+    ready = (cot_ring.last(0), cot_ring.last(1))
     weight_scratch = pltpu.VMEM((27 * channels, channels), BF16)
-    mixed = call(
-        mix_body,
-        sds((per_device, channels), BF16),
-        [HBM, HBM, VMEM],
-        [pltpu.VMEM(cols_shape(bricks), BF16), weight_scratch, pltpu.SemaphoreType.DMA((3, 4))],
-        cost=6,
-        name="mix",
-    )(mix_cols, conv_weight, features)
-    cot_ring.go(0)
-    cot_ring.go(1)
-    third = (cot_ring.last(0), cot_ring.last(1))
-    sent = sums_ring.go((third, mixed))
-    cot_ring.go(0, sent)
+    mixed = []
+    for brick in range(bricks):
+        mix_cols = lax.optimization_barrier((cols, sent))[0]
+        mixed.append(
+            call(
+                functools.partial(mix_body, brick),
+                sds((per_device, channels), BF16),
+                [HBM, HBM, VMEM] + [HBM] * len(mixed[-1:]),
+                [
+                    pltpu.VMEM(cols_shape(1), BF16),
+                    weight_scratch,
+                    pltpu.VMEM((512, channels), BF16),
+                    pltpu.SemaphoreType.DMA((3, 4)),
+                    pltpu.SemaphoreType.DMA((1,)),
+                ],
+                cost=3,
+                name="mix_" + str(brick),
+                out_specs=HBM,
+                aliases={3: 0} if mixed else None,
+            )(mix_cols, conv_weight, features, *mixed[-1:])
+        )
+        sent = sums_ring.go((ready, mixed[-1]))
+        cot_ring.go(0)
+        cot_ring.go(1)
+        ready = (cot_ring.last(0), cot_ring.last(1))
     cot_parts = cot_ring.places(cols)
     sent = sums_ring.go(tuple(t for k, t in enumerate(cot_parts) if k != peers // 2 + peers // 4))
     served = lax.optimization_barrier((served, sent))[0]
@@ -720,7 +735,7 @@
     )(served, send_face, table, cotangent, features, gain, conv_weight, *cot_parts)
     for _ in range(chips // 2 - 4):
         sums_ring.go()
-    return (mixed, grad_features, sums_ring.total(grad_features))
+    return (mixed[-1], grad_features, sums_ring.total(grad_features))
 
 
 def solution(mesh):

time: 111 us -> 114 us (1.027)
  Pallas kernels: 36 us -> 43 us
  waiting for transfers between devices: 32.6 us -> 30.9 us
  other arithmetic: 3.66 us -> 2.51 us
    pallas_call x1 -> x2, Pallas kernels: 7.69 us -> 13.6 us  [local(): call(functools.partial(mix_body, brick), sds((per_device, channels), BF16...]
    ppermute x21, waiting for transfers between devices: 32.5 us -> 30.9 us  [ring_step(): return lax.ppermute(x, 'morton', pairs)]
    pallas_call x1, Pallas kernels: 11.7 us -> 12.9 us  [local(): call(functools.partial(input_grad_body, slots, peers, count), sds((per_de...]
    ppermute x21, starting transfers between devices: 30.1 us -> 28.9 us  [ring_step(): return lax.ppermute(x, 'morton', pairs)]
    convert_element_type x4, other arithmetic: 2.79 us -> 1.64 us  [go(): part = part.astype(BF16)]
  transfers between devices with their start and end apart: 41 -> 41, of which waited for: 11 -> 11; matrix products, arithmetic and copies ran while one was open for 4% -> 3% of each run, Pallas kernels for 30% -> 35%
where the time goes in v11:
time: 114 us
  Pallas kernels  43 us (38%)
  starting transfers between devices  33.3 us (29%)
  waiting for transfers between devices  30.9 us (27%)
  local copies, waits for them, and re-layouts  2.88 us (3%)
  other arithmetic  2.51 us (2%)
  between operations  1.19 us (1%)
    ppermute x21, waiting for transfers between devices, ring_step(): return lax.ppermute(x, 'morton', pairs)  30.9 us
    ppermute x21, starting transfers between devices, ring_step(): return lax.ppermute(x, 'morton', pairs)  28.9 us
    pallas_call x2, Pallas kernels, local(): call(functools.partial(mix_body, brick), sds((per_device, channels), BF16...  13.6 us
    pallas_call x1, Pallas kernels, local(): call(functools.partial(input_grad_body, slots, peers, count), sds((per_de...  12.9 us
    pallas_call x1, Pallas kernels, local(): call(functools.partial(weight_grad_body, slots, factor, peers, count), (s...  12 us
    ppermute x20, starting transfers between devices, swap_cores(): return lax.ppermute(x, 'morton', [(m, m ^ 1) for m in range(peers)])  4.48 us
    pallas_call x1, Pallas kernels, local(): call(norm_body, (sds((per_device, channels), BF16), sds((bricks * ROWS +...  2.68 us
  transfers between devices with their start and end apart: 41, of which 11 were waited for; matrix products, arithmetic and copies ran while one was open for 3% of the time, Pallas kernels for 35%

profile of v11, /device:TPU:0, one launch (start us, length us, event | category | flops | bytes accessed | tf_op | source)
XLA Modules:
  0.0 113.9 jit_solution(6951456263043012744)
XLA Ops:
  0.6 2.7 %norm.1 = (bf16[1024,256]{1,0:T(8,128)(2,1)}, bf16[656,256]{1,0:T(8,128)(2,1)}) custom-call(s32[2,26]{1,0:T(2,128)} %refs_0_.1, s32[1,64]{1,0:T(1,128)} %refs_1_.5, bf16[1024,256]{1,0:T(8,128)(2,1)} %refs_4_.1, f32[1,256]{1,0:T(1,128)} %bitcast.94), custom_call_target="tpu_custom_call" | custom-call | flops 2000000000 | tf_op jit(solution)/shard_map/norm/pallas_call | solution.py:622
  3.3 3.0 %collective-permute-start.1 = (bf16[656,256]{1,0:T(8,128)(2,1)}, bf16[656,256]{1,0:T(8,128)(2,1)S(1)}, u32[]{:S(2)}, u32[]{:S(2)}) collective-permute-start(bf16[656,256]{1,0:T(8,128)(2,1)} %get-tuple-element.38), channel_id=1, source_target_pairs={{0,4},{1,3},{4,8},{5,1},{8,12},{9,5},{12,14},{13,9},{14,10},{15,13... | collective-permute-start | bytes 1007624 | tf_op jit(solution)/shard_map/ppermute | solution.py:72
  7.0 1.9 %extract.1 = bf16[640,256]{1,0:T(8,128)(2,1)} custom-call(bf16[1024,256]{1,0:T(8,128)(2,1)} %refs_3_.3), custom_call_target="tpu_custom_call" | custom-call | flops 2000000000 | tf_op jit(solution)/shard_map/extract/pallas_call | solution.py:630
  8.9 5.0 %collective-permute-done.1 = bf16[656,256]{1,0:T(8,128)(2,1)S(1)} collective-permute-done((bf16[656,256]{1,0:T(8,128)(2,1)}, bf16[656,256]{1,0:T(8,128)(2,1)S(1)}, u32[]{:S(2)}, u32[]{:S(2)}) %collective-permute-start.1) | collective-permute-done | bytes 335904 | tf_op jit(solution)/shard_map/ppermute | solution.py:72
  13.9 2.4 %collective-permute-start.2 = (bf16[656,256]{1,0:T(8,128)(2,1)S(1)}, bf16[656,256]{1,0:T(8,128)(2,1)S(1)}, u32[]{:S(2)}, u32[]{:S(2)}) collective-permute-start(bf16[656,256]{1,0:T(8,128)(2,1)S(1)} %collective-permute-done.1), channel_id=1, source_target_pairs={{0,4},{1,3},{4,8},{5,1},{8,12},{9,5},{12,14},{13,9},{14,10},{15,13... | collective-permute-start | bytes 1007624 | tf_op jit(solution)/shard_map/ppermute | solution.py:72
  19.2 3.2 %collective-permute-done.2 = bf16[656,256]{1,0:T(8,128)(2,1)S(1)} collective-permute-done((bf16[656,256]{1,0:T(8,128)(2,1)S(1)}, bf16[656,256]{1,0:T(8,128)(2,1)S(1)}, u32[]{:S(2)}, u32[]{:S(2)}) %collective-permute-start.2) | collective-permute-done | bytes 335904 | tf_op jit(solution)/shard_map/ppermute | solution.py:72
  24.0 2.0 %collective-permute-done.6 = bf16[656,256]{1,0:T(8,128)(2,1)S(1)} collective-permute-done((bf16[656,256]{1,0:T(8,128)(2,1)S(1)}, bf16[656,256]{1,0:T(8,128)(2,1)S(1)}, u32[]{:S(2)}, u32[]{:S(2)}) %collective-permute-start.6) | collective-permute-done | bytes 335904 | tf_op jit(solution)/shard_map/ppermute | solution.py:72
  27.1 2.5 %collective-permute-done.3 = bf16[656,256]{1,0:T(8,128)(2,1)S(1)} collective-permute-done((bf16[656,256]{1,0:T(8,128)(2,1)S(1)}, bf16[656,256]{1,0:T(8,128)(2,1)S(1)}, u32[]{:S(2)}, u32[]{:S(2)}) %collective-permute-start.3) | collective-permute-done | bytes 335904 | tf_op jit(solution)/shard_map/ppermute | solution.py:72
  31.3 1.9 %collective-permute-done.7 = bf16[656,256]{1,0:T(8,128)(2,1)S(1)} collective-permute-done((bf16[656,256]{1,0:T(8,128)(2,1)S(1)}, bf16[656,256]{1,0:T(8,128)(2,1)S(1)}, u32[]{:S(2)}, u32[]{:S(2)}) %collective-permute-start.7) | collective-permute-done | bytes 335904 | tf_op jit(solution)/shard_map/ppermute | solution.py:72
  33.2 3.6 %collective-permute-done.4 = bf16[656,256]{1,0:T(8,128)(2,1)S(1)} collective-permute-done((bf16[656,256]{1,0:T(8,128)(2,1)S(1)}, bf16[656,256]{1,0:T(8,128)(2,1)S(1)}, u32[]{:S(2)}, u32[]{:S(2)}) %collective-permute-start.4) | collective-permute-done | bytes 335904 | tf_op jit(solution)/shard_map/ppermute | solution.py:72
  37.9 2.3 %collective-permute-start.16 = (bf16[640,256]{1,0:T(8,128)(2,1)}, bf16[640,256]{1,0:T(8,128)(2,1)S(1)}, u32[]{:S(2)}, u32[]{:S(2)}) collective-permute-start(bf16[640,256]{1,0:T(8,128)(2,1)} %extract.1), channel_id=1, source_target_pairs={{1,4},{0,3},{5,8},{4,1},{9,12},{8,5},{13,14},{12,9},{15,10},{14,13... | collective-permute-start | bytes 983048 | tf_op jit(solution)/shard_map/ppermute | solution.py:72
  41.2 12.0 %weight_grad.1 = (f32[8,432,256]{2,1,0:T(8,128)}, bf16[2,432,256]{2,1,0:T(8,128)(2,1)}, bf16[2,432,256]{2,1,0:T(8,128)(2,1)}, bf16[2,432,256]{2,1,0:T(8,128)(2,1...) custom-call(s32[2,26]{1,0:T(2,128)} %refs_0_.1, ...), custom_call_target="tpu_custom_call" | custom-call | flops 8999999488 | tf_op jit(solution)/shard_map/weight_grad/pallas_call | solution.py:653
  55.1 2.2 %collective-permute-start.20 = (bf16[640,256]{1,0:T(8,128)(2,1)S(1)}, bf16[640,256]{1,0:T(8,128)(2,1)S(1)}, u32[]{:S(2)}, u32[]{:S(2)}) collective-permute-start(bf16[640,256]{1,0:T(8,128)(2,1)S(1)} %collective-permute-done.15), channel_id=1, source_target_pairs={{0,4},{1,3},{4,8},{5,1},{8,12},{9,5},{12,14},{13,9},{14,10},{15,13... | collective-permute-start | bytes 983048 | tf_op jit(solution)/shard_map/ppermute | solution.py:72
  60.5 2.3 %collective-permute-start.22 = (bf16[432,256]{1,0:T(8,128)(2,1)S(1)}, bf16[432,256]{1,0:T(8,128)(2,1)S(1)}, u32[]{:S(2)}, u32[]{:S(2)}) collective-permute-start(bf16[432,256]{1,0:T(8,128)(2,1)S(1)} %get-tuple-element.75), channel_id=1, source_target_pairs={{0,2},{1,3},{4,0},{5,1},{8,4},{9,5},{12,8},{13,9},{14,12},{15,13},... | collective-permute-start | bytes 663560 | tf_op jit(solution)/shard_map/ppermute | solution.py:72
  62.8 6.8 %mix_0.1.refs_3_ = bf16[1024,256]{1,0:T(8,128)(2,1)} custom-call(bf16[20,64,2304]{2,1,0:T(8,128)(2,1)} %get-tuple-element.54.refs_0_, bf16[6912,256]{1,0:T(8,128)(2,1)} %refs_6_.1, bf16[1024,256]{1,0:T(8,128)(2,1)} %refs_4_.1), custom_call_target="tpu_custom_call" | custom-call | flops 3000000000 | tf_op jit(solution)/shard_map/mix_0/pallas_call | solution.py:694
  69.7 2.0 %collective-permute-start.26 = (bf16[640,256]{1,0:T(8,128)(2,1)S(1)}, bf16[640,256]{1,0:T(8,128)(2,1)}, u32[]{:S(2)}, u32[]{:S(2)}) collective-permute-start(bf16[640,256]{1,0:T(8,128)(2,1)S(1)} %collective-permute-done.20), channel_id=1, source_target_pairs={{0,4},{1,3},{4,8},{5,1},{8,12},{9,5},{12,14},{13,9},{14,10},{15,13... | collective-permute-start | bytes 983048 | tf_op jit(solution)/shard_map/ppermute | solution.py:72
  72.0 2.1 %collective-permute-start.25 = (bf16[432,256]{1,0:T(8,128)(2,1)S(1)}, bf16[432,256]{1,0:T(8,128)(2,1)S(1)}, u32[]{:S(2)}, u32[]{:S(2)}) collective-permute-start(bf16[432,256]{1,0:T(8,128)(2,1)S(1)} %get-tuple-element.52), channel_id=1, source_target_pairs={{0,4},{1,5},{4,8},{5,9},{8,12},{9,13},{12,14},{13,15},{14,10},{15,... | collective-permute-start | bytes 663560 | tf_op jit(solution)/shard_map/ppermute | solution.py:72
  74.1 6.8 %mix_1.1 = bf16[1024,256]{1,0:T(8,128)(2,1)} custom-call(bf16[20,64,2304]{2,1,0:T(8,128)(2,1)} %get-tuple-element.54.refs_0_, bf16[6912,256]{1,0:T(8,128)(2,1)} %refs_6_.1, bf16[1024,256]{1,0:T(8,128)(2,1)} %refs_4_.1, bf16[1024,256]{1,0:T(8,128)(2,1)} %mix_0.1.refs_3_), custom_call_target="tpu_custom_call", output_to_operand_aliasing={{}: (3, {})} | custom-call | flops 3000000000 | tf_op jit(solution)/shard_map/mix_1/pallas_call | solution.py:694
  81.0 1.8 %collective-permute-done.26 = bf16[640,256]{1,0:T(8,128)(2,1)} collective-permute-done((bf16[640,256]{1,0:T(8,128)(2,1)S(1)}, bf16[640,256]{1,0:T(8,128)(2,1)}, u32[]{:S(2)}, u32[]{:S(2)}) %collective-permute-start.26) | collective-permute-done | bytes 327712 | tf_op jit(solution)/shard_map/ppermute | solution.py:72
  82.8 1.8 %collective-permute-start.23 = (bf16[2,432,256]{2,1,0:T(8,128)(2,1)S(1)}, bf16[2,432,256]{2,1,0:T(8,128)(2,1)S(1)}, u32[]{:S(2)}, u32[]{:S(2)}) collective-permute-start(bf16[2,432,256]{2,1,0:T(8,128)(2,1)S(1)} %copy-done.1), channel_id=1, source_target_pairs={{0,1},{1,0},{2,3},{3,2},{4,5},{5,4},{6,7},{7,6},{8,9},{9,8},{10,11... | collective-permute-start | bytes 1327112 | tf_op jit(solution)/shard_map/ppermute | solution.py:76
  85.2 2.1 %collective-permute-start.28 = (bf16[432,256]{1,0:T(8,128)(2,1)S(1)}, bf16[432,256]{1,0:T(8,128)(2,1)S(1)}, u32[]{:S(2)}, u32[]{:S(2)}) collective-permute-start(bf16[432,256]{1,0:T(8,128)(2,1)S(1)} %get-tuple-element.60), channel_id=1, source_target_pairs={{0,4},{1,5},{4,8},{5,9},{8,12},{9,13},{12,14},{13,15},{14,10},{15,... | collective-permute-start | bytes 663560 | tf_op jit(solution)/shard_map/ppermute | solution.py:72
  88.0 6.7 %collective-permute-done.30 = bf16[640,256]{1,0:T(8,128)(2,1)S(1)} collective-permute-done((bf16[640,256]{1,0:T(8,128)(2,1)}, bf16[640,256]{1,0:T(8,128)(2,1)S(1)}, u32[]{:S(2)}, u32[]{:S(2)}) %collective-permute-start.30) | collective-permute-done | bytes 327712 | tf_op jit(solution)/shard_map/ppermute | solution.py:72
  94.7 2.4 %collective-permute-done.28 = bf16[432,256]{1,0:T(8,128)(2,1)S(1)} collective-permute-done((bf16[432,256]{1,0:T(8,128)(2,1)S(1)}, bf16[432,256]{1,0:T(8,128)(2,1)S(1)}, u32[]{:S(2)}, u32[]{:S(2)}) %collective-permute-start.28) | collective-permute-done | bytes 221216 | tf_op jit(solution)/shard_map/ppermute | solution.py:72
  100.1 12.9 %input_grad.1 = bf16[1024,256]{1,0:T(8,128)(2,1)} custom-call(s32[16,256]{1,0:T(8,128)} %get-tuple-element.66.refs_0_, s32[1,64]{1,0:T(1,128)} %refs_1_.5, s32[33]{0:T(128)} %dynamic-slice_bitcast_fusion.refs_1_.refs_2_, bf16[1024,256]{1,0:T(8,128)(2,1)} %refs_3_.3, bf16[1024,256]{1,0:T(8,128)(2,1)} %refs_4_.1, f32[1,256]{1,0:T(1,128)} %bitcast.95, ...), custom_call_target="tpu_custom_call" | custom-call | flops 12999999488 | tf_op jit(solution)/shard_map/input_grad/pallas_call | solution.py:719
  (136 shorter events, 20.6 us)
Async XLA Ops:
  3.3 10.6 %collective-permute-start.1 = (bf16[656,256]{1,0:T(8,128)(2,1)}, bf16[656,256]{1,0:T(8,128)(2,1)S(1)}, u32[]{:S(2)}, u32[]{:S(2)}) collective-permute-start(bf16[656,256]{1,0:T(8,128)(2,1)} %get-tuple-element.38), channel_id=1, source_target_pairs={{0,4},{1,3},{4,8},{5,1},{8,12},{9,5},{12,14},{13,9},{14,10},{15,13... | collective-permute-start | bytes 1007624 | tf_op jit(solution)/shard_map/ppermute | solution.py:72
  6.3 11.2 %collective-permute-start.5 = (bf16[656,256]{1,0:T(8,128)(2,1)}, bf16[656,256]{1,0:T(8,128)(2,1)S(1)}, u32[]{:S(2)}, u32[]{:S(2)}) collective-permute-start(bf16[656,256]{1,0:T(8,128)(2,1)} %get-tuple-element.38), channel_id=1, source_target_pairs={{1,4},{0,3},{5,8},{4,1},{9,12},{8,5},{13,14},{12,9},{15,10},{14,13... | collective-permute-start | bytes 1007624 | tf_op jit(solution)/shard_map/ppermute | solution.py:72
  13.9 8.4 %collective-permute-start.2 = (bf16[656,256]{1,0:T(8,128)(2,1)S(1)}, bf16[656,256]{1,0:T(8,128)(2,1)S(1)}, u32[]{:S(2)}, u32[]{:S(2)}) collective-permute-start(bf16[656,256]{1,0:T(8,128)(2,1)S(1)} %collective-permute-done.1), channel_id=1, source_target_pairs={{0,4},{1,3},{4,8},{5,1},{8,12},{9,5},{12,14},{13,9},{14,10},{15,13... | collective-permute-start | bytes 1007624 | tf_op jit(solution)/shard_map/ppermute | solution.py:72
  17.6 8.4 %collective-permute-start.6 = (bf16[656,256]{1,0:T(8,128)(2,1)S(1)}, bf16[656,256]{1,0:T(8,128)(2,1)S(1)}, u32[]{:S(2)}, u32[]{:S(2)}) collective-permute-start(bf16[656,256]{1,0:T(8,128)(2,1)S(1)} %collective-permute-done.5), channel_id=1, source_target_pairs={{0,4},{1,3},{4,8},{5,1},{8,12},{9,5},{12,14},{13,9},{14,10},{15,13... | collective-permute-start | bytes 1007624 | tf_op jit(solution)/shard_map/ppermute | solution.py:72
  31.2 9.0 %collective-permute-start.10 = (bf16[656,256]{1,0:T(8,128)(2,1)S(1)}, bf16[656,256]{1,0:T(8,128)(2,1)S(1)}, u32[]{:S(2)}, u32[]{:S(2)}) collective-permute-start(bf16[656,256]{1,0:T(8,128)(2,1)S(1)} %collective-permute-done.3), channel_id=1, source_target_pairs={{0,1},{1,0},{2,3},{3,2},{4,5},{5,4},{6,7},{7,6},{8,9},{9,8},{10,11... | collective-permute-start | bytes 1007624 | tf_op jit(solution)/shard_map/ppermute | solution.py:76
  36.8 16.4 %collective-permute-start.15 = (bf16[640,256]{1,0:T(8,128)(2,1)}, bf16[640,256]{1,0:T(8,128)(2,1)S(1)}, u32[]{:S(2)}, u32[]{:S(2)}) collective-permute-start(bf16[640,256]{1,0:T(8,128)(2,1)} %extract.1), channel_id=1, source_target_pairs={{0,4},{1,3},{4,8},{5,1},{8,12},{9,5},{12,14},{13,9},{14,10},{15,13... | collective-permute-start | bytes 983048 | tf_op jit(solution)/shard_map/ppermute | solution.py:72
  37.9 15.3 %collective-permute-start.16 = (bf16[640,256]{1,0:T(8,128)(2,1)}, bf16[640,256]{1,0:T(8,128)(2,1)S(1)}, u32[]{:S(2)}, u32[]{:S(2)}) collective-permute-start(bf16[640,256]{1,0:T(8,128)(2,1)} %extract.1), channel_id=1, source_target_pairs={{1,4},{0,3},{5,8},{4,1},{9,12},{8,5},{13,14},{12,9},{15,10},{14,13... | collective-permute-start | bytes 983048 | tf_op jit(solution)/shard_map/ppermute | solution.py:72
  54.4 17.6 %collective-permute-start.24 = (bf16[2,432,256]{2,1,0:T(8,128)(2,1)}, bf16[2,432,256]{2,1,0:T(8,128)(2,1)S(1)}, u32[]{:S(2)}, u32[]{:S(2)}) collective-permute-start(bf16[2,432,256]{2,1,0:T(8,128)(2,1)} %get-tuple-element.59), channel_id=1, source_target_pairs={{0,1},{1,0},{2,3},{3,2},{4,5},{5,4},{6,7},{7,6},{8,9},{9,8},{10,11... | collective-permute-start | bytes 1327112 | tf_op jit(solution)/shard_map/ppermute | solution.py:76
  55.1 14.6 %collective-permute-start.17 = (bf16[2,432,256]{2,1,0:T(8,128)(2,1)}, bf16[2,432,256]{2,1,0:T(8,128)(2,1)S(1)}, u32[]{:S(2)}, u32[]{:S(2)}) collective-permute-start(bf16[2,432,256]{2,1,0:T(8,128)(2,1)} %get-tuple-element.46), channel_id=1, source_target_pairs={{0,1},{1,0},{2,3},{3,2},{4,5},{5,4},{6,7},{7,6},{8,9},{9,8},{10,11... | collective-permute-start | bytes 1327112 | tf_op jit(solution)/shard_map/ppermute | solution.py:76
  55.1 14.5 %collective-permute-start.20 = (bf16[640,256]{1,0:T(8,128)(2,1)S(1)}, bf16[640,256]{1,0:T(8,128)(2,1)S(1)}, u32[]{:S(2)}, u32[]{:S(2)}) collective-permute-start(bf16[640,256]{1,0:T(8,128)(2,1)S(1)} %collective-permute-done.15), channel_id=1, source_target_pairs={{0,4},{1,3},{4,8},{5,1},{8,12},{9,5},{12,14},{13,9},{14,10},{15,13... | collective-permute-start | bytes 983048 | tf_op jit(solution)/shard_map/ppermute | solution.py:72
  58.5 11.2 %collective-permute-start.19 = (bf16[432,256]{1,0:T(8,128)(2,1)S(1)}, bf16[432,256]{1,0:T(8,128)(2,1)S(1)}, u32[]{:S(2)}, u32[]{:S(2)}) collective-permute-start(bf16[432,256]{1,0:T(8,128)(2,1)S(1)} %get-tuple-element.76), channel_id=1, source_target_pairs={{0,4},{1,5},{4,8},{5,9},{8,12},{9,13},{12,14},{13,15},{14,10},{15,... | collective-permute-start | bytes 663560 | tf_op jit(solution)/shard_map/ppermute | solution.py:72
  60.5 11.3 %collective-permute-start.22 = (bf16[432,256]{1,0:T(8,128)(2,1)S(1)}, bf16[432,256]{1,0:T(8,128)(2,1)S(1)}, u32[]{:S(2)}, u32[]{:S(2)}) collective-permute-start(bf16[432,256]{1,0:T(8,128)(2,1)S(1)} %get-tuple-element.75), channel_id=1, source_target_pairs={{0,2},{1,3},{4,0},{5,1},{8,4},{9,5},{12,8},{13,9},{14,12},{15,13},... | collective-permute-start | bytes 663560 | tf_op jit(solution)/shard_map/ppermute | solution.py:72
  69.6 15.6 %collective-permute-start.29 = (bf16[640,256]{1,0:T(8,128)(2,1)S(1)}, bf16[640,256]{1,0:T(8,128)(2,1)S(1)}, u32[]{:S(2)}, u32[]{:S(2)}) collective-permute-start(bf16[640,256]{1,0:T(8,128)(2,1)S(1)} %copy-done.18), channel_id=1, source_target_pairs={{0,1},{1,0},{2,3},{3,2},{4,5},{5,4},{6,7},{7,6},{8,9},{9,8},{10,11... | collective-permute-start | bytes 983048 | tf_op jit(solution)/shard_map/ppermute | solution.py:76
  69.7 11.2 %collective-permute-start.27 = (bf16[640,256]{1,0:T(8,128)(2,1)S(1)}, bf16[640,256]{1,0:T(8,128)(2,1)S(1)}, u32[]{:S(2)}, u32[]{:S(2)}) collective-permute-start(bf16[640,256]{1,0:T(8,128)(2,1)S(1)} %collective-permute-done.21), channel_id=1, source_target_pairs={{0,4},{1,3},{4,8},{5,1},{8,12},{9,5},{12,14},{13,9},{14,10},{15,13... | collective-permute-start | bytes 983048 | tf_op jit(solution)/shard_map/ppermute | solution.py:72
  69.7 13.0 %collective-permute-start.26 = (bf16[640,256]{1,0:T(8,128)(2,1)S(1)}, bf16[640,256]{1,0:T(8,128)(2,1)}, u32[]{:S(2)}, u32[]{:S(2)}) collective-permute-start(bf16[640,256]{1,0:T(8,128)(2,1)S(1)} %collective-permute-done.20), channel_id=1, source_target_pairs={{0,4},{1,3},{4,8},{5,1},{8,12},{9,5},{12,14},{13,9},{14,10},{15,13... | collective-permute-start | bytes 983048 | tf_op jit(solution)/shard_map/ppermute | solution.py:72
  71.9 10.9 %collective-permute-start.39 = (bf16[432,256]{1,0:T(8,128)(2,1)S(1)}, bf16[432,256]{1,0:T(8,128)(2,1)S(1)}, u32[]{:S(2)}, u32[]{:S(2)}) collective-permute-start(bf16[432,256]{1,0:T(8,128)(2,1)S(1)} %get-tuple-element.53), channel_id=1, source_target_pairs={{0,2},{1,3},{4,0},{5,1},{8,4},{9,5},{12,8},{13,9},{14,12},{15,13},... | collective-permute-start | bytes 663560 | tf_op jit(solution)/shard_map/ppermute | solution.py:72
  72.0 13.0 %collective-permute-start.25 = (bf16[432,256]{1,0:T(8,128)(2,1)S(1)}, bf16[432,256]{1,0:T(8,128)(2,1)S(1)}, u32[]{:S(2)}, u32[]{:S(2)}) collective-permute-start(bf16[432,256]{1,0:T(8,128)(2,1)S(1)} %get-tuple-element.52), channel_id=1, source_target_pairs={{0,4},{1,5},{4,8},{5,9},{8,12},{9,13},{12,14},{13,15},{14,10},{15,... | collective-permute-start | bytes 663560 | tf_op jit(solution)/shard_map/ppermute | solution.py:72
  85.0 9.7 %collective-permute-start.30 = (bf16[640,256]{1,0:T(8,128)(2,1)}, bf16[640,256]{1,0:T(8,128)(2,1)S(1)}, u32[]{:S(2)}, u32[]{:S(2)}) collective-permute-start(bf16[640,256]{1,0:T(8,128)(2,1)} %collective-permute-done.26), channel_id=1, source_target_pairs={{0,4},{1,3},{4,8},{5,1},{8,12},{9,5},{12,14},{13,9},{14,10},{15,13... | collective-permute-start | bytes 983048 | tf_op jit(solution)/shard_map/ppermute | solution.py:72
  85.2 11.8 %collective-permute-start.28 = (bf16[432,256]{1,0:T(8,128)(2,1)S(1)}, bf16[432,256]{1,0:T(8,128)(2,1)S(1)}, u32[]{:S(2)}, u32[]{:S(2)}) collective-permute-start(bf16[432,256]{1,0:T(8,128)(2,1)S(1)} %get-tuple-element.60), channel_id=1, source_target_pairs={{0,4},{1,5},{4,8},{5,9},{8,12},{9,13},{12,14},{13,15},{14,10},{15,... | collective-permute-start | bytes 663560 | tf_op jit(solution)/shard_map/ppermute | solution.py:72
  87.3 9.9 %collective-permute-start.35 = (bf16[640,256]{1,0:T(8,128)(2,1)S(1)}, bf16[640,256]{1,0:T(8,128)(2,1)S(1)}, u32[]{:S(2)}, u32[]{:S(2)}) collective-permute-start(bf16[640,256]{1,0:T(8,128)(2,1)S(1)} %collective-permute-done.21), channel_id=1, source_target_pairs={{0,1},{1,0},{2,3},{3,2},{4,5},{5,4},{6,7},{7,6},{8,9},{9,8},{10,11... | collective-permute-start | bytes 983048 | tf_op jit(solution)/shard_map/ppermute | solution.py:76
  87.4 10.3 %collective-permute-start.32 = (bf16[640,256]{1,0:T(8,128)(2,1)S(1)}, bf16[640,256]{1,0:T(8,128)(2,1)S(1)}, u32[]{:S(2)}, u32[]{:S(2)}) collective-permute-start(bf16[640,256]{1,0:T(8,128)(2,1)S(1)} %collective-permute-done.20), channel_id=1, source_target_pairs={{0,1},{1,0},{2,3},{3,2},{4,5},{5,4},{6,7},{7,6},{8,9},{9,8},{10,11... | collective-permute-start | bytes 983048 | tf_op jit(solution)/shard_map/ppermute | solution.py:76
  87.9 9.7 %collective-permute-start.36 = (bf16[640,256]{1,0:T(8,128)(2,1)S(1)}, bf16[640,256]{1,0:T(8,128)(2,1)S(1)}, u32[]{:S(2)}, u32[]{:S(2)}) collective-permute-start(bf16[640,256]{1,0:T(8,128)(2,1)S(1)} %collective-permute-done.27), channel_id=1, source_target_pairs={{0,1},{1,0},{2,3},{3,2},{4,5},{5,4},{6,7},{7,6},{8,9},{9,8},{10,11... | collective-permute-start | bytes 983048 | tf_op jit(solution)/shard_map/ppermute | solution.py:76
  97.2 15.9 %collective-permute-start.40 = (bf16[432,256]{1,0:T(8,128)(2,1)S(1)}, bf16[432,256]{1,0:T(8,128)(2,1)S(1)}, u32[]{:S(2)}, u32[]{:S(2)}) collective-permute-start(bf16[432,256]{1,0:T(8,128)(2,1)S(1)} %get-tuple-element.68), channel_id=1, source_target_pairs={{0,2},{1,3},{4,0},{5,1},{8,4},{9,5},{12,8},{13,9},{14,12},{15,13},... | collective-permute-start | bytes 663560 | tf_op jit(solution)/shard_map/ppermute | solution.py:72
  97.7 15.3 %collective-permute-start.38 = (bf16[432,256]{1,0:T(8,128)(2,1)S(1)}, bf16[432,256]{1,0:T(8,128)(2,1)S(1)}, u32[]{:S(2)}, u32[]{:S(2)}) collective-permute-start(bf16[432,256]{1,0:T(8,128)(2,1)S(1)} %fusion.3), channel_id=1, source_target_pairs={{0,4},{1,5},{4,8},{5,9},{8,12},{9,13},{12,14},{13,15},{14,10},{15,... | collective-permute-start | bytes 663560 | tf_op jit(solution)/shard_map/ppermute | solution.py:72
  (50 other events, 464.6 us)

commit v12 on v10

--- a/solution.py
+++ b/solution.py
@@ -45,21 +45,23 @@
     behind = (spot[device // 2][:, None] - spot[None, :]) % chips
     half = chips // 2
     turn = np.where(behind >= half, 2 * (behind - half), 2 * (half - 1 - behind) + 1)
-    place_of = np.broadcast_to(device, (peers, peers)).copy()
+    places = np.broadcast_to(device, (2, peers, peers)).copy()
     if chips <= 8:
         for me in range(peers):
             for other in range(peers):
                 away = behind[me, other // 2] if me % 2 == 0 else -behind[me, other // 2] % chips
                 same = me % 2 == other % 2
                 if away == 0:
-                    place = 0 if same else 1
+                    place = (0, 0) if same else (1, 1)
                 elif away < half or (away == half and same):
-                    place = 1 + away if same else 1 + half + away
+                    place = (1 + away, 2 * away) if same else (1 + half + away, 2 * away + 1)
                 else:
                     away = chips - away
-                    place = half + (away if not same else half + away) + half
-                place_of[me, other] = place
-    return np.concatenate([place_of, behind, turn, device[:, None]], axis=1).astype(np.int32)
+                    place = (2 * half + away, 2 * half + 2 * away - 1)
+                    if same:
+                        place = (3 * half + away, 2 * half + 2 * away)
+                places[:, me, other] = place
+    return np.concatenate([*places, behind, turn, device[:, None]], axis=1).astype(np.int32)
 
 
 def ring_step(x, peers, step, cross=0):
@@ -106,6 +108,39 @@
             held = [lax.optimization_barrier((t, gate))[0] for t in mine]
         others = [swap_cores(t, self.peers) for t in [self.x] + held]
         return [t[None] for t in [self.x] + others[:1] + mine + others[1:]]
+
+
+class PairGather:
+    def __init__(self, x, peers, gate):
+        self.peers, self.chips = peers, peers // 2
+        self.whole = None
+        if self.chips > 8:
+            self.whole = lax.all_gather(x[None], "morton", axis=0, tiled=True)
+            return
+        self.rows = x.shape[0]
+        x = lax.optimization_barrier((x, gate))[0]
+        self.hops = [jnp.concatenate([x, swap_cores(x, peers)], axis=0)]
+
+    def go(self, gate=None):
+        if self.whole is not None:
+            return
+        held = self.hops[-1]
+        if len(self.hops) == self.chips // 2:
+            held = held[: self.rows]
+        if gate is not None:
+            held = lax.optimization_barrier((held, gate))[0]
+        self.hops.append(ring_step(held, self.peers, 0))
+
+    def last(self):
+        return self.whole if self.whole is not None else self.hops[-1]
+
+    def places(self, gate):
+        if self.whole is not None:
+            return [self.whole], [self.whole]
+        held = [lax.optimization_barrier((t, gate))[0] for t in self.hops[1:]]
+        got = self.hops + [swap_cores(t, self.peers) for t in held]
+        got = [t.reshape(-1, self.rows, t.shape[1]) for t in got]
+        return got, got[: self.chips // 2] + got[self.chips // 2 + 1 : -1]
 
 
 class RingScatter:
@@ -327,7 +362,7 @@
         add_cell(pads[0], cell(facing))
 
 
-def windows(cells, halo, cols, bricks, out=None, sems=None):
+def windows(cells, halo, cols, bricks):
     row = lax.broadcasted_iota(jnp.int32, (8, C), 0)
 
     def step(k, _):
@@ -344,45 +379,39 @@
                 block = jnp.concatenate(shifted[l][j : j + 8], axis=0).astype(BF16)
                 at = (3 * j + l) * C
                 cols[k, :, at : at + C] = block
-        if out is not None:
-            pltpu.make_async_copy(cols.at[k], out.at[k], sems.at[k]).start()
         return 0
 
     lax.fori_loop(0, bricks * 10, step, 0)
 
 
-def wait_windows(cols, out, sems, bricks):
-    def step(k, _):
-        pltpu.make_async_copy(cols.at[k], out.at[k], sems.at[k]).wait()
-        return 0
-
-    lax.fori_loop(0, bricks * 10, step, 0)
-
-
 def fetch(parts, share, sems, first=0, rows=None):
-    size = parts[0].shape[0]
     lines = pl.ds(first, rows or parts[0].shape[1])
-    copies = [
-        pltpu.make_async_copy(part.at[:, lines], share.at[pl.ds(k * size, size), lines], sems.at[k])
-        for k, part in enumerate(parts)
-    ]
+    copies = []
+    place = 0
+    for k, part in enumerate(parts):
+        size = part.shape[0]
+        to = share.at[pl.ds(place, size), lines]
+        copies.append(pltpu.make_async_copy(part.at[:, lines], to, sems.at[k]))
+        place += size
     for copy in copies:
         copy.start()
     return copies
 
 
 def weight_grad_body(slots, factor, peers, count, *refs):
-    recv, table, own_ref, cot_ref = refs[:4]
-    parts = refs[4 : 4 + count]
-    keep_ref = refs[4 + count]
-    give_refs = refs[5 + count : 5 + count + peers // 4]
-    out_cols, codes_ref, served_ref = refs[-16:-13]
-    cells, halo, share, cols, sums, narrow, turned, codes = refs[-13:-5]
-    sems, cols_sems, codes_sem, out_sems, notes_sems = refs[-5:]
+    recv, table, own_ref, cot_ref, x_ref, weight_ref = refs[:6]
+    parts = refs[6 : 6 + count]
+    keep_ref = refs[6 + count]
+    give_refs = refs[7 + count : 7 + count + peers // 4]
+    mix_ref, codes_ref, served_ref = refs[-16:-13]
+    cells, halo, share, cols, sums, narrow, turned, weight, codes = refs[-13:-4]
+    sems, codes_sem, out_sems, notes_sems = refs[-4:]
     bricks = own_ref.shape[0] // 512
-    me = table[2 * peers]
+    me = table[3 * peers]
     notes_copies = fetch(parts, share, notes_sems, bricks * ROWS, NOTES)
     copies = fetch(parts, share, sems, 0, bricks * ROWS)
+    weight_copy = pltpu.make_async_copy(weight_ref, weight, codes_sem.at[1])
+    weight_copy.start()
     for part in range(bricks * 2):
         at = slice(part * 256, part * 256 + 256)
         turned[:, at] = cot_ref[at, :].astype(F32).T.astype(BF16)
@@ -407,7 +436,7 @@
             code = codes[at, me * slots + safe - sender * slots]
             kind = tuple(abs(t) for t in e)
             place(kind, e, slot >= 0, at, code // 6, brick, share, cells, halo)
-    windows(cells, halo, cols, bricks, out_cols, cols_sems)
+    windows(cells, halo, cols, bricks)
 
     rows = 27 * C // peers
     for tap in range(27):
@@ -425,78 +454,33 @@
             stop = min((tap + 1) * C, (owner + 1) * rows)
             piece = total[start - tap * C : stop - tap * C]
             bucket = jnp.bitwise_xor(me % 2, owner % 2)
-            behind = table[peers + owner // 2]
+            behind = table[2 * peers + owner // 2]
             where = slice(start - owner * rows, stop - owner * rows)
             sums[bucket, behind, where, :] = piece
-            narrow[bucket, behind, where, :] = piece.astype(BF16)
+            turn = table[2 * peers + peers // 2 + owner // 2]
+            narrow[bucket, turn, where, :] = piece.astype(BF16)
             start = stop
-            if stop == (owner + 1) * rows:
-
-                @pl.when(bucket == 0)
-                def _():
-                    pltpu.make_async_copy(
-                        sums.at[0, behind], keep_ref.at[behind], out_sems.at[0, behind]
-                    ).start()
-
-                turn = table[peers + peers // 2 + owner // 2]
-                for hop, give_ref in enumerate(give_refs):
-
-                    @pl.when((bucket == 1) & (turn // 2 == hop))
-                    def _():
-                        pltpu.make_async_copy(
-                            narrow.at[1, behind], give_ref.at[turn % 2], out_sems.at[1, turn]
-                        ).start()
-
+
+    out_copies = []
     for k in range(peers // 2):
-        pltpu.make_async_copy(sums.at[0, k], keep_ref.at[k], out_sems.at[0, k]).wait()
-        pltpu.make_async_copy(narrow.at[1, k], give_refs[k // 2].at[k % 2], out_sems.at[1, k]).wait()
-    wait_windows(cols, out_cols, cols_sems, bricks)
-
-
-GROUP = 3 * C
-
-
-def start_stream(cols_ref, first, cols, weight_ref, weight, sems):
-    copies = []
-    planes = cols.shape[0]
-    for g in range(3):
-        lanes = pl.ds(g * GROUP, GROUP)
-        group = [
-            pltpu.make_async_copy(
-                cols_ref.at[pl.ds(first, planes), :, lanes], cols.at[:, :, lanes], sems.at[g, 3]
-            )
-        ]
+        give_ref = give_refs[k // 2].at[k % 2]
+        out_copies.append(pltpu.make_async_copy(narrow.at[1, k], give_ref, out_sems.at[1, k]))
+    for k in range(peers // 2):
+        out_copies.append(pltpu.make_async_copy(sums.at[0, k], keep_ref.at[k], out_sems.at[0, k]))
+    for copy in out_copies:
+        copy.start()
+    weight_copy.wait()
+    for brick in range(bricks):
+        at = slice(brick * 512, brick * 512 + 512)
+        total = None
         for i in range(3):
-            at = pl.ds((i * 3 + g) * GROUP, GROUP)
-            group.append(pltpu.make_async_copy(weight_ref.at[at], weight.at[at], sems.at[g, i]))
-        copies.append(group)
-    for group in copies:
-        for copy in group:
-            copy.start()
-    return copies
-
-
-def tap_sum(copies, cols, weight):
-    bricks = cols.shape[0] // 10
-    totals = [None] * bricks
-    for g in range(3):
-        for copy in copies[g]:
-            copy.wait()
-        for brick in range(bricks):
-            for i in range(3):
-                at = brick * 10 + i
-                left = cols[at : at + 8, :, g * GROUP : g * GROUP + GROUP].reshape(512, GROUP)
-                right = weight[(i * 3 + g) * GROUP : (i * 3 + g + 1) * GROUP, :]
-                term = jnp.dot(left, right, preferred_element_type=F32)
-                totals[brick] = term if totals[brick] is None else totals[brick] + term
-    return totals
-
-
-def mix_body(cols_ref, weight_ref, x_ref, out_ref, cols, weight, sems):
-    copies = start_stream(cols_ref, 0, cols, weight_ref, weight, sems)
-    for brick, total in enumerate(tap_sum(copies, cols, weight)):
-        at = slice(brick * 512, brick * 512 + 512)
-        out_ref[at, :] = (x_ref[at, :].astype(F32) + total).astype(BF16)
+            left = cols[brick * 10 + i : brick * 10 + i + 8].reshape(512, 9 * C)
+            right = weight[i * 9 * C : (i + 1) * 9 * C, :]
+            term = jnp.dot(left, right, preferred_element_type=F32)
+            total = term if total is None else total + term
+        mix_ref[at, :] = (x_ref[at, :].astype(F32) + total).astype(BF16)
+    for copy in out_copies:
+        copy.wait()
 
 
 def input_grad_body(slots, peers, count, *refs):
@@ -504,7 +488,7 @@
     parts = refs[7 : 7 + count]
     out_ref, cells, halo, cols, share, weight, heads, more, sems, weight_sem = refs[7 + count :]
     bricks = cot_ref.shape[0] // 512
-    me = table[2 * peers]
+    me = table[3 * peers]
     copies = fetch(parts, share, sems)
     weight_copy = pltpu.make_async_copy(weight_ref, weight, weight_sem.at[0])
     weight_copy.start()
@@ -517,8 +501,8 @@
 
     def source_of(k):
         receiver = k // slots
-        at = table[receiver]
-        return at, served[at, me * slots + k - receiver * slots] - 1
+        entry = served[table[receiver], me * slots + k - receiver * slots] - 1
+        return table[peers + receiver], entry
 
     def sort(k, found):
         _, entry = source_of(k)
@@ -633,28 +617,27 @@
     hidden_ring.go(1)
     hidden_ring.go(0, cot_share)
     hidden_ring.go(1)
+    cot_ring = PairGather(cot_share, peers, hidden_ring.last(0))
     hidden_ring.go(0, table)
     hidden_ring.go(1)
-    hidden_ring.go(0)
+    hidden_ring.go(0, cot_ring.last())
     hidden_parts = hidden_ring.places()
-
-    cot_ring = RingGather(cot_share, peers)
-    cot_ring.go(0, hidden_ring.last(1))
-    cot_ring.go(1, hidden_ring.last(0))
+    cot_ring.go(hidden_ring.last(0))
 
     count = len(hidden_parts)
     rows = 27 * channels // peers
     chips = peers // 2
-    keep, *give, cols, _, served = call(
+    weight_scratch = pltpu.VMEM((27 * channels, channels), BF16)
+    keep, *give, mixed, _, served = call(
         functools.partial(weight_grad_body, slots, factor, peers, count),
         (
             sds((chips, rows, channels), F32),
             *[sds((2, rows, channels), BF16)] * (chips // 2),
-            sds(cols_shape(bricks), BF16),
+            sds((per_device, channels), BF16),
             sds((peers, channels), jnp.int32),
             sds((peers, channels), jnp.int32),
         ),
-        [SMEM] * 2 + [VMEM] * 2 + [HBM] * count,
+        [SMEM] * 2 + [VMEM] * 3 + [HBM] * (1 + count),
         padded(bricks)
         + [
             pltpu.VMEM((peers, bricks * ROWS + NOTES, channels), BF16),
@@ -662,49 +645,35 @@
             pltpu.VMEM((2, chips, rows, channels), F32),
             pltpu.VMEM((2, chips, rows, channels), BF16),
             pltpu.VMEM((channels, per_device), BF16),
+            weight_scratch,
             pltpu.SMEM((peers, channels), jnp.int32),
             pltpu.SemaphoreType.DMA((count,)),
-            pltpu.SemaphoreType.DMA((bricks * 10,)),
-            pltpu.SemaphoreType.DMA((1,)),
+            pltpu.SemaphoreType.DMA((2,)),
             pltpu.SemaphoreType.DMA((2, chips)),
             pltpu.SemaphoreType.DMA((count,)),
         ],
-        cost=9,
+        cost=13,
         name="weight_grad",
-        out_specs=(*[HBM] * (2 + chips // 2), VMEM, VMEM),
-    )(recv_slot, table, hidden, cotangent, *hidden_parts)
-
-    first = (cot_ring.last(0), cot_ring.last(1))
-    give = [lax.optimization_barrier((t, first))[0] for t in give]
+        out_specs=(*[HBM] * (1 + chips // 2), VMEM, VMEM, VMEM),
+    )(recv_slot, table, hidden, cotangent, features, conv_weight, *hidden_parts)
+
+    give = [lax.optimization_barrier((t, cot_ring.last()))[0] for t in give]
     sums_ring = RingScatter(keep, give, peers)
+    cot_ring.go(served)
     sums_ring.go()
-    cot_ring.go(0, cols)
-    cot_ring.go(1, cols)
-    second = (cot_ring.last(0), cot_ring.last(1))
-    sent = sums_ring.go(second)
-    mix_cols = lax.optimization_barrier((cols, sent))[0]
-    weight_scratch = pltpu.VMEM((27 * channels, channels), BF16)
-    mixed = call(
-        mix_body,
+    gate = cot_ring.last()
+    cot_ring.go(sums_ring.held[0])
+    sums_ring.go(gate)
+    sent = sums_ring.go(cot_ring.last())
+    cot_ring.go(sent)
+    cot_parts, early = cot_ring.places(served)
+    sent = sums_ring.go(early)
+    served = lax.optimization_barrier((served, sent))[0]
+
+    grad_features = call(
+        functools.partial(input_grad_body, slots, peers, len(cot_parts)),
         sds((per_device, channels), BF16),
-        [HBM, HBM, VMEM],
-        [pltpu.VMEM(cols_shape(bricks), BF16), weight_scratch, pltpu.SemaphoreType.DMA((3, 4))],
-        cost=6,
-        name="mix",
-    )(mix_cols, conv_weight, features)
-    cot_ring.go(0)
-    cot_ring.go(1)
-    third = (cot_ring.last(0), cot_ring.last(1))
-    sent = sums_ring.go((third, mixed))
-    cot_ring.go(0, sent)
-    cot_parts = cot_ring.places(cols)
-    sent = sums_ring.go(tuple(t for k, t in enumerate(cot_parts) if k != peers // 2 + peers // 4))
-    served = lax.optimization_barrier((served, sent))[0]
-
-    grad_features = call(
-        functools.partial(input_grad_body, slots, peers, count),
-        sds((per_device, channels), BF16),
-        [SMEM] * 3 + [VMEM] * 3 + [HBM] * (1 + count),
+        [SMEM] * 3 + [VMEM] * 3 + [HBM] * (1 + len(cot_parts)),
         padded(bricks)
         + [
             pltpu.VMEM(cols_shape(bricks), BF16),
@@ -712,7 +681,7 @@
             weight_scratch,
             pltpu.SMEM((bricks * 26,), jnp.int32),
             pltpu.SMEM((peers * slots,), jnp.int32),
-            pltpu.SemaphoreType.DMA((count,)),
+            pltpu.SemaphoreType.DMA((len(cot_parts),)),
             pltpu.SemaphoreType.DMA((1,)),
         ],
         cost=13,

time: 111 us -> 120 us (1.081)
  waiting for transfers between devices: 32.6 us -> 54.2 us
  starting transfers between devices: 33.7 us -> 24.9 us
  Pallas kernels: 36 us -> 31.2 us
    ppermute x21 -> x18, waiting for transfers between devices: 32.5 us -> 53.2 us  [ring_step(): return lax.ppermute(x, 'morton', pairs)]
    ppermute x21 -> x18, starting transfers between devices: 30.1 us -> 19.7 us  [ring_step(): return lax.ppermute(x, 'morton', pairs)]
    pallas_call x2 -> x1, Pallas kernels: 19.4 us -> 12 us  [local(): call(functools.partial(input_grad_body, slots, peers, len(cot_parts)), sd...]
    pallas_call x1, Pallas kernels: 12 us -> 14.7 us  [local(): call(functools.partial(weight_grad_body, slots, factor, peers, count), (s...]
    ppermute x20 -> x17, starting transfers between devices: 3.64 us -> 5.22 us  [swap_cores(): return lax.ppermute(x, 'morton', [(m, m ^ 1) for m in range(peers)])]
    unnamed x68 -> x55, local copies, waits for them, and re-layouts: 1.65 us -> 2.71 us
  transfers between devices with their start and end apart: 41 -> 35, of which waited for: 11 -> 12; matrix products, arithmetic and copies ran while one was open for 4% -> 4% of each run, Pallas kernels for 30% -> 24%
where the time goes in v12:
time: 120 us; the launch traced here: 119 us
  waiting for transfers between devices  54.2 us (45%)
  Pallas kernels  31.2 us (26%)
  starting transfers between devices  24.9 us (21%)
  local copies, waits for them, and re-layouts  4.04 us (3%)
  other arithmetic  3.66 us (3%)
    ppermute x18, waiting for transfers between devices, ring_step(): return lax.ppermute(x, 'morton', pairs)  53.2 us
    ppermute x18, starting transfers between devices, ring_step(): return lax.ppermute(x, 'morton', pairs)  19.7 us
    pallas_call x1, Pallas kernels, local(): call(functools.partial(weight_grad_body, slots, factor, peers, count), (s...  14.7 us
    pallas_call x1, Pallas kernels, local(): call(functools.partial(input_grad_body, slots, peers, len(cot_parts)), sd...  12 us
    ppermute x17, starting transfers between devices, swap_cores(): return lax.ppermute(x, 'morton', [(m, m ^ 1) for m in range(peers)])  5.22 us
    convert_element_type x4, other arithmetic, go(): part = part.astype(BF16)  2.79 us
    unnamed x55, local copies, waits for them, and re-layouts  2.71 us
    pallas_call x1, Pallas kernels, local(): call(norm_body, (sds((per_device, channels), BF16), sds((bricks * ROWS +...  2.69 us
  transfers between devices with their start and end apart: 35, of which 12 were waited for; matrix products, arithmetic and copies ran while one was open for 4% of the time, Pallas kernels for 24%

profile of v12, /device:TPU:0, one launch (start us, length us, event | category | flops | bytes accessed | tf_op | source)
XLA Modules:
  0.0 119.0 jit_solution(12046830699500993570)
XLA Ops:
  0.6 2.7 %norm.1 = (bf16[1024,256]{1,0:T(8,128)(2,1)}, bf16[656,256]{1,0:T(8,128)(2,1)}) custom-call(s32[2,26]{1,0:T(2,128)} %refs_0_.1, s32[1,64]{1,0:T(1,128)} %refs_1_.1, bf16[1024,256]{1,0:T(8,128)(2,1)} %refs_4_.3, f32[1,256]{1,0:T(1,128)} %bitcast.81), custom_call_target="tpu_custom_call" | custom-call | flops 2000000000 | tf_op jit(solution)/shard_map/norm/pallas_call | solution.py:601
  3.3 3.0 %collective-permute-start.1 = (bf16[656,256]{1,0:T(8,128)(2,1)}, bf16[656,256]{1,0:T(8,128)(2,1)S(1)}, u32[]{:S(2)}, u32[]{:S(2)}) collective-permute-start(bf16[656,256]{1,0:T(8,128)(2,1)} %get-tuple-element.36), channel_id=1, source_target_pairs={{0,4},{1,3},{4,8},{5,1},{8,12},{9,5},{12,14},{13,9},{14,10},{15,13... | collective-permute-start | bytes 1007624 | tf_op jit(solution)/shard_map/ppermute | solution.py:74
  7.0 1.9 %extract.1 = bf16[640,256]{1,0:T(8,128)(2,1)} custom-call(bf16[1024,256]{1,0:T(8,128)(2,1)} %refs_3_.3), custom_call_target="tpu_custom_call" | custom-call | flops 2000000000 | tf_op jit(solution)/shard_map/extract/pallas_call | solution.py:609
  8.9 5.0 %collective-permute-done.1 = bf16[656,256]{1,0:T(8,128)(2,1)S(1)} collective-permute-done((bf16[656,256]{1,0:T(8,128)(2,1)}, bf16[656,256]{1,0:T(8,128)(2,1)S(1)}, u32[]{:S(2)}, u32[]{:S(2)}) %collective-permute-start.1) | collective-permute-done | bytes 335904 | tf_op jit(solution)/shard_map/ppermute | solution.py:74
  13.9 2.4 %collective-permute-start.2 = (bf16[656,256]{1,0:T(8,128)(2,1)S(1)}, bf16[656,256]{1,0:T(8,128)(2,1)S(1)}, u32[]{:S(2)}, u32[]{:S(2)}) collective-permute-start(bf16[656,256]{1,0:T(8,128)(2,1)S(1)} %collective-permute-done.1), channel_id=1, source_target_pairs={{0,4},{1,3},{4,8},{5,1},{8,12},{9,5},{12,14},{13,9},{14,10},{15,13... | collective-permute-start | bytes 1007624 | tf_op jit(solution)/shard_map/ppermute | solution.py:74
  16.3 1.6 %collective-permute-start.7 = (bf16[656,256]{1,0:T(8,128)(2,1)S(1)}, bf16[656,256]{1,0:T(8,128)(2,1)S(1)}, u32[]{:S(2)}, u32[]{:S(2)}) collective-permute-start(bf16[656,256]{1,0:T(8,128)(2,1)S(1)} %collective-permute-done.6), channel_id=1, source_target_pairs={{0,4},{1,3},{4,8},{5,1},{8,12},{9,5},{12,14},{13,9},{14,10},{15,13... | collective-permute-start | bytes 1007624 | tf_op jit(solution)/shard_map/ppermute | solution.py:74
  17.9 4.5 %collective-permute-done.2 = bf16[656,256]{1,0:T(8,128)(2,1)S(1)} collective-permute-done((bf16[656,256]{1,0:T(8,128)(2,1)S(1)}, bf16[656,256]{1,0:T(8,128)(2,1)S(1)}, u32[]{:S(2)}, u32[]{:S(2)}) %collective-permute-start.2) | collective-permute-done | bytes 335904 | tf_op jit(solution)/shard_map/ppermute | solution.py:74
  22.4 1.3 %dynamic-slice_bitcast_fusion.refs_1_.refs_2_ = s32[49]{0:T(128)} fusion(s32[16,49]{1,0:T(8,128)} %constant.10.clone, s32[]{:T(128)S(6)} %select_n.3), kind=kLoop, calls=%fused_computation.18 | loop fusion | bytes 396 | tf_op jit(solution)/shard_map/squeeze | solution.py:599
  23.7 1.1 collective-permute-start.3
  24.8 1.1 collective-permute-start
  28.1 2.8 %collective-permute-done.3 = bf16[656,256]{1,0:T(8,128)(2,1)S(1)} collective-permute-done((bf16[656,256]{1,0:T(8,128)(2,1)S(1)}, bf16[656,256]{1,0:T(8,128)(2,1)S(1)}, u32[]{:S(2)}, u32[]{:S(2)}) %collective-permute-start.3) | collective-permute-done | bytes 335904 | tf_op jit(solution)/shard_map/ppermute | solution.py:74
  32.7 1.9 %collective-permute-done.8 = bf16[656,256]{1,0:T(8,128)(2,1)S(1)} collective-permute-done((bf16[656,256]{1,0:T(8,128)(2,1)S(1)}, bf16[656,256]{1,0:T(8,128)(2,1)S(1)}, u32[]{:S(2)}, u32[]{:S(2)}) %collective-permute-start.8) | collective-permute-done | bytes 335904 | tf_op jit(solution)/shard_map/ppermute | solution.py:74
  34.7 3.6 %collective-permute-done.5 = bf16[656,256]{1,0:T(8,128)(2,1)S(1)} collective-permute-done((bf16[656,256]{1,0:T(8,128)(2,1)S(1)}, bf16[656,256]{1,0:T(8,128)(2,1)S(1)}, u32[]{:S(2)}, u32[]{:S(2)}) %collective-permute-start.5) | collective-permute-done | bytes 335904 | tf_op jit(solution)/shard_map/ppermute | solution.py:74
  40.7 14.7 %weight_grad.1 = (f32[8,432,256]{2,1,0:T(8,128)}, bf16[2,432,256]{2,1,0:T(8,128)(2,1)}, bf16[2,432,256]{2,1,0:T(8,128)(2,1)}, bf16[2,432,256]{2,1,0:T(8,128)(2,1...) custom-call(s32[2,26]{1,0:T(2,128)} %refs_0_.1, ...), custom_call_target="tpu_custom_call" | custom-call | flops 12999999488 | tf_op jit(solution)/shard_map/weight_grad/pallas_call | solution.py:631
  57.8 1.2 %fusion.7 = (bf16[432,256]{1,0:T(8,128)(2,1)S(1)}, bf16[432,256]{1,0:T(8,128)(2,1)S(1)}) fusion(f32[8,432,256]{2,1,0:T(8,128)} %get-tuple-element.43, bf16[2,432,256]{2,1,0:T(8,128)(2,1)S(1)} %collective-permute-done.20), kind=kLoop, calls=%fused_computation.15 | loop fusion | flops 663552 | bytes 1769472 | tf_op jit(solution)/shard_map/convert_element_type | solution.py:167
  61.2 8.0 %collective-permute-done.22 = bf16[1280,256]{1,0:T(8,128)(2,1)S(1)} collective-permute-done((bf16[1280,256]{1,0:T(8,128)(2,1)S(1)}, bf16[1280,256]{1,0:T(8,128)(2,1)S(1)}, u32[]{:S(2)}, u32[]{:S(2)}) %collective-permute-start.22) | collective-permute-done | bytes 655392 | tf_op jit(solution)/shard_map/ppermute | solution.py:74
  69.2 2.4 %collective-permute-done.21 = bf16[432,256]{1,0:T(8,128)(2,1)S(1)} collective-permute-done((bf16[432,256]{1,0:T(8,128)(2,1)S(1)}, bf16[432,256]{1,0:T(8,128)(2,1)S(1)}, u32[]{:S(2)}, u32[]{:S(2)}) %collective-permute-start.21) | collective-permute-done | bytes 221216 | tf_op jit(solution)/shard_map/ppermute | solution.py:74
  72.1 1.3 %fusion.1 = (bf16[432,256]{1,0:T(8,128)(2,1)S(1)}, bf16[432,256]{1,0:T(8,128)(2,1)S(1)}) fusion(bf16[432,256]{1,0:T(8,128)(2,1)S(1)} %collective-permute-done.29, f32[8,432,256]{2,1,0:T(8,128)} %get-tuple-element.43, bf16[2,432,256]{2,1,0:T(8,128)(2,1)S(1)} %collective-permute-done.19, bf16[432,256]{1,0:T(8,128)(2,1)S(1)} %collective-permute-done.21), kind=kLoop, calls=%fused_computation.3 | loop fusion | flops 1105920 | bytes 2211840 | tf_op jit(solution)/shard_map/convert_element_type | solution.py:167
  73.4 2.1 %collective-permute-start.23 = (bf16[432,256]{1,0:T(8,128)(2,1)S(1)}, bf16[432,256]{1,0:T(8,128)(2,1)S(1)}, u32[]{:S(2)}, u32[]{:S(2)}) collective-permute-start(bf16[432,256]{1,0:T(8,128)(2,1)S(1)} %get-tuple-element.54), channel_id=1, source_target_pairs={{0,4},{1,5},{4,8},{5,9},{8,12},{9,13},{12,14},{13,15},{14,10},{15,... | collective-permute-start | bytes 663560 | tf_op jit(solution)/shard_map/ppermute | solution.py:74
  75.5 11.0 %collective-permute-done.23 = bf16[432,256]{1,0:T(8,128)(2,1)S(1)} collective-permute-done((bf16[432,256]{1,0:T(8,128)(2,1)S(1)}, bf16[432,256]{1,0:T(8,128)(2,1)S(1)}, u32[]{:S(2)}, u32[]{:S(2)}) %collective-permute-start.23) | collective-permute-done | bytes 221216 | tf_op jit(solution)/shard_map/ppermute | solution.py:74
  88.7 7.4 %collective-permute-done.31 = bf16[640,256]{1,0:T(8,128)(2,1)S(1)} collective-permute-done((bf16[640,256]{1,0:T(8,128)(2,1)S(1)}, bf16[640,256]{1,0:T(8,128)(2,1)S(1)}, u32[]{:S(2)}, u32[]{:S(2)}) %collective-permute-start.31) | collective-permute-done | bytes 327712 | tf_op jit(solution)/shard_map/ppermute | solution.py:74
  96.2 6.7 %collective-permute-done.25 = bf16[432,256]{1,0:T(8,128)(2,1)S(1)} collective-permute-done((bf16[432,256]{1,0:T(8,128)(2,1)S(1)}, bf16[432,256]{1,0:T(8,128)(2,1)S(1)}, u32[]{:S(2)}, u32[]{:S(2)}) %collective-permute-start.25) | collective-permute-done | bytes 221216 | tf_op jit(solution)/shard_map/ppermute | solution.py:74
  102.9 1.4 %collective-permute-start.34 = (bf16[432,256]{1,0:T(8,128)(2,1)S(1)}, bf16[432,256]{1,0:T(8,128)(2,1)S(1)}, u32[]{:S(2)}, u32[]{:S(2)}) collective-permute-start(bf16[432,256]{1,0:T(8,128)(2,1)S(1)} %get-tuple-element.62), channel_id=1, source_target_pairs={{0,2},{1,3},{4,0},{5,1},{8,4},{9,5},{12,8},{13,9},{14,12},{15,13},... | collective-permute-start | bytes 663560 | tf_op jit(solution)/shard_map/ppermute | solution.py:74
  106.1 12.0 %input_grad.1 = bf16[1024,256]{1,0:T(8,128)(2,1)} custom-call(s32[16,256]{1,0:T(8,128)} %get-tuple-element.60.refs_0_, s32[1,64]{1,0:T(1,128)} %refs_1_.1, s32[49]{0:T(128)} %dynamic-slice_bitcast_fusion.refs_1_.refs_2_, bf16[1024,256]{1,0:T(8,128)(2,1)} %refs_3_.3, bf16[1024,256]{1,0:T(8,128)(2,1)} %refs_4_.3, f32[1,256]{1,0:T(1,128)} %bitcast.82, ...), custom_call_target="tpu_custom_call" | custom-call | flops 12999999488 | tf_op jit(solution)/shard_map/input_grad/pallas_call | solution.py:673
  (113 shorter events, 17.0 us)
Async XLA Ops:
  3.3 10.6 %collective-permute-start.1 = (bf16[656,256]{1,0:T(8,128)(2,1)}, bf16[656,256]{1,0:T(8,128)(2,1)S(1)}, u32[]{:S(2)}, u32[]{:S(2)}) collective-permute-start(bf16[656,256]{1,0:T(8,128)(2,1)} %get-tuple-element.36), channel_id=1, source_target_pairs={{0,4},{1,3},{4,8},{5,1},{8,12},{9,5},{12,14},{13,9},{14,10},{15,13... | collective-permute-start | bytes 1007624 | tf_op jit(solution)/shard_map/ppermute | solution.py:74
  6.3 10.0 %collective-permute-start.6 = (bf16[656,256]{1,0:T(8,128)(2,1)}, bf16[656,256]{1,0:T(8,128)(2,1)S(1)}, u32[]{:S(2)}, u32[]{:S(2)}) collective-permute-start(bf16[656,256]{1,0:T(8,128)(2,1)} %get-tuple-element.36), channel_id=1, source_target_pairs={{1,4},{0,3},{5,8},{4,1},{9,12},{8,5},{13,14},{12,9},{15,10},{14,13... | collective-permute-start | bytes 1007624 | tf_op jit(solution)/shard_map/ppermute | solution.py:74
  13.9 8.4 %collective-permute-start.2 = (bf16[656,256]{1,0:T(8,128)(2,1)S(1)}, bf16[656,256]{1,0:T(8,128)(2,1)S(1)}, u32[]{:S(2)}, u32[]{:S(2)}) collective-permute-start(bf16[656,256]{1,0:T(8,128)(2,1)S(1)} %collective-permute-done.1), channel_id=1, source_target_pairs={{0,4},{1,3},{4,8},{5,1},{8,12},{9,5},{12,14},{13,9},{14,10},{15,13... | collective-permute-start | bytes 1007624 | tf_op jit(solution)/shard_map/ppermute | solution.py:74
  16.3 10.6 %collective-permute-start.7 = (bf16[656,256]{1,0:T(8,128)(2,1)S(1)}, bf16[656,256]{1,0:T(8,128)(2,1)S(1)}, u32[]{:S(2)}, u32[]{:S(2)}) collective-permute-start(bf16[656,256]{1,0:T(8,128)(2,1)S(1)} %collective-permute-done.6), channel_id=1, source_target_pairs={{0,4},{1,3},{4,8},{5,1},{8,12},{9,5},{12,14},{13,9},{14,10},{15,13... | collective-permute-start | bytes 1007624 | tf_op jit(solution)/shard_map/ppermute | solution.py:74
  24.8 7.2 %collective-permute-start = (bf16[656,256]{1,0:T(8,128)(2,1)S(1)}, bf16[656,256]{1,0:T(8,128)(2,1)S(1)}, u32[]{:S(2)}, u32[]{:S(2)}) collective-permute-start(bf16[656,256]{1,0:T(8,128)(2,1)S(1)} %copy-done.9), channel_id=1, source_target_pairs={{0,1},{1,0},{2,3},{3,2},{4,5},{5,4},{6,7},{7,6},{8,9},{9,8},{10,11... | collective-permute-start | bytes 1007624 | tf_op jit(solution)/shard_map/ppermute | solution.py:78
  27.5 7.2 %collective-permute-start.8 = (bf16[656,256]{1,0:T(8,128)(2,1)S(1)}, bf16[656,256]{1,0:T(8,128)(2,1)S(1)}, u32[]{:S(2)}, u32[]{:S(2)}) collective-permute-start(bf16[656,256]{1,0:T(8,128)(2,1)S(1)} %collective-permute-done.7), channel_id=1, source_target_pairs={{0,4},{1,3},{4,8},{5,1},{8,12},{9,5},{12,14},{13,9},{14,10},{15,13... | collective-permute-start | bytes 1007624 | tf_op jit(solution)/shard_map/ppermute | solution.py:74
  30.8 7.4 %collective-permute-start.5 = (bf16[656,256]{1,0:T(8,128)(2,1)S(1)}, bf16[656,256]{1,0:T(8,128)(2,1)S(1)}, u32[]{:S(2)}, u32[]{:S(2)}) collective-permute-start(bf16[656,256]{1,0:T(8,128)(2,1)S(1)} %collective-permute-done.3), channel_id=1, source_target_pairs={{0,4},{1,3},{4,8},{5,1},{8,12},{9,5},{12,14},{13,9},{14,10},{15,13... | collective-permute-start | bytes 1007624 | tf_op jit(solution)/shard_map/ppermute | solution.py:74
  38.3 17.1 %collective-permute-start.16 = (bf16[1280,256]{1,0:T(8,128)(2,1)S(1)}, bf16[1280,256]{1,0:T(8,128)(2,1)S(1)}, u32[]{:S(2)}, u32[]{:S(2)}) collective-permute-start(bf16[1280,256]{1,0:T(8,128)(2,1)S(1)} %constant_dynamic-update-slice_fusion), channel_id=1, source_target_pairs={{0,4},{1,3},{4,8},{5,1},{8,12},{9,5},{12,14},{13,9},{14,10},{15,13... | collective-permute-start | bytes 1966088 | tf_op jit(solution)/shard_map/ppermute | solution.py:74
  56.2 13.0 %collective-permute-start.22 = (bf16[1280,256]{1,0:T(8,128)(2,1)S(1)}, bf16[1280,256]{1,0:T(8,128)(2,1)S(1)}, u32[]{:S(2)}, u32[]{:S(2)}) collective-permute-start(bf16[1280,256]{1,0:T(8,128)(2,1)S(1)} %collective-permute-done.16), channel_id=1, source_target_pairs={{0,4},{1,3},{4,8},{5,1},{8,12},{9,5},{12,14},{13,9},{14,10},{15,13... | collective-permute-start | bytes 1966088 | tf_op jit(solution)/shard_map/ppermute | solution.py:74
  56.8 15.3 %collective-permute-start.19 = (bf16[2,432,256]{2,1,0:T(8,128)(2,1)}, bf16[2,432,256]{2,1,0:T(8,128)(2,1)S(1)}, u32[]{:S(2)}, u32[]{:S(2)}) collective-permute-start(bf16[2,432,256]{2,1,0:T(8,128)(2,1)} %get-tuple-element.50), channel_id=1, source_target_pairs={{0,1},{1,0},{2,3},{3,2},{4,5},{5,4},{6,7},{7,6},{8,9},{9,8},{10,11... | collective-permute-start | bytes 1327112 | tf_op jit(solution)/shard_map/ppermute | solution.py:78
  59.1 12.4 %collective-permute-start.21 = (bf16[432,256]{1,0:T(8,128)(2,1)S(1)}, bf16[432,256]{1,0:T(8,128)(2,1)S(1)}, u32[]{:S(2)}, u32[]{:S(2)}) collective-permute-start(bf16[432,256]{1,0:T(8,128)(2,1)S(1)} %get-tuple-element.72), channel_id=1, source_target_pairs={{0,4},{1,5},{4,8},{5,9},{8,12},{9,13},{12,14},{13,15},{14,10},{15,... | collective-permute-start | bytes 663560 | tf_op jit(solution)/shard_map/ppermute | solution.py:74
  60.1 12.0 %collective-permute-start.29 = (bf16[432,256]{1,0:T(8,128)(2,1)S(1)}, bf16[432,256]{1,0:T(8,128)(2,1)S(1)}, u32[]{:S(2)}, u32[]{:S(2)}) collective-permute-start(bf16[432,256]{1,0:T(8,128)(2,1)S(1)} %get-tuple-element.71), channel_id=1, source_target_pairs={{0,2},{1,3},{4,0},{5,1},{8,4},{9,5},{12,8},{13,9},{14,12},{15,13},... | collective-permute-start | bytes 663560 | tf_op jit(solution)/shard_map/ppermute | solution.py:74
  61.2 14.3 %collective-permute-start.18 = (bf16[2,432,256]{2,1,0:T(8,128)(2,1)}, bf16[2,432,256]{2,1,0:T(8,128)(2,1)S(1)}, u32[]{:S(2)}, u32[]{:S(2)}) collective-permute-start(bf16[2,432,256]{2,1,0:T(8,128)(2,1)} %get-tuple-element.48), channel_id=1, source_target_pairs={{0,1},{1,0},{2,3},{3,2},{4,5},{5,4},{6,7},{7,6},{8,9},{9,8},{10,11... | collective-permute-start | bytes 1327112 | tf_op jit(solution)/shard_map/ppermute | solution.py:78
  71.5 15.1 %collective-permute-start.24 = (bf16[1280,256]{1,0:T(8,128)(2,1)S(1)}, bf16[1280,256]{1,0:T(8,128)(2,1)S(1)}, u32[]{:S(2)}, u32[]{:S(2)}) collective-permute-start(bf16[1280,256]{1,0:T(8,128)(2,1)S(1)} %collective-permute-done.22), channel_id=1, source_target_pairs={{0,4},{1,3},{4,8},{5,1},{8,12},{9,5},{12,14},{13,9},{14,10},{15,13... | collective-permute-start | bytes 1966088 | tf_op jit(solution)/shard_map/ppermute | solution.py:74
  73.4 13.1 %collective-permute-start.23 = (bf16[432,256]{1,0:T(8,128)(2,1)S(1)}, bf16[432,256]{1,0:T(8,128)(2,1)S(1)}, u32[]{:S(2)}, u32[]{:S(2)}) collective-permute-start(bf16[432,256]{1,0:T(8,128)(2,1)S(1)} %get-tuple-element.54), channel_id=1, source_target_pairs={{0,4},{1,5},{4,8},{5,9},{8,12},{9,13},{12,14},{13,15},{14,10},{15,... | collective-permute-start | bytes 663560 | tf_op jit(solution)/shard_map/ppermute | solution.py:74
  75.5 11.0 %collective-permute-start.30 = (bf16[432,256]{1,0:T(8,128)(2,1)S(1)}, bf16[432,256]{1,0:T(8,128)(2,1)S(1)}, u32[]{:S(2)}, u32[]{:S(2)}) collective-permute-start(bf16[432,256]{1,0:T(8,128)(2,1)S(1)} %get-tuple-element.61), channel_id=1, source_target_pairs={{0,2},{1,3},{4,0},{5,1},{8,4},{9,5},{12,8},{13,9},{14,12},{15,13},... | collective-permute-start | bytes 663560 | tf_op jit(solution)/shard_map/ppermute | solution.py:74
  86.7 9.4 %collective-permute-start.31 = (bf16[640,256]{1,0:T(8,128)(2,1)S(1)}, bf16[640,256]{1,0:T(8,128)(2,1)S(1)}, u32[]{:S(2)}, u32[]{:S(2)}) collective-permute-start(bf16[640,256]{1,0:T(8,128)(2,1)S(1)} %slice.72), channel_id=1, source_target_pairs={{0,4},{1,3},{4,8},{5,1},{8,12},{9,5},{12,14},{13,9},{14,10},{15,13... | collective-permute-start | bytes 983048 | tf_op jit(solution)/shard_map/ppermute | solution.py:74
  87.7 8.4 %collective-permute-start.17 = (bf16[2,432,256]{2,1,0:T(8,128)(2,1)S(1)}, bf16[2,432,256]{2,1,0:T(8,128)(2,1)S(1)}, u32[]{:S(2)}, u32[]{:S(2)}) collective-permute-start(bf16[2,432,256]{2,1,0:T(8,128)(2,1)S(1)} %copy-done.8), channel_id=1, source_target_pairs={{0,1},{1,0},{2,3},{3,2},{4,5},{5,4},{6,7},{7,6},{8,9},{9,8},{10,11... | collective-permute-start | bytes 1327112 | tf_op jit(solution)/shard_map/ppermute | solution.py:78
  87.7 16.7 %collective-permute-start.26 = (bf16[1280,256]{1,0:T(8,128)(2,1)S(1)}, bf16[1280,256]{1,0:T(8,128)(2,1)S(1)}, u32[]{:S(2)}, u32[]{:S(2)}) collective-permute-start(bf16[1280,256]{1,0:T(8,128)(2,1)S(1)} %collective-permute-done.16), channel_id=1, source_target_pairs={{0,1},{1,0},{2,3},{3,2},{4,5},{5,4},{6,7},{7,6},{8,9},{9,8},{10,11... | collective-permute-start | bytes 1966088 | tf_op jit(solution)/shard_map/ppermute | solution.py:78
  88.2 16.2 %collective-permute-start.27 = (bf16[1280,256]{1,0:T(8,128)(2,1)S(1)}, bf16[1280,256]{1,0:T(8,128)(2,1)S(1)}, u32[]{:S(2)}, u32[]{:S(2)}) collective-permute-start(bf16[1280,256]{1,0:T(8,128)(2,1)S(1)} %collective-permute-done.22), channel_id=1, source_target_pairs={{0,1},{1,0},{2,3},{3,2},{4,5},{5,4},{6,7},{7,6},{8,9},{9,8},{10,11... | collective-permute-start | bytes 1966088 | tf_op jit(solution)/shard_map/ppermute | solution.py:78
  88.2 16.2 %collective-permute-start.28 = (bf16[1280,256]{1,0:T(8,128)(2,1)S(1)}, bf16[1280,256]{1,0:T(8,128)(2,1)S(1)}, u32[]{:S(2)}, u32[]{:S(2)}) collective-permute-start(bf16[1280,256]{1,0:T(8,128)(2,1)S(1)} %collective-permute-done.24), channel_id=1, source_target_pairs={{0,1},{1,0},{2,3},{3,2},{4,5},{5,4},{6,7},{7,6},{8,9},{9,8},{10,11... | collective-permute-start | bytes 1966088 | tf_op jit(solution)/shard_map/ppermute | solution.py:78
  96.1 9.2 %collective-permute-start.32 = (bf16[640,256]{1,0:T(8,128)(2,1)S(1)}, bf16[640,256]{1,0:T(8,128)(2,1)S(1)}, u32[]{:S(2)}, u32[]{:S(2)}) collective-permute-start(bf16[640,256]{1,0:T(8,128)(2,1)S(1)} %collective-permute-done.31), channel_id=1, source_target_pairs={{0,1},{1,0},{2,3},{3,2},{4,5},{5,4},{6,7},{7,6},{8,9},{9,8},{10,11... | collective-permute-start | bytes 983048 | tf_op jit(solution)/shard_map/ppermute | solution.py:78
  102.9 15.2 %collective-permute-start.34 = (bf16[432,256]{1,0:T(8,128)(2,1)S(1)}, bf16[432,256]{1,0:T(8,128)(2,1)S(1)}, u32[]{:S(2)}, u32[]{:S(2)}) collective-permute-start(bf16[432,256]{1,0:T(8,128)(2,1)S(1)} %get-tuple-element.62), channel_id=1, source_target_pairs={{0,2},{1,3},{4,0},{5,1},{8,4},{9,5},{12,8},{13,9},{14,12},{15,13},... | collective-permute-start | bytes 663560 | tf_op jit(solution)/shard_map/ppermute | solution.py:74
  104.4 13.7 %collective-permute-start.33 = (bf16[432,256]{1,0:T(8,128)(2,1)S(1)}, bf16[432,256]{1,0:T(8,128)(2,1)S(1)}, u32[]{:S(2)}, u32[]{:S(2)}) collective-permute-start(bf16[432,256]{1,0:T(8,128)(2,1)S(1)} %fusion.5), channel_id=1, source_target_pairs={{0,4},{1,5},{4,8},{5,9},{8,12},{9,13},{12,14},{13,15},{14,10},{15,... | collective-permute-start | bytes 663560 | tf_op jit(solution)/shard_map/ppermute | solution.py:74
  (38 other events, 415.9 us)

commit v13 on v12

--- a/solution.py
+++ b/solution.py
@@ -45,23 +45,20 @@
     behind = (spot[device // 2][:, None] - spot[None, :]) % chips
     half = chips // 2
     turn = np.where(behind >= half, 2 * (behind - half), 2 * (half - 1 - behind) + 1)
-    places = np.broadcast_to(device, (2, peers, peers)).copy()
+    place_of = np.broadcast_to(device, (peers, peers)).copy()
     if chips <= 8:
         for me in range(peers):
             for other in range(peers):
                 away = behind[me, other // 2] if me % 2 == 0 else -behind[me, other // 2] % chips
                 same = me % 2 == other % 2
                 if away == 0:
-                    place = (0, 0) if same else (1, 1)
+                    place = 0 if same else 1
                 elif away < half or (away == half and same):
-                    place = (1 + away, 2 * away) if same else (1 + half + away, 2 * away + 1)
+                    place = 1 + away if same else 1 + half + away
                 else:
-                    away = chips - away
-                    place = (2 * half + away, 2 * half + 2 * away - 1)
-                    if same:
-                        place = (3 * half + away, 2 * half + 2 * away)
-                places[:, me, other] = place
-    return np.concatenate([*places, behind, turn, device[:, None]], axis=1).astype(np.int32)
+                    place = 3 * half + chips - away if same else 2 * half + chips - away
+                place_of[me, other] = place
+    return np.concatenate([place_of, behind, turn, device[:, None]], axis=1).astype(np.int32)
 
 
 def ring_step(x, peers, step, cross=0):
@@ -82,6 +79,7 @@
     def __init__(self, x, peers):
         self.x, self.peers, self.chips = x, peers, peers // 2
         self.whole = None
+        self.swaps = {}
         if self.chips > 8:
             self.whole = lax.all_gather(x[None], "morton", axis=0, tiled=True)
             return
@@ -99,48 +97,20 @@
     def last(self, chain):
         return self.x if self.whole is not None else self.chains[chain][-1]
 
-    def places(self, gate=None):
+    def swap(self, chain, hop, gate=None):
+        if self.whole is None and (chain, hop) not in self.swaps:
+            held = self.chains[chain][hop]
+            if gate is not None:
+                held = lax.optimization_barrier((held, gate))[0]
+            self.swaps[chain, hop] = swap_cores(held, self.peers)
+        return self.swaps.get((chain, hop), self.x)
+
+    def places(self):
         if self.whole is not None:
             return [self.whole]
-        mine = self.chains[0][1:] + self.chains[1][1:]
-        held = mine
-        if gate is not None:
-            held = [lax.optimization_barrier((t, gate))[0] for t in mine]
-        others = [swap_cores(t, self.peers) for t in [self.x] + held]
-        return [t[None] for t in [self.x] + others[:1] + mine + others[1:]]
-
-
-class PairGather:
-    def __init__(self, x, peers, gate):
-        self.peers, self.chips = peers, peers // 2
-        self.whole = None
-        if self.chips > 8:
-            self.whole = lax.all_gather(x[None], "morton", axis=0, tiled=True)
-            return
-        self.rows = x.shape[0]
-        x = lax.optimization_barrier((x, gate))[0]
-        self.hops = [jnp.concatenate([x, swap_cores(x, peers)], axis=0)]
-
-    def go(self, gate=None):
-        if self.whole is not None:
-            return
-        held = self.hops[-1]
-        if len(self.hops) == self.chips // 2:
-            held = held[: self.rows]
-        if gate is not None:
-            held = lax.optimization_barrier((held, gate))[0]
-        self.hops.append(ring_step(held, self.peers, 0))
-
-    def last(self):
-        return self.whole if self.whole is not None else self.hops[-1]
-
-    def places(self, gate):
-        if self.whole is not None:
-            return [self.whole], [self.whole]
-        held = [lax.optimization_barrier((t, gate))[0] for t in self.hops[1:]]
-        got = self.hops + [swap_cores(t, self.peers) for t in held]
-        got = [t.reshape(-1, self.rows, t.shape[1]) for t in got]
-        return got, got[: self.chips // 2] + got[self.chips // 2 + 1 : -1]
+        keys = [(c, h) for c in (0, 1) for h in range(1, len(self.chains[c]))]
+        mine = [self.x, self.swap(0, 0)] + [self.chains[c][h] for c, h in keys]
+        return [t[None] for t in mine + [self.swap(c, h) for c, h in keys]]
 
 
 class RingScatter:
@@ -407,7 +377,7 @@
     cells, halo, share, cols, sums, narrow, turned, weight, codes = refs[-13:-4]
     sems, codes_sem, out_sems, notes_sems = refs[-4:]
     bricks = own_ref.shape[0] // 512
-    me = table[3 * peers]
+    me = table[2 * peers]
     notes_copies = fetch(parts, share, notes_sems, bricks * ROWS, NOTES)
     copies = fetch(parts, share, sems, 0, bricks * ROWS)
     weight_copy = pltpu.make_async_copy(weight_ref, weight, codes_sem.at[1])
@@ -454,10 +424,10 @@
             stop = min((tap + 1) * C, (owner + 1) * rows)
             piece = total[start - tap * C : stop - tap * C]
             bucket = jnp.bitwise_xor(me % 2, owner % 2)
-            behind = table[2 * peers + owner // 2]
+            behind = table[peers + owner // 2]
             where = slice(start - owner * rows, stop - owner * rows)
             sums[bucket, behind, where, :] = piece
-            turn = table[2 * peers + peers // 2 + owner // 2]
+            turn = table[peers + peers // 2 + owner // 2]
             narrow[bucket, turn, where, :] = piece.astype(BF16)
             start = stop
 
@@ -488,7 +458,7 @@
     parts = refs[7 : 7 + count]
     out_ref, cells, halo, cols, share, weight, heads, more, sems, weight_sem = refs[7 + count :]
     bricks = cot_ref.shape[0] // 512
-    me = table[3 * peers]
+    me = table[2 * peers]
     copies = fetch(parts, share, sems)
     weight_copy = pltpu.make_async_copy(weight_ref, weight, weight_sem.at[0])
     weight_copy.start()
@@ -501,8 +471,8 @@
 
     def source_of(k):
         receiver = k // slots
-        entry = served[table[receiver], me * slots + k - receiver * slots] - 1
-        return table[peers + receiver], entry
+        at = table[receiver]
+        return at, served[at, me * slots + k - receiver * slots] - 1
 
     def sort(k, found):
         _, entry = source_of(k)
@@ -617,12 +587,13 @@
     hidden_ring.go(1)
     hidden_ring.go(0, cot_share)
     hidden_ring.go(1)
-    cot_ring = PairGather(cot_share, peers, hidden_ring.last(0))
     hidden_ring.go(0, table)
     hidden_ring.go(1)
-    hidden_ring.go(0, cot_ring.last())
+    hidden_ring.go(0)
     hidden_parts = hidden_ring.places()
-    cot_ring.go(hidden_ring.last(0))
+    cot_ring = RingGather(cot_share, peers)
+    cot_ring.go(0, hidden_ring.last(1))
+    cot_ring.go(1, hidden_ring.last(0))
 
     count = len(hidden_parts)
     rows = 27 * channels // peers
@@ -657,17 +628,22 @@
         out_specs=(*[HBM] * (1 + chips // 2), VMEM, VMEM, VMEM),
     )(recv_slot, table, hidden, cotangent, features, conv_weight, *hidden_parts)
 
-    give = [lax.optimization_barrier((t, cot_ring.last()))[0] for t in give]
+    first = (cot_ring.last(0), cot_ring.last(1), cot_ring.swap(0, 0))
+    give = [lax.optimization_barrier((t, first))[0] for t in give]
     sums_ring = RingScatter(keep, give, peers)
-    cot_ring.go(served)
+    cot_ring.go(0, served)
+    cot_ring.go(1, served)
     sums_ring.go()
-    gate = cot_ring.last()
-    cot_ring.go(sums_ring.held[0])
+    gate = (cot_ring.last(0), cot_ring.last(1))
+    cot_ring.go(0)
+    cot_ring.go(1)
     sums_ring.go(gate)
-    sent = sums_ring.go(cot_ring.last())
-    cot_ring.go(sent)
-    cot_parts, early = cot_ring.places(served)
-    sent = sums_ring.go(early)
+    gate = (cot_ring.last(0), cot_ring.last(1), cot_ring.swap(0, 1), cot_ring.swap(1, 1))
+    cot_ring.go(0, cot_ring.last(1))
+    sums_ring.go(gate)
+    cot_ring.swap(0, 4, sums_ring.held[0])
+    sent = sums_ring.go(tuple(cot_ring.swap(chain, hop) for chain in (0, 1) for hop in (2, 3)))
+    cot_parts = cot_ring.places()
     served = lax.optimization_barrier((served, sent))[0]
 
     grad_features = call(

time: 120 us -> 113 us (0.942)
  waiting for transfers between devices: 54.2 us -> 37.9 us
  starting transfers between devices: 24.9 us -> 34.9 us
  local copies, waits for them, and re-layouts: 4.04 us -> 2.84 us
    ppermute x18 -> x21, waiting for transfers between devices: 53.2 us -> 37.8 us  [ring_step(): return lax.ppermute(x, 'morton', pairs)]
    ppermute x18 -> x21, starting transfers between devices: 19.7 us -> 31.4 us  [ring_step(): return lax.ppermute(x, 'morton', pairs)]
    ppermute x17 -> x20, starting transfers between devices: 5.22 us -> 3.45 us  [swap_cores(): return lax.ppermute(x, 'morton', [(m, m ^ 1) for m in range(peers)])]
    unnamed x55 -> x66, local copies, waits for them, and re-layouts: 2.71 us -> 1.55 us
  transfers between devices with their start and end apart: 35 -> 41, of which waited for: 12 -> 13; matrix products, arithmetic and copies ran while one was open for 4% -> 4% of each run, Pallas kernels for 24% -> 26%
where the time goes in v13:
time: 113 us; the launch traced here: 112 us
  waiting for transfers between devices  37.9 us (34%)
  starting transfers between devices  34.9 us (31%)
  Pallas kernels  31.4 us (28%)
  other arithmetic  3.67 us (3%)
  local copies, waits for them, and re-layouts  2.84 us (3%)
    ppermute x21, waiting for transfers between devices, ring_step(): return lax.ppermute(x, 'morton', pairs)  37.8 us
    ppermute x21, starting transfers between devices, ring_step(): return lax.ppermute(x, 'morton', pairs)  31.4 us
    pallas_call x1, Pallas kernels, local(): call(functools.partial(weight_grad_body, slots, factor, peers, count), (s...  14.7 us
    pallas_call x1, Pallas kernels, local(): call(functools.partial(input_grad_body, slots, peers, len(cot_parts)), sd...  12.2 us
    ppermute x20, starting transfers between devices, swap_cores(): return lax.ppermute(x, 'morton', [(m, m ^ 1) for m in range(peers)])  3.45 us
    convert_element_type x4, other arithmetic, go(): part = part.astype(BF16)  2.79 us
    pallas_call x1, Pallas kernels, local(): call(norm_body, (sds((per_device, channels), BF16), sds((bricks * ROWS +...  2.67 us
  transfers between devices with their start and end apart: 41, of which 13 were waited for; matrix products, arithmetic and copies ran while one was open for 4% of the time, Pallas kernels for 26%

profile of v13, /device:TPU:0, one launch (start us, length us, event | category | flops | bytes accessed | tf_op | source)
XLA Modules:
  0.0 111.7 jit_solution(11683821379066134100)
XLA Ops:
  0.6 2.7 %norm.1 = (bf16[1024,256]{1,0:T(8,128)(2,1)}, bf16[656,256]{1,0:T(8,128)(2,1)}) custom-call(s32[2,26]{1,0:T(2,128)} %refs_0_.1, s32[1,64]{1,0:T(1,128)} %refs_1_.1, bf16[1024,256]{1,0:T(8,128)(2,1)} %refs_4_.3, f32[1,256]{1,0:T(1,128)} %bitcast.95), custom_call_target="tpu_custom_call" | custom-call | flops 2000000000 | tf_op jit(solution)/shard_map/norm/pallas_call | solution.py:571
  3.3 3.0 %collective-permute-start.1 = (bf16[656,256]{1,0:T(8,128)(2,1)}, bf16[656,256]{1,0:T(8,128)(2,1)S(1)}, u32[]{:S(2)}, u32[]{:S(2)}) collective-permute-start(bf16[656,256]{1,0:T(8,128)(2,1)} %get-tuple-element.33), channel_id=1, source_target_pairs={{0,4},{1,3},{4,8},{5,1},{8,12},{9,5},{12,14},{13,9},{14,10},{15,13... | collective-permute-start | bytes 1007624 | tf_op jit(solution)/shard_map/ppermute | solution.py:71
  7.0 1.9 %extract.1 = bf16[640,256]{1,0:T(8,128)(2,1)} custom-call(bf16[1024,256]{1,0:T(8,128)(2,1)} %refs_3_.3), custom_call_target="tpu_custom_call" | custom-call | flops 2000000000 | tf_op jit(solution)/shard_map/extract/pallas_call | solution.py:579
  8.9 5.0 %collective-permute-done.1 = bf16[656,256]{1,0:T(8,128)(2,1)S(1)} collective-permute-done((bf16[656,256]{1,0:T(8,128)(2,1)}, bf16[656,256]{1,0:T(8,128)(2,1)S(1)}, u32[]{:S(2)}, u32[]{:S(2)}) %collective-permute-start.1) | collective-permute-done | bytes 335904 | tf_op jit(solution)/shard_map/ppermute | solution.py:71
  13.9 2.4 %collective-permute-start.2 = (bf16[656,256]{1,0:T(8,128)(2,1)S(1)}, bf16[656,256]{1,0:T(8,128)(2,1)S(1)}, u32[]{:S(2)}, u32[]{:S(2)}) collective-permute-start(bf16[656,256]{1,0:T(8,128)(2,1)S(1)} %collective-permute-done.1), channel_id=1, source_target_pairs={{0,4},{1,3},{4,8},{5,1},{8,12},{9,5},{12,14},{13,9},{14,10},{15,13... | collective-permute-start | bytes 1007624 | tf_op jit(solution)/shard_map/ppermute | solution.py:71
  17.6 1.6 %collective-permute-start.6 = (bf16[656,256]{1,0:T(8,128)(2,1)S(1)}, bf16[656,256]{1,0:T(8,128)(2,1)S(1)}, u32[]{:S(2)}, u32[]{:S(2)}) collective-permute-start(bf16[656,256]{1,0:T(8,128)(2,1)S(1)} %collective-permute-done.5), channel_id=1, source_target_pairs={{0,4},{1,3},{4,8},{5,1},{8,12},{9,5},{12,14},{13,9},{14,10},{15,13... | collective-permute-start | bytes 1007624 | tf_op jit(solution)/shard_map/ppermute | solution.py:71
  19.2 3.2 %collective-permute-done.2 = bf16[656,256]{1,0:T(8,128)(2,1)S(1)} collective-permute-done((bf16[656,256]{1,0:T(8,128)(2,1)S(1)}, bf16[656,256]{1,0:T(8,128)(2,1)S(1)}, u32[]{:S(2)}, u32[]{:S(2)}) %collective-permute-start.2) | collective-permute-done | bytes 335904 | tf_op jit(solution)/shard_map/ppermute | solution.py:71
  24.0 2.0 %collective-permute-done.6 = bf16[656,256]{1,0:T(8,128)(2,1)S(1)} collective-permute-done((bf16[656,256]{1,0:T(8,128)(2,1)S(1)}, bf16[656,256]{1,0:T(8,128)(2,1)S(1)}, u32[]{:S(2)}, u32[]{:S(2)}) %collective-permute-start.6) | collective-permute-done | bytes 335904 | tf_op jit(solution)/shard_map/ppermute | solution.py:71
  27.1 2.5 %collective-permute-done.3 = bf16[656,256]{1,0:T(8,128)(2,1)S(1)} collective-permute-done((bf16[656,256]{1,0:T(8,128)(2,1)S(1)}, bf16[656,256]{1,0:T(8,128)(2,1)S(1)}, u32[]{:S(2)}, u32[]{:S(2)}) %collective-permute-start.3) | collective-permute-done | bytes 335904 | tf_op jit(solution)/shard_map/ppermute | solution.py:71
  31.3 1.9 %collective-permute-done.7 = bf16[656,256]{1,0:T(8,128)(2,1)S(1)} collective-permute-done((bf16[656,256]{1,0:T(8,128)(2,1)S(1)}, bf16[656,256]{1,0:T(8,128)(2,1)S(1)}, u32[]{:S(2)}, u32[]{:S(2)}) %collective-permute-start.7) | collective-permute-done | bytes 335904 | tf_op jit(solution)/shard_map/ppermute | solution.py:71
  33.2 3.6 %collective-permute-done.4 = bf16[656,256]{1,0:T(8,128)(2,1)S(1)} collective-permute-done((bf16[656,256]{1,0:T(8,128)(2,1)S(1)}, bf16[656,256]{1,0:T(8,128)(2,1)S(1)}, u32[]{:S(2)}, u32[]{:S(2)}) %collective-permute-start.4) | collective-permute-done | bytes 335904 | tf_op jit(solution)/shard_map/ppermute | solution.py:71
  38.4 1.9 %collective-permute-start.16 = (bf16[640,256]{1,0:T(8,128)(2,1)}, bf16[640,256]{1,0:T(8,128)(2,1)S(1)}, u32[]{:S(2)}, u32[]{:S(2)}) collective-permute-start(bf16[640,256]{1,0:T(8,128)(2,1)} %extract.1), channel_id=1, source_target_pairs={{1,4},{0,3},{5,8},{4,1},{9,12},{8,5},{13,14},{12,9},{15,10},{14,13... | collective-permute-start | bytes 983048 | tf_op jit(solution)/shard_map/ppermute | solution.py:71
  41.1 14.7 %weight_grad.1 = (f32[8,432,256]{2,1,0:T(8,128)}, bf16[2,432,256]{2,1,0:T(8,128)(2,1)}, bf16[2,432,256]{2,1,0:T(8,128)(2,1)}, bf16[2,432,256]{2,1,0:T(8,128)(2,1...) custom-call(s32[2,26]{1,0:T(2,128)} %refs_0_.1, ...), custom_call_target="tpu_custom_call" | custom-call | flops 12999999488 | tf_op jit(solution)/shard_map/weight_grad/pallas_call | solution.py:602
  57.7 2.1 %collective-permute-start.23 = (bf16[640,256]{1,0:T(8,128)(2,1)S(1)}, bf16[640,256]{1,0:T(8,128)(2,1)S(1)}, u32[]{:S(2)}, u32[]{:S(2)}) collective-permute-start(bf16[640,256]{1,0:T(8,128)(2,1)S(1)} %collective-permute-done.15), channel_id=1, source_target_pairs={{0,4},{1,3},{4,8},{5,1},{8,12},{9,5},{12,14},{13,9},{14,10},{15,13... | collective-permute-start | bytes 983048 | tf_op jit(solution)/shard_map/ppermute | solution.py:71
  63.3 5.7 %collective-permute-done.23 = bf16[640,256]{1,0:T(8,128)(2,1)S(1)} collective-permute-done((bf16[640,256]{1,0:T(8,128)(2,1)S(1)}, bf16[640,256]{1,0:T(8,128)(2,1)S(1)}, u32[]{:S(2)}, u32[]{:S(2)}) %collective-permute-start.23) | collective-permute-done | bytes 327712 | tf_op jit(solution)/shard_map/ppermute | solution.py:71
  70.4 2.3 %collective-permute-start.26 = (bf16[640,256]{1,0:T(8,128)(2,1)S(1)}, bf16[640,256]{1,0:T(8,128)(2,1)S(1)}, u32[]{:S(2)}, u32[]{:S(2)}) collective-permute-start(bf16[640,256]{1,0:T(8,128)(2,1)S(1)} %collective-permute-done.23), channel_id=1, source_target_pairs={{0,4},{1,3},{4,8},{5,1},{8,12},{9,5},{12,14},{13,9},{14,10},{15,13... | collective-permute-start | bytes 983048 | tf_op jit(solution)/shard_map/ppermute | solution.py:71
  74.5 1.6 %collective-permute-start.39 = (bf16[432,256]{1,0:T(8,128)(2,1)S(1)}, bf16[432,256]{1,0:T(8,128)(2,1)S(1)}, u32[]{:S(2)}, u32[]{:S(2)}) collective-permute-start(bf16[432,256]{1,0:T(8,128)(2,1)S(1)} %get-tuple-element.57), channel_id=1, source_target_pairs={{0,2},{1,3},{4,0},{5,1},{8,4},{9,5},{12,8},{13,9},{14,12},{15,13},... | collective-permute-start | bytes 663560 | tf_op jit(solution)/shard_map/ppermute | solution.py:71
  77.0 4.9 %collective-permute-done.26 = bf16[640,256]{1,0:T(8,128)(2,1)S(1)} collective-permute-done((bf16[640,256]{1,0:T(8,128)(2,1)S(1)}, bf16[640,256]{1,0:T(8,128)(2,1)S(1)}, u32[]{:S(2)}, u32[]{:S(2)}) %collective-permute-start.26) | collective-permute-done | bytes 327712 | tf_op jit(solution)/shard_map/ppermute | solution.py:71
  82.5 1.8 %collective-permute-done.25 = bf16[432,256]{1,0:T(8,128)(2,1)S(1)} collective-permute-done((bf16[432,256]{1,0:T(8,128)(2,1)S(1)}, bf16[432,256]{1,0:T(8,128)(2,1)S(1)}, u32[]{:S(2)}, u32[]{:S(2)}) %collective-permute-start.25) | collective-permute-done | bytes 221216 | tf_op jit(solution)/shard_map/ppermute | solution.py:71
  85.9 2.5 %collective-permute-start.30 = (bf16[432,256]{1,0:T(8,128)(2,1)S(1)}, bf16[432,256]{1,0:T(8,128)(2,1)S(1)}, u32[]{:S(2)}, u32[]{:S(2)}) collective-permute-start(bf16[432,256]{1,0:T(8,128)(2,1)S(1)} %get-tuple-element.52), channel_id=1, source_target_pairs={{0,4},{1,5},{4,8},{5,9},{8,12},{9,13},{12,14},{13,15},{14,10},{15,... | collective-permute-start | bytes 663560 | tf_op jit(solution)/shard_map/ppermute | solution.py:71
  89.0 3.7 %collective-permute-done.35 = bf16[640,256]{1,0:T(8,128)(2,1)S(1)} collective-permute-done((bf16[640,256]{1,0:T(8,128)(2,1)S(1)}, bf16[640,256]{1,0:T(8,128)(2,1)S(1)}, u32[]{:S(2)}, u32[]{:S(2)}) %collective-permute-start.35) | collective-permute-done | bytes 327712 | tf_op jit(solution)/shard_map/ppermute | solution.py:71
  92.7 2.4 %collective-permute-done.30 = bf16[432,256]{1,0:T(8,128)(2,1)S(1)} collective-permute-done((bf16[432,256]{1,0:T(8,128)(2,1)S(1)}, bf16[432,256]{1,0:T(8,128)(2,1)S(1)}, u32[]{:S(2)}, u32[]{:S(2)}) %collective-permute-start.30) | collective-permute-done | bytes 221216 | tf_op jit(solution)/shard_map/ppermute | solution.py:71
  95.7 1.6 %collective-permute-start.40 = (bf16[432,256]{1,0:T(8,128)(2,1)S(1)}, bf16[432,256]{1,0:T(8,128)(2,1)S(1)}, u32[]{:S(2)}, u32[]{:S(2)}) collective-permute-start(bf16[432,256]{1,0:T(8,128)(2,1)S(1)} %get-tuple-element.58), channel_id=1, source_target_pairs={{0,2},{1,3},{4,0},{5,1},{8,4},{9,5},{12,8},{13,9},{14,12},{15,13},... | collective-permute-start | bytes 663560 | tf_op jit(solution)/shard_map/ppermute | solution.py:71
  98.6 12.2 %input_grad.1 = bf16[1024,256]{1,0:T(8,128)(2,1)} custom-call(s32[16,256]{1,0:T(8,128)} %get-tuple-element.54.refs_0_, s32[1,64]{1,0:T(1,128)} %refs_1_.1, s32[33]{0:T(128)} %dynamic-slice_bitcast_fusion.refs_1_.refs_2_, bf16[1024,256]{1,0:T(8,128)(2,1)} %refs_3_.3, bf16[1024,256]{1,0:T(8,128)(2,1)} %refs_4_.3, f32[1,256]{1,0:T(1,128)} %bitcast.96, ...), custom_call_target="tpu_custom_call" | custom-call | flops 12999999488 | tf_op jit(solution)/shard_map/input_grad/pallas_call | solution.py:649
  (134 shorter events, 23.5 us)
Async XLA Ops:
  3.3 10.6 %collective-permute-start.1 = (bf16[656,256]{1,0:T(8,128)(2,1)}, bf16[656,256]{1,0:T(8,128)(2,1)S(1)}, u32[]{:S(2)}, u32[]{:S(2)}) collective-permute-start(bf16[656,256]{1,0:T(8,128)(2,1)} %get-tuple-element.33), channel_id=1, source_target_pairs={{0,4},{1,3},{4,8},{5,1},{8,12},{9,5},{12,14},{13,9},{14,10},{15,13... | collective-permute-start | bytes 1007624 | tf_op jit(solution)/shard_map/ppermute | solution.py:71
  6.3 11.3 %collective-permute-start.5 = (bf16[656,256]{1,0:T(8,128)(2,1)}, bf16[656,256]{1,0:T(8,128)(2,1)S(1)}, u32[]{:S(2)}, u32[]{:S(2)}) collective-permute-start(bf16[656,256]{1,0:T(8,128)(2,1)} %get-tuple-element.33), channel_id=1, source_target_pairs={{1,4},{0,3},{5,8},{4,1},{9,12},{8,5},{13,14},{12,9},{15,10},{14,13... | collective-permute-start | bytes 1007624 | tf_op jit(solution)/shard_map/ppermute | solution.py:71
  13.9 8.4 %collective-permute-start.2 = (bf16[656,256]{1,0:T(8,128)(2,1)S(1)}, bf16[656,256]{1,0:T(8,128)(2,1)S(1)}, u32[]{:S(2)}, u32[]{:S(2)}) collective-permute-start(bf16[656,256]{1,0:T(8,128)(2,1)S(1)} %collective-permute-done.1), channel_id=1, source_target_pairs={{0,4},{1,3},{4,8},{5,1},{8,12},{9,5},{12,14},{13,9},{14,10},{15,13... | collective-permute-start | bytes 1007624 | tf_op jit(solution)/shard_map/ppermute | solution.py:71
  17.6 8.4 %collective-permute-start.6 = (bf16[656,256]{1,0:T(8,128)(2,1)S(1)}, bf16[656,256]{1,0:T(8,128)(2,1)S(1)}, u32[]{:S(2)}, u32[]{:S(2)}) collective-permute-start(bf16[656,256]{1,0:T(8,128)(2,1)S(1)} %collective-permute-done.5), channel_id=1, source_target_pairs={{0,4},{1,3},{4,8},{5,1},{8,12},{9,5},{12,14},{13,9},{14,10},{15,13... | collective-permute-start | bytes 1007624 | tf_op jit(solution)/shard_map/ppermute | solution.py:71
  36.8 19.1 %collective-permute-start.17 = (bf16[640,256]{1,0:T(8,128)(2,1)}, bf16[640,256]{1,0:T(8,128)(2,1)S(1)}, u32[]{:S(2)}, u32[]{:S(2)}) collective-permute-start(bf16[640,256]{1,0:T(8,128)(2,1)} %extract.1), channel_id=1, source_target_pairs={{0,1},{1,0},{2,3},{3,2},{4,5},{5,4},{6,7},{7,6},{8,9},{9,8},{10,11... | collective-permute-start | bytes 983048 | tf_op jit(solution)/shard_map/ppermute | solution.py:75
  37.3 18.6 %collective-permute-start.15 = (bf16[640,256]{1,0:T(8,128)(2,1)}, bf16[640,256]{1,0:T(8,128)(2,1)S(1)}, u32[]{:S(2)}, u32[]{:S(2)}) collective-permute-start(bf16[640,256]{1,0:T(8,128)(2,1)} %extract.1), channel_id=1, source_target_pairs={{0,4},{1,3},{4,8},{5,1},{8,12},{9,5},{12,14},{13,9},{14,10},{15,13... | collective-permute-start | bytes 983048 | tf_op jit(solution)/shard_map/ppermute | solution.py:71
  38.4 17.5 %collective-permute-start.16 = (bf16[640,256]{1,0:T(8,128)(2,1)}, bf16[640,256]{1,0:T(8,128)(2,1)S(1)}, u32[]{:S(2)}, u32[]{:S(2)}) collective-permute-start(bf16[640,256]{1,0:T(8,128)(2,1)} %extract.1), channel_id=1, source_target_pairs={{1,4},{0,3},{5,8},{4,1},{9,12},{8,5},{13,14},{12,9},{15,10},{14,13... | collective-permute-start | bytes 983048 | tf_op jit(solution)/shard_map/ppermute | solution.py:71
  56.0 7.3 %collective-permute-start.24 = (bf16[640,256]{1,0:T(8,128)(2,1)S(1)}, bf16[640,256]{1,0:T(8,128)(2,1)S(1)}, u32[]{:S(2)}, u32[]{:S(2)}) collective-permute-start(bf16[640,256]{1,0:T(8,128)(2,1)S(1)} %collective-permute-done.16), channel_id=1, source_target_pairs={{0,4},{1,3},{4,8},{5,1},{8,12},{9,5},{12,14},{13,9},{14,10},{15,13... | collective-permute-start | bytes 983048 | tf_op jit(solution)/shard_map/ppermute | solution.py:71
  57.4 13.0 %collective-permute-start.20 = (bf16[2,432,256]{2,1,0:T(8,128)(2,1)}, bf16[2,432,256]{2,1,0:T(8,128)(2,1)S(1)}, u32[]{:S(2)}, u32[]{:S(2)}) collective-permute-start(bf16[2,432,256]{2,1,0:T(8,128)(2,1)} %get-tuple-element.46), channel_id=1, source_target_pairs={{0,1},{1,0},{2,3},{3,2},{4,5},{5,4},{6,7},{7,6},{8,9},{9,8},{10,11... | collective-permute-start | bytes 1327112 | tf_op jit(solution)/shard_map/ppermute | solution.py:75
  57.7 11.3 %collective-permute-start.23 = (bf16[640,256]{1,0:T(8,128)(2,1)S(1)}, bf16[640,256]{1,0:T(8,128)(2,1)S(1)}, u32[]{:S(2)}, u32[]{:S(2)}) collective-permute-start(bf16[640,256]{1,0:T(8,128)(2,1)S(1)} %collective-permute-done.15), channel_id=1, source_target_pairs={{0,4},{1,3},{4,8},{5,1},{8,12},{9,5},{12,14},{13,9},{14,10},{15,13... | collective-permute-start | bytes 983048 | tf_op jit(solution)/shard_map/ppermute | solution.py:71
  61.0 11.7 %collective-permute-start.22 = (bf16[432,256]{1,0:T(8,128)(2,1)S(1)}, bf16[432,256]{1,0:T(8,128)(2,1)S(1)}, u32[]{:S(2)}, u32[]{:S(2)}) collective-permute-start(bf16[432,256]{1,0:T(8,128)(2,1)S(1)} %get-tuple-element.66), channel_id=1, source_target_pairs={{0,4},{1,5},{4,8},{5,9},{8,12},{9,13},{12,14},{13,15},{14,10},{15,... | collective-permute-start | bytes 663560 | tf_op jit(solution)/shard_map/ppermute | solution.py:71
  61.5 11.2 %collective-permute-start.38 = (bf16[432,256]{1,0:T(8,128)(2,1)S(1)}, bf16[432,256]{1,0:T(8,128)(2,1)S(1)}, u32[]{:S(2)}, u32[]{:S(2)}) collective-permute-start(bf16[432,256]{1,0:T(8,128)(2,1)S(1)} %get-tuple-element.65), channel_id=1, source_target_pairs={{0,2},{1,3},{4,0},{5,1},{8,4},{9,5},{12,8},{13,9},{14,12},{15,13},... | collective-permute-start | bytes 663560 | tf_op jit(solution)/shard_map/ppermute | solution.py:71
  63.2 18.7 %collective-permute-start.19 = (bf16[2,432,256]{2,1,0:T(8,128)(2,1)}, bf16[2,432,256]{2,1,0:T(8,128)(2,1)S(1)}, u32[]{:S(2)}, u32[]{:S(2)}) collective-permute-start(bf16[2,432,256]{2,1,0:T(8,128)(2,1)} %get-tuple-element.44), channel_id=1, source_target_pairs={{0,1},{1,0},{2,3},{3,2},{4,5},{5,4},{6,7},{7,6},{8,9},{9,8},{10,11... | collective-permute-start | bytes 1327112 | tf_op jit(solution)/shard_map/ppermute | solution.py:75
  69.0 8.0 %collective-permute-start.27 = (bf16[640,256]{1,0:T(8,128)(2,1)S(1)}, bf16[640,256]{1,0:T(8,128)(2,1)S(1)}, u32[]{:S(2)}, u32[]{:S(2)}) collective-permute-start(bf16[640,256]{1,0:T(8,128)(2,1)S(1)} %collective-permute-done.24), channel_id=1, source_target_pairs={{0,4},{1,3},{4,8},{5,1},{8,12},{9,5},{12,14},{13,9},{14,10},{15,13... | collective-permute-start | bytes 983048 | tf_op jit(solution)/shard_map/ppermute | solution.py:71
  70.4 11.6 %collective-permute-start.26 = (bf16[640,256]{1,0:T(8,128)(2,1)S(1)}, bf16[640,256]{1,0:T(8,128)(2,1)S(1)}, u32[]{:S(2)}, u32[]{:S(2)}) collective-permute-start(bf16[640,256]{1,0:T(8,128)(2,1)S(1)} %collective-permute-done.23), channel_id=1, source_target_pairs={{0,4},{1,3},{4,8},{5,1},{8,12},{9,5},{12,14},{13,9},{14,10},{15,13... | collective-permute-start | bytes 983048 | tf_op jit(solution)/shard_map/ppermute | solution.py:71
  74.0 10.3 %collective-permute-start.25 = (bf16[432,256]{1,0:T(8,128)(2,1)S(1)}, bf16[432,256]{1,0:T(8,128)(2,1)S(1)}, u32[]{:S(2)}, u32[]{:S(2)}) collective-permute-start(bf16[432,256]{1,0:T(8,128)(2,1)S(1)} %get-tuple-element.51), channel_id=1, source_target_pairs={{0,4},{1,5},{4,8},{5,9},{8,12},{9,13},{12,14},{13,15},{14,10},{15,... | collective-permute-start | bytes 663560 | tf_op jit(solution)/shard_map/ppermute | solution.py:71
  74.5 11.2 %collective-permute-start.39 = (bf16[432,256]{1,0:T(8,128)(2,1)S(1)}, bf16[432,256]{1,0:T(8,128)(2,1)S(1)}, u32[]{:S(2)}, u32[]{:S(2)}) collective-permute-start(bf16[432,256]{1,0:T(8,128)(2,1)S(1)} %get-tuple-element.57), channel_id=1, source_target_pairs={{0,2},{1,3},{4,0},{5,1},{8,4},{9,5},{12,8},{13,9},{14,12},{15,13},... | collective-permute-start | bytes 663560 | tf_op jit(solution)/shard_map/ppermute | solution.py:71
  77.0 8.9 %collective-permute-start.28 = (bf16[640,256]{1,0:T(8,128)(2,1)S(1)}, bf16[640,256]{1,0:T(8,128)(2,1)S(1)}, u32[]{:S(2)}, u32[]{:S(2)}) collective-permute-start(bf16[640,256]{1,0:T(8,128)(2,1)S(1)} %collective-permute-done.15), channel_id=1, source_target_pairs={{0,1},{1,0},{2,3},{3,2},{4,5},{5,4},{6,7},{7,6},{8,9},{9,8},{10,11... | collective-permute-start | bytes 983048 | tf_op jit(solution)/shard_map/ppermute | solution.py:75
  82.0 13.1 %collective-permute-start.18 = (bf16[2,432,256]{2,1,0:T(8,128)(2,1)S(1)}, bf16[2,432,256]{2,1,0:T(8,128)(2,1)S(1)}, u32[]{:S(2)}, u32[]{:S(2)}) collective-permute-start(bf16[2,432,256]{2,1,0:T(8,128)(2,1)S(1)} %copy-done.1), channel_id=1, source_target_pairs={{0,1},{1,0},{2,3},{3,2},{4,5},{5,4},{6,7},{7,6},{8,9},{9,8},{10,11... | collective-permute-start | bytes 1327112 | tf_op jit(solution)/shard_map/ppermute | solution.py:75
  84.3 8.4 %collective-permute-start.35 = (bf16[640,256]{1,0:T(8,128)(2,1)S(1)}, bf16[640,256]{1,0:T(8,128)(2,1)S(1)}, u32[]{:S(2)}, u32[]{:S(2)}) collective-permute-start(bf16[640,256]{1,0:T(8,128)(2,1)S(1)} %collective-permute-done.26), channel_id=1, source_target_pairs={{0,4},{1,3},{4,8},{5,1},{8,12},{9,5},{12,14},{13,9},{14,10},{15,13... | collective-permute-start | bytes 983048 | tf_op jit(solution)/shard_map/ppermute | solution.py:71
  85.9 9.1 %collective-permute-start.30 = (bf16[432,256]{1,0:T(8,128)(2,1)S(1)}, bf16[432,256]{1,0:T(8,128)(2,1)S(1)}, u32[]{:S(2)}, u32[]{:S(2)}) collective-permute-start(bf16[432,256]{1,0:T(8,128)(2,1)S(1)} %get-tuple-element.52), channel_id=1, source_target_pairs={{0,4},{1,5},{4,8},{5,9},{8,12},{9,13},{12,14},{13,15},{14,10},{15,... | collective-permute-start | bytes 663560 | tf_op jit(solution)/shard_map/ppermute | solution.py:71
  88.5 8.8 %collective-permute-start.31 = (bf16[640,256]{1,0:T(8,128)(2,1)S(1)}, bf16[640,256]{1,0:T(8,128)(2,1)S(1)}, u32[]{:S(2)}, u32[]{:S(2)}) collective-permute-start(bf16[640,256]{1,0:T(8,128)(2,1)S(1)} %collective-permute-done.23), channel_id=1, source_target_pairs={{0,1},{1,0},{2,3},{3,2},{4,5},{5,4},{6,7},{7,6},{8,9},{9,8},{10,11... | collective-permute-start | bytes 983048 | tf_op jit(solution)/shard_map/ppermute | solution.py:75
  95.7 15.1 %collective-permute-start.40 = (bf16[432,256]{1,0:T(8,128)(2,1)S(1)}, bf16[432,256]{1,0:T(8,128)(2,1)S(1)}, u32[]{:S(2)}, u32[]{:S(2)}) collective-permute-start(bf16[432,256]{1,0:T(8,128)(2,1)S(1)} %get-tuple-element.58), channel_id=1, source_target_pairs={{0,2},{1,3},{4,0},{5,1},{8,4},{9,5},{12,8},{13,9},{14,12},{15,13},... | collective-permute-start | bytes 663560 | tf_op jit(solution)/shard_map/ppermute | solution.py:71
  97.3 13.5 %collective-permute-start.37 = (bf16[432,256]{1,0:T(8,128)(2,1)S(1)}, bf16[432,256]{1,0:T(8,128)(2,1)S(1)}, u32[]{:S(2)}, u32[]{:S(2)}) collective-permute-start(bf16[432,256]{1,0:T(8,128)(2,1)S(1)} %fusion.5), channel_id=1, source_target_pairs={{0,4},{1,5},{4,8},{5,9},{8,12},{9,13},{12,14},{13,15},{14,10},{15,... | collective-permute-start | bytes 663560 | tf_op jit(solution)/shard_map/ppermute | solution.py:71
  (50 other events, 575.7 us)

commit v14 on v9

--- a/solution.py
+++ b/solution.py
@@ -80,6 +80,7 @@
     def __init__(self, x, peers):
         self.x, self.peers, self.chips = x, peers, peers // 2
         self.whole = None
+        self.swaps = {}
         if self.chips > 8:
             self.whole = lax.all_gather(x[None], "morton", axis=0, tiled=True)
             return
@@ -97,15 +98,20 @@
     def last(self, chain):
         return self.x if self.whole is not None else self.chains[chain][-1]
 
-    def places(self, gate=None):
+    def swap(self, chain, hop, gate=None):
+        if self.whole is None and (chain, hop) not in self.swaps:
+            held = self.chains[chain][hop]
+            if gate is not None:
+                held = lax.optimization_barrier((held, gate))[0]
+            self.swaps[chain, hop] = swap_cores(held, self.peers)
+        return self.swaps.get((chain, hop), self.x)
+
+    def places(self):
         if self.whole is not None:
             return [self.whole]
-        mine = self.chains[0][1:] + self.chains[1][1:]
-        held = mine
-        if gate is not None:
-            held = [lax.optimization_barrier((t, gate))[0] for t in mine]
-        others = [swap_cores(t, self.peers) for t in [self.x] + held]
-        return [t[None] for t in [self.x] + others[:1] + mine + others[1:]]
+        keys = [(c, h) for c in (0, 1) for h in range(1, len(self.chains[c]))]
+        mine = [self.x, self.swap(0, 0)] + [self.chains[c][h] for c, h in keys]
+        return [t[None] for t in mine + [self.swap(c, h) for c, h in keys]]
 
 
 class RingScatter:
@@ -137,8 +143,9 @@
         self.hop += 1
         return sent
 
-    def total(self):
-        return sum((t.astype(F32) for t in self.held if t is not None), self.term(0))
+    def total(self, gate):
+        held = lax.optimization_barrier((*self.held, gate))[:2]
+        return sum((t.astype(F32) for t in held), self.term(0))
 
 
 def call(body, out_shape, in_specs, scratch=(), cost=2, name=None, out_specs=None, aliases=None):
@@ -673,7 +680,7 @@
         out_specs=(*[HBM] * (2 + chips // 2), VMEM, VMEM),
     )(recv_slot, table, hidden, cotangent, *hidden_parts)
 
-    first = (cot_ring.last(0), cot_ring.last(1))
+    first = (cot_ring.last(0), cot_ring.last(1), cot_ring.swap(0, 0))
     give = [lax.optimization_barrier((t, first))[0] for t in give]
     sums_ring = RingScatter(keep, give, peers)
     sent = sums_ring.go()
@@ -693,14 +700,15 @@
         cost=6,
         name="mix",
     )(mix_cols, conv_weight, features)
-    sent = sums_ring.go((second, mixed))
+    sums_ring.go((second, mixed))
     cot_ring.go(0)
     cot_ring.go(1)
-    third = (cot_ring.last(0), cot_ring.last(1))
+    third = (cot_ring.last(0), cot_ring.last(1), cot_ring.swap(0, 1), cot_ring.swap(1, 1))
+    cot_ring.go(0, cot_ring.last(1))
     sums_ring.go(third)
-    cot_ring.go(0)
-    sent = sums_ring.go(cot_ring.last(0))
-    cot_parts = cot_ring.places(cols)
+    cot_ring.swap(0, 4, sums_ring.held[0])
+    sent = sums_ring.go(tuple(cot_ring.swap(chain, hop) for chain in (0, 1) for hop in (2, 3)))
+    cot_parts = cot_ring.places()
     served = lax.optimization_barrier((served, sent))[0]
 
     grad_features = call(
@@ -722,7 +730,7 @@
     )(served, send_face, table, cotangent, features, gain, conv_weight, *cot_parts)
     for _ in range(chips // 2 - 4):
         sums_ring.go()
-    return (mixed, grad_features, sums_ring.total())
+    return (mixed, grad_features, sums_ring.total(grad_features))
 
 
 def solution(mesh):

time: 111 us -> 111 us (level)
  waiting for transfers between devices: 36.3 us -> 37.7 us
  transfers between devices with their start and end apart: 41 -> 41, of which waited for: 10 -> 12; matrix products, arithmetic and copies ran while one was open for 3% -> 3% of each run, Pallas kernels for 31% -> 30%
where the time goes in v14:
time: 111 us
  waiting for transfers between devices  37.7 us (34%)
  Pallas kernels  35.9 us (32%)
  starting transfers between devices  30.5 us (27%)
  local copies, waits for them, and re-layouts  2.79 us (3%)
  other arithmetic  2.5 us (2%)
  between operations  1.15 us (1%)
    ppermute x21, waiting for transfers between devices, ring_step(): return lax.ppermute(x, 'morton', pairs)  37.2 us
    ppermute x21, starting transfers between devices, ring_step(): return lax.ppermute(x, 'morton', pairs)  26.8 us
    pallas_call x1, Pallas kernels, local(): call(functools.partial(weight_grad_body, slots, factor, peers, count), (s...  12 us
    pallas_call x1, Pallas kernels, local(): call(functools.partial(input_grad_body, slots, peers, count), sds((per_de...  11.6 us
    pallas_call x1, Pallas kernels, local(): call(mix_body, sds((per_device, channels), BF16), [HBM, HBM, VMEM], [pltp...  7.69 us
    ppermute x20, starting transfers between devices, swap_cores(): return lax.ppermute(x, 'morton', [(m, m ^ 1) for m in range(peers)])  3.75 us
    pallas_call x1, Pallas kernels, local(): call(norm_body, (sds((per_device, channels), BF16), sds((bricks * ROWS +...  2.68 us
  transfers between devices with their start and end apart: 41, of which 12 were waited for; matrix products, arithmetic and copies ran while one was open for 3% of the time, Pallas kernels for 30%

profile of v14, /device:TPU:0, one launch (start us, length us, event | category | flops | bytes accessed | tf_op | source)
XLA Modules:
  0.0 110.6 jit_solution(3353182095084761715)
XLA Ops:
  0.6 2.7 %norm.1 = (bf16[1024,256]{1,0:T(8,128)(2,1)}, bf16[656,256]{1,0:T(8,128)(2,1)}) custom-call(s32[2,26]{1,0:T(2,128)} %refs_0_.1, s32[1,64]{1,0:T(1,128)} %refs_1_.1, bf16[1024,256]{1,0:T(8,128)(2,1)} %refs_4_.1, f32[1,256]{1,0:T(1,128)} %bitcast.95), custom_call_target="tpu_custom_call" | custom-call | flops 2000000000 | tf_op jit(solution)/shard_map/norm/pallas_call | solution.py:623
  3.3 3.0 %collective-permute-start.1 = (bf16[656,256]{1,0:T(8,128)(2,1)}, bf16[656,256]{1,0:T(8,128)(2,1)S(1)}, u32[]{:S(2)}, u32[]{:S(2)}) collective-permute-start(bf16[656,256]{1,0:T(8,128)(2,1)} %get-tuple-element.34), channel_id=1, source_target_pairs={{0,4},{1,3},{4,8},{5,1},{8,12},{9,5},{12,14},{13,9},{14,10},{15,13... | collective-permute-start | bytes 1007624 | tf_op jit(solution)/shard_map/ppermute | solution.py:72
  7.0 1.9 %extract.1 = bf16[640,256]{1,0:T(8,128)(2,1)} custom-call(bf16[1024,256]{1,0:T(8,128)(2,1)} %refs_3_.3), custom_call_target="tpu_custom_call" | custom-call | flops 2000000000 | tf_op jit(solution)/shard_map/extract/pallas_call | solution.py:631
  8.9 5.0 %collective-permute-done.1 = bf16[656,256]{1,0:T(8,128)(2,1)S(1)} collective-permute-done((bf16[656,256]{1,0:T(8,128)(2,1)}, bf16[656,256]{1,0:T(8,128)(2,1)S(1)}, u32[]{:S(2)}, u32[]{:S(2)}) %collective-permute-start.1) | collective-permute-done | bytes 335904 | tf_op jit(solution)/shard_map/ppermute | solution.py:72
  13.9 2.4 %collective-permute-start.2 = (bf16[656,256]{1,0:T(8,128)(2,1)S(1)}, bf16[656,256]{1,0:T(8,128)(2,1)S(1)}, u32[]{:S(2)}, u32[]{:S(2)}) collective-permute-start(bf16[656,256]{1,0:T(8,128)(2,1)S(1)} %collective-permute-done.1), channel_id=1, source_target_pairs={{0,4},{1,3},{4,8},{5,1},{8,12},{9,5},{12,14},{13,9},{14,10},{15,13... | collective-permute-start | bytes 1007624 | tf_op jit(solution)/shard_map/ppermute | solution.py:72
  16.3 1.3 %dynamic-slice_bitcast_fusion.refs_1_.refs_2_ = s32[33]{0:T(128)} fusion(s32[16,33]{1,0:T(8,128)} %constant.10.clone, s32[]{:T(128)S(6)} %select_n.3), kind=kLoop, calls=%fused_computation.16 | loop fusion | bytes 268 | tf_op jit(solution)/shard_map/squeeze | solution.py:621
  17.6 1.6 %collective-permute-start.6 = (bf16[656,256]{1,0:T(8,128)(2,1)S(1)}, bf16[656,256]{1,0:T(8,128)(2,1)S(1)}, u32[]{:S(2)}, u32[]{:S(2)}) collective-permute-start(bf16[656,256]{1,0:T(8,128)(2,1)S(1)} %collective-permute-done.5), channel_id=1, source_target_pairs={{0,4},{1,3},{4,8},{5,1},{8,12},{9,5},{12,14},{13,9},{14,10},{15,13... | collective-permute-start | bytes 1007624 | tf_op jit(solution)/shard_map/ppermute | solution.py:72
  19.1 3.2 %collective-permute-done.2 = bf16[656,256]{1,0:T(8,128)(2,1)S(1)} collective-permute-done((bf16[656,256]{1,0:T(8,128)(2,1)S(1)}, bf16[656,256]{1,0:T(8,128)(2,1)S(1)}, u32[]{:S(2)}, u32[]{:S(2)}) %collective-permute-start.2) | collective-permute-done | bytes 335904 | tf_op jit(solution)/shard_map/ppermute | solution.py:72
  24.0 2.0 %collective-permute-done.6 = bf16[656,256]{1,0:T(8,128)(2,1)S(1)} collective-permute-done((bf16[656,256]{1,0:T(8,128)(2,1)S(1)}, bf16[656,256]{1,0:T(8,128)(2,1)S(1)}, u32[]{:S(2)}, u32[]{:S(2)}) %collective-permute-start.6) | collective-permute-done | bytes 335904 | tf_op jit(solution)/shard_map/ppermute | solution.py:72
  27.1 2.5 %collective-permute-done.3 = bf16[656,256]{1,0:T(8,128)(2,1)S(1)} collective-permute-done((bf16[656,256]{1,0:T(8,128)(2,1)S(1)}, bf16[656,256]{1,0:T(8,128)(2,1)S(1)}, u32[]{:S(2)}, u32[]{:S(2)}) %collective-permute-start.3) | collective-permute-done | bytes 335904 | tf_op jit(solution)/shard_map/ppermute | solution.py:72
  31.3 1.9 %collective-permute-done.7 = bf16[656,256]{1,0:T(8,128)(2,1)S(1)} collective-permute-done((bf16[656,256]{1,0:T(8,128)(2,1)S(1)}, bf16[656,256]{1,0:T(8,128)(2,1)S(1)}, u32[]{:S(2)}, u32[]{:S(2)}) %collective-permute-start.7) | collective-permute-done | bytes 335904 | tf_op jit(solution)/shard_map/ppermute | solution.py:72
  33.2 3.6 %collective-permute-done.4 = bf16[656,256]{1,0:T(8,128)(2,1)S(1)} collective-permute-done((bf16[656,256]{1,0:T(8,128)(2,1)S(1)}, bf16[656,256]{1,0:T(8,128)(2,1)S(1)}, u32[]{:S(2)}, u32[]{:S(2)}) %collective-permute-start.4) | collective-permute-done | bytes 335904 | tf_op jit(solution)/shard_map/ppermute | solution.py:72
  38.4 1.9 %collective-permute-start.16 = (bf16[640,256]{1,0:T(8,128)(2,1)}, bf16[640,256]{1,0:T(8,128)(2,1)S(1)}, u32[]{:S(2)}, u32[]{:S(2)}) collective-permute-start(bf16[640,256]{1,0:T(8,128)(2,1)} %extract.1), channel_id=1, source_target_pairs={{1,4},{0,3},{5,8},{4,1},{9,12},{8,5},{13,14},{12,9},{15,10},{14,13... | collective-permute-start | bytes 983048 | tf_op jit(solution)/shard_map/ppermute | solution.py:72
  41.2 12.0 %weight_grad.1 = (f32[8,432,256]{2,1,0:T(8,128)}, bf16[2,432,256]{2,1,0:T(8,128)(2,1)}, bf16[2,432,256]{2,1,0:T(8,128)(2,1)}, bf16[2,432,256]{2,1,0:T(8,128)(2,1...) custom-call(s32[2,26]{1,0:T(2,128)} %refs_0_.1, ...), custom_call_target="tpu_custom_call" | custom-call | flops 8999999488 | tf_op jit(solution)/shard_map/weight_grad/pallas_call | solution.py:654
  54.8 2.3 %collective-permute-start.23 = (bf16[640,256]{1,0:T(8,128)(2,1)S(1)}, bf16[640,256]{1,0:T(8,128)(2,1)S(1)}, u32[]{:S(2)}, u32[]{:S(2)}) collective-permute-start(bf16[640,256]{1,0:T(8,128)(2,1)S(1)} %collective-permute-done.15), channel_id=1, source_target_pairs={{0,4},{1,3},{4,8},{5,1},{8,12},{9,5},{12,14},{13,9},{14,10},{15,13... | collective-permute-start | bytes 983048 | tf_op jit(solution)/shard_map/ppermute | solution.py:72
  58.9 1.5 %collective-permute-start.38 = (bf16[432,256]{1,0:T(8,128)(2,1)S(1)}, bf16[432,256]{1,0:T(8,128)(2,1)S(1)}, u32[]{:S(2)}, u32[]{:S(2)}) collective-permute-start(bf16[432,256]{1,0:T(8,128)(2,1)S(1)} %get-tuple-element.67), channel_id=1, source_target_pairs={{0,2},{1,3},{4,0},{5,1},{8,4},{9,5},{12,8},{13,9},{14,12},{15,13},... | collective-permute-start | bytes 663560 | tf_op jit(solution)/shard_map/ppermute | solution.py:72
  60.5 7.7 %mix.1 = bf16[1024,256]{1,0:T(8,128)(2,1)} custom-call(bf16[20,64,2304]{2,1,0:T(8,128)(2,1)} %get-tuple-element.43.cols_ref, bf16[6912,256]{1,0:T(8,128)(2,1)} %refs_6_.1, bf16[1024,256]{1,0:T(8,128)(2,1)} %refs_4_.1), custom_call_target="tpu_custom_call" | custom-call | flops 6000000000 | tf_op jit(solution)/shard_map/mix/pallas_call | solution.py:695
  70.9 1.4 %collective-permute-start.39 = (bf16[432,256]{1,0:T(8,128)(2,1)S(1)}, bf16[432,256]{1,0:T(8,128)(2,1)S(1)}, u32[]{:S(2)}, u32[]{:S(2)}) collective-permute-start(bf16[432,256]{1,0:T(8,128)(2,1)S(1)} %get-tuple-element.59), channel_id=1, source_target_pairs={{0,2},{1,3},{4,0},{5,1},{8,4},{9,5},{12,8},{13,9},{14,12},{15,13},... | collective-permute-start | bytes 663560 | tf_op jit(solution)/shard_map/ppermute | solution.py:72
  72.4 5.5 %collective-permute-done.27 = bf16[640,256]{1,0:T(8,128)(2,1)S(1)} collective-permute-done((bf16[640,256]{1,0:T(8,128)(2,1)S(1)}, bf16[640,256]{1,0:T(8,128)(2,1)S(1)}, u32[]{:S(2)}, u32[]{:S(2)}) %collective-permute-start.27) | collective-permute-done | bytes 327712 | tf_op jit(solution)/shard_map/ppermute | solution.py:72
  77.8 3.5 %collective-permute-done.26 = bf16[640,256]{1,0:T(8,128)(2,1)S(1)} collective-permute-done((bf16[640,256]{1,0:T(8,128)(2,1)S(1)}, bf16[640,256]{1,0:T(8,128)(2,1)S(1)}, u32[]{:S(2)}, u32[]{:S(2)}) %collective-permute-start.26) | collective-permute-done | bytes 327712 | tf_op jit(solution)/shard_map/ppermute | solution.py:72
  81.9 1.8 %collective-permute-done.25 = bf16[432,256]{1,0:T(8,128)(2,1)S(1)} collective-permute-done((bf16[432,256]{1,0:T(8,128)(2,1)S(1)}, bf16[432,256]{1,0:T(8,128)(2,1)S(1)}, u32[]{:S(2)}, u32[]{:S(2)}) %collective-permute-start.25) | collective-permute-done | bytes 221216 | tf_op jit(solution)/shard_map/ppermute | solution.py:72
  86.4 5.8 %collective-permute-done.35 = bf16[640,256]{1,0:T(8,128)(2,1)S(1)} collective-permute-done((bf16[640,256]{1,0:T(8,128)(2,1)S(1)}, bf16[640,256]{1,0:T(8,128)(2,1)S(1)}, u32[]{:S(2)}, u32[]{:S(2)}) %collective-permute-start.35) | collective-permute-done | bytes 327712 | tf_op jit(solution)/shard_map/ppermute | solution.py:72
  92.2 2.4 %collective-permute-done.30 = bf16[432,256]{1,0:T(8,128)(2,1)S(1)} collective-permute-done((bf16[432,256]{1,0:T(8,128)(2,1)S(1)}, bf16[432,256]{1,0:T(8,128)(2,1)S(1)}, u32[]{:S(2)}, u32[]{:S(2)}) %collective-permute-start.30) | collective-permute-done | bytes 221216 | tf_op jit(solution)/shard_map/ppermute | solution.py:72
  98.1 11.6 %input_grad.1 = bf16[1024,256]{1,0:T(8,128)(2,1)} custom-call(s32[16,256]{1,0:T(8,128)} %get-tuple-element.56.refs_0_, s32[1,64]{1,0:T(1,128)} %refs_1_.1, s32[33]{0:T(128)} %dynamic-slice_bitcast_fusion.refs_1_.refs_2_, bf16[1024,256]{1,0:T(8,128)(2,1)} %refs_3_.3, bf16[1024,256]{1,0:T(8,128)(2,1)} %refs_4_.1, f32[1,256]{1,0:T(1,128)} %bitcast.96, ...), custom_call_target="tpu_custom_call" | custom-call | flops 12999999488 | tf_op jit(solution)/shard_map/input_grad/pallas_call | solution.py:714
  (137 shorter events, 21.0 us)
Async XLA Ops:
  3.3 10.6 %collective-permute-start.1 = (bf16[656,256]{1,0:T(8,128)(2,1)}, bf16[656,256]{1,0:T(8,128)(2,1)S(1)}, u32[]{:S(2)}, u32[]{:S(2)}) collective-permute-start(bf16[656,256]{1,0:T(8,128)(2,1)} %get-tuple-element.34), channel_id=1, source_target_pairs={{0,4},{1,3},{4,8},{5,1},{8,12},{9,5},{12,14},{13,9},{14,10},{15,13... | collective-permute-start | bytes 1007624 | tf_op jit(solution)/shard_map/ppermute | solution.py:72
  6.3 11.2 %collective-permute-start.5 = (bf16[656,256]{1,0:T(8,128)(2,1)}, bf16[656,256]{1,0:T(8,128)(2,1)S(1)}, u32[]{:S(2)}, u32[]{:S(2)}) collective-permute-start(bf16[656,256]{1,0:T(8,128)(2,1)} %get-tuple-element.34), channel_id=1, source_target_pairs={{1,4},{0,3},{5,8},{4,1},{9,12},{8,5},{13,14},{12,9},{15,10},{14,13... | collective-permute-start | bytes 1007624 | tf_op jit(solution)/shard_map/ppermute | solution.py:72
  13.9 8.4 %collective-permute-start.2 = (bf16[656,256]{1,0:T(8,128)(2,1)S(1)}, bf16[656,256]{1,0:T(8,128)(2,1)S(1)}, u32[]{:S(2)}, u32[]{:S(2)}) collective-permute-start(bf16[656,256]{1,0:T(8,128)(2,1)S(1)} %collective-permute-done.1), channel_id=1, source_target_pairs={{0,4},{1,3},{4,8},{5,1},{8,12},{9,5},{12,14},{13,9},{14,10},{15,13... | collective-permute-start | bytes 1007624 | tf_op jit(solution)/shard_map/ppermute | solution.py:72
  17.6 8.4 %collective-permute-start.6 = (bf16[656,256]{1,0:T(8,128)(2,1)S(1)}, bf16[656,256]{1,0:T(8,128)(2,1)S(1)}, u32[]{:S(2)}, u32[]{:S(2)}) collective-permute-start(bf16[656,256]{1,0:T(8,128)(2,1)S(1)} %collective-permute-done.5), channel_id=1, source_target_pairs={{0,4},{1,3},{4,8},{5,1},{8,12},{9,5},{12,14},{13,9},{14,10},{15,13... | collective-permute-start | bytes 1007624 | tf_op jit(solution)/shard_map/ppermute | solution.py:72
  36.8 16.4 %collective-permute-start.17 = (bf16[640,256]{1,0:T(8,128)(2,1)}, bf16[640,256]{1,0:T(8,128)(2,1)S(1)}, u32[]{:S(2)}, u32[]{:S(2)}) collective-permute-start(bf16[640,256]{1,0:T(8,128)(2,1)} %extract.1), channel_id=1, source_target_pairs={{0,1},{1,0},{2,3},{3,2},{4,5},{5,4},{6,7},{7,6},{8,9},{9,8},{10,11... | collective-permute-start | bytes 983048 | tf_op jit(solution)/shard_map/ppermute | solution.py:76
  37.3 16.0 %collective-permute-start.15 = (bf16[640,256]{1,0:T(8,128)(2,1)}, bf16[640,256]{1,0:T(8,128)(2,1)S(1)}, u32[]{:S(2)}, u32[]{:S(2)}) collective-permute-start(bf16[640,256]{1,0:T(8,128)(2,1)} %extract.1), channel_id=1, source_target_pairs={{0,4},{1,3},{4,8},{5,1},{8,12},{9,5},{12,14},{13,9},{14,10},{15,13... | collective-permute-start | bytes 983048 | tf_op jit(solution)/shard_map/ppermute | solution.py:72
  38.4 14.9 %collective-permute-start.16 = (bf16[640,256]{1,0:T(8,128)(2,1)}, bf16[640,256]{1,0:T(8,128)(2,1)S(1)}, u32[]{:S(2)}, u32[]{:S(2)}) collective-permute-start(bf16[640,256]{1,0:T(8,128)(2,1)} %extract.1), channel_id=1, source_target_pairs={{1,4},{0,3},{5,8},{4,1},{9,12},{8,5},{13,14},{12,9},{15,10},{14,13... | collective-permute-start | bytes 983048 | tf_op jit(solution)/shard_map/ppermute | solution.py:72
  53.4 15.9 %collective-permute-start.21 = (bf16[2,432,256]{2,1,0:T(8,128)(2,1)}, bf16[2,432,256]{2,1,0:T(8,128)(2,1)S(1)}, u32[]{:S(2)}, u32[]{:S(2)}) collective-permute-start(bf16[2,432,256]{2,1,0:T(8,128)(2,1)} %get-tuple-element.50), channel_id=1, source_target_pairs={{0,1},{1,0},{2,3},{3,2},{4,5},{5,4},{6,7},{7,6},{8,9},{9,8},{10,11... | collective-permute-start | bytes 1327112 | tf_op jit(solution)/shard_map/ppermute | solution.py:76
  53.9 14.3 %collective-permute-start.24 = (bf16[640,256]{1,0:T(8,128)(2,1)S(1)}, bf16[640,256]{1,0:T(8,128)(2,1)S(1)}, u32[]{:S(2)}, u32[]{:S(2)}) collective-permute-start(bf16[640,256]{1,0:T(8,128)(2,1)S(1)} %collective-permute-done.16), channel_id=1, source_target_pairs={{0,4},{1,3},{4,8},{5,1},{8,12},{9,5},{12,14},{13,9},{14,10},{15,13... | collective-permute-start | bytes 983048 | tf_op jit(solution)/shard_map/ppermute | solution.py:72
  54.8 13.5 %collective-permute-start.23 = (bf16[640,256]{1,0:T(8,128)(2,1)S(1)}, bf16[640,256]{1,0:T(8,128)(2,1)S(1)}, u32[]{:S(2)}, u32[]{:S(2)}) collective-permute-start(bf16[640,256]{1,0:T(8,128)(2,1)S(1)} %collective-permute-done.15), channel_id=1, source_target_pairs={{0,4},{1,3},{4,8},{5,1},{8,12},{9,5},{12,14},{13,9},{14,10},{15,13... | collective-permute-start | bytes 983048 | tf_op jit(solution)/shard_map/ppermute | solution.py:72
  58.4 11.7 %collective-permute-start.22 = (bf16[432,256]{1,0:T(8,128)(2,1)S(1)}, bf16[432,256]{1,0:T(8,128)(2,1)S(1)}, u32[]{:S(2)}, u32[]{:S(2)}) collective-permute-start(bf16[432,256]{1,0:T(8,128)(2,1)S(1)} %get-tuple-element.68), channel_id=1, source_target_pairs={{0,4},{1,5},{4,8},{5,9},{8,12},{9,13},{12,14},{13,15},{14,10},{15,... | collective-permute-start | bytes 663560 | tf_op jit(solution)/shard_map/ppermute | solution.py:72
  58.9 11.2 %collective-permute-start.38 = (bf16[432,256]{1,0:T(8,128)(2,1)S(1)}, bf16[432,256]{1,0:T(8,128)(2,1)S(1)}, u32[]{:S(2)}, u32[]{:S(2)}) collective-permute-start(bf16[432,256]{1,0:T(8,128)(2,1)S(1)} %get-tuple-element.67), channel_id=1, source_target_pairs={{0,2},{1,3},{4,0},{5,1},{8,4},{9,5},{12,8},{13,9},{14,12},{15,13},... | collective-permute-start | bytes 663560 | tf_op jit(solution)/shard_map/ppermute | solution.py:72
  68.2 13.1 %collective-permute-start.20 = (bf16[2,432,256]{2,1,0:T(8,128)(2,1)S(1)}, bf16[2,432,256]{2,1,0:T(8,128)(2,1)S(1)}, u32[]{:S(2)}, u32[]{:S(2)}) collective-permute-start(bf16[2,432,256]{2,1,0:T(8,128)(2,1)S(1)} %copy-done.2), channel_id=1, source_target_pairs={{0,1},{1,0},{2,3},{3,2},{4,5},{5,4},{6,7},{7,6},{8,9},{9,8},{10,11... | collective-permute-start | bytes 1327112 | tf_op jit(solution)/shard_map/ppermute | solution.py:76
  68.3 9.5 %collective-permute-start.27 = (bf16[640,256]{1,0:T(8,128)(2,1)S(1)}, bf16[640,256]{1,0:T(8,128)(2,1)S(1)}, u32[]{:S(2)}, u32[]{:S(2)}) collective-permute-start(bf16[640,256]{1,0:T(8,128)(2,1)S(1)} %collective-permute-done.24), channel_id=1, source_target_pairs={{0,4},{1,3},{4,8},{5,1},{8,12},{9,5},{12,14},{13,9},{14,10},{15,13... | collective-permute-start | bytes 983048 | tf_op jit(solution)/shard_map/ppermute | solution.py:72
  69.2 12.1 %collective-permute-start.26 = (bf16[640,256]{1,0:T(8,128)(2,1)S(1)}, bf16[640,256]{1,0:T(8,128)(2,1)S(1)}, u32[]{:S(2)}, u32[]{:S(2)}) collective-permute-start(bf16[640,256]{1,0:T(8,128)(2,1)S(1)} %collective-permute-done.23), channel_id=1, source_target_pairs={{0,4},{1,3},{4,8},{5,1},{8,12},{9,5},{12,14},{13,9},{14,10},{15,13... | collective-permute-start | bytes 983048 | tf_op jit(solution)/shard_map/ppermute | solution.py:72
  70.3 13.4 %collective-permute-start.25 = (bf16[432,256]{1,0:T(8,128)(2,1)S(1)}, bf16[432,256]{1,0:T(8,128)(2,1)S(1)}, u32[]{:S(2)}, u32[]{:S(2)}) collective-permute-start(bf16[432,256]{1,0:T(8,128)(2,1)S(1)} %get-tuple-element.53), channel_id=1, source_target_pairs={{0,4},{1,5},{4,8},{5,9},{8,12},{9,13},{12,14},{13,15},{14,10},{15,... | collective-permute-start | bytes 663560 | tf_op jit(solution)/shard_map/ppermute | solution.py:72
  70.9 13.6 %collective-permute-start.39 = (bf16[432,256]{1,0:T(8,128)(2,1)S(1)}, bf16[432,256]{1,0:T(8,128)(2,1)S(1)}, u32[]{:S(2)}, u32[]{:S(2)}) collective-permute-start(bf16[432,256]{1,0:T(8,128)(2,1)S(1)} %get-tuple-element.59), channel_id=1, source_target_pairs={{0,2},{1,3},{4,0},{5,1},{8,4},{9,5},{12,8},{13,9},{14,12},{15,13},... | collective-permute-start | bytes 663560 | tf_op jit(solution)/shard_map/ppermute | solution.py:72
  81.4 13.2 %collective-permute-start.19 = (bf16[2,432,256]{2,1,0:T(8,128)(2,1)S(1)}, bf16[2,432,256]{2,1,0:T(8,128)(2,1)S(1)}, u32[]{:S(2)}, u32[]{:S(2)}) collective-permute-start(bf16[2,432,256]{2,1,0:T(8,128)(2,1)S(1)} %copy-done.1), channel_id=1, source_target_pairs={{0,1},{1,0},{2,3},{3,2},{4,5},{5,4},{6,7},{7,6},{8,9},{9,8},{10,11... | collective-permute-start | bytes 1327112 | tf_op jit(solution)/shard_map/ppermute | solution.py:76
  83.7 8.5 %collective-permute-start.35 = (bf16[640,256]{1,0:T(8,128)(2,1)S(1)}, bf16[640,256]{1,0:T(8,128)(2,1)S(1)}, u32[]{:S(2)}, u32[]{:S(2)}) collective-permute-start(bf16[640,256]{1,0:T(8,128)(2,1)S(1)} %collective-permute-done.26), channel_id=1, source_target_pairs={{0,4},{1,3},{4,8},{5,1},{8,12},{9,5},{12,14},{13,9},{14,10},{15,13... | collective-permute-start | bytes 983048 | tf_op jit(solution)/shard_map/ppermute | solution.py:72
  84.7 9.8 %collective-permute-start.30 = (bf16[432,256]{1,0:T(8,128)(2,1)S(1)}, bf16[432,256]{1,0:T(8,128)(2,1)S(1)}, u32[]{:S(2)}, u32[]{:S(2)}) collective-permute-start(bf16[432,256]{1,0:T(8,128)(2,1)S(1)} %get-tuple-element.54), channel_id=1, source_target_pairs={{0,4},{1,5},{4,8},{5,9},{8,12},{9,13},{12,14},{13,15},{14,10},{15,... | collective-permute-start | bytes 663560 | tf_op jit(solution)/shard_map/ppermute | solution.py:72
  85.8 9.3 %collective-permute-start.33 = (bf16[640,256]{1,0:T(8,128)(2,1)S(1)}, bf16[640,256]{1,0:T(8,128)(2,1)S(1)}, u32[]{:S(2)}, u32[]{:S(2)}) collective-permute-start(bf16[640,256]{1,0:T(8,128)(2,1)S(1)} %collective-permute-done.24), channel_id=1, source_target_pairs={{0,1},{1,0},{2,3},{3,2},{4,5},{5,4},{6,7},{7,6},{8,9},{9,8},{10,11... | collective-permute-start | bytes 983048 | tf_op jit(solution)/shard_map/ppermute | solution.py:76
  85.8 9.8 %collective-permute-start.31 = (bf16[640,256]{1,0:T(8,128)(2,1)S(1)}, bf16[640,256]{1,0:T(8,128)(2,1)S(1)}, u32[]{:S(2)}, u32[]{:S(2)}) collective-permute-start(bf16[640,256]{1,0:T(8,128)(2,1)S(1)} %collective-permute-done.23), channel_id=1, source_target_pairs={{0,1},{1,0},{2,3},{3,2},{4,5},{5,4},{6,7},{7,6},{8,9},{9,8},{10,11... | collective-permute-start | bytes 983048 | tf_op jit(solution)/shard_map/ppermute | solution.py:76
  95.2 14.6 %collective-permute-start.40 = (bf16[432,256]{1,0:T(8,128)(2,1)S(1)}, bf16[432,256]{1,0:T(8,128)(2,1)S(1)}, u32[]{:S(2)}, u32[]{:S(2)}) collective-permute-start(bf16[432,256]{1,0:T(8,128)(2,1)S(1)} %get-tuple-element.60), channel_id=1, source_target_pairs={{0,2},{1,3},{4,0},{5,1},{8,4},{9,5},{12,8},{13,9},{14,12},{15,13},... | collective-permute-start | bytes 663560 | tf_op jit(solution)/shard_map/ppermute | solution.py:72
  96.2 13.6 %collective-permute-start.37 = (bf16[432,256]{1,0:T(8,128)(2,1)S(1)}, bf16[432,256]{1,0:T(8,128)(2,1)S(1)}, u32[]{:S(2)}, u32[]{:S(2)}) collective-permute-start(bf16[432,256]{1,0:T(8,128)(2,1)S(1)} %fusion.5), channel_id=1, source_target_pairs={{0,4},{1,5},{4,8},{5,9},{8,12},{9,13},{12,14},{13,15},{14,10},{15,... | collective-permute-start | bytes 663560 | tf_op jit(solution)/shard_map/ppermute | solution.py:72
  (51 other events, 500.6 us)

commit v15 on v13

--- a/solution.py
+++ b/solution.py
@@ -61,10 +61,11 @@
     return np.concatenate([place_of, behind, turn, device[:, None]], axis=1).astype(np.int32)
 
 
-def ring_step(x, peers, step, cross=0):
+def ring_step(x, peers, step, cross=0, reach=1):
     order = ring_order(peers // 2)
+    chips = len(order)
     pairs = [
-        (2 * order[i] + (core ^ cross), 2 * order[(i + (step or 1 - 2 * core)) % len(order)] + core)
+        (2 * order[i] + (core ^ cross), 2 * order[(i + reach * (step or 1 - 2 * core)) % chips] + core)
         for i in range(len(order))
         for core in range(2)
     ]
@@ -93,6 +94,10 @@
             held = lax.optimization_barrier((held, gate))[0]
         cross = int(chain == 1 and len(self.chains[chain]) == 1)
         self.chains[chain].append(ring_step(held, self.peers, 0, cross))
+
+    def go_far(self, chain):
+        if self.whole is None and len(self.chains[chain]) == 2 <= self.chips // 2 - chain:
+            self.chains[chain].append(ring_step(self.x, self.peers, 0, chain, 2))
 
     def last(self, chain):
         return self.x if self.whole is not None else self.chains[chain][-1]
@@ -594,6 +599,8 @@
     cot_ring = RingGather(cot_share, peers)
     cot_ring.go(0, hidden_ring.last(1))
     cot_ring.go(1, hidden_ring.last(0))
+    cot_ring.go_far(0)
+    cot_ring.go_far(1)
 
     count = len(hidden_parts)
     rows = 27 * channels // peers
@@ -628,21 +635,18 @@
         out_specs=(*[HBM] * (1 + chips // 2), VMEM, VMEM, VMEM),
     )(recv_slot, table, hidden, cotangent, features, conv_weight, *hidden_parts)
 
-    first = (cot_ring.last(0), cot_ring.last(1), cot_ring.swap(0, 0))
-    give = [lax.optimization_barrier((t, first))[0] for t in give]
+    first = [t for chain in (0, 1) for t in cot_ring.chains[chain][1:]] if cot_ring.whole is None else []
+    give = [lax.optimization_barrier((t, cot_ring.swap(0, 0), *first))[0] for t in give]
     sums_ring = RingScatter(keep, give, peers)
     cot_ring.go(0, served)
     cot_ring.go(1, served)
     sums_ring.go()
     gate = (cot_ring.last(0), cot_ring.last(1))
-    cot_ring.go(0)
-    cot_ring.go(1)
-    sums_ring.go(gate)
-    gate = (cot_ring.last(0), cot_ring.last(1), cot_ring.swap(0, 1), cot_ring.swap(1, 1))
     cot_ring.go(0, cot_ring.last(1))
     sums_ring.go(gate)
     cot_ring.swap(0, 4, sums_ring.held[0])
-    sent = sums_ring.go(tuple(cot_ring.swap(chain, hop) for chain in (0, 1) for hop in (2, 3)))
+    sums_ring.go(tuple(cot_ring.swap(chain, hop) for chain in (0, 1) for hop in (1, 2)))
+    sent = sums_ring.go((cot_ring.swap(0, 3), cot_ring.swap(1, 3)))
     cot_parts = cot_ring.places()
     served = lax.optimization_barrier((served, sent))[0]
 

time: 113 us -> 117 us (1.035)
  waiting for transfers between devices: 37.9 us -> 43.3 us
    ppermute x21, waiting for transfers between devices: 37.8 us -> 41.6 us  [ring_step(): return lax.ppermute(x, 'morton', pairs)]
    ppermute x21, starting transfers between devices: 31.4 us -> 29.6 us  [ring_step(): return lax.ppermute(x, 'morton', pairs)]
    ppermute x20, waiting for transfers between devices: 0.05 us -> 1.68 us  [swap_cores(): return lax.ppermute(x, 'morton', [(m, m ^ 1) for m in range(peers)])]
    ppermute x20, starting transfers between devices: 3.45 us -> 5.04 us  [swap_cores(): return lax.ppermute(x, 'morton', [(m, m ^ 1) for m in range(peers)])]
  transfers between devices with their start and end apart: 41 -> 41, of which waited for: 13 -> 15; matrix products, arithmetic and copies ran while one was open for 4% -> 4% of each run, Pallas kernels for 26% -> 24%
where the time goes in v15:
time: 117 us; the launch traced here: 116 us
  waiting for transfers between devices  43.3 us (37%)
  starting transfers between devices  34.7 us (30%)
  Pallas kernels  30.9 us (26%)
  other arithmetic  3.68 us (3%)
  local copies, waits for them, and re-layouts  2.73 us (2%)
    ppermute x21, waiting for transfers between devices, ring_step(): return lax.ppermute(x, 'morton', pairs)  41.6 us
    ppermute x21, starting transfers between devices, ring_step(): return lax.ppermute(x, 'morton', pairs)  29.6 us
    pallas_call x1, Pallas kernels, local(): call(functools.partial(weight_grad_body, slots, factor, peers, count), (s...  14.7 us
    pallas_call x1, Pallas kernels, local(): call(functools.partial(input_grad_body, slots, peers, len(cot_parts)), sd...  11.7 us
    ppermute x20, starting transfers between devices, swap_cores(): return lax.ppermute(x, 'morton', [(m, m ^ 1) for m in range(peers)])  5.04 us
    convert_element_type x4, other arithmetic, go(): part = part.astype(BF16)  2.8 us
    pallas_call x1, Pallas kernels, local(): call(norm_body, (sds((per_device, channels), BF16), sds((bricks * ROWS +...  2.67 us
  transfers between devices with their start and end apart: 41, of which 15 were waited for; matrix products, arithmetic and copies ran while one was open for 4% of the time, Pallas kernels for 24%

profile of v15, /device:TPU:0, one launch (start us, length us, event | category | flops | bytes accessed | tf_op | source)
XLA Modules:
  0.0 116.3 jit_solution(6804987953669799825)
XLA Ops:
  0.6 2.7 %norm.1 = (bf16[1024,256]{1,0:T(8,128)(2,1)}, bf16[656,256]{1,0:T(8,128)(2,1)}) custom-call(s32[2,26]{1,0:T(2,128)} %refs_0_.1, s32[1,64]{1,0:T(1,128)} %refs_1_.1, bf16[1024,256]{1,0:T(8,128)(2,1)} %refs_4_.3, f32[1,256]{1,0:T(1,128)} %bitcast.95), custom_call_target="tpu_custom_call" | custom-call | flops 2000000000 | tf_op jit(solution)/shard_map/norm/pallas_call | solution.py:576
  3.3 3.0 %collective-permute-start.1 = (bf16[656,256]{1,0:T(8,128)(2,1)}, bf16[656,256]{1,0:T(8,128)(2,1)S(1)}, u32[]{:S(2)}, u32[]{:S(2)}) collective-permute-start(bf16[656,256]{1,0:T(8,128)(2,1)} %get-tuple-element.33), channel_id=1, source_target_pairs={{0,4},{1,3},{4,8},{5,1},{8,12},{9,5},{12,14},{13,9},{14,10},{15,13... | collective-permute-start | bytes 1007624 | tf_op jit(solution)/shard_map/ppermute | solution.py:72
  7.0 1.9 %extract.1 = bf16[640,256]{1,0:T(8,128)(2,1)} custom-call(bf16[1024,256]{1,0:T(8,128)(2,1)} %refs_3_.3), custom_call_target="tpu_custom_call" | custom-call | flops 2000000000 | tf_op jit(solution)/shard_map/extract/pallas_call | solution.py:584
  8.9 5.0 %collective-permute-done.1 = bf16[656,256]{1,0:T(8,128)(2,1)S(1)} collective-permute-done((bf16[656,256]{1,0:T(8,128)(2,1)}, bf16[656,256]{1,0:T(8,128)(2,1)S(1)}, u32[]{:S(2)}, u32[]{:S(2)}) %collective-permute-start.1) | collective-permute-done | bytes 335904 | tf_op jit(solution)/shard_map/ppermute | solution.py:72
  13.9 2.4 %collective-permute-start.2 = (bf16[656,256]{1,0:T(8,128)(2,1)S(1)}, bf16[656,256]{1,0:T(8,128)(2,1)S(1)}, u32[]{:S(2)}, u32[]{:S(2)}) collective-permute-start(bf16[656,256]{1,0:T(8,128)(2,1)S(1)} %collective-permute-done.1), channel_id=1, source_target_pairs={{0,4},{1,3},{4,8},{5,1},{8,12},{9,5},{12,14},{13,9},{14,10},{15,13... | collective-permute-start | bytes 1007624 | tf_op jit(solution)/shard_map/ppermute | solution.py:72
  19.2 3.2 %collective-permute-done.2 = bf16[656,256]{1,0:T(8,128)(2,1)S(1)} collective-permute-done((bf16[656,256]{1,0:T(8,128)(2,1)S(1)}, bf16[656,256]{1,0:T(8,128)(2,1)S(1)}, u32[]{:S(2)}, u32[]{:S(2)}) %collective-permute-start.2) | collective-permute-done | bytes 335904 | tf_op jit(solution)/shard_map/ppermute | solution.py:72
  24.0 2.0 %collective-permute-done.6 = bf16[656,256]{1,0:T(8,128)(2,1)S(1)} collective-permute-done((bf16[656,256]{1,0:T(8,128)(2,1)S(1)}, bf16[656,256]{1,0:T(8,128)(2,1)S(1)}, u32[]{:S(2)}, u32[]{:S(2)}) %collective-permute-start.6) | collective-permute-done | bytes 335904 | tf_op jit(solution)/shard_map/ppermute | solution.py:72
  27.1 2.5 %collective-permute-done.3 = bf16[656,256]{1,0:T(8,128)(2,1)S(1)} collective-permute-done((bf16[656,256]{1,0:T(8,128)(2,1)S(1)}, bf16[656,256]{1,0:T(8,128)(2,1)S(1)}, u32[]{:S(2)}, u32[]{:S(2)}) %collective-permute-start.3) | collective-permute-done | bytes 335904 | tf_op jit(solution)/shard_map/ppermute | solution.py:72
  31.3 1.9 %collective-permute-done.7 = bf16[656,256]{1,0:T(8,128)(2,1)S(1)} collective-permute-done((bf16[656,256]{1,0:T(8,128)(2,1)S(1)}, bf16[656,256]{1,0:T(8,128)(2,1)S(1)}, u32[]{:S(2)}, u32[]{:S(2)}) %collective-permute-start.7) | collective-permute-done | bytes 335904 | tf_op jit(solution)/shard_map/ppermute | solution.py:72
  33.2 3.6 %collective-permute-done.4 = bf16[656,256]{1,0:T(8,128)(2,1)S(1)} collective-permute-done((bf16[656,256]{1,0:T(8,128)(2,1)S(1)}, bf16[656,256]{1,0:T(8,128)(2,1)S(1)}, u32[]{:S(2)}, u32[]{:S(2)}) %collective-permute-start.4) | collective-permute-done | bytes 335904 | tf_op jit(solution)/shard_map/ppermute | solution.py:72
  36.8 2.2 %collective-permute-start.17 = (bf16[640,256]{1,0:T(8,128)(2,1)}, bf16[640,256]{1,0:T(8,128)(2,1)S(1)}, u32[]{:S(2)}, u32[]{:S(2)}) collective-permute-start(bf16[640,256]{1,0:T(8,128)(2,1)} %extract.1), channel_id=1, source_target_pairs={{0,8},{1,7},{4,12},{5,3},{8,14},{9,1},{12,10},{13,5},{14,6},{15,9}... | collective-permute-start | bytes 983048 | tf_op jit(solution)/shard_map/ppermute | solution.py:72
  38.9 3.2 %collective-permute-start.19 = (bf16[640,256]{1,0:T(8,128)(2,1)}, bf16[640,256]{1,0:T(8,128)(2,1)S(1)}, u32[]{:S(2)}, u32[]{:S(2)}) collective-permute-start(bf16[640,256]{1,0:T(8,128)(2,1)} %extract.1), channel_id=1, source_target_pairs={{1,8},{0,7},{5,12},{4,3},{9,14},{8,1},{13,10},{12,5},{15,6},{14,9}... | collective-permute-start | bytes 983048 | tf_op jit(solution)/shard_map/ppermute | solution.py:72
  43.7 14.7 %weight_grad.1 = (f32[8,432,256]{2,1,0:T(8,128)}, bf16[2,432,256]{2,1,0:T(8,128)(2,1)}, bf16[2,432,256]{2,1,0:T(8,128)(2,1)}, bf16[2,432,256]{2,1,0:T(8,128)(2,1...) custom-call(s32[2,26]{1,0:T(2,128)} %refs_0_.1, ...), custom_call_target="tpu_custom_call" | custom-call | flops 12999999488 | tf_op jit(solution)/shard_map/weight_grad/pallas_call | solution.py:609
  58.4 2.7 %collective-permute-done.16 = bf16[640,256]{1,0:T(8,128)(2,1)S(1)} collective-permute-done((bf16[640,256]{1,0:T(8,128)(2,1)}, bf16[640,256]{1,0:T(8,128)(2,1)S(1)}, u32[]{:S(2)}, u32[]{:S(2)}) %collective-permute-start.16) | collective-permute-done | bytes 327712 | tf_op jit(solution)/shard_map/ppermute | solution.py:72
  64.7 2.3 %collective-permute-start.24 = (bf16[432,256]{1,0:T(8,128)(2,1)S(1)}, bf16[432,256]{1,0:T(8,128)(2,1)S(1)}, u32[]{:S(2)}, u32[]{:S(2)}) collective-permute-start(bf16[432,256]{1,0:T(8,128)(2,1)S(1)} %get-tuple-element.66), channel_id=1, source_target_pairs={{0,4},{1,5},{4,8},{5,9},{8,12},{9,13},{12,14},{13,15},{14,10},{15,... | collective-permute-start | bytes 663560 | tf_op jit(solution)/shard_map/ppermute | solution.py:72
  67.1 2.0 %collective-permute-start.25 = (bf16[640,256]{1,0:T(8,128)(2,1)S(1)}, bf16[640,256]{1,0:T(8,128)(2,1)S(1)}, u32[]{:S(2)}, u32[]{:S(2)}) collective-permute-start(bf16[640,256]{1,0:T(8,128)(2,1)S(1)} %collective-permute-done.17), channel_id=1, source_target_pairs={{0,4},{1,3},{4,8},{5,1},{8,12},{9,5},{12,14},{13,9},{14,10},{15,13... | collective-permute-start | bytes 983048 | tf_op jit(solution)/shard_map/ppermute | solution.py:72
  70.7 1.8 %collective-permute-done.24 = bf16[432,256]{1,0:T(8,128)(2,1)S(1)} collective-permute-done((bf16[432,256]{1,0:T(8,128)(2,1)S(1)}, bf16[432,256]{1,0:T(8,128)(2,1)S(1)}, u32[]{:S(2)}, u32[]{:S(2)}) %collective-permute-start.24) | collective-permute-done | bytes 221216 | tf_op jit(solution)/shard_map/ppermute | solution.py:72
  72.5 2.9 %collective-permute-done.38 = bf16[432,256]{1,0:T(8,128)(2,1)S(1)} collective-permute-done((bf16[432,256]{1,0:T(8,128)(2,1)S(1)}, bf16[432,256]{1,0:T(8,128)(2,1)S(1)}, u32[]{:S(2)}, u32[]{:S(2)}) %collective-permute-start.38) | collective-permute-done | bytes 221216 | tf_op jit(solution)/shard_map/ppermute | solution.py:72
  76.8 2.8 %collective-permute-done.26 = bf16[640,256]{1,0:T(8,128)(2,1)S(1)} collective-permute-done((bf16[640,256]{1,0:T(8,128)(2,1)S(1)}, bf16[640,256]{1,0:T(8,128)(2,1)S(1)}, u32[]{:S(2)}, u32[]{:S(2)}) %collective-permute-start.26) | collective-permute-done | bytes 327712 | tf_op jit(solution)/shard_map/ppermute | solution.py:72
  79.5 2.1 %collective-permute-start.27 = (bf16[432,256]{1,0:T(8,128)(2,1)S(1)}, bf16[432,256]{1,0:T(8,128)(2,1)S(1)}, u32[]{:S(2)}, u32[]{:S(2)}) collective-permute-start(bf16[432,256]{1,0:T(8,128)(2,1)S(1)} %get-tuple-element.51), channel_id=1, source_target_pairs={{0,4},{1,5},{4,8},{5,9},{8,12},{9,13},{12,14},{13,15},{14,10},{15,... | collective-permute-start | bytes 663560 | tf_op jit(solution)/shard_map/ppermute | solution.py:72
  83.2 4.0 %collective-permute-done.27 = bf16[432,256]{1,0:T(8,128)(2,1)S(1)} collective-permute-done((bf16[432,256]{1,0:T(8,128)(2,1)S(1)}, bf16[432,256]{1,0:T(8,128)(2,1)S(1)}, u32[]{:S(2)}, u32[]{:S(2)}) %collective-permute-start.27) | collective-permute-done | bytes 221216 | tf_op jit(solution)/shard_map/ppermute | solution.py:72
  93.1 5.5 %collective-permute-done.35 = bf16[640,256]{1,0:T(8,128)(2,1)S(1)} collective-permute-done((bf16[640,256]{1,0:T(8,128)(2,1)S(1)}, bf16[640,256]{1,0:T(8,128)(2,1)S(1)}, u32[]{:S(2)}, u32[]{:S(2)}) %collective-permute-start.35) | collective-permute-done | bytes 327712 | tf_op jit(solution)/shard_map/ppermute | solution.py:72
  99.0 2.0 %collective-permute-done.32 = bf16[432,256]{1,0:T(8,128)(2,1)S(1)} collective-permute-done((bf16[432,256]{1,0:T(8,128)(2,1)S(1)}, bf16[432,256]{1,0:T(8,128)(2,1)S(1)}, u32[]{:S(2)}, u32[]{:S(2)}) %collective-permute-start.32) | collective-permute-done | bytes 221216 | tf_op jit(solution)/shard_map/ppermute | solution.py:72
  103.7 11.7 %input_grad.1 = bf16[1024,256]{1,0:T(8,128)(2,1)} custom-call(s32[16,256]{1,0:T(8,128)} %get-tuple-element.54.refs_0_, s32[1,64]{1,0:T(1,128)} %refs_1_.1, s32[33]{0:T(128)} %dynamic-slice_bitcast_fusion.refs_1_.refs_2_, bf16[1024,256]{1,0:T(8,128)(2,1)} %refs_3_.3, bf16[1024,256]{1,0:T(8,128)(2,1)} %refs_4_.3, f32[1,256]{1,0:T(1,128)} %bitcast.96, ...), custom_call_target="tpu_custom_call" | custom-call | flops 12999999488 | tf_op jit(solution)/shard_map/input_grad/pallas_call | solution.py:653
  (134 shorter events, 27.4 us)
Async XLA Ops:
  3.3 10.6 %collective-permute-start.1 = (bf16[656,256]{1,0:T(8,128)(2,1)}, bf16[656,256]{1,0:T(8,128)(2,1)S(1)}, u32[]{:S(2)}, u32[]{:S(2)}) collective-permute-start(bf16[656,256]{1,0:T(8,128)(2,1)} %get-tuple-element.33), channel_id=1, source_target_pairs={{0,4},{1,3},{4,8},{5,1},{8,12},{9,5},{12,14},{13,9},{14,10},{15,13... | collective-permute-start | bytes 1007624 | tf_op jit(solution)/shard_map/ppermute | solution.py:72
  6.3 11.3 %collective-permute-start.5 = (bf16[656,256]{1,0:T(8,128)(2,1)}, bf16[656,256]{1,0:T(8,128)(2,1)S(1)}, u32[]{:S(2)}, u32[]{:S(2)}) collective-permute-start(bf16[656,256]{1,0:T(8,128)(2,1)} %get-tuple-element.33), channel_id=1, source_target_pairs={{1,4},{0,3},{5,8},{4,1},{9,12},{8,5},{13,14},{12,9},{15,10},{14,13... | collective-permute-start | bytes 1007624 | tf_op jit(solution)/shard_map/ppermute | solution.py:72
  31.2 10.9 %collective-permute-start.10 = (bf16[656,256]{1,0:T(8,128)(2,1)S(1)}, bf16[656,256]{1,0:T(8,128)(2,1)S(1)}, u32[]{:S(2)}, u32[]{:S(2)}) collective-permute-start(bf16[656,256]{1,0:T(8,128)(2,1)S(1)} %collective-permute-done.3), channel_id=1, source_target_pairs={{0,1},{1,0},{2,3},{3,2},{4,5},{5,4},{6,7},{7,6},{8,9},{9,8},{10,11... | collective-permute-start | bytes 1007624 | tf_op jit(solution)/shard_map/ppermute | solution.py:76
  33.2 9.3 %collective-permute-start.14 = (bf16[656,256]{1,0:T(8,128)(2,1)S(1)}, bf16[656,256]{1,0:T(8,128)(2,1)S(1)}, u32[]{:S(2)}, u32[]{:S(2)}) collective-permute-start(bf16[656,256]{1,0:T(8,128)(2,1)S(1)} %collective-permute-done.7), channel_id=1, source_target_pairs={{0,1},{1,0},{2,3},{3,2},{4,5},{5,4},{6,7},{7,6},{8,9},{9,8},{10,11... | collective-permute-start | bytes 1007624 | tf_op jit(solution)/shard_map/ppermute | solution.py:76
  36.8 21.6 %collective-permute-start.17 = (bf16[640,256]{1,0:T(8,128)(2,1)}, bf16[640,256]{1,0:T(8,128)(2,1)S(1)}, u32[]{:S(2)}, u32[]{:S(2)}) collective-permute-start(bf16[640,256]{1,0:T(8,128)(2,1)} %extract.1), channel_id=1, source_target_pairs={{0,8},{1,7},{4,12},{5,3},{8,14},{9,1},{12,10},{13,5},{14,6},{15,9}... | collective-permute-start | bytes 983048 | tf_op jit(solution)/shard_map/ppermute | solution.py:72
  38.9 19.5 %collective-permute-start.19 = (bf16[640,256]{1,0:T(8,128)(2,1)}, bf16[640,256]{1,0:T(8,128)(2,1)S(1)}, u32[]{:S(2)}, u32[]{:S(2)}) collective-permute-start(bf16[640,256]{1,0:T(8,128)(2,1)} %extract.1), channel_id=1, source_target_pairs={{1,8},{0,7},{5,12},{4,3},{9,14},{8,1},{13,10},{12,5},{15,6},{14,9}... | collective-permute-start | bytes 983048 | tf_op jit(solution)/shard_map/ppermute | solution.py:72
  42.1 16.3 %collective-permute-start.15 = (bf16[640,256]{1,0:T(8,128)(2,1)}, bf16[640,256]{1,0:T(8,128)(2,1)S(1)}, u32[]{:S(2)}, u32[]{:S(2)}) collective-permute-start(bf16[640,256]{1,0:T(8,128)(2,1)} %extract.1), channel_id=1, source_target_pairs={{0,1},{1,0},{2,3},{3,2},{4,5},{5,4},{6,7},{7,6},{8,9},{9,8},{10,11... | collective-permute-start | bytes 983048 | tf_op jit(solution)/shard_map/ppermute | solution.py:76
  42.5 18.6 %collective-permute-start.16 = (bf16[640,256]{1,0:T(8,128)(2,1)}, bf16[640,256]{1,0:T(8,128)(2,1)S(1)}, u32[]{:S(2)}, u32[]{:S(2)}) collective-permute-start(bf16[640,256]{1,0:T(8,128)(2,1)} %extract.1), channel_id=1, source_target_pairs={{0,4},{1,3},{4,8},{5,1},{8,12},{9,5},{12,14},{13,9},{14,10},{15,13... | collective-permute-start | bytes 983048 | tf_op jit(solution)/shard_map/ppermute | solution.py:72
  42.9 18.2 %collective-permute-start.18 = (bf16[640,256]{1,0:T(8,128)(2,1)}, bf16[640,256]{1,0:T(8,128)(2,1)S(1)}, u32[]{:S(2)}, u32[]{:S(2)}) collective-permute-start(bf16[640,256]{1,0:T(8,128)(2,1)} %extract.1), channel_id=1, source_target_pairs={{1,4},{0,3},{5,8},{4,1},{9,12},{8,5},{13,14},{12,9},{15,10},{14,13... | collective-permute-start | bytes 983048 | tf_op jit(solution)/shard_map/ppermute | solution.py:72
  61.9 8.8 %collective-permute-start.22 = (bf16[2,432,256]{2,1,0:T(8,128)(2,1)}, bf16[2,432,256]{2,1,0:T(8,128)(2,1)S(1)}, u32[]{:S(2)}, u32[]{:S(2)}) collective-permute-start(bf16[2,432,256]{2,1,0:T(8,128)(2,1)} %get-tuple-element.46), channel_id=1, source_target_pairs={{0,1},{1,0},{2,3},{3,2},{4,5},{5,4},{6,7},{7,6},{8,9},{9,8},{10,11... | collective-permute-start | bytes 1327112 | tf_op jit(solution)/shard_map/ppermute | solution.py:76
  67.1 9.6 %collective-permute-start.25 = (bf16[640,256]{1,0:T(8,128)(2,1)S(1)}, bf16[640,256]{1,0:T(8,128)(2,1)S(1)}, u32[]{:S(2)}, u32[]{:S(2)}) collective-permute-start(bf16[640,256]{1,0:T(8,128)(2,1)S(1)} %collective-permute-done.17), channel_id=1, source_target_pairs={{0,4},{1,3},{4,8},{5,1},{8,12},{9,5},{12,14},{13,9},{14,10},{15,13... | collective-permute-start | bytes 983048 | tf_op jit(solution)/shard_map/ppermute | solution.py:72
  69.1 10.4 %collective-permute-start.26 = (bf16[640,256]{1,0:T(8,128)(2,1)S(1)}, bf16[640,256]{1,0:T(8,128)(2,1)S(1)}, u32[]{:S(2)}, u32[]{:S(2)}) collective-permute-start(bf16[640,256]{1,0:T(8,128)(2,1)S(1)} %collective-permute-done.19), channel_id=1, source_target_pairs={{0,4},{1,3},{4,8},{5,1},{8,12},{9,5},{12,14},{13,9},{14,10},{15,13... | collective-permute-start | bytes 983048 | tf_op jit(solution)/shard_map/ppermute | solution.py:72
  70.7 12.1 %collective-permute-start.21 = (bf16[2,432,256]{2,1,0:T(8,128)(2,1)}, bf16[2,432,256]{2,1,0:T(8,128)(2,1)S(1)}, u32[]{:S(2)}, u32[]{:S(2)}) collective-permute-start(bf16[2,432,256]{2,1,0:T(8,128)(2,1)} %get-tuple-element.44), channel_id=1, source_target_pairs={{0,1},{1,0},{2,3},{3,2},{4,5},{5,4},{6,7},{7,6},{8,9},{9,8},{10,11... | collective-permute-start | bytes 1327112 | tf_op jit(solution)/shard_map/ppermute | solution.py:76
  72.5 10.2 %collective-permute-start.29 = (bf16[640,256]{1,0:T(8,128)(2,1)S(1)}, bf16[640,256]{1,0:T(8,128)(2,1)S(1)}, u32[]{:S(2)}, u32[]{:S(2)}) collective-permute-start(bf16[640,256]{1,0:T(8,128)(2,1)S(1)} %collective-permute-done.17), channel_id=1, source_target_pairs={{0,1},{1,0},{2,3},{3,2},{4,5},{5,4},{6,7},{7,6},{8,9},{9,8},{10,11... | collective-permute-start | bytes 983048 | tf_op jit(solution)/shard_map/ppermute | solution.py:76
  81.6 9.7 %collective-permute-start.31 = (bf16[640,256]{1,0:T(8,128)(2,1)S(1)}, bf16[640,256]{1,0:T(8,128)(2,1)S(1)}, u32[]{:S(2)}, u32[]{:S(2)}) collective-permute-start(bf16[640,256]{1,0:T(8,128)(2,1)S(1)} %collective-permute-done.19), channel_id=1, source_target_pairs={{0,1},{1,0},{2,3},{3,2},{4,5},{5,4},{6,7},{7,6},{8,9},{9,8},{10,11... | collective-permute-start | bytes 983048 | tf_op jit(solution)/shard_map/ppermute | solution.py:76
  82.7 8.6 %collective-permute-start.28 = (bf16[640,256]{1,0:T(8,128)(2,1)S(1)}, bf16[640,256]{1,0:T(8,128)(2,1)S(1)}, u32[]{:S(2)}, u32[]{:S(2)}) collective-permute-start(bf16[640,256]{1,0:T(8,128)(2,1)S(1)} %collective-permute-done.16), channel_id=1, source_target_pairs={{0,1},{1,0},{2,3},{3,2},{4,5},{5,4},{6,7},{7,6},{8,9},{9,8},{10,11... | collective-permute-start | bytes 983048 | tf_op jit(solution)/shard_map/ppermute | solution.py:76
  82.8 8.6 %collective-permute-start.30 = (bf16[640,256]{1,0:T(8,128)(2,1)S(1)}, bf16[640,256]{1,0:T(8,128)(2,1)S(1)}, u32[]{:S(2)}, u32[]{:S(2)}) collective-permute-start(bf16[640,256]{1,0:T(8,128)(2,1)S(1)} %collective-permute-done.18), channel_id=1, source_target_pairs={{0,1},{1,0},{2,3},{3,2},{4,5},{5,4},{6,7},{7,6},{8,9},{9,8},{10,11... | collective-permute-start | bytes 983048 | tf_op jit(solution)/shard_map/ppermute | solution.py:76
  87.3 11.4 %collective-permute-start.20 = (bf16[2,432,256]{2,1,0:T(8,128)(2,1)S(1)}, bf16[2,432,256]{2,1,0:T(8,128)(2,1)S(1)}, u32[]{:S(2)}, u32[]{:S(2)}) collective-permute-start(bf16[2,432,256]{2,1,0:T(8,128)(2,1)S(1)} %copy-done.1), channel_id=1, source_target_pairs={{0,1},{1,0},{2,3},{3,2},{4,5},{5,4},{6,7},{7,6},{8,9},{9,8},{10,11... | collective-permute-start | bytes 1327112 | tf_op jit(solution)/shard_map/ppermute | solution.py:76
  89.7 8.9 %collective-permute-start.35 = (bf16[640,256]{1,0:T(8,128)(2,1)S(1)}, bf16[640,256]{1,0:T(8,128)(2,1)S(1)}, u32[]{:S(2)}, u32[]{:S(2)}) collective-permute-start(bf16[640,256]{1,0:T(8,128)(2,1)S(1)} %collective-permute-done.25), channel_id=1, source_target_pairs={{0,4},{1,3},{4,8},{5,1},{8,12},{9,5},{12,14},{13,9},{14,10},{15,13... | collective-permute-start | bytes 983048 | tf_op jit(solution)/shard_map/ppermute | solution.py:72
  91.4 9.6 %collective-permute-start.32 = (bf16[432,256]{1,0:T(8,128)(2,1)S(1)}, bf16[432,256]{1,0:T(8,128)(2,1)S(1)}, u32[]{:S(2)}, u32[]{:S(2)}) collective-permute-start(bf16[432,256]{1,0:T(8,128)(2,1)S(1)} %get-tuple-element.52), channel_id=1, source_target_pairs={{0,4},{1,5},{4,8},{5,9},{8,12},{9,13},{12,14},{13,15},{14,10},{15,... | collective-permute-start | bytes 663560 | tf_op jit(solution)/shard_map/ppermute | solution.py:72
  92.6 8.5 %collective-permute-start.33 = (bf16[640,256]{1,0:T(8,128)(2,1)S(1)}, bf16[640,256]{1,0:T(8,128)(2,1)S(1)}, u32[]{:S(2)}, u32[]{:S(2)}) collective-permute-start(bf16[640,256]{1,0:T(8,128)(2,1)S(1)} %collective-permute-done.25), channel_id=1, source_target_pairs={{0,1},{1,0},{2,3},{3,2},{4,5},{5,4},{6,7},{7,6},{8,9},{9,8},{10,11... | collective-permute-start | bytes 983048 | tf_op jit(solution)/shard_map/ppermute | solution.py:76
  92.6 8.5 %collective-permute-start.34 = (bf16[640,256]{1,0:T(8,128)(2,1)S(1)}, bf16[640,256]{1,0:T(8,128)(2,1)S(1)}, u32[]{:S(2)}, u32[]{:S(2)}) collective-permute-start(bf16[640,256]{1,0:T(8,128)(2,1)S(1)} %collective-permute-done.26), channel_id=1, source_target_pairs={{0,1},{1,0},{2,3},{3,2},{4,5},{5,4},{6,7},{7,6},{8,9},{9,8},{10,11... | collective-permute-start | bytes 983048 | tf_op jit(solution)/shard_map/ppermute | solution.py:76
  98.7 16.8 %collective-permute-start.40 = (bf16[432,256]{1,0:T(8,128)(2,1)S(1)}, bf16[432,256]{1,0:T(8,128)(2,1)S(1)}, u32[]{:S(2)}, u32[]{:S(2)}) collective-permute-start(bf16[432,256]{1,0:T(8,128)(2,1)S(1)} %get-tuple-element.58), channel_id=1, source_target_pairs={{0,2},{1,3},{4,0},{5,1},{8,4},{9,5},{12,8},{13,9},{14,12},{15,13},... | collective-permute-start | bytes 663560 | tf_op jit(solution)/shard_map/ppermute | solution.py:72
  101.2 14.3 %collective-permute-start.37 = (bf16[432,256]{1,0:T(8,128)(2,1)S(1)}, bf16[432,256]{1,0:T(8,128)(2,1)S(1)}, u32[]{:S(2)}, u32[]{:S(2)}) collective-permute-start(bf16[432,256]{1,0:T(8,128)(2,1)S(1)} %fusion.5), channel_id=1, source_target_pairs={{0,4},{1,5},{4,8},{5,9},{8,12},{9,13},{12,14},{13,15},{14,10},{15,... | collective-permute-start | bytes 663560 | tf_op jit(solution)/shard_map/ppermute | solution.py:72
  (50 other events, 696.5 us)

commit v16 on v9

--- a/solution.py
+++ b/solution.py
@@ -12,10 +12,16 @@
 F32 = jnp.float32
 BF16 = jnp.bfloat16
 C = 256
-C_LINES = 128
-B_LINES = 224
-ROWS = 320
+B_LINES = 128
+ROWS = 224
+C_ROWS = 72
 NOTES = 16
+
+
+def payload_rows(bricks):
+    return -(-bricks * (ROWS + C_ROWS) // 16) * 16
+
+
 HB = 24
 VMEM_LIMIT = 56 * 1024 * 1024
 DIRECTIONS = [
@@ -158,39 +164,34 @@
 PLANES = 4
 
 
-def put_boundary(rows, base, a, out_ref, stage):
+def put_boundary(rows, brick, a, out_ref, stage, ends):
+    base = brick * ROWS
+    if a in (0, 7):
+        at = base if a == 0 else base + 64
+        out_ref[at : at + 64, :] = rows
+        return
     wide = rows.astype(F32)
-
-    def put(at, value, lanes=slice(None)):
-        out_ref[pl.ds(pl.multiple_of(base + at, 16), value.shape[0]), lanes] = value
-
-    if a in (0, 7):
-        put(0 if a == 0 else 64, rows)
-        return
+    at = base + B_LINES - 16 + 16 * a
+    out_ref[at : at + 16, :] = jnp.concatenate([wide[:8], wide[56:]], axis=0).astype(BF16)
+    at = brick * C_ROWS + 12 * (a - 1)
     for half in range(2):
         lanes = slice(half * 128, half * 128 + 128)
         stage[half] = wide[:, lanes]
-        first = stage[half, pl.ds(0, 8, stride=8), :]
-        last = stage[half, pl.ds(7, 8, stride=8), :]
-        put(C_LINES - 16 + 16 * a, jnp.concatenate([first, last], axis=0).astype(BF16), lanes)
-    pair = jnp.concatenate([wide[:8], wide[56:]], axis=0).astype(BF16)
-    put(B_LINES - 16 + 16 * a, pair)
-
-
-def each_brick(rows_of, bricks, out_ref, stage):
-    def step(brick, _):
+        ends[at : at + 6, lanes] = stage[half, pl.ds(8, 6, stride=8), :]
+        ends[at + 6 : at + 12, lanes] = stage[half, pl.ds(15, 6, stride=8), :]
+
+
+def each_brick(rows_of, bricks, out_ref, stage, ends):
+    for brick in range(bricks):
         for first in range(0, 8, PLANES):
-            at = pl.multiple_of(brick * 512 + first * 64, 64)
-            rows = rows_of(pl.ds(at, PLANES * 64))
+            rows = rows_of(pl.ds(brick * 512 + first * 64, PLANES * 64))
             for t in range(PLANES):
                 plane = rows[t * 64 : t * 64 + 64]
-                put_boundary(plane, brick * ROWS, first + t, out_ref, stage.at[first + t])
-        return 0
-
-    lax.fori_loop(0, bricks, step, 0)
-
-
-def norm_body(recv, send, x_ref, gain_ref, hidden_ref, out_ref, stage):
+                put_boundary(plane, brick, first + t, out_ref, stage.at[first + t], ends)
+    out_ref[bricks * ROWS : payload_rows(bricks), :] = ends[...].astype(BF16)
+
+
+def norm_body(recv, send, x_ref, gain_ref, hidden_ref, out_ref, stage, ends):
     bricks, directions = recv.shape
     gain = gain_ref[...]
     lane = lax.broadcasted_iota(jnp.int32, (1, C), 1)
@@ -203,7 +204,7 @@
             served = jnp.where(lane == recv[brick, number], brick * directions + number + 1, served)
     row = lax.broadcasted_iota(jnp.int32, (NOTES, C), 0)
     notes = jnp.where(row == 0, codes, jnp.where(row == 1, served, 0))
-    out_ref[bricks * ROWS :, :] = notes.astype(F32).astype(BF16)
+    out_ref[payload_rows(bricks) :, :] = notes.astype(F32).astype(BF16)
 
     def rows_of(at):
         x = x_ref[at, :].astype(F32)
@@ -213,11 +214,11 @@
         hidden_ref[at, :] = rows
         return rows
 
-    each_brick(rows_of, bricks, out_ref, stage)
-
-
-def extract_body(x_ref, out_ref, stage):
-    each_brick(lambda at: x_ref[at, :], x_ref.shape[0] // 512, out_ref, stage)
+    each_brick(rows_of, bricks, out_ref, stage, ends)
+
+
+def extract_body(x_ref, out_ref, stage, ends):
+    each_brick(lambda at: x_ref[at, :], x_ref.shape[0] // 512, out_ref, stage, ends)
 
 
 def start_padded(own_ref, cells, halo, bricks):
@@ -265,6 +266,16 @@
 
     def half(pair, axis):
         return pick(flags[axis], pair[8:], pair[:8])
+
+    def ends(a):
+        value = None
+        for number in range(cells.shape[0] // 100):
+            at = cells.shape[0] // 100 * ROWS + number * C_ROWS + 12 * (a - 1)
+            block = share[place_at, at // 16 * 16 : -(-(at + 12) // 16) * 16, :].astype(F32)
+            block = block[at % 16 : at % 16 + 12]
+            block = pick(flags[2], block[6:], block[:6])
+            value = block if value is None else jnp.where(source_brick == number, block, value)
+        return value if keep is None else jnp.where(keep, value, 0.0)
 
     def line_b(at):
         plane = rows(at, 64)
@@ -308,7 +319,10 @@
             if a in (0, 7):
                 line = line_c(0 if a == 0 else 64)
             else:
-                line = half(rows(C_LINES - 16 + 16 * a, 16), 2)
+                pair = rows(B_LINES - 16 + 16 * a, 16)
+                low = pick(flags[2], pair[7:8], pair[0:1])
+                high = pick(flags[2], pair[15:], pair[8:9])
+                line = jnp.concatenate([low, ends(a), high], axis=0)
             add_halo(a + 1, line)
     elif kind == (1, 1, 0):
         add_line(cells, (base + pads[0]) * 10 + pads[1], line_b(facing))
@@ -319,8 +333,8 @@
             if a in (0, 7):
                 value = cell(0 if a == 0 else 64)
             else:
-                line = half(rows(C_LINES - 16 + 16 * a, 16), 2)
-                value = pick(flags[1], line[7:8], line[0:1])
+                line = half(rows(B_LINES - 16 + 16 * a, 16), 1)
+                value = pick(flags[2], line[7:8], line[0:1])
             add_cell(a + 1, value)
     else:
         add_cell(pads[0], cell(facing))
@@ -380,15 +394,15 @@
     sems, cols_sems, codes_sem, out_sems, notes_sems = refs[-5:]
     bricks = own_ref.shape[0] // 512
     me = table[2 * peers]
-    notes_copies = fetch(parts, share, notes_sems, bricks * ROWS, NOTES)
-    copies = fetch(parts, share, sems, 0, bricks * ROWS)
+    notes_copies = fetch(parts, share, notes_sems, payload_rows(bricks), NOTES)
+    copies = fetch(parts, share, sems, 0, payload_rows(bricks))
     for part in range(bricks * 2):
         at = slice(part * 256, part * 256 + 256)
         turned[:, at] = cot_ref[at, :].astype(F32).T.astype(BF16)
     for copy in notes_copies:
         copy.wait()
     for k in range(peers):
-        notes = share[k, bricks * ROWS :, :].astype(F32).astype(jnp.int32)
+        notes = share[k, payload_rows(bricks) :, :].astype(F32).astype(jnp.int32)
         codes_ref[k : k + 1, :] = notes[0:1]
         served_ref[k : k + 1, :] = notes[1:2]
     codes_copy = pltpu.make_async_copy(codes_ref, codes, codes_sem.at[0])
@@ -599,7 +613,11 @@
     factor = 1.0 / math.sqrt(peers * per_device)
     gain = norm_gain.reshape(1, channels)
     sds = jax.ShapeDtypeStruct
-    stage = pltpu.VMEM((8, 2, 64, 128), F32)
+    share_rows = payload_rows(bricks)
+    stage = [
+        pltpu.VMEM((8, 2, 64, 128), F32),
+        pltpu.VMEM((share_rows - bricks * ROWS, channels), F32),
+    ]
 
     def padded(n):
         return [
@@ -615,17 +633,17 @@
 
     hidden, share = call(
         norm_body,
-        (sds((per_device, channels), BF16), sds((bricks * ROWS + NOTES, channels), BF16)),
+        (sds((per_device, channels), BF16), sds((share_rows + NOTES, channels), BF16)),
         [SMEM, SMEM, VMEM, VMEM],
-        [stage],
+        stage,
         name="norm",
     )(recv_slot, send_face, features, gain)
     hidden_ring = RingGather(share, peers)
     cot_share = call(
         extract_body,
-        sds((bricks * ROWS, channels), BF16),
+        sds((share_rows, channels), BF16),
         [VMEM],
-        [stage],
+        stage,
         name="extract",
     )(cotangent)
     hidden_ring.go(0)
@@ -656,7 +674,7 @@
         [SMEM] * 2 + [VMEM] * 2 + [HBM] * count,
         padded(bricks)
         + [
-            pltpu.VMEM((peers, bricks * ROWS + NOTES, channels), BF16),
+            pltpu.VMEM((peers, share_rows + NOTES, channels), BF16),
             pltpu.VMEM(cols_shape(bricks), BF16),
             pltpu.VMEM((2, chips, rows, channels), F32),
             pltpu.VMEM((2, chips, rows, channels), BF16),
@@ -710,7 +728,7 @@
         padded(bricks)
         + [
             pltpu.VMEM(cols_shape(bricks), BF16),
-            pltpu.VMEM((peers, bricks * ROWS, channels), BF16),
+            pltpu.VMEM((peers, share_rows, channels), BF16),
             weight_scratch[0],
             pltpu.SMEM((bricks * 26,), jnp.int32),
             pltpu.SMEM((peers * slots,), jnp.int32),

time: 111 us -> 108 us (0.973)
  waiting for transfers between devices: 36.3 us -> 34 us
    ppermute x21, waiting for transfers between devices: 36.2 us -> 33.9 us  [ring_step(): return lax.ppermute(x, 'morton', pairs)]
where the time goes in v16:
time: 108 us
  Pallas kernels  36.1 us (33%)
  waiting for transfers between devices  34 us (31%)
  starting transfers between devices  31.2 us (29%)
  local copies, waits for them, and re-layouts  2.89 us (3%)
  other arithmetic  2.53 us (2%)
  between operations  1.14 us (1%)
    ppermute x21, waiting for transfers between devices, ring_step(): return lax.ppermute(x, 'morton', pairs)  33.9 us
    ppermute x21, starting transfers between devices, ring_step(): return lax.ppermute(x, 'morton', pairs)  27.4 us
    pallas_call x1, Pallas kernels, local(): call(functools.partial(input_grad_body, slots, peers, count), sds((per_de...  12.1 us
    pallas_call x1, Pallas kernels, local(): call(functools.partial(weight_grad_body, slots, factor, peers, count), (s...  11.9 us
    pallas_call x1, Pallas kernels, local(): call(mix_body, sds((per_device, channels), BF16), [HBM, HBM, VMEM], [pltp...  7.69 us
    ppermute x20, starting transfers between devices, swap_cores(): return lax.ppermute(x, 'morton', [(m, m ^ 1) for m in range(peers)])  3.79 us
    pallas_call x1, Pallas kernels, local(): call(norm_body, (sds((per_device, channels), BF16), sds((share_rows + NOT...  2.5 us
  transfers between devices with their start and end apart: 41, of which 10 were waited for; matrix products, arithmetic and copies ran while one was open for 3% of the time, Pallas kernels for 31%

profile of v16, /device:TPU:0, one launch (start us, length us, event | category | flops | bytes accessed | tf_op | source)
XLA Modules:
  0.0 107.8 jit_solution(13519405678260693569)
XLA Ops:
  0.6 2.5 %norm.1 = (bf16[1024,256]{1,0:T(8,128)(2,1)}, bf16[608,256]{1,0:T(8,128)(2,1)}) custom-call(s32[2,26]{1,0:T(2,128)} %refs_0_.1, s32[1,64]{1,0:T(1,128)} %refs_1_.1, bf16[1024,256]{1,0:T(8,128)(2,1)} %refs_4_.1, f32[1,256]{1,0:T(1,128)} %bitcast.95), custom_call_target="tpu_custom_call" | custom-call | flops 2000000000 | tf_op jit(solution)/shard_map/norm/pallas_call | solution.py:634
  3.1 3.0 %collective-permute-start.1 = (bf16[608,256]{1,0:T(8,128)(2,1)}, bf16[608,256]{1,0:T(8,128)(2,1)S(1)}, u32[]{:S(2)}, u32[]{:S(2)}) collective-permute-start(bf16[608,256]{1,0:T(8,128)(2,1)} %get-tuple-element.35), channel_id=1, source_target_pairs={{0,4},{1,3},{4,8},{5,1},{8,12},{9,5},{12,14},{13,9},{14,10},{15,13... | collective-permute-start | bytes 933896 | tf_op jit(solution)/shard_map/ppermute | solution.py:78
  6.8 1.8 %extract.1 = bf16[592,256]{1,0:T(8,128)(2,1)} custom-call(bf16[1024,256]{1,0:T(8,128)(2,1)} %refs_3_.3), custom_call_target="tpu_custom_call" | custom-call | flops 2000000000 | tf_op jit(solution)/shard_map/extract/pallas_call | solution.py:642
  8.7 4.5 %collective-permute-done.1 = bf16[608,256]{1,0:T(8,128)(2,1)S(1)} collective-permute-done((bf16[608,256]{1,0:T(8,128)(2,1)}, bf16[608,256]{1,0:T(8,128)(2,1)S(1)}, u32[]{:S(2)}, u32[]{:S(2)}) %collective-permute-start.1) | collective-permute-done | bytes 311328 | tf_op jit(solution)/shard_map/ppermute | solution.py:78
  13.2 2.4 %collective-permute-start.2 = (bf16[608,256]{1,0:T(8,128)(2,1)S(1)}, bf16[608,256]{1,0:T(8,128)(2,1)S(1)}, u32[]{:S(2)}, u32[]{:S(2)}) collective-permute-start(bf16[608,256]{1,0:T(8,128)(2,1)S(1)} %collective-permute-done.1), channel_id=1, source_target_pairs={{0,4},{1,3},{4,8},{5,1},{8,12},{9,5},{12,14},{13,9},{14,10},{15,13... | collective-permute-start | bytes 933896 | tf_op jit(solution)/shard_map/ppermute | solution.py:78
  15.6 1.2 %dynamic-slice_bitcast_fusion.refs_1_.refs_2_ = s32[33]{0:T(128)} fusion(s32[16,33]{1,0:T(8,128)} %constant.10.clone, s32[]{:T(128)S(6)} %select_n.3), kind=kLoop, calls=%fused_computation.16 | loop fusion | bytes 268 | tf_op jit(solution)/shard_map/squeeze | solution.py:632
  16.8 1.6 %collective-permute-start.6 = (bf16[608,256]{1,0:T(8,128)(2,1)S(1)}, bf16[608,256]{1,0:T(8,128)(2,1)S(1)}, u32[]{:S(2)}, u32[]{:S(2)}) collective-permute-start(bf16[608,256]{1,0:T(8,128)(2,1)S(1)} %collective-permute-done.5), channel_id=1, source_target_pairs={{0,4},{1,3},{4,8},{5,1},{8,12},{9,5},{12,14},{13,9},{14,10},{15,13... | collective-permute-start | bytes 933896 | tf_op jit(solution)/shard_map/ppermute | solution.py:78
  18.4 3.0 %collective-permute-done.2 = bf16[608,256]{1,0:T(8,128)(2,1)S(1)} collective-permute-done((bf16[608,256]{1,0:T(8,128)(2,1)S(1)}, bf16[608,256]{1,0:T(8,128)(2,1)S(1)}, u32[]{:S(2)}, u32[]{:S(2)}) %collective-permute-start.2) | collective-permute-done | bytes 311328 | tf_op jit(solution)/shard_map/ppermute | solution.py:78
  23.0 1.7 %collective-permute-done.6 = bf16[608,256]{1,0:T(8,128)(2,1)S(1)} collective-permute-done((bf16[608,256]{1,0:T(8,128)(2,1)S(1)}, bf16[608,256]{1,0:T(8,128)(2,1)S(1)}, u32[]{:S(2)}, u32[]{:S(2)}) %collective-permute-start.6) | collective-permute-done | bytes 311328 | tf_op jit(solution)/shard_map/ppermute | solution.py:78
  25.8 2.5 %collective-permute-done.3 = bf16[608,256]{1,0:T(8,128)(2,1)S(1)} collective-permute-done((bf16[608,256]{1,0:T(8,128)(2,1)S(1)}, bf16[608,256]{1,0:T(8,128)(2,1)S(1)}, u32[]{:S(2)}, u32[]{:S(2)}) %collective-permute-start.3) | collective-permute-done | bytes 311328 | tf_op jit(solution)/shard_map/ppermute | solution.py:78
  30.0 1.6 %collective-permute-done.7 = bf16[608,256]{1,0:T(8,128)(2,1)S(1)} collective-permute-done((bf16[608,256]{1,0:T(8,128)(2,1)S(1)}, bf16[608,256]{1,0:T(8,128)(2,1)S(1)}, u32[]{:S(2)}, u32[]{:S(2)}) %collective-permute-start.7) | collective-permute-done | bytes 311328 | tf_op jit(solution)/shard_map/ppermute | solution.py:78
  31.6 3.6 %collective-permute-done.4 = bf16[608,256]{1,0:T(8,128)(2,1)S(1)} collective-permute-done((bf16[608,256]{1,0:T(8,128)(2,1)S(1)}, bf16[608,256]{1,0:T(8,128)(2,1)S(1)}, u32[]{:S(2)}, u32[]{:S(2)}) %collective-permute-start.4) | collective-permute-done | bytes 311328 | tf_op jit(solution)/shard_map/ppermute | solution.py:78
  36.4 2.3 %collective-permute-start.16 = (bf16[592,256]{1,0:T(8,128)(2,1)}, bf16[592,256]{1,0:T(8,128)(2,1)S(1)}, u32[]{:S(2)}, u32[]{:S(2)}) collective-permute-start(bf16[592,256]{1,0:T(8,128)(2,1)} %extract.1), channel_id=1, source_target_pairs={{1,4},{0,3},{5,8},{4,1},{9,12},{8,5},{13,14},{12,9},{15,10},{14,13... | collective-permute-start | bytes 909320 | tf_op jit(solution)/shard_map/ppermute | solution.py:78
  39.6 11.9 %weight_grad.1 = (f32[8,432,256]{2,1,0:T(8,128)}, bf16[2,432,256]{2,1,0:T(8,128)(2,1)}, bf16[2,432,256]{2,1,0:T(8,128)(2,1)}, bf16[2,432,256]{2,1,0:T(8,128)(2,1...) custom-call(s32[2,26]{1,0:T(2,128)} %refs_0_.1, ...), custom_call_target="tpu_custom_call" | custom-call | flops 8999999488 | tf_op jit(solution)/shard_map/weight_grad/pallas_call | solution.py:665
  52.8 2.3 %collective-permute-start.22 = (bf16[592,256]{1,0:T(8,128)(2,1)S(1)}, bf16[592,256]{1,0:T(8,128)(2,1)S(1)}, u32[]{:S(2)}, u32[]{:S(2)}) collective-permute-start(bf16[592,256]{1,0:T(8,128)(2,1)S(1)} %collective-permute-done.15), channel_id=1, source_target_pairs={{0,4},{1,3},{4,8},{5,1},{8,12},{9,5},{12,14},{13,9},{14,10},{15,13... | collective-permute-start | bytes 909320 | tf_op jit(solution)/shard_map/ppermute | solution.py:78
  55.1 1.2 %fusion.7 = (bf16[432,256]{1,0:T(8,128)(2,1)S(1)}, bf16[432,256]{1,0:T(8,128)(2,1)S(1)}) fusion(f32[8,432,256]{2,1,0:T(8,128)} %get-tuple-element.39, bf16[2,432,256]{2,1,0:T(8,128)(2,1)S(1)} %collective-permute-done.17), kind=kLoop, calls=%fused_computation.15 | loop fusion | flops 663552 | bytes 1769472 | tf_op jit(solution)/shard_map/convert_element_type | solution.py:138
  56.9 1.6 %collective-permute-start.38 = (bf16[432,256]{1,0:T(8,128)(2,1)S(1)}, bf16[432,256]{1,0:T(8,128)(2,1)S(1)}, u32[]{:S(2)}, u32[]{:S(2)}) collective-permute-start(bf16[432,256]{1,0:T(8,128)(2,1)S(1)} %get-tuple-element.69), channel_id=1, source_target_pairs={{0,2},{1,3},{4,0},{5,1},{8,4},{9,5},{12,8},{13,9},{14,12},{15,13},... | collective-permute-start | bytes 663560 | tf_op jit(solution)/shard_map/ppermute | solution.py:78
  58.5 7.7 %mix.1 = bf16[1024,256]{1,0:T(8,128)(2,1)} custom-call(bf16[20,64,2304]{2,1,0:T(8,128)(2,1)} %get-tuple-element.44.cols_ref, bf16[6912,256]{1,0:T(8,128)(2,1)} %refs_6_.1, bf16[1024,256]{1,0:T(8,128)(2,1)} %refs_4_.1), custom_call_target="tpu_custom_call" | custom-call | flops 6000000000 | tf_op jit(solution)/shard_map/mix/pallas_call | solution.py:706
  69.3 1.2 %collective-permute-start.39 = (bf16[432,256]{1,0:T(8,128)(2,1)S(1)}, bf16[432,256]{1,0:T(8,128)(2,1)S(1)}, u32[]{:S(2)}, u32[]{:S(2)}) collective-permute-start(bf16[432,256]{1,0:T(8,128)(2,1)S(1)} %get-tuple-element.63), channel_id=1, source_target_pairs={{0,2},{1,3},{4,0},{5,1},{8,4},{9,5},{12,8},{13,9},{14,12},{15,13},... | collective-permute-start | bytes 663560 | tf_op jit(solution)/shard_map/ppermute | solution.py:78
  70.4 8.3 %collective-permute-done.25 = bf16[592,256]{1,0:T(8,128)(2,1)S(1)} collective-permute-done((bf16[592,256]{1,0:T(8,128)(2,1)S(1)}, bf16[592,256]{1,0:T(8,128)(2,1)S(1)}, u32[]{:S(2)}, u32[]{:S(2)}) %collective-permute-start.25) | collective-permute-done | bytes 303136 | tf_op jit(solution)/shard_map/ppermute | solution.py:78
  81.8 3.8 %collective-permute-done.28 = bf16[592,256]{1,0:T(8,128)(2,1)S(1)} collective-permute-done((bf16[592,256]{1,0:T(8,128)(2,1)S(1)}, bf16[592,256]{1,0:T(8,128)(2,1)S(1)}, u32[]{:S(2)}, u32[]{:S(2)}) %collective-permute-start.28) | collective-permute-done | bytes 303136 | tf_op jit(solution)/shard_map/ppermute | solution.py:78
  87.6 4.1 %collective-permute-done.27 = bf16[432,256]{1,0:T(8,128)(2,1)S(1)} collective-permute-done((bf16[432,256]{1,0:T(8,128)(2,1)S(1)}, bf16[432,256]{1,0:T(8,128)(2,1)S(1)}, u32[]{:S(2)}, u32[]{:S(2)}) %collective-permute-start.27) | collective-permute-done | bytes 221216 | tf_op jit(solution)/shard_map/ppermute | solution.py:78
  92.2 1.6 %collective-permute-start.37 = (bf16[432,256]{1,0:T(8,128)(2,1)S(1)}, bf16[432,256]{1,0:T(8,128)(2,1)S(1)}, u32[]{:S(2)}, u32[]{:S(2)}) collective-permute-start(bf16[432,256]{1,0:T(8,128)(2,1)S(1)} %fusion.5), channel_id=1, source_target_pairs={{0,4},{1,5},{4,8},{5,9},{8,12},{9,13},{12,14},{13,15},{14,10},{15,... | collective-permute-start | bytes 663560 | tf_op jit(solution)/shard_map/ppermute | solution.py:78
  94.8 12.1 %input_grad.1 = bf16[1024,256]{1,0:T(8,128)(2,1)} custom-call(s32[16,256]{1,0:T(8,128)} %get-tuple-element.57.refs_0_, s32[1,64]{1,0:T(1,128)} %refs_1_.1, s32[33]{0:T(128)} %dynamic-slice_bitcast_fusion.refs_1_.refs_2_, bf16[1024,256]{1,0:T(8,128)(2,1)} %refs_3_.3, bf16[1024,256]{1,0:T(8,128)(2,1)} %refs_4_.1, f32[1,256]{1,0:T(1,128)} %bitcast.96, ...), custom_call_target="tpu_custom_call" | custom-call | flops 12999999488 | tf_op jit(solution)/shard_map/input_grad/pallas_call | solution.py:724
  (139 shorter events, 19.1 us)
Async XLA Ops:
  3.1 10.1 %collective-permute-start.1 = (bf16[608,256]{1,0:T(8,128)(2,1)}, bf16[608,256]{1,0:T(8,128)(2,1)S(1)}, u32[]{:S(2)}, u32[]{:S(2)}) collective-permute-start(bf16[608,256]{1,0:T(8,128)(2,1)} %get-tuple-element.35), channel_id=1, source_target_pairs={{0,4},{1,3},{4,8},{5,1},{8,12},{9,5},{12,14},{13,9},{14,10},{15,13... | collective-permute-start | bytes 933896 | tf_op jit(solution)/shard_map/ppermute | solution.py:78
  6.2 10.7 %collective-permute-start.5 = (bf16[608,256]{1,0:T(8,128)(2,1)}, bf16[608,256]{1,0:T(8,128)(2,1)S(1)}, u32[]{:S(2)}, u32[]{:S(2)}) collective-permute-start(bf16[608,256]{1,0:T(8,128)(2,1)} %get-tuple-element.35), channel_id=1, source_target_pairs={{1,4},{0,3},{5,8},{4,1},{9,12},{8,5},{13,14},{12,9},{15,10},{14,13... | collective-permute-start | bytes 933896 | tf_op jit(solution)/shard_map/ppermute | solution.py:78
  13.2 8.2 %collective-permute-start.2 = (bf16[608,256]{1,0:T(8,128)(2,1)S(1)}, bf16[608,256]{1,0:T(8,128)(2,1)S(1)}, u32[]{:S(2)}, u32[]{:S(2)}) collective-permute-start(bf16[608,256]{1,0:T(8,128)(2,1)S(1)} %collective-permute-done.1), channel_id=1, source_target_pairs={{0,4},{1,3},{4,8},{5,1},{8,12},{9,5},{12,14},{13,9},{14,10},{15,13... | collective-permute-start | bytes 933896 | tf_op jit(solution)/shard_map/ppermute | solution.py:78
  16.8 7.9 %collective-permute-start.6 = (bf16[608,256]{1,0:T(8,128)(2,1)S(1)}, bf16[608,256]{1,0:T(8,128)(2,1)S(1)}, u32[]{:S(2)}, u32[]{:S(2)}) collective-permute-start(bf16[608,256]{1,0:T(8,128)(2,1)S(1)} %collective-permute-done.5), channel_id=1, source_target_pairs={{0,4},{1,3},{4,8},{5,1},{8,12},{9,5},{12,14},{13,9},{14,10},{15,13... | collective-permute-start | bytes 933896 | tf_op jit(solution)/shard_map/ppermute | solution.py:78
  22.5 6.9 %collective-permute-start = (bf16[608,256]{1,0:T(8,128)(2,1)S(1)}, bf16[608,256]{1,0:T(8,128)(2,1)S(1)}, u32[]{:S(2)}, u32[]{:S(2)}) collective-permute-start(bf16[608,256]{1,0:T(8,128)(2,1)S(1)} %copy-done.3), channel_id=1, source_target_pairs={{0,1},{1,0},{2,3},{3,2},{4,5},{5,4},{6,7},{7,6},{8,9},{9,8},{10,11... | collective-permute-start | bytes 933896 | tf_op jit(solution)/shard_map/ppermute | solution.py:82
  22.5 6.9 %collective-permute-start.8 = (bf16[608,256]{1,0:T(8,128)(2,1)S(1)}, bf16[608,256]{1,0:T(8,128)(2,1)S(1)}, u32[]{:S(2)}, u32[]{:S(2)}) collective-permute-start(bf16[608,256]{1,0:T(8,128)(2,1)S(1)} %collective-permute-done.1), channel_id=1, source_target_pairs={{0,1},{1,0},{2,3},{3,2},{4,5},{5,4},{6,7},{7,6},{8,9},{9,8},{10,11... | collective-permute-start | bytes 933896 | tf_op jit(solution)/shard_map/ppermute | solution.py:82
  23.0 6.9 %collective-permute-start.12 = (bf16[608,256]{1,0:T(8,128)(2,1)S(1)}, bf16[608,256]{1,0:T(8,128)(2,1)S(1)}, u32[]{:S(2)}, u32[]{:S(2)}) collective-permute-start(bf16[608,256]{1,0:T(8,128)(2,1)S(1)} %collective-permute-done.5), channel_id=1, source_target_pairs={{0,1},{1,0},{2,3},{3,2},{4,5},{5,4},{6,7},{7,6},{8,9},{9,8},{10,11... | collective-permute-start | bytes 933896 | tf_op jit(solution)/shard_map/ppermute | solution.py:82
  29.4 6.9 %collective-permute-start.13 = (bf16[608,256]{1,0:T(8,128)(2,1)S(1)}, bf16[608,256]{1,0:T(8,128)(2,1)S(1)}, u32[]{:S(2)}, u32[]{:S(2)}) collective-permute-start(bf16[608,256]{1,0:T(8,128)(2,1)S(1)} %collective-permute-done.6), channel_id=1, source_target_pairs={{0,1},{1,0},{2,3},{3,2},{4,5},{5,4},{6,7},{7,6},{8,9},{9,8},{10,11... | collective-permute-start | bytes 933896 | tf_op jit(solution)/shard_map/ppermute | solution.py:82
  29.9 8.7 %collective-permute-start.10 = (bf16[608,256]{1,0:T(8,128)(2,1)S(1)}, bf16[608,256]{1,0:T(8,128)(2,1)S(1)}, u32[]{:S(2)}, u32[]{:S(2)}) collective-permute-start(bf16[608,256]{1,0:T(8,128)(2,1)S(1)} %collective-permute-done.3), channel_id=1, source_target_pairs={{0,1},{1,0},{2,3},{3,2},{4,5},{5,4},{6,7},{7,6},{8,9},{9,8},{10,11... | collective-permute-start | bytes 933896 | tf_op jit(solution)/shard_map/ppermute | solution.py:82
  31.6 7.0 %collective-permute-start.14 = (bf16[608,256]{1,0:T(8,128)(2,1)S(1)}, bf16[608,256]{1,0:T(8,128)(2,1)S(1)}, u32[]{:S(2)}, u32[]{:S(2)}) collective-permute-start(bf16[608,256]{1,0:T(8,128)(2,1)S(1)} %collective-permute-done.7), channel_id=1, source_target_pairs={{0,1},{1,0},{2,3},{3,2},{4,5},{5,4},{6,7},{7,6},{8,9},{9,8},{10,11... | collective-permute-start | bytes 933896 | tf_op jit(solution)/shard_map/ppermute | solution.py:82
  35.2 16.3 %collective-permute-start.15 = (bf16[592,256]{1,0:T(8,128)(2,1)}, bf16[592,256]{1,0:T(8,128)(2,1)S(1)}, u32[]{:S(2)}, u32[]{:S(2)}) collective-permute-start(bf16[592,256]{1,0:T(8,128)(2,1)} %extract.1), channel_id=1, source_target_pairs={{0,4},{1,3},{4,8},{5,1},{8,12},{9,5},{12,14},{13,9},{14,10},{15,13... | collective-permute-start | bytes 909320 | tf_op jit(solution)/shard_map/ppermute | solution.py:78
  36.4 15.2 %collective-permute-start.16 = (bf16[592,256]{1,0:T(8,128)(2,1)}, bf16[592,256]{1,0:T(8,128)(2,1)S(1)}, u32[]{:S(2)}, u32[]{:S(2)}) collective-permute-start(bf16[592,256]{1,0:T(8,128)(2,1)} %extract.1), channel_id=1, source_target_pairs={{1,4},{0,3},{5,8},{4,1},{9,12},{8,5},{13,14},{12,9},{15,10},{14,13... | collective-permute-start | bytes 909320 | tf_op jit(solution)/shard_map/ppermute | solution.py:78
  51.6 15.7 %collective-permute-start.20 = (bf16[2,432,256]{2,1,0:T(8,128)(2,1)}, bf16[2,432,256]{2,1,0:T(8,128)(2,1)S(1)}, u32[]{:S(2)}, u32[]{:S(2)}) collective-permute-start(bf16[2,432,256]{2,1,0:T(8,128)(2,1)} %get-tuple-element.51), channel_id=1, source_target_pairs={{0,1},{1,0},{2,3},{3,2},{4,5},{5,4},{6,7},{7,6},{8,9},{9,8},{10,11... | collective-permute-start | bytes 1327112 | tf_op jit(solution)/shard_map/ppermute | solution.py:82
  52.1 14.0 %collective-permute-start.23 = (bf16[592,256]{1,0:T(8,128)(2,1)S(1)}, bf16[592,256]{1,0:T(8,128)(2,1)S(1)}, u32[]{:S(2)}, u32[]{:S(2)}) collective-permute-start(bf16[592,256]{1,0:T(8,128)(2,1)S(1)} %collective-permute-done.16), channel_id=1, source_target_pairs={{0,4},{1,3},{4,8},{5,1},{8,12},{9,5},{12,14},{13,9},{14,10},{15,13... | collective-permute-start | bytes 909320 | tf_op jit(solution)/shard_map/ppermute | solution.py:78
  52.8 13.5 %collective-permute-start.22 = (bf16[592,256]{1,0:T(8,128)(2,1)S(1)}, bf16[592,256]{1,0:T(8,128)(2,1)S(1)}, u32[]{:S(2)}, u32[]{:S(2)}) collective-permute-start(bf16[592,256]{1,0:T(8,128)(2,1)S(1)} %collective-permute-done.15), channel_id=1, source_target_pairs={{0,4},{1,3},{4,8},{5,1},{8,12},{9,5},{12,14},{13,9},{14,10},{15,13... | collective-permute-start | bytes 909320 | tf_op jit(solution)/shard_map/ppermute | solution.py:78
  56.3 11.9 %collective-permute-start.21 = (bf16[432,256]{1,0:T(8,128)(2,1)S(1)}, bf16[432,256]{1,0:T(8,128)(2,1)S(1)}, u32[]{:S(2)}, u32[]{:S(2)}) collective-permute-start(bf16[432,256]{1,0:T(8,128)(2,1)S(1)} %get-tuple-element.70), channel_id=1, source_target_pairs={{0,4},{1,5},{4,8},{5,9},{8,12},{9,13},{12,14},{13,15},{14,10},{15,... | collective-permute-start | bytes 663560 | tf_op jit(solution)/shard_map/ppermute | solution.py:78
  56.9 11.3 %collective-permute-start.38 = (bf16[432,256]{1,0:T(8,128)(2,1)S(1)}, bf16[432,256]{1,0:T(8,128)(2,1)S(1)}, u32[]{:S(2)}, u32[]{:S(2)}) collective-permute-start(bf16[432,256]{1,0:T(8,128)(2,1)S(1)} %get-tuple-element.69), channel_id=1, source_target_pairs={{0,2},{1,3},{4,0},{5,1},{8,4},{9,5},{12,8},{13,9},{14,12},{15,13},... | collective-permute-start | bytes 663560 | tf_op jit(solution)/shard_map/ppermute | solution.py:78
  66.2 13.5 %collective-permute-start.19 = (bf16[2,432,256]{2,1,0:T(8,128)(2,1)S(1)}, bf16[2,432,256]{2,1,0:T(8,128)(2,1)S(1)}, u32[]{:S(2)}, u32[]{:S(2)}) collective-permute-start(bf16[2,432,256]{2,1,0:T(8,128)(2,1)S(1)} %copy-done.2), channel_id=1, source_target_pairs={{0,1},{1,0},{2,3},{3,2},{4,5},{5,4},{6,7},{7,6},{8,9},{9,8},{10,11... | collective-permute-start | bytes 1327112 | tf_op jit(solution)/shard_map/ppermute | solution.py:82
  66.3 13.4 %collective-permute-start.26 = (bf16[592,256]{1,0:T(8,128)(2,1)S(1)}, bf16[592,256]{1,0:T(8,128)(2,1)S(1)}, u32[]{:S(2)}, u32[]{:S(2)}) collective-permute-start(bf16[592,256]{1,0:T(8,128)(2,1)S(1)} %collective-permute-done.23), channel_id=1, source_target_pairs={{0,4},{1,3},{4,8},{5,1},{8,12},{9,5},{12,14},{13,9},{14,10},{15,13... | collective-permute-start | bytes 909320 | tf_op jit(solution)/shard_map/ppermute | solution.py:78
  67.3 11.5 %collective-permute-start.25 = (bf16[592,256]{1,0:T(8,128)(2,1)S(1)}, bf16[592,256]{1,0:T(8,128)(2,1)S(1)}, u32[]{:S(2)}, u32[]{:S(2)}) collective-permute-start(bf16[592,256]{1,0:T(8,128)(2,1)S(1)} %collective-permute-done.22), channel_id=1, source_target_pairs={{0,4},{1,3},{4,8},{5,1},{8,12},{9,5},{12,14},{13,9},{14,10},{15,13... | collective-permute-start | bytes 909320 | tf_op jit(solution)/shard_map/ppermute | solution.py:78
  68.4 12.8 %collective-permute-start.24 = (bf16[432,256]{1,0:T(8,128)(2,1)S(1)}, bf16[432,256]{1,0:T(8,128)(2,1)S(1)}, u32[]{:S(2)}, u32[]{:S(2)}) collective-permute-start(bf16[432,256]{1,0:T(8,128)(2,1)S(1)} %get-tuple-element.54), channel_id=1, source_target_pairs={{0,4},{1,5},{4,8},{5,9},{8,12},{9,13},{12,14},{13,15},{14,10},{15,... | collective-permute-start | bytes 663560 | tf_op jit(solution)/shard_map/ppermute | solution.py:78
  69.3 11.9 %collective-permute-start.39 = (bf16[432,256]{1,0:T(8,128)(2,1)S(1)}, bf16[432,256]{1,0:T(8,128)(2,1)S(1)}, u32[]{:S(2)}, u32[]{:S(2)}) collective-permute-start(bf16[432,256]{1,0:T(8,128)(2,1)S(1)} %get-tuple-element.63), channel_id=1, source_target_pairs={{0,2},{1,3},{4,0},{5,1},{8,4},{9,5},{12,8},{13,9},{14,12},{15,13},... | collective-permute-start | bytes 663560 | tf_op jit(solution)/shard_map/ppermute | solution.py:78
  91.8 15.1 %collective-permute-start.40 = (bf16[432,256]{1,0:T(8,128)(2,1)S(1)}, bf16[432,256]{1,0:T(8,128)(2,1)S(1)}, u32[]{:S(2)}, u32[]{:S(2)}) collective-permute-start(bf16[432,256]{1,0:T(8,128)(2,1)S(1)} %get-tuple-element.64), channel_id=1, source_target_pairs={{0,2},{1,3},{4,0},{5,1},{8,4},{9,5},{12,8},{13,9},{14,12},{15,13},... | collective-permute-start | bytes 663560 | tf_op jit(solution)/shard_map/ppermute | solution.py:78
  92.2 14.7 %collective-permute-start.37 = (bf16[432,256]{1,0:T(8,128)(2,1)S(1)}, bf16[432,256]{1,0:T(8,128)(2,1)S(1)}, u32[]{:S(2)}, u32[]{:S(2)}) collective-permute-start(bf16[432,256]{1,0:T(8,128)(2,1)S(1)} %fusion.5), channel_id=1, source_target_pairs={{0,4},{1,5},{4,8},{5,9},{8,12},{9,13},{12,14},{13,15},{14,10},{15,... | collective-permute-start | bytes 663560 | tf_op jit(solution)/shard_map/ppermute | solution.py:78
  (52 other events, 506.4 us)

commit v17 on v16

--- a/solution.py
+++ b/solution.py
@@ -103,13 +103,15 @@
     def last(self, chain):
         return self.x if self.whole is not None else self.chains[chain][-1]
 
-    def places(self, gate=None):
+    def places(self, gate=None, last_gate=None):
         if self.whole is not None:
             return [self.whole]
         mine = self.chains[0][1:] + self.chains[1][1:]
         held = mine
         if gate is not None:
-            held = [lax.optimization_barrier((t, gate))[0] for t in mine]
+            last = self.chips // 2 - 1
+            gates = [last_gate if k == last else gate for k in range(len(mine))]
+            held = [lax.optimization_barrier(pair)[0] for pair in zip(mine, gates)]
         others = [swap_cores(t, self.peers) for t in [self.x] + held]
         return [t[None] for t in [self.x] + others[:1] + mine + others[1:]]
 
@@ -143,8 +145,9 @@
         self.hop += 1
         return sent
 
-    def total(self):
-        return sum((t.astype(F32) for t in self.held if t is not None), self.term(0))
+    def total(self, gate):
+        held = lax.optimization_barrier((*self.held, gate))[:2]
+        return sum((t.astype(F32) for t in held), self.term(0))
 
 
 def call(body, out_shape, in_specs, scratch=(), cost=2, name=None, out_specs=None, aliases=None):
@@ -716,9 +719,11 @@
     cot_ring.go(1)
     third = (cot_ring.last(0), cot_ring.last(1))
     sums_ring.go(third)
+    arrived = sums_ring.held[0]
     cot_ring.go(0)
-    sent = sums_ring.go(cot_ring.last(0))
-    cot_parts = cot_ring.places(cols)
+    cot_parts = cot_ring.places(cols, arrived)
+    early = [t for k, t in enumerate(cot_parts) if k != peers // 2 + peers // 4]
+    sent = sums_ring.go(early)
     served = lax.optimization_barrier((served, sent))[0]
 
     grad_features = call(
@@ -740,7 +745,7 @@
     )(served, send_face, table, cotangent, features, gain, conv_weight, *cot_parts)
     for _ in range(chips // 2 - 4):
         sums_ring.go()
-    return (mixed, grad_features, sums_ring.total())
+    return (mixed, grad_features, sums_ring.total(grad_features))
 
 
 def solution(mesh):

time: 108 us -> 110 us (1.019)
  waiting for transfers between devices: 34 us -> 36.9 us
  starting transfers between devices: 31.2 us -> 30 us
    ppermute x21, waiting for transfers between devices: 33.9 us -> 36.4 us  [ring_step(): return lax.ppermute(x, 'morton', pairs)]
  transfers between devices with their start and end apart: 41 -> 41, of which waited for: 10 -> 12; matrix products, arithmetic and copies ran while one was open for 3% -> 3% of each run, Pallas kernels for 31% -> 31%
where the time goes in v17:
time: 110 us
  waiting for transfers between devices  36.9 us (34%)
  Pallas kernels  36.8 us (33%)
  starting transfers between devices  30 us (27%)
  local copies, waits for them, and re-layouts  2.73 us (2%)
  other arithmetic  2.53 us (2%)
  between operations  1.12 us (1%)
    ppermute x21, waiting for transfers between devices, ring_step(): return lax.ppermute(x, 'morton', pairs)  36.4 us
    ppermute x21, starting transfers between devices, ring_step(): return lax.ppermute(x, 'morton', pairs)  27.2 us
    pallas_call x1, Pallas kernels, local(): call(functools.partial(input_grad_body, slots, peers, count), sds((per_de...  12.8 us
    pallas_call x1, Pallas kernels, local(): call(functools.partial(weight_grad_body, slots, factor, peers, count), (s...  11.9 us
    pallas_call x1, Pallas kernels, local(): call(mix_body, sds((per_device, channels), BF16), [HBM, HBM, VMEM], [pltp...  7.69 us
    ppermute x20, starting transfers between devices, swap_cores(): return lax.ppermute(x, 'morton', [(m, m ^ 1) for m in range(peers)])  2.77 us
    pallas_call x1, Pallas kernels, local(): call(norm_body, (sds((per_device, channels), BF16), sds((share_rows + NOT...  2.5 us
  transfers between devices with their start and end apart: 41, of which 12 were waited for; matrix products, arithmetic and copies ran while one was open for 3% of the time, Pallas kernels for 31%

profile of v17, /device:TPU:0, one launch (start us, length us, event | category | flops | bytes accessed | tf_op | source)
XLA Modules:
  0.0 110.0 jit_solution(5140074957232212770)
XLA Ops:
  0.6 2.5 %norm.1 = (bf16[1024,256]{1,0:T(8,128)(2,1)}, bf16[608,256]{1,0:T(8,128)(2,1)}) custom-call(s32[2,26]{1,0:T(2,128)} %refs_0_.1, s32[1,64]{1,0:T(1,128)} %refs_1_.1, bf16[1024,256]{1,0:T(8,128)(2,1)} %refs_4_.1, f32[1,256]{1,0:T(1,128)} %bitcast.95), custom_call_target="tpu_custom_call" | custom-call | flops 2000000000 | tf_op jit(solution)/shard_map/norm/pallas_call | solution.py:637
  3.1 3.0 %collective-permute-start.1 = (bf16[608,256]{1,0:T(8,128)(2,1)}, bf16[608,256]{1,0:T(8,128)(2,1)S(1)}, u32[]{:S(2)}, u32[]{:S(2)}) collective-permute-start(bf16[608,256]{1,0:T(8,128)(2,1)} %get-tuple-element.37), channel_id=1, source_target_pairs={{0,4},{1,3},{4,8},{5,1},{8,12},{9,5},{12,14},{13,9},{14,10},{15,13... | collective-permute-start | bytes 933896 | tf_op jit(solution)/shard_map/ppermute | solution.py:78
  6.8 1.8 %extract.1 = bf16[592,256]{1,0:T(8,128)(2,1)} custom-call(bf16[1024,256]{1,0:T(8,128)(2,1)} %refs_3_.3), custom_call_target="tpu_custom_call" | custom-call | flops 2000000000 | tf_op jit(solution)/shard_map/extract/pallas_call | solution.py:645
  8.7 4.5 %collective-permute-done.1 = bf16[608,256]{1,0:T(8,128)(2,1)S(1)} collective-permute-done((bf16[608,256]{1,0:T(8,128)(2,1)}, bf16[608,256]{1,0:T(8,128)(2,1)S(1)}, u32[]{:S(2)}, u32[]{:S(2)}) %collective-permute-start.1) | collective-permute-done | bytes 311328 | tf_op jit(solution)/shard_map/ppermute | solution.py:78
  13.2 2.4 %collective-permute-start.2 = (bf16[608,256]{1,0:T(8,128)(2,1)S(1)}, bf16[608,256]{1,0:T(8,128)(2,1)S(1)}, u32[]{:S(2)}, u32[]{:S(2)}) collective-permute-start(bf16[608,256]{1,0:T(8,128)(2,1)S(1)} %collective-permute-done.1), channel_id=1, source_target_pairs={{0,4},{1,3},{4,8},{5,1},{8,12},{9,5},{12,14},{13,9},{14,10},{15,13... | collective-permute-start | bytes 933896 | tf_op jit(solution)/shard_map/ppermute | solution.py:78
  15.6 1.2 %dynamic-slice_bitcast_fusion.refs_1_.refs_2_ = s32[33]{0:T(128)} fusion(s32[16,33]{1,0:T(8,128)} %constant.10.clone, s32[]{:T(128)S(6)} %select_n.3), kind=kLoop, calls=%fused_computation.16 | loop fusion | bytes 268 | tf_op jit(solution)/shard_map/squeeze | solution.py:635
  16.8 1.6 %collective-permute-start.6 = (bf16[608,256]{1,0:T(8,128)(2,1)S(1)}, bf16[608,256]{1,0:T(8,128)(2,1)S(1)}, u32[]{:S(2)}, u32[]{:S(2)}) collective-permute-start(bf16[608,256]{1,0:T(8,128)(2,1)S(1)} %collective-permute-done.5), channel_id=1, source_target_pairs={{0,4},{1,3},{4,8},{5,1},{8,12},{9,5},{12,14},{13,9},{14,10},{15,13... | collective-permute-start | bytes 933896 | tf_op jit(solution)/shard_map/ppermute | solution.py:78
  18.4 3.0 %collective-permute-done.2 = bf16[608,256]{1,0:T(8,128)(2,1)S(1)} collective-permute-done((bf16[608,256]{1,0:T(8,128)(2,1)S(1)}, bf16[608,256]{1,0:T(8,128)(2,1)S(1)}, u32[]{:S(2)}, u32[]{:S(2)}) %collective-permute-start.2) | collective-permute-done | bytes 311328 | tf_op jit(solution)/shard_map/ppermute | solution.py:78
  23.0 1.7 %collective-permute-done.6 = bf16[608,256]{1,0:T(8,128)(2,1)S(1)} collective-permute-done((bf16[608,256]{1,0:T(8,128)(2,1)S(1)}, bf16[608,256]{1,0:T(8,128)(2,1)S(1)}, u32[]{:S(2)}, u32[]{:S(2)}) %collective-permute-start.6) | collective-permute-done | bytes 311328 | tf_op jit(solution)/shard_map/ppermute | solution.py:78
  25.8 2.5 %collective-permute-done.3 = bf16[608,256]{1,0:T(8,128)(2,1)S(1)} collective-permute-done((bf16[608,256]{1,0:T(8,128)(2,1)S(1)}, bf16[608,256]{1,0:T(8,128)(2,1)S(1)}, u32[]{:S(2)}, u32[]{:S(2)}) %collective-permute-start.3) | collective-permute-done | bytes 311328 | tf_op jit(solution)/shard_map/ppermute | solution.py:78
  30.0 1.6 %collective-permute-done.7 = bf16[608,256]{1,0:T(8,128)(2,1)S(1)} collective-permute-done((bf16[608,256]{1,0:T(8,128)(2,1)S(1)}, bf16[608,256]{1,0:T(8,128)(2,1)S(1)}, u32[]{:S(2)}, u32[]{:S(2)}) %collective-permute-start.7) | collective-permute-done | bytes 311328 | tf_op jit(solution)/shard_map/ppermute | solution.py:78
  31.6 3.6 %collective-permute-done.4 = bf16[608,256]{1,0:T(8,128)(2,1)S(1)} collective-permute-done((bf16[608,256]{1,0:T(8,128)(2,1)S(1)}, bf16[608,256]{1,0:T(8,128)(2,1)S(1)}, u32[]{:S(2)}, u32[]{:S(2)}) %collective-permute-start.4) | collective-permute-done | bytes 311328 | tf_op jit(solution)/shard_map/ppermute | solution.py:78
  36.4 2.3 %collective-permute-start.16 = (bf16[592,256]{1,0:T(8,128)(2,1)}, bf16[592,256]{1,0:T(8,128)(2,1)S(1)}, u32[]{:S(2)}, u32[]{:S(2)}) collective-permute-start(bf16[592,256]{1,0:T(8,128)(2,1)} %extract.1), channel_id=1, source_target_pairs={{1,4},{0,3},{5,8},{4,1},{9,12},{8,5},{13,14},{12,9},{15,10},{14,13... | collective-permute-start | bytes 909320 | tf_op jit(solution)/shard_map/ppermute | solution.py:78
  39.6 11.9 %weight_grad.1 = (f32[8,432,256]{2,1,0:T(8,128)}, bf16[2,432,256]{2,1,0:T(8,128)(2,1)}, bf16[2,432,256]{2,1,0:T(8,128)(2,1)}, bf16[2,432,256]{2,1,0:T(8,128)(2,1...) custom-call(s32[2,26]{1,0:T(2,128)} %refs_0_.1, ...), custom_call_target="tpu_custom_call" | custom-call | flops 8999999488 | tf_op jit(solution)/shard_map/weight_grad/pallas_call | solution.py:668
  52.8 2.3 %collective-permute-start.22 = (bf16[592,256]{1,0:T(8,128)(2,1)S(1)}, bf16[592,256]{1,0:T(8,128)(2,1)S(1)}, u32[]{:S(2)}, u32[]{:S(2)}) collective-permute-start(bf16[592,256]{1,0:T(8,128)(2,1)S(1)} %collective-permute-done.15), channel_id=1, source_target_pairs={{0,4},{1,3},{4,8},{5,1},{8,12},{9,5},{12,14},{13,9},{14,10},{15,13... | collective-permute-start | bytes 909320 | tf_op jit(solution)/shard_map/ppermute | solution.py:78
  55.1 1.2 %fusion.7 = (bf16[432,256]{1,0:T(8,128)(2,1)S(1)}, bf16[432,256]{1,0:T(8,128)(2,1)S(1)}) fusion(f32[8,432,256]{2,1,0:T(8,128)} %get-tuple-element.41, bf16[2,432,256]{2,1,0:T(8,128)(2,1)S(1)} %collective-permute-done.17), kind=kLoop, calls=%fused_computation.15 | loop fusion | flops 663552 | bytes 1769472 | tf_op jit(solution)/shard_map/convert_element_type | solution.py:140
  56.9 1.6 %collective-permute-start.38 = (bf16[432,256]{1,0:T(8,128)(2,1)S(1)}, bf16[432,256]{1,0:T(8,128)(2,1)S(1)}, u32[]{:S(2)}, u32[]{:S(2)}) collective-permute-start(bf16[432,256]{1,0:T(8,128)(2,1)S(1)} %get-tuple-element.73), channel_id=1, source_target_pairs={{0,2},{1,3},{4,0},{5,1},{8,4},{9,5},{12,8},{13,9},{14,12},{15,13},... | collective-permute-start | bytes 663560 | tf_op jit(solution)/shard_map/ppermute | solution.py:78
  58.5 7.7 %mix.1 = bf16[1024,256]{1,0:T(8,128)(2,1)} custom-call(bf16[20,64,2304]{2,1,0:T(8,128)(2,1)} %get-tuple-element.46.cols_ref, bf16[6912,256]{1,0:T(8,128)(2,1)} %refs_6_.1, bf16[1024,256]{1,0:T(8,128)(2,1)} %refs_4_.1), custom_call_target="tpu_custom_call" | custom-call | flops 6000000000 | tf_op jit(solution)/shard_map/mix/pallas_call | solution.py:709
  70.5 5.1 %collective-permute-done.26 = bf16[592,256]{1,0:T(8,128)(2,1)S(1)} collective-permute-done((bf16[592,256]{1,0:T(8,128)(2,1)S(1)}, bf16[592,256]{1,0:T(8,128)(2,1)S(1)}, u32[]{:S(2)}, u32[]{:S(2)}) %collective-permute-start.26) | collective-permute-done | bytes 303136 | tf_op jit(solution)/shard_map/ppermute | solution.py:78
  75.6 3.2 %collective-permute-done.25 = bf16[592,256]{1,0:T(8,128)(2,1)S(1)} collective-permute-done((bf16[592,256]{1,0:T(8,128)(2,1)S(1)}, bf16[592,256]{1,0:T(8,128)(2,1)S(1)}, u32[]{:S(2)}, u32[]{:S(2)}) %collective-permute-start.25) | collective-permute-done | bytes 303136 | tf_op jit(solution)/shard_map/ppermute | solution.py:78
  78.8 2.4 %collective-permute-done.24 = bf16[432,256]{1,0:T(8,128)(2,1)S(1)} collective-permute-done((bf16[432,256]{1,0:T(8,128)(2,1)S(1)}, bf16[432,256]{1,0:T(8,128)(2,1)S(1)}, u32[]{:S(2)}, u32[]{:S(2)}) %collective-permute-start.24) | collective-permute-done | bytes 221216 | tf_op jit(solution)/shard_map/ppermute | solution.py:78
  84.0 6.4 %collective-permute-done.29 = bf16[592,256]{1,0:T(8,128)(2,1)S(1)} collective-permute-done((bf16[592,256]{1,0:T(8,128)(2,1)S(1)}, bf16[592,256]{1,0:T(8,128)(2,1)S(1)}, u32[]{:S(2)}, u32[]{:S(2)}) %collective-permute-start.29) | collective-permute-done | bytes 303136 | tf_op jit(solution)/shard_map/ppermute | solution.py:78
  90.4 2.4 %collective-permute-done.27 = bf16[432,256]{1,0:T(8,128)(2,1)S(1)} collective-permute-done((bf16[432,256]{1,0:T(8,128)(2,1)S(1)}, bf16[432,256]{1,0:T(8,128)(2,1)S(1)}, u32[]{:S(2)}, u32[]{:S(2)}) %collective-permute-start.27) | collective-permute-done | bytes 221216 | tf_op jit(solution)/shard_map/ppermute | solution.py:78
  96.3 12.8 %input_grad.1 = bf16[1024,256]{1,0:T(8,128)(2,1)} custom-call(s32[16,256]{1,0:T(8,128)} %get-tuple-element.63.refs_0_, s32[1,64]{1,0:T(1,128)} %refs_1_.1, s32[33]{0:T(128)} %dynamic-slice_bitcast_fusion.refs_1_.refs_2_, bf16[1024,256]{1,0:T(8,128)(2,1)} %refs_3_.3, bf16[1024,256]{1,0:T(8,128)(2,1)} %refs_4_.1, f32[1,256]{1,0:T(1,128)} %bitcast.96, ...), custom_call_target="tpu_custom_call" | custom-call | flops 12999999488 | tf_op jit(solution)/shard_map/input_grad/pallas_call | solution.py:729
  (139 shorter events, 20.2 us)
Async XLA Ops:
  3.1 10.1 %collective-permute-start.1 = (bf16[608,256]{1,0:T(8,128)(2,1)}, bf16[608,256]{1,0:T(8,128)(2,1)S(1)}, u32[]{:S(2)}, u32[]{:S(2)}) collective-permute-start(bf16[608,256]{1,0:T(8,128)(2,1)} %get-tuple-element.37), channel_id=1, source_target_pairs={{0,4},{1,3},{4,8},{5,1},{8,12},{9,5},{12,14},{13,9},{14,10},{15,13... | collective-permute-start | bytes 933896 | tf_op jit(solution)/shard_map/ppermute | solution.py:78
  6.2 10.7 %collective-permute-start.5 = (bf16[608,256]{1,0:T(8,128)(2,1)}, bf16[608,256]{1,0:T(8,128)(2,1)S(1)}, u32[]{:S(2)}, u32[]{:S(2)}) collective-permute-start(bf16[608,256]{1,0:T(8,128)(2,1)} %get-tuple-element.37), channel_id=1, source_target_pairs={{1,4},{0,3},{5,8},{4,1},{9,12},{8,5},{13,14},{12,9},{15,10},{14,13... | collective-permute-start | bytes 933896 | tf_op jit(solution)/shard_map/ppermute | solution.py:78
  13.2 8.2 %collective-permute-start.2 = (bf16[608,256]{1,0:T(8,128)(2,1)S(1)}, bf16[608,256]{1,0:T(8,128)(2,1)S(1)}, u32[]{:S(2)}, u32[]{:S(2)}) collective-permute-start(bf16[608,256]{1,0:T(8,128)(2,1)S(1)} %collective-permute-done.1), channel_id=1, source_target_pairs={{0,4},{1,3},{4,8},{5,1},{8,12},{9,5},{12,14},{13,9},{14,10},{15,13... | collective-permute-start | bytes 933896 | tf_op jit(solution)/shard_map/ppermute | solution.py:78
  29.9 8.7 %collective-permute-start.10 = (bf16[608,256]{1,0:T(8,128)(2,1)S(1)}, bf16[608,256]{1,0:T(8,128)(2,1)S(1)}, u32[]{:S(2)}, u32[]{:S(2)}) collective-permute-start(bf16[608,256]{1,0:T(8,128)(2,1)S(1)} %collective-permute-done.3), channel_id=1, source_target_pairs={{0,1},{1,0},{2,3},{3,2},{4,5},{5,4},{6,7},{7,6},{8,9},{9,8},{10,11... | collective-permute-start | bytes 933896 | tf_op jit(solution)/shard_map/ppermute | solution.py:82
  35.2 16.3 %collective-permute-start.15 = (bf16[592,256]{1,0:T(8,128)(2,1)}, bf16[592,256]{1,0:T(8,128)(2,1)S(1)}, u32[]{:S(2)}, u32[]{:S(2)}) collective-permute-start(bf16[592,256]{1,0:T(8,128)(2,1)} %extract.1), channel_id=1, source_target_pairs={{0,4},{1,3},{4,8},{5,1},{8,12},{9,5},{12,14},{13,9},{14,10},{15,13... | collective-permute-start | bytes 909320 | tf_op jit(solution)/shard_map/ppermute | solution.py:78
  36.4 15.2 %collective-permute-start.16 = (bf16[592,256]{1,0:T(8,128)(2,1)}, bf16[592,256]{1,0:T(8,128)(2,1)S(1)}, u32[]{:S(2)}, u32[]{:S(2)}) collective-permute-start(bf16[592,256]{1,0:T(8,128)(2,1)} %extract.1), channel_id=1, source_target_pairs={{1,4},{0,3},{5,8},{4,1},{9,12},{8,5},{13,14},{12,9},{15,10},{14,13... | collective-permute-start | bytes 909320 | tf_op jit(solution)/shard_map/ppermute | solution.py:78
  51.6 15.7 %collective-permute-start.20 = (bf16[2,432,256]{2,1,0:T(8,128)(2,1)}, bf16[2,432,256]{2,1,0:T(8,128)(2,1)S(1)}, u32[]{:S(2)}, u32[]{:S(2)}) collective-permute-start(bf16[2,432,256]{2,1,0:T(8,128)(2,1)} %get-tuple-element.53), channel_id=1, source_target_pairs={{0,1},{1,0},{2,3},{3,2},{4,5},{5,4},{6,7},{7,6},{8,9},{9,8},{10,11... | collective-permute-start | bytes 1327112 | tf_op jit(solution)/shard_map/ppermute | solution.py:82
  52.1 14.0 %collective-permute-start.23 = (bf16[592,256]{1,0:T(8,128)(2,1)S(1)}, bf16[592,256]{1,0:T(8,128)(2,1)S(1)}, u32[]{:S(2)}, u32[]{:S(2)}) collective-permute-start(bf16[592,256]{1,0:T(8,128)(2,1)S(1)} %collective-permute-done.16), channel_id=1, source_target_pairs={{0,4},{1,3},{4,8},{5,1},{8,12},{9,5},{12,14},{13,9},{14,10},{15,13... | collective-permute-start | bytes 909320 | tf_op jit(solution)/shard_map/ppermute | solution.py:78
  52.8 13.5 %collective-permute-start.22 = (bf16[592,256]{1,0:T(8,128)(2,1)S(1)}, bf16[592,256]{1,0:T(8,128)(2,1)S(1)}, u32[]{:S(2)}, u32[]{:S(2)}) collective-permute-start(bf16[592,256]{1,0:T(8,128)(2,1)S(1)} %collective-permute-done.15), channel_id=1, source_target_pairs={{0,4},{1,3},{4,8},{5,1},{8,12},{9,5},{12,14},{13,9},{14,10},{15,13... | collective-permute-start | bytes 909320 | tf_op jit(solution)/shard_map/ppermute | solution.py:78
  56.3 11.9 %collective-permute-start.21 = (bf16[432,256]{1,0:T(8,128)(2,1)S(1)}, bf16[432,256]{1,0:T(8,128)(2,1)S(1)}, u32[]{:S(2)}, u32[]{:S(2)}) collective-permute-start(bf16[432,256]{1,0:T(8,128)(2,1)S(1)} %get-tuple-element.74), channel_id=1, source_target_pairs={{0,4},{1,5},{4,8},{5,9},{8,12},{9,13},{12,14},{13,15},{14,10},{15,... | collective-permute-start | bytes 663560 | tf_op jit(solution)/shard_map/ppermute | solution.py:78
  56.9 11.3 %collective-permute-start.38 = (bf16[432,256]{1,0:T(8,128)(2,1)S(1)}, bf16[432,256]{1,0:T(8,128)(2,1)S(1)}, u32[]{:S(2)}, u32[]{:S(2)}) collective-permute-start(bf16[432,256]{1,0:T(8,128)(2,1)S(1)} %get-tuple-element.73), channel_id=1, source_target_pairs={{0,2},{1,3},{4,0},{5,1},{8,4},{9,5},{12,8},{13,9},{14,12},{15,13},... | collective-permute-start | bytes 663560 | tf_op jit(solution)/shard_map/ppermute | solution.py:78
  66.3 9.2 %collective-permute-start.26 = (bf16[592,256]{1,0:T(8,128)(2,1)S(1)}, bf16[592,256]{1,0:T(8,128)(2,1)S(1)}, u32[]{:S(2)}, u32[]{:S(2)}) collective-permute-start(bf16[592,256]{1,0:T(8,128)(2,1)S(1)} %collective-permute-done.23), channel_id=1, source_target_pairs={{0,4},{1,3},{4,8},{5,1},{8,12},{9,5},{12,14},{13,9},{14,10},{15,13... | collective-permute-start | bytes 909320 | tf_op jit(solution)/shard_map/ppermute | solution.py:78
  67.3 11.5 %collective-permute-start.25 = (bf16[592,256]{1,0:T(8,128)(2,1)S(1)}, bf16[592,256]{1,0:T(8,128)(2,1)S(1)}, u32[]{:S(2)}, u32[]{:S(2)}) collective-permute-start(bf16[592,256]{1,0:T(8,128)(2,1)S(1)} %collective-permute-done.22), channel_id=1, source_target_pairs={{0,4},{1,3},{4,8},{5,1},{8,12},{9,5},{12,14},{13,9},{14,10},{15,13... | collective-permute-start | bytes 909320 | tf_op jit(solution)/shard_map/ppermute | solution.py:78
  68.4 12.8 %collective-permute-start.24 = (bf16[432,256]{1,0:T(8,128)(2,1)S(1)}, bf16[432,256]{1,0:T(8,128)(2,1)S(1)}, u32[]{:S(2)}, u32[]{:S(2)}) collective-permute-start(bf16[432,256]{1,0:T(8,128)(2,1)S(1)} %get-tuple-element.56), channel_id=1, source_target_pairs={{0,4},{1,5},{4,8},{5,9},{8,12},{9,13},{12,14},{13,15},{14,10},{15,... | collective-permute-start | bytes 663560 | tf_op jit(solution)/shard_map/ppermute | solution.py:78
  69.3 11.9 %collective-permute-start.39 = (bf16[432,256]{1,0:T(8,128)(2,1)S(1)}, bf16[432,256]{1,0:T(8,128)(2,1)S(1)}, u32[]{:S(2)}, u32[]{:S(2)}) collective-permute-start(bf16[432,256]{1,0:T(8,128)(2,1)S(1)} %get-tuple-element.65), channel_id=1, source_target_pairs={{0,2},{1,3},{4,0},{5,1},{8,4},{9,5},{12,8},{13,9},{14,12},{15,13},... | collective-permute-start | bytes 663560 | tf_op jit(solution)/shard_map/ppermute | solution.py:78
  70.4 11.9 %collective-permute-start.28 = (bf16[592,256]{1,0:T(8,128)(2,1)S(1)}, bf16[592,256]{1,0:T(8,128)(2,1)S(1)}, u32[]{:S(2)}, u32[]{:S(2)}) collective-permute-start(bf16[592,256]{1,0:T(8,128)(2,1)S(1)} %copy-done.19), channel_id=1, source_target_pairs={{0,1},{1,0},{2,3},{3,2},{4,5},{5,4},{6,7},{7,6},{8,9},{9,8},{10,11... | collective-permute-start | bytes 909320 | tf_op jit(solution)/shard_map/ppermute | solution.py:82
  75.5 7.9 %collective-permute-start.33 = (bf16[592,256]{1,0:T(8,128)(2,1)S(1)}, bf16[592,256]{1,0:T(8,128)(2,1)S(1)}, u32[]{:S(2)}, u32[]{:S(2)}) collective-permute-start(bf16[592,256]{1,0:T(8,128)(2,1)S(1)} %collective-permute-done.16), channel_id=1, source_target_pairs={{0,1},{1,0},{2,3},{3,2},{4,5},{5,4},{6,7},{7,6},{8,9},{9,8},{10,11... | collective-permute-start | bytes 909320 | tf_op jit(solution)/shard_map/ppermute | solution.py:82
  81.2 11.6 %collective-permute-start.18 = (bf16[2,432,256]{2,1,0:T(8,128)(2,1)S(1)}, bf16[2,432,256]{2,1,0:T(8,128)(2,1)S(1)}, u32[]{:S(2)}, u32[]{:S(2)}) collective-permute-start(bf16[2,432,256]{2,1,0:T(8,128)(2,1)S(1)} %copy-done.1), channel_id=1, source_target_pairs={{0,1},{1,0},{2,3},{3,2},{4,5},{5,4},{6,7},{7,6},{8,9},{9,8},{10,11... | collective-permute-start | bytes 1327112 | tf_op jit(solution)/shard_map/ppermute | solution.py:82
  81.2 9.2 %collective-permute-start.29 = (bf16[592,256]{1,0:T(8,128)(2,1)S(1)}, bf16[592,256]{1,0:T(8,128)(2,1)S(1)}, u32[]{:S(2)}, u32[]{:S(2)}) collective-permute-start(bf16[592,256]{1,0:T(8,128)(2,1)S(1)} %collective-permute-done.25), channel_id=1, source_target_pairs={{0,4},{1,3},{4,8},{5,1},{8,12},{9,5},{12,14},{13,9},{14,10},{15,13... | collective-permute-start | bytes 909320 | tf_op jit(solution)/shard_map/ppermute | solution.py:78
  82.4 10.4 %collective-permute-start.27 = (bf16[432,256]{1,0:T(8,128)(2,1)S(1)}, bf16[432,256]{1,0:T(8,128)(2,1)S(1)}, u32[]{:S(2)}, u32[]{:S(2)}) collective-permute-start(bf16[432,256]{1,0:T(8,128)(2,1)S(1)} %get-tuple-element.57), channel_id=1, source_target_pairs={{0,4},{1,5},{4,8},{5,9},{8,12},{9,13},{12,14},{13,15},{14,10},{15,... | collective-permute-start | bytes 663560 | tf_op jit(solution)/shard_map/ppermute | solution.py:78
  83.5 9.9 %collective-permute-start.34 = (bf16[592,256]{1,0:T(8,128)(2,1)S(1)}, bf16[592,256]{1,0:T(8,128)(2,1)S(1)}, u32[]{:S(2)}, u32[]{:S(2)}) collective-permute-start(bf16[592,256]{1,0:T(8,128)(2,1)S(1)} %collective-permute-done.23), channel_id=1, source_target_pairs={{0,1},{1,0},{2,3},{3,2},{4,5},{5,4},{6,7},{7,6},{8,9},{9,8},{10,11... | collective-permute-start | bytes 909320 | tf_op jit(solution)/shard_map/ppermute | solution.py:82
  83.6 10.4 %collective-permute-start.31 = (bf16[592,256]{1,0:T(8,128)(2,1)S(1)}, bf16[592,256]{1,0:T(8,128)(2,1)S(1)}, u32[]{:S(2)}, u32[]{:S(2)}) collective-permute-start(bf16[592,256]{1,0:T(8,128)(2,1)S(1)} %collective-permute-done.22), channel_id=1, source_target_pairs={{0,1},{1,0},{2,3},{3,2},{4,5},{5,4},{6,7},{7,6},{8,9},{9,8},{10,11... | collective-permute-start | bytes 909320 | tf_op jit(solution)/shard_map/ppermute | solution.py:82
  93.4 15.7 %collective-permute-start.40 = (bf16[432,256]{1,0:T(8,128)(2,1)S(1)}, bf16[432,256]{1,0:T(8,128)(2,1)S(1)}, u32[]{:S(2)}, u32[]{:S(2)}) collective-permute-start(bf16[432,256]{1,0:T(8,128)(2,1)S(1)} %get-tuple-element.66), channel_id=1, source_target_pairs={{0,2},{1,3},{4,0},{5,1},{8,4},{9,5},{12,8},{13,9},{14,12},{15,13},... | collective-permute-start | bytes 663560 | tf_op jit(solution)/shard_map/ppermute | solution.py:78
  94.4 14.7 %collective-permute-start.37 = (bf16[432,256]{1,0:T(8,128)(2,1)S(1)}, bf16[432,256]{1,0:T(8,128)(2,1)S(1)}, u32[]{:S(2)}, u32[]{:S(2)}) collective-permute-start(bf16[432,256]{1,0:T(8,128)(2,1)S(1)} %fusion.5), channel_id=1, source_target_pairs={{0,4},{1,5},{4,8},{5,9},{8,12},{9,13},{12,14},{13,15},{14,10},{15,... | collective-permute-start | bytes 663560 | tf_op jit(solution)/shard_map/ppermute | solution.py:78
  (52 other events, 503.9 us)

commit v18 on v16

--- a/solution.py
+++ b/solution.py
@@ -23,7 +23,7 @@
 
 
 HB = 24
-VMEM_LIMIT = 56 * 1024 * 1024
+VMEM_LIMIT = 60 * 1024 * 1024
 DIRECTIONS = [
     (i, j, l)
     for i in (-1, 0, 1)
@@ -648,9 +648,9 @@
     )(cotangent)
     hidden_ring.go(0)
     hidden_ring.go(1)
-    hidden_ring.go(0, cot_share)
+    hidden_ring.go(0, (cot_share, table))
     hidden_ring.go(1)
-    hidden_ring.go(0, table)
+    hidden_ring.go(0)
     hidden_ring.go(1)
     hidden_ring.go(0)
     hidden_parts = hidden_ring.places()

time: 108 us -> 111 us (1.028)
  other arithmetic: 2.53 us -> 6.65 us
    convert_element_type x4, other arithmetic: 1.65 us -> 4.76 us  [go(): part = part.astype(BF16)]
    unnamed x70 -> x56, local copies, waits for them, and re-layouts: 1.68 us -> 2.34 us
  transfers between devices with their start and end apart: 41 -> 41, of which waited for: 10 -> 10; matrix products, arithmetic and copies ran while one was open for 3% -> 5% of each run, Pallas kernels for 31% -> 31%
where the time goes in v18:
time: 111 us
  Pallas kernels  36.4 us (33%)
  waiting for transfers between devices  33.4 us (30%)
  starting transfers between devices  30.1 us (27%)
  other arithmetic  6.65 us (6%)
  local copies, waits for them, and re-layouts  3.57 us (3%)
    ppermute x21, waiting for transfers between devices, ring_step(): return lax.ppermute(x, 'morton', pairs)  33.3 us
    ppermute x21, starting transfers between devices, ring_step(): return lax.ppermute(x, 'morton', pairs)  26.3 us
    pallas_call x1, Pallas kernels, local(): call(functools.partial(input_grad_body, slots, peers, count), sds((per_de...  12.4 us
    pallas_call x1, Pallas kernels, local(): call(functools.partial(weight_grad_body, slots, factor, peers, count), (s...  12 us
    pallas_call x1, Pallas kernels, local(): call(mix_body, sds((per_device, channels), BF16), [HBM, HBM, VMEM], [pltp...  7.69 us
    convert_element_type x4, other arithmetic, go(): part = part.astype(BF16)  4.76 us
    ppermute x20, starting transfers between devices, swap_cores(): return lax.ppermute(x, 'morton', [(m, m ^ 1) for m in range(peers)])  3.75 us
    pallas_call x1, Pallas kernels, local(): call(norm_body, (sds((per_device, channels), BF16), sds((share_rows + NOT...  2.5 us
  transfers between devices with their start and end apart: 41, of which 10 were waited for; matrix products, arithmetic and copies ran while one was open for 5% of the time, Pallas kernels for 31%

profile of v18, /device:TPU:0, one launch (start us, length us, event | category | flops | bytes accessed | tf_op | source)
XLA Modules:
  0.0 111.1 jit_solution(17369845364211752979)
XLA Ops:
  0.6 2.5 %norm.1 = (bf16[1024,256]{1,0:T(8,128)(2,1)}, bf16[608,256]{1,0:T(8,128)(2,1)}) custom-call(s32[2,26]{1,0:T(2,128)} %refs_0_.1, s32[1,64]{1,0:T(1,128)} %refs_1_.1, bf16[1024,256]{1,0:T(8,128)(2,1)} %refs_4_.1, f32[1,256]{1,0:T(1,128)} %bitcast.91), custom_call_target="tpu_custom_call" | custom-call | flops 2000000000 | tf_op jit(solution)/shard_map/norm/pallas_call | solution.py:634
  3.1 3.0 %collective-permute-start.1 = (bf16[608,256]{1,0:T(8,128)(2,1)}, bf16[608,256]{1,0:T(8,128)(2,1)S(1)}, u32[]{:S(2)}, u32[]{:S(2)}) collective-permute-start(bf16[608,256]{1,0:T(8,128)(2,1)} %get-tuple-element.34), channel_id=1, source_target_pairs={{0,4},{1,3},{4,8},{5,1},{8,12},{9,5},{12,14},{13,9},{14,10},{15,13... | collective-permute-start | bytes 933896 | tf_op jit(solution)/shard_map/ppermute | solution.py:78
  8.1 1.9 %extract.1 = bf16[592,256]{1,0:T(8,128)(2,1)} custom-call(bf16[1024,256]{1,0:T(8,128)(2,1)} %refs_3_.3), custom_call_target="tpu_custom_call" | custom-call | flops 2000000000 | tf_op jit(solution)/shard_map/extract/pallas_call | solution.py:642
  10.0 3.3 %collective-permute-done.1 = bf16[608,256]{1,0:T(8,128)(2,1)S(1)} collective-permute-done((bf16[608,256]{1,0:T(8,128)(2,1)}, bf16[608,256]{1,0:T(8,128)(2,1)S(1)}, u32[]{:S(2)}, u32[]{:S(2)}) %collective-permute-start.1) | collective-permute-done | bytes 311328 | tf_op jit(solution)/shard_map/ppermute | solution.py:78
  13.2 2.4 %collective-permute-start.2 = (bf16[608,256]{1,0:T(8,128)(2,1)S(1)}, bf16[608,256]{1,0:T(8,128)(2,1)S(1)}, u32[]{:S(2)}, u32[]{:S(2)}) collective-permute-start(bf16[608,256]{1,0:T(8,128)(2,1)S(1)} %collective-permute-done.1), channel_id=1, source_target_pairs={{0,4},{1,3},{4,8},{5,1},{8,12},{9,5},{12,14},{13,9},{14,10},{15,13... | collective-permute-start | bytes 933896 | tf_op jit(solution)/shard_map/ppermute | solution.py:78
  15.6 1.6 %collective-permute-start.6 = (bf16[608,256]{1,0:T(8,128)(2,1)S(1)}, bf16[608,256]{1,0:T(8,128)(2,1)S(1)}, u32[]{:S(2)}, u32[]{:S(2)}) collective-permute-start(bf16[608,256]{1,0:T(8,128)(2,1)S(1)} %collective-permute-done.5), channel_id=1, source_target_pairs={{0,4},{1,3},{4,8},{5,1},{8,12},{9,5},{12,14},{13,9},{14,10},{15,13... | collective-permute-start | bytes 933896 | tf_op jit(solution)/shard_map/ppermute | solution.py:78
  17.2 4.2 %collective-permute-done.2 = bf16[608,256]{1,0:T(8,128)(2,1)S(1)} collective-permute-done((bf16[608,256]{1,0:T(8,128)(2,1)S(1)}, bf16[608,256]{1,0:T(8,128)(2,1)S(1)}, u32[]{:S(2)}, u32[]{:S(2)}) %collective-permute-start.2) | collective-permute-done | bytes 311328 | tf_op jit(solution)/shard_map/ppermute | solution.py:78
  23.0 1.7 %collective-permute-done.6 = bf16[608,256]{1,0:T(8,128)(2,1)S(1)} collective-permute-done((bf16[608,256]{1,0:T(8,128)(2,1)S(1)}, bf16[608,256]{1,0:T(8,128)(2,1)S(1)}, u32[]{:S(2)}, u32[]{:S(2)}) %collective-permute-start.6) | collective-permute-done | bytes 311328 | tf_op jit(solution)/shard_map/ppermute | solution.py:78
  25.8 2.5 %collective-permute-done.3 = bf16[608,256]{1,0:T(8,128)(2,1)S(1)} collective-permute-done((bf16[608,256]{1,0:T(8,128)(2,1)S(1)}, bf16[608,256]{1,0:T(8,128)(2,1)S(1)}, u32[]{:S(2)}, u32[]{:S(2)}) %collective-permute-start.3) | collective-permute-done | bytes 311328 | tf_op jit(solution)/shard_map/ppermute | solution.py:78
  30.0 1.6 %collective-permute-done.7 = bf16[608,256]{1,0:T(8,128)(2,1)S(1)} collective-permute-done((bf16[608,256]{1,0:T(8,128)(2,1)S(1)}, bf16[608,256]{1,0:T(8,128)(2,1)S(1)}, u32[]{:S(2)}, u32[]{:S(2)}) %collective-permute-start.7) | collective-permute-done | bytes 311328 | tf_op jit(solution)/shard_map/ppermute | solution.py:78
  31.6 3.6 %collective-permute-done.4 = bf16[608,256]{1,0:T(8,128)(2,1)S(1)} collective-permute-done((bf16[608,256]{1,0:T(8,128)(2,1)S(1)}, bf16[608,256]{1,0:T(8,128)(2,1)S(1)}, u32[]{:S(2)}, u32[]{:S(2)}) %collective-permute-start.4) | collective-permute-done | bytes 311328 | tf_op jit(solution)/shard_map/ppermute | solution.py:78
  36.4 2.3 %collective-permute-start.16 = (bf16[592,256]{1,0:T(8,128)(2,1)}, bf16[592,256]{1,0:T(8,128)(2,1)}, u32[]{:S(2)}, u32[]{:S(2)}) collective-permute-start(bf16[592,256]{1,0:T(8,128)(2,1)} %extract.1), channel_id=1, source_target_pairs={{1,4},{0,3},{5,8},{4,1},{9,12},{8,5},{13,14},{12,9},{15,10},{14,13... | collective-permute-start | bytes 909320 | tf_op jit(solution)/shard_map/ppermute | solution.py:78
  40.2 12.0 %weight_grad.1 = (f32[8,432,256]{2,1,0:T(8,128)}, bf16[2,432,256]{2,1,0:T(8,128)(2,1)}, bf16[2,432,256]{2,1,0:T(8,128)(2,1)}, bf16[2,432,256]{2,1,0:T(8,128)(2,1...) custom-call(s32[2,26]{1,0:T(2,128)} %refs_0_.1, ...), custom_call_target="tpu_custom_call" | custom-call | flops 8999999488 | tf_op jit(solution)/shard_map/weight_grad/pallas_call | solution.py:665
  53.4 2.3 %collective-permute-start.22 = (bf16[592,256]{1,0:T(8,128)(2,1)}, bf16[592,256]{1,0:T(8,128)(2,1)}, u32[]{:S(2)}, u32[]{:S(2)}) collective-permute-start(bf16[592,256]{1,0:T(8,128)(2,1)} %collective-permute-done.15), channel_id=1, source_target_pairs={{0,4},{1,3},{4,8},{5,1},{8,12},{9,5},{12,14},{13,9},{14,10},{15,13... | collective-permute-start | bytes 909320 | tf_op jit(solution)/shard_map/ppermute | solution.py:78
  55.7 2.0 %fusion.7 = (bf16[432,256]{1,0:T(8,128)(2,1)}, bf16[432,256]{1,0:T(8,128)(2,1)}) fusion(f32[8,432,256]{2,1,0:T(8,128)} %get-tuple-element.37, bf16[2,432,256]{2,1,0:T(8,128)(2,1)S(1)} %collective-permute-done.17), kind=kLoop, calls=%fused_computation.15 | loop fusion | flops 663552 | bytes 1769472 | tf_op jit(solution)/shard_map/convert_element_type | solution.py:138
  58.2 1.6 %collective-permute-start.38 = (bf16[432,256]{1,0:T(8,128)(2,1)}, bf16[432,256]{1,0:T(8,128)(2,1)}, u32[]{:S(2)}, u32[]{:S(2)}) collective-permute-start(bf16[432,256]{1,0:T(8,128)(2,1)} %get-tuple-element.67), channel_id=1, source_target_pairs={{0,2},{1,3},{4,0},{5,1},{8,4},{9,5},{12,8},{13,9},{14,12},{15,13},... | collective-permute-start | bytes 663560 | tf_op jit(solution)/shard_map/ppermute | solution.py:78
  59.8 7.7 %mix.1 = bf16[1024,256]{1,0:T(8,128)(2,1)} custom-call(bf16[20,64,2304]{2,1,0:T(8,128)(2,1)} %get-tuple-element.42.cols_ref, bf16[6912,256]{1,0:T(8,128)(2,1)} %refs_6_.1, bf16[1024,256]{1,0:T(8,128)(2,1)} %refs_4_.1), custom_call_target="tpu_custom_call" | custom-call | flops 6000000000 | tf_op jit(solution)/shard_map/mix/pallas_call | solution.py:706
  72.5 7.8 %collective-permute-done.25 = bf16[592,256]{1,0:T(8,128)(2,1)S(1)} collective-permute-done((bf16[592,256]{1,0:T(8,128)(2,1)}, bf16[592,256]{1,0:T(8,128)(2,1)S(1)}, u32[]{:S(2)}, u32[]{:S(2)}) %collective-permute-start.25) | collective-permute-done | bytes 303136 | tf_op jit(solution)/shard_map/ppermute | solution.py:78
  81.4 1.2 %collective-permute-done.24 = bf16[432,256]{1,0:T(8,128)(2,1)S(1)} collective-permute-done((bf16[432,256]{1,0:T(8,128)(2,1)S(1)}, bf16[432,256]{1,0:T(8,128)(2,1)S(1)}, u32[]{:S(2)}, u32[]{:S(2)}) %collective-permute-start.24) | collective-permute-done | bytes 221216 | tf_op jit(solution)/shard_map/ppermute | solution.py:78
  84.0 3.1 %collective-permute-done.28 = bf16[592,256]{1,0:T(8,128)(2,1)S(1)} collective-permute-done((bf16[592,256]{1,0:T(8,128)(2,1)S(1)}, bf16[592,256]{1,0:T(8,128)(2,1)S(1)}, u32[]{:S(2)}, u32[]{:S(2)}) %collective-permute-start.28) | collective-permute-done | bytes 303136 | tf_op jit(solution)/shard_map/ppermute | solution.py:78
  88.7 4.3 %collective-permute-done.27 = bf16[432,256]{1,0:T(8,128)(2,1)S(1)} collective-permute-done((bf16[432,256]{1,0:T(8,128)(2,1)S(1)}, bf16[432,256]{1,0:T(8,128)(2,1)S(1)}, u32[]{:S(2)}, u32[]{:S(2)}) %collective-permute-start.27) | collective-permute-done | bytes 221216 | tf_op jit(solution)/shard_map/ppermute | solution.py:78
  94.1 1.7 %collective-permute-start.37 = (bf16[432,256]{1,0:T(8,128)(2,1)}, bf16[432,256]{1,0:T(8,128)(2,1)}, u32[]{:S(2)}, u32[]{:S(2)}) collective-permute-start(bf16[432,256]{1,0:T(8,128)(2,1)} %fusion.5), channel_id=1, source_target_pairs={{0,4},{1,5},{4,8},{5,9},{8,12},{9,13},{12,14},{13,15},{14,10},{15,... | collective-permute-start | bytes 663560 | tf_op jit(solution)/shard_map/ppermute | solution.py:78
  96.8 12.4 %input_grad.1 = bf16[1024,256]{1,0:T(8,128)(2,1)} custom-call(s32[16,256]{1,0:T(8,128)} %get-tuple-element.55.refs_0_, s32[1,64]{1,0:T(1,128)} %refs_1_.1, s32[33]{0:T(128)} %dynamic-slice_bitcast_fusion.refs_1_.refs_2_, bf16[1024,256]{1,0:T(8,128)(2,1)} %refs_3_.3, bf16[1024,256]{1,0:T(8,128)(2,1)} %refs_4_.1, f32[1,256]{1,0:T(1,128)} %bitcast.92, ...), custom_call_target="tpu_custom_call" | custom-call | flops 12999999488 | tf_op jit(solution)/shard_map/input_grad/pallas_call | solution.py:724
  109.2 1.9 %fusion.2 = f32[432,256]{1,0:T(8,128)} fusion(bf16[432,256]{1,0:T(8,128)(2,1)} %collective-permute-done.40, bf16[432,256]{1,0:T(8,128)(2,1)} %collective-permute-done.37, f32[8,432,256]{2,1,0:T(8,128)S(1)} %copy-done, bf16[2,432,256]{2,1,0:T(8,128)(2,1)S(1)} %collective-permute-done.18), kind=kLoop, calls=%fused_computation.5 | loop fusion | flops 663552 | bytes 1548288 | tf_op jit(solution)/shard_map/add | solution.py:147
  (125 shorter events, 21.5 us)
Async XLA Ops:
  3.1 10.1 %collective-permute-start.1 = (bf16[608,256]{1,0:T(8,128)(2,1)}, bf16[608,256]{1,0:T(8,128)(2,1)S(1)}, u32[]{:S(2)}, u32[]{:S(2)}) collective-permute-start(bf16[608,256]{1,0:T(8,128)(2,1)} %get-tuple-element.34), channel_id=1, source_target_pairs={{0,4},{1,3},{4,8},{5,1},{8,12},{9,5},{12,14},{13,9},{14,10},{15,13... | collective-permute-start | bytes 933896 | tf_op jit(solution)/shard_map/ppermute | solution.py:78
  6.2 9.4 %collective-permute-start.5 = (bf16[608,256]{1,0:T(8,128)(2,1)}, bf16[608,256]{1,0:T(8,128)(2,1)S(1)}, u32[]{:S(2)}, u32[]{:S(2)}) collective-permute-start(bf16[608,256]{1,0:T(8,128)(2,1)} %get-tuple-element.34), channel_id=1, source_target_pairs={{1,4},{0,3},{5,8},{4,1},{9,12},{8,5},{13,14},{12,9},{15,10},{14,13... | collective-permute-start | bytes 933896 | tf_op jit(solution)/shard_map/ppermute | solution.py:78
  13.2 8.2 %collective-permute-start.2 = (bf16[608,256]{1,0:T(8,128)(2,1)S(1)}, bf16[608,256]{1,0:T(8,128)(2,1)S(1)}, u32[]{:S(2)}, u32[]{:S(2)}) collective-permute-start(bf16[608,256]{1,0:T(8,128)(2,1)S(1)} %collective-permute-done.1), channel_id=1, source_target_pairs={{0,4},{1,3},{4,8},{5,1},{8,12},{9,5},{12,14},{13,9},{14,10},{15,13... | collective-permute-start | bytes 933896 | tf_op jit(solution)/shard_map/ppermute | solution.py:78
  15.6 9.1 %collective-permute-start.6 = (bf16[608,256]{1,0:T(8,128)(2,1)S(1)}, bf16[608,256]{1,0:T(8,128)(2,1)S(1)}, u32[]{:S(2)}, u32[]{:S(2)}) collective-permute-start(bf16[608,256]{1,0:T(8,128)(2,1)S(1)} %collective-permute-done.5), channel_id=1, source_target_pairs={{0,4},{1,3},{4,8},{5,1},{8,12},{9,5},{12,14},{13,9},{14,10},{15,13... | collective-permute-start | bytes 933896 | tf_op jit(solution)/shard_map/ppermute | solution.py:78
  23.0 6.9 %collective-permute-start.12 = (bf16[608,256]{1,0:T(8,128)(2,1)S(1)}, bf16[608,256]{1,0:T(8,128)(2,1)S(1)}, u32[]{:S(2)}, u32[]{:S(2)}) collective-permute-start(bf16[608,256]{1,0:T(8,128)(2,1)S(1)} %collective-permute-done.5), channel_id=1, source_target_pairs={{0,1},{1,0},{2,3},{3,2},{4,5},{5,4},{6,7},{7,6},{8,9},{9,8},{10,11... | collective-permute-start | bytes 933896 | tf_op jit(solution)/shard_map/ppermute | solution.py:82
  29.4 6.9 %collective-permute-start.13 = (bf16[608,256]{1,0:T(8,128)(2,1)S(1)}, bf16[608,256]{1,0:T(8,128)(2,1)S(1)}, u32[]{:S(2)}, u32[]{:S(2)}) collective-permute-start(bf16[608,256]{1,0:T(8,128)(2,1)S(1)} %collective-permute-done.6), channel_id=1, source_target_pairs={{0,1},{1,0},{2,3},{3,2},{4,5},{5,4},{6,7},{7,6},{8,9},{9,8},{10,11... | collective-permute-start | bytes 933896 | tf_op jit(solution)/shard_map/ppermute | solution.py:82
  29.9 8.7 %collective-permute-start.10 = (bf16[608,256]{1,0:T(8,128)(2,1)S(1)}, bf16[608,256]{1,0:T(8,128)(2,1)S(1)}, u32[]{:S(2)}, u32[]{:S(2)}) collective-permute-start(bf16[608,256]{1,0:T(8,128)(2,1)S(1)} %collective-permute-done.3), channel_id=1, source_target_pairs={{0,1},{1,0},{2,3},{3,2},{4,5},{5,4},{6,7},{7,6},{8,9},{9,8},{10,11... | collective-permute-start | bytes 933896 | tf_op jit(solution)/shard_map/ppermute | solution.py:82
  31.6 7.0 %collective-permute-start.14 = (bf16[608,256]{1,0:T(8,128)(2,1)S(1)}, bf16[608,256]{1,0:T(8,128)(2,1)S(1)}, u32[]{:S(2)}, u32[]{:S(2)}) collective-permute-start(bf16[608,256]{1,0:T(8,128)(2,1)S(1)} %collective-permute-done.7), channel_id=1, source_target_pairs={{0,1},{1,0},{2,3},{3,2},{4,5},{5,4},{6,7},{7,6},{8,9},{9,8},{10,11... | collective-permute-start | bytes 933896 | tf_op jit(solution)/shard_map/ppermute | solution.py:82
  35.2 17.0 %collective-permute-start.15 = (bf16[592,256]{1,0:T(8,128)(2,1)}, bf16[592,256]{1,0:T(8,128)(2,1)}, u32[]{:S(2)}, u32[]{:S(2)}) collective-permute-start(bf16[592,256]{1,0:T(8,128)(2,1)} %extract.1), channel_id=1, source_target_pairs={{0,4},{1,3},{4,8},{5,1},{8,12},{9,5},{12,14},{13,9},{14,10},{15,13... | collective-permute-start | bytes 909320 | tf_op jit(solution)/shard_map/ppermute | solution.py:78
  36.4 15.8 %collective-permute-start.16 = (bf16[592,256]{1,0:T(8,128)(2,1)}, bf16[592,256]{1,0:T(8,128)(2,1)}, u32[]{:S(2)}, u32[]{:S(2)}) collective-permute-start(bf16[592,256]{1,0:T(8,128)(2,1)} %extract.1), channel_id=1, source_target_pairs={{1,4},{0,3},{5,8},{4,1},{9,12},{8,5},{13,14},{12,9},{15,10},{14,13... | collective-permute-start | bytes 909320 | tf_op jit(solution)/shard_map/ppermute | solution.py:78
  52.3 15.9 %collective-permute-start.20 = (bf16[2,432,256]{2,1,0:T(8,128)(2,1)}, bf16[2,432,256]{2,1,0:T(8,128)(2,1)S(1)}, u32[]{:S(2)}, u32[]{:S(2)}) collective-permute-start(bf16[2,432,256]{2,1,0:T(8,128)(2,1)} %get-tuple-element.49), channel_id=1, source_target_pairs={{0,1},{1,0},{2,3},{3,2},{4,5},{5,4},{6,7},{7,6},{8,9},{9,8},{10,11... | collective-permute-start | bytes 1327112 | tf_op jit(solution)/shard_map/ppermute | solution.py:82
  52.8 14.7 %collective-permute-start.23 = (bf16[592,256]{1,0:T(8,128)(2,1)}, bf16[592,256]{1,0:T(8,128)(2,1)}, u32[]{:S(2)}, u32[]{:S(2)}) collective-permute-start(bf16[592,256]{1,0:T(8,128)(2,1)} %collective-permute-done.16), channel_id=1, source_target_pairs={{0,4},{1,3},{4,8},{5,1},{8,12},{9,5},{12,14},{13,9},{14,10},{15,13... | collective-permute-start | bytes 909320 | tf_op jit(solution)/shard_map/ppermute | solution.py:78
  53.4 14.1 %collective-permute-start.22 = (bf16[592,256]{1,0:T(8,128)(2,1)}, bf16[592,256]{1,0:T(8,128)(2,1)}, u32[]{:S(2)}, u32[]{:S(2)}) collective-permute-start(bf16[592,256]{1,0:T(8,128)(2,1)} %collective-permute-done.15), channel_id=1, source_target_pairs={{0,4},{1,3},{4,8},{5,1},{8,12},{9,5},{12,14},{13,9},{14,10},{15,13... | collective-permute-start | bytes 909320 | tf_op jit(solution)/shard_map/ppermute | solution.py:78
  57.7 11.5 %collective-permute-start.21 = (bf16[432,256]{1,0:T(8,128)(2,1)}, bf16[432,256]{1,0:T(8,128)(2,1)}, u32[]{:S(2)}, u32[]{:S(2)}) collective-permute-start(bf16[432,256]{1,0:T(8,128)(2,1)} %get-tuple-element.68), channel_id=1, source_target_pairs={{0,4},{1,5},{4,8},{5,9},{8,12},{9,13},{12,14},{13,15},{14,10},{15,... | collective-permute-start | bytes 663560 | tf_op jit(solution)/shard_map/ppermute | solution.py:78
  58.2 11.0 %collective-permute-start.38 = (bf16[432,256]{1,0:T(8,128)(2,1)}, bf16[432,256]{1,0:T(8,128)(2,1)}, u32[]{:S(2)}, u32[]{:S(2)}) collective-permute-start(bf16[432,256]{1,0:T(8,128)(2,1)} %get-tuple-element.67), channel_id=1, source_target_pairs={{0,2},{1,3},{4,0},{5,1},{8,4},{9,5},{12,8},{13,9},{14,12},{15,13},... | collective-permute-start | bytes 663560 | tf_op jit(solution)/shard_map/ppermute | solution.py:78
  67.5 13.4 %collective-permute-start.19 = (bf16[2,432,256]{2,1,0:T(8,128)(2,1)}, bf16[2,432,256]{2,1,0:T(8,128)(2,1)S(1)}, u32[]{:S(2)}, u32[]{:S(2)}) collective-permute-start(bf16[2,432,256]{2,1,0:T(8,128)(2,1)} %get-tuple-element.47), channel_id=1, source_target_pairs={{0,1},{1,0},{2,3},{3,2},{4,5},{5,4},{6,7},{7,6},{8,9},{9,8},{10,11... | collective-permute-start | bytes 1327112 | tf_op jit(solution)/shard_map/ppermute | solution.py:82
  67.6 13.3 %collective-permute-start.26 = (bf16[592,256]{1,0:T(8,128)(2,1)}, bf16[592,256]{1,0:T(8,128)(2,1)S(1)}, u32[]{:S(2)}, u32[]{:S(2)}) collective-permute-start(bf16[592,256]{1,0:T(8,128)(2,1)} %collective-permute-done.23), channel_id=1, source_target_pairs={{0,4},{1,3},{4,8},{5,1},{8,12},{9,5},{12,14},{13,9},{14,10},{15,13... | collective-permute-start | bytes 909320 | tf_op jit(solution)/shard_map/ppermute | solution.py:78
  68.2 12.0 %collective-permute-start.25 = (bf16[592,256]{1,0:T(8,128)(2,1)}, bf16[592,256]{1,0:T(8,128)(2,1)S(1)}, u32[]{:S(2)}, u32[]{:S(2)}) collective-permute-start(bf16[592,256]{1,0:T(8,128)(2,1)} %collective-permute-done.22), channel_id=1, source_target_pairs={{0,4},{1,3},{4,8},{5,1},{8,12},{9,5},{12,14},{13,9},{14,10},{15,13... | collective-permute-start | bytes 909320 | tf_op jit(solution)/shard_map/ppermute | solution.py:78
  70.4 12.2 %collective-permute-start.24 = (bf16[432,256]{1,0:T(8,128)(2,1)S(1)}, bf16[432,256]{1,0:T(8,128)(2,1)S(1)}, u32[]{:S(2)}, u32[]{:S(2)}) collective-permute-start(bf16[432,256]{1,0:T(8,128)(2,1)S(1)} %get-tuple-element.52), channel_id=1, source_target_pairs={{0,4},{1,5},{4,8},{5,9},{8,12},{9,13},{12,14},{13,15},{14,10},{15,... | collective-permute-start | bytes 663560 | tf_op jit(solution)/shard_map/ppermute | solution.py:78
  71.5 11.1 %collective-permute-start.39 = (bf16[432,256]{1,0:T(8,128)(2,1)S(1)}, bf16[432,256]{1,0:T(8,128)(2,1)S(1)}, u32[]{:S(2)}, u32[]{:S(2)}) collective-permute-start(bf16[432,256]{1,0:T(8,128)(2,1)S(1)} %get-tuple-element.61), channel_id=1, source_target_pairs={{0,2},{1,3},{4,0},{5,1},{8,4},{9,5},{12,8},{13,9},{14,12},{15,13},... | collective-permute-start | bytes 663560 | tf_op jit(solution)/shard_map/ppermute | solution.py:78
  88.2 7.7 %collective-permute-start.36 = (bf16[592,256]{1,0:T(8,128)(2,1)S(1)}, bf16[592,256]{1,0:T(8,128)(2,1)S(1)}, u32[]{:S(2)}, u32[]{:S(2)}) collective-permute-start(bf16[592,256]{1,0:T(8,128)(2,1)S(1)} %collective-permute-done.26), channel_id=1, source_target_pairs={{0,1},{1,0},{2,3},{3,2},{4,5},{5,4},{6,7},{7,6},{8,9},{9,8},{10,11... | collective-permute-start | bytes 909320 | tf_op jit(solution)/shard_map/ppermute | solution.py:82
  88.3 7.6 %collective-permute-start.32 = (bf16[592,256]{1,0:T(8,128)(2,1)S(1)}, bf16[592,256]{1,0:T(8,128)(2,1)S(1)}, u32[]{:S(2)}, u32[]{:S(2)}) collective-permute-start(bf16[592,256]{1,0:T(8,128)(2,1)S(1)} %collective-permute-done.25), channel_id=1, source_target_pairs={{0,1},{1,0},{2,3},{3,2},{4,5},{5,4},{6,7},{7,6},{8,9},{9,8},{10,11... | collective-permute-start | bytes 909320 | tf_op jit(solution)/shard_map/ppermute | solution.py:82
  93.8 15.4 %collective-permute-start.40 = (bf16[432,256]{1,0:T(8,128)(2,1)}, bf16[432,256]{1,0:T(8,128)(2,1)}, u32[]{:S(2)}, u32[]{:S(2)}) collective-permute-start(bf16[432,256]{1,0:T(8,128)(2,1)} %get-tuple-element.62), channel_id=1, source_target_pairs={{0,2},{1,3},{4,0},{5,1},{8,4},{9,5},{12,8},{13,9},{14,12},{15,13},... | collective-permute-start | bytes 663560 | tf_op jit(solution)/shard_map/ppermute | solution.py:78
  94.1 15.1 %collective-permute-start.37 = (bf16[432,256]{1,0:T(8,128)(2,1)}, bf16[432,256]{1,0:T(8,128)(2,1)}, u32[]{:S(2)}, u32[]{:S(2)}) collective-permute-start(bf16[432,256]{1,0:T(8,128)(2,1)} %fusion.5), channel_id=1, source_target_pairs={{0,4},{1,5},{4,8},{5,9},{8,12},{9,13},{12,14},{13,15},{14,10},{15,... | collective-permute-start | bytes 663560 | tf_op jit(solution)/shard_map/ppermute | solution.py:78
  (45 other events, 347.3 us)

commit v19 on v16

--- a/solution.py
+++ b/solution.py
@@ -23,7 +23,7 @@
 
 
 HB = 24
-VMEM_LIMIT = 56 * 1024 * 1024
+VMEM_LIMIT = 40 * 1024 * 1024
 DIRECTIONS = [
     (i, j, l)
     for i in (-1, 0, 1)

time: 108 us -> 117 us (1.083)
  Pallas kernels: 36.1 us -> 40.6 us
  local copies, waits for them, and re-layouts: 2.89 us -> 6.45 us
  waiting for transfers between devices: 34 us -> 37.1 us
    pallas_call x1, Pallas kernels: 11.9 us -> 19.5 us  [local(): call(functools.partial(weight_grad_body, slots, factor, peers, count), (s...]
    unnamed x70 -> x22, local copies, waits for them, and re-layouts: 1.68 us -> 5.76 us
    ppermute x21, waiting for transfers between devices: 33.9 us -> 37 us  [ring_step(): return lax.ppermute(x, 'morton', pairs)]
    pallas_call x1, Pallas kernels: 1.84 us -> 0.09 us  [local(): call(extract_body, sds((share_rows, channels), BF16), [VMEM], stage, name...]
    pallas_call x1, Pallas kernels: 2.5 us -> 1.14 us  [local(): call(norm_body, (sds((per_device, channels), BF16), sds((share_rows + NOT...]
  transfers between devices with their start and end apart: 41 -> 41, of which waited for: 10 -> 10; matrix products, arithmetic and copies ran while one was open for 3% -> 1% of each run, Pallas kernels for 31% -> 34%
where the time goes in v19:
time: 117 us
  Pallas kernels  40.6 us (35%)
  waiting for transfers between devices  37.1 us (32%)
  starting transfers between devices  30.2 us (26%)
  local copies, waits for them, and re-layouts  6.45 us (6%)
  other arithmetic  1.44 us (1%)
    ppermute x21, waiting for transfers between devices, ring_step(): return lax.ppermute(x, 'morton', pairs)  37 us
    ppermute x21, starting transfers between devices, ring_step(): return lax.ppermute(x, 'morton', pairs)  26.4 us
    pallas_call x1, Pallas kernels, local(): call(functools.partial(weight_grad_body, slots, factor, peers, count), (s...  19.5 us
    pallas_call x1, Pallas kernels, local(): call(functools.partial(input_grad_body, slots, peers, count), sds((per_de...  13 us
    pallas_call x1, Pallas kernels, local(): call(mix_body, sds((per_device, channels), BF16), [HBM, HBM, VMEM], [pltp...  6.89 us
    unnamed x22, local copies, waits for them, and re-layouts  5.76 us
    ppermute x20, starting transfers between devices, swap_cores(): return lax.ppermute(x, 'morton', [(m, m ^ 1) for m in range(peers)])  3.78 us
  transfers between devices with their start and end apart: 41, of which 10 were waited for; matrix products, arithmetic and copies ran while one was open for 1% of the time, Pallas kernels for 34%

profile of v19, /device:TPU:0, one launch (start us, length us, event | category | flops | bytes accessed | tf_op | source)
XLA Modules:
  0.0 116.6 jit_solution(12603057787748807911)
XLA Ops:
  3.7 1.1 norm.1
  4.8 3.1 %collective-permute-start.1 = (bf16[608,256]{1,0:T(8,128)(2,1)S(1)}, bf16[608,256]{1,0:T(8,128)(2,1)S(1)}, u32[]{:S(2)}, u32[]{:S(2)}) collective-permute-start(bf16[608,256]{1,0:T(8,128)(2,1)S(1)} %get-tuple-element.35), channel_id=1, source_target_pairs={{0,4},{1,3},{4,8},{5,1},{8,12},{9,5},{12,14},{13,9},{14,10},{15,13... | collective-permute-start | bytes 933896 | tf_op jit(solution)/shard_map/ppermute | solution.py:78
  8.7 6.0 %collective-permute-done.1 = bf16[608,256]{1,0:T(8,128)(2,1)S(1)} collective-permute-done((bf16[608,256]{1,0:T(8,128)(2,1)S(1)}, bf16[608,256]{1,0:T(8,128)(2,1)S(1)}, u32[]{:S(2)}, u32[]{:S(2)}) %collective-permute-start.1) | collective-permute-done | bytes 311328 | tf_op jit(solution)/shard_map/ppermute | solution.py:78
  14.7 2.5 %collective-permute-start.2 = (bf16[608,256]{1,0:T(8,128)(2,1)S(1)}, bf16[608,256]{1,0:T(8,128)(2,1)S(1)}, u32[]{:S(2)}, u32[]{:S(2)}) collective-permute-start(bf16[608,256]{1,0:T(8,128)(2,1)S(1)} %collective-permute-done.1), channel_id=1, source_target_pairs={{0,4},{1,3},{4,8},{5,1},{8,12},{9,5},{12,14},{13,9},{14,10},{15,13... | collective-permute-start | bytes 933896 | tf_op jit(solution)/shard_map/ppermute | solution.py:78
  17.8 1.6 %collective-permute-start.6 = (bf16[608,256]{1,0:T(8,128)(2,1)S(1)}, bf16[608,256]{1,0:T(8,128)(2,1)S(1)}, u32[]{:S(2)}, u32[]{:S(2)}) collective-permute-start(bf16[608,256]{1,0:T(8,128)(2,1)S(1)} %collective-permute-done.5), channel_id=1, source_target_pairs={{0,4},{1,3},{4,8},{5,1},{8,12},{9,5},{12,14},{13,9},{14,10},{15,13... | collective-permute-start | bytes 933896 | tf_op jit(solution)/shard_map/ppermute | solution.py:78
  19.4 3.5 %collective-permute-done.2 = bf16[608,256]{1,0:T(8,128)(2,1)S(1)} collective-permute-done((bf16[608,256]{1,0:T(8,128)(2,1)S(1)}, bf16[608,256]{1,0:T(8,128)(2,1)S(1)}, u32[]{:S(2)}, u32[]{:S(2)}) %collective-permute-start.2) | collective-permute-done | bytes 311328 | tf_op jit(solution)/shard_map/ppermute | solution.py:78
  24.6 1.7 %collective-permute-done.6 = bf16[608,256]{1,0:T(8,128)(2,1)S(1)} collective-permute-done((bf16[608,256]{1,0:T(8,128)(2,1)S(1)}, bf16[608,256]{1,0:T(8,128)(2,1)S(1)}, u32[]{:S(2)}, u32[]{:S(2)}) %collective-permute-start.6) | collective-permute-done | bytes 311328 | tf_op jit(solution)/shard_map/ppermute | solution.py:78
  27.4 2.5 %collective-permute-done.3 = bf16[608,256]{1,0:T(8,128)(2,1)S(1)} collective-permute-done((bf16[608,256]{1,0:T(8,128)(2,1)S(1)}, bf16[608,256]{1,0:T(8,128)(2,1)S(1)}, u32[]{:S(2)}, u32[]{:S(2)}) %collective-permute-start.3) | collective-permute-done | bytes 311328 | tf_op jit(solution)/shard_map/ppermute | solution.py:78
  31.5 1.7 %collective-permute-done.7 = bf16[608,256]{1,0:T(8,128)(2,1)S(1)} collective-permute-done((bf16[608,256]{1,0:T(8,128)(2,1)S(1)}, bf16[608,256]{1,0:T(8,128)(2,1)S(1)}, u32[]{:S(2)}, u32[]{:S(2)}) %collective-permute-start.7) | collective-permute-done | bytes 311328 | tf_op jit(solution)/shard_map/ppermute | solution.py:78
  33.2 3.6 %collective-permute-done.4 = bf16[608,256]{1,0:T(8,128)(2,1)S(1)} collective-permute-done((bf16[608,256]{1,0:T(8,128)(2,1)S(1)}, bf16[608,256]{1,0:T(8,128)(2,1)S(1)}, u32[]{:S(2)}, u32[]{:S(2)}) %collective-permute-start.4) | collective-permute-done | bytes 311328 | tf_op jit(solution)/shard_map/ppermute | solution.py:78
  37.9 2.4 %collective-permute-start.16 = (bf16[592,256]{1,0:T(8,128)(2,1)S(1)}, bf16[592,256]{1,0:T(8,128)(2,1)S(1)}, u32[]{:S(2)}, u32[]{:S(2)}) collective-permute-start(bf16[592,256]{1,0:T(8,128)(2,1)S(1)} %extract.1), channel_id=1, source_target_pairs={{1,4},{0,3},{5,8},{4,1},{9,12},{8,5},{13,14},{12,9},{15,10},{14,13... | collective-permute-start | bytes 909320 | tf_op jit(solution)/shard_map/ppermute | solution.py:78
  40.3 19.5 %weight_grad.1 = (f32[8,432,256]{2,1,0:T(8,128)S(1)}, bf16[2,432,256]{2,1,0:T(8,128)(2,1)S(1)}, bf16[2,432,256]{2,1,0:T(8,128)(2,1)S(1)}, bf16[2,432,256]{2,1,0:...) custom-call(s32[2,26]{1,0:T(2,128)S(1)} %copy-done.5, ...), custom_call_target="tpu_custom_call" | custom-call | flops 8999999488 | tf_op jit(solution)/shard_map/weight_grad/pallas_call | solution.py:665
  60.9 2.3 %collective-permute-start.22 = (bf16[592,256]{1,0:T(8,128)(2,1)S(1)}, bf16[592,256]{1,0:T(8,128)(2,1)S(1)}, u32[]{:S(2)}, u32[]{:S(2)}) collective-permute-start(bf16[592,256]{1,0:T(8,128)(2,1)S(1)} %collective-permute-done.15), channel_id=1, source_target_pairs={{0,4},{1,3},{4,8},{5,1},{8,12},{9,5},{12,14},{13,9},{14,10},{15,13... | collective-permute-start | bytes 909320 | tf_op jit(solution)/shard_map/ppermute | solution.py:78
  63.8 1.6 %collective-permute-start.38 = (bf16[432,256]{1,0:T(8,128)(2,1)S(1)}, bf16[432,256]{1,0:T(8,128)(2,1)S(1)}, u32[]{:S(2)}, u32[]{:S(2)}) collective-permute-start(bf16[432,256]{1,0:T(8,128)(2,1)S(1)} %get-tuple-element.69), channel_id=1, source_target_pairs={{0,2},{1,3},{4,0},{5,1},{8,4},{9,5},{12,8},{13,9},{14,12},{15,13},... | collective-permute-start | bytes 663560 | tf_op jit(solution)/shard_map/ppermute | solution.py:78
  65.4 2.7 %copy-done.10 = bf16[20,64,2304]{2,1,0:T(8,128)(2,1)S(1)} copy-done((bf16[20,64,2304]{2,1,0:T(8,128)(2,1)S(1)}, bf16[20,64,2304]{2,1,0:T(8,128)(2,1)}, u32[]{:S(2)}) %copy-start.10) | copy-done | bytes 5898264
  68.1 6.9 %mix.1 = bf16[1024,256]{1,0:T(8,128)(2,1)} custom-call(bf16[20,64,2304]{2,1,0:T(8,128)(2,1)S(1)} %copy-done.10, bf16[6912,256]{1,0:T(8,128)(2,1)S(1)} %copy-done, bf16[1024,256]{1,0:T(8,128)(2,1)S(1)} %copy-done.2), custom_call_target="tpu_custom_call" | custom-call | flops 6000000000 | tf_op jit(solution)/shard_map/mix/pallas_call | solution.py:706
  75.6 1.4 %collective-permute-start.25 = (bf16[592,256]{1,0:T(8,128)(2,1)S(1)}, bf16[592,256]{1,0:T(8,128)(2,1)S(1)}, u32[]{:S(2)}, u32[]{:S(2)}) collective-permute-start(bf16[592,256]{1,0:T(8,128)(2,1)S(1)} %collective-permute-done.22), channel_id=1, source_target_pairs={{0,4},{1,3},{4,8},{5,1},{8,12},{9,5},{12,14},{13,9},{14,10},{15,13... | collective-permute-start | bytes 909320 | tf_op jit(solution)/shard_map/ppermute | solution.py:78
  77.9 1.4 %collective-permute-start.39 = (bf16[432,256]{1,0:T(8,128)(2,1)S(1)}, bf16[432,256]{1,0:T(8,128)(2,1)S(1)}, u32[]{:S(2)}, u32[]{:S(2)}) collective-permute-start(bf16[432,256]{1,0:T(8,128)(2,1)S(1)} %get-tuple-element.63), channel_id=1, source_target_pairs={{0,2},{1,3},{4,0},{5,1},{8,4},{9,5},{12,8},{13,9},{14,12},{15,13},... | collective-permute-start | bytes 663560 | tf_op jit(solution)/shard_map/ppermute | solution.py:78
  79.3 8.3 %collective-permute-done.25 = bf16[592,256]{1,0:T(8,128)(2,1)S(1)} collective-permute-done((bf16[592,256]{1,0:T(8,128)(2,1)S(1)}, bf16[592,256]{1,0:T(8,128)(2,1)S(1)}, u32[]{:S(2)}, u32[]{:S(2)}) %collective-permute-start.25) | collective-permute-done | bytes 303136 | tf_op jit(solution)/shard_map/ppermute | solution.py:78
  88.6 1.4 %collective-permute-done.24 = bf16[432,256]{1,0:T(8,128)(2,1)S(1)} collective-permute-done((bf16[432,256]{1,0:T(8,128)(2,1)S(1)}, bf16[432,256]{1,0:T(8,128)(2,1)S(1)}, u32[]{:S(2)}, u32[]{:S(2)}) %collective-permute-start.24) | collective-permute-done | bytes 221216 | tf_op jit(solution)/shard_map/ppermute | solution.py:78
  90.7 3.7 %collective-permute-done.28 = bf16[592,256]{1,0:T(8,128)(2,1)S(1)} collective-permute-done((bf16[592,256]{1,0:T(8,128)(2,1)S(1)}, bf16[592,256]{1,0:T(8,128)(2,1)S(1)}, u32[]{:S(2)}, u32[]{:S(2)}) %collective-permute-start.28) | collective-permute-done | bytes 303136 | tf_op jit(solution)/shard_map/ppermute | solution.py:78
  95.9 4.6 %collective-permute-done.27 = bf16[432,256]{1,0:T(8,128)(2,1)S(1)} collective-permute-done((bf16[432,256]{1,0:T(8,128)(2,1)S(1)}, bf16[432,256]{1,0:T(8,128)(2,1)S(1)}, u32[]{:S(2)}, u32[]{:S(2)}) %collective-permute-start.27) | collective-permute-done | bytes 221216 | tf_op jit(solution)/shard_map/ppermute | solution.py:78
  100.9 1.7 %collective-permute-start.37 = (bf16[432,256]{1,0:T(8,128)(2,1)S(1)}, bf16[432,256]{1,0:T(8,128)(2,1)S(1)}, u32[]{:S(2)}, u32[]{:S(2)}) collective-permute-start(bf16[432,256]{1,0:T(8,128)(2,1)S(1)} %fusion.5), channel_id=1, source_target_pairs={{0,4},{1,5},{4,8},{5,9},{8,12},{9,13},{12,14},{13,15},{14,10},{15,... | collective-permute-start | bytes 663560 | tf_op jit(solution)/shard_map/ppermute | solution.py:78
  102.7 13.0 %input_grad.1 = bf16[1024,256]{1,0:T(8,128)(2,1)} custom-call(s32[16,256]{1,0:T(8,128)S(1)} %get-tuple-element.57.refs_0_, s32[1,64]{1,0:T(1,128)S(1)} %copy-done.9, s32[33]{0:T(128)S(1)} %dynamic-slice_bitcast_fusion.refs_1_.refs_2_, bf16[1024,256]{1,0:T(8,128)(2,1)S(1)} %copy-done.3, bf16[1024,256]{1,0:T(8,128)(2,1)S(1)} %copy-done.2, ...), custom_call_target="tpu_custom_call" | custom-call | flops 12999999488 | tf_op jit(solution)/shard_map/input_grad/pallas_call | solution.py:724
  (91 shorter events, 17.7 us)
Async XLA Ops:
  4.8 9.8 %collective-permute-start.1 = (bf16[608,256]{1,0:T(8,128)(2,1)S(1)}, bf16[608,256]{1,0:T(8,128)(2,1)S(1)}, u32[]{:S(2)}, u32[]{:S(2)}) collective-permute-start(bf16[608,256]{1,0:T(8,128)(2,1)S(1)} %get-tuple-element.35), channel_id=1, source_target_pairs={{0,4},{1,3},{4,8},{5,1},{8,12},{9,5},{12,14},{13,9},{14,10},{15,13... | collective-permute-start | bytes 933896 | tf_op jit(solution)/shard_map/ppermute | solution.py:78
  7.9 9.9 %collective-permute-start.5 = (bf16[608,256]{1,0:T(8,128)(2,1)S(1)}, bf16[608,256]{1,0:T(8,128)(2,1)S(1)}, u32[]{:S(2)}, u32[]{:S(2)}) collective-permute-start(bf16[608,256]{1,0:T(8,128)(2,1)S(1)} %get-tuple-element.35), channel_id=1, source_target_pairs={{1,4},{0,3},{5,8},{4,1},{9,12},{8,5},{13,14},{12,9},{15,10},{14,13... | collective-permute-start | bytes 933896 | tf_op jit(solution)/shard_map/ppermute | solution.py:78
  14.7 8.3 %collective-permute-start.2 = (bf16[608,256]{1,0:T(8,128)(2,1)S(1)}, bf16[608,256]{1,0:T(8,128)(2,1)S(1)}, u32[]{:S(2)}, u32[]{:S(2)}) collective-permute-start(bf16[608,256]{1,0:T(8,128)(2,1)S(1)} %collective-permute-done.1), channel_id=1, source_target_pairs={{0,4},{1,3},{4,8},{5,1},{8,12},{9,5},{12,14},{13,9},{14,10},{15,13... | collective-permute-start | bytes 933896 | tf_op jit(solution)/shard_map/ppermute | solution.py:78
  17.8 8.5 %collective-permute-start.6 = (bf16[608,256]{1,0:T(8,128)(2,1)S(1)}, bf16[608,256]{1,0:T(8,128)(2,1)S(1)}, u32[]{:S(2)}, u32[]{:S(2)}) collective-permute-start(bf16[608,256]{1,0:T(8,128)(2,1)S(1)} %collective-permute-done.5), channel_id=1, source_target_pairs={{0,4},{1,3},{4,8},{5,1},{8,12},{9,5},{12,14},{13,9},{14,10},{15,13... | collective-permute-start | bytes 933896 | tf_op jit(solution)/shard_map/ppermute | solution.py:78
  24.1 6.9 %collective-permute-start.8 = (bf16[608,256]{1,0:T(8,128)(2,1)S(1)}, bf16[608,256]{1,0:T(8,128)(2,1)S(1)}, u32[]{:S(2)}, u32[]{:S(2)}) collective-permute-start(bf16[608,256]{1,0:T(8,128)(2,1)S(1)} %collective-permute-done.1), channel_id=1, source_target_pairs={{0,1},{1,0},{2,3},{3,2},{4,5},{5,4},{6,7},{7,6},{8,9},{9,8},{10,11... | collective-permute-start | bytes 933896 | tf_op jit(solution)/shard_map/ppermute | solution.py:82
  24.6 6.9 %collective-permute-start.12 = (bf16[608,256]{1,0:T(8,128)(2,1)S(1)}, bf16[608,256]{1,0:T(8,128)(2,1)S(1)}, u32[]{:S(2)}, u32[]{:S(2)}) collective-permute-start(bf16[608,256]{1,0:T(8,128)(2,1)S(1)} %collective-permute-done.5), channel_id=1, source_target_pairs={{0,1},{1,0},{2,3},{3,2},{4,5},{5,4},{6,7},{7,6},{8,9},{9,8},{10,11... | collective-permute-start | bytes 933896 | tf_op jit(solution)/shard_map/ppermute | solution.py:82
  31.5 8.7 %collective-permute-start.10 = (bf16[608,256]{1,0:T(8,128)(2,1)S(1)}, bf16[608,256]{1,0:T(8,128)(2,1)S(1)}, u32[]{:S(2)}, u32[]{:S(2)}) collective-permute-start(bf16[608,256]{1,0:T(8,128)(2,1)S(1)} %collective-permute-done.3), channel_id=1, source_target_pairs={{0,1},{1,0},{2,3},{3,2},{4,5},{5,4},{6,7},{7,6},{8,9},{9,8},{10,11... | collective-permute-start | bytes 933896 | tf_op jit(solution)/shard_map/ppermute | solution.py:82
  33.2 7.0 %collective-permute-start.14 = (bf16[608,256]{1,0:T(8,128)(2,1)S(1)}, bf16[608,256]{1,0:T(8,128)(2,1)S(1)}, u32[]{:S(2)}, u32[]{:S(2)}) collective-permute-start(bf16[608,256]{1,0:T(8,128)(2,1)S(1)} %collective-permute-done.7), channel_id=1, source_target_pairs={{0,1},{1,0},{2,3},{3,2},{4,5},{5,4},{6,7},{7,6},{8,9},{9,8},{10,11... | collective-permute-start | bytes 933896 | tf_op jit(solution)/shard_map/ppermute | solution.py:82
  36.8 23.0 %collective-permute-start.15 = (bf16[592,256]{1,0:T(8,128)(2,1)S(1)}, bf16[592,256]{1,0:T(8,128)(2,1)S(1)}, u32[]{:S(2)}, u32[]{:S(2)}) collective-permute-start(bf16[592,256]{1,0:T(8,128)(2,1)S(1)} %extract.1), channel_id=1, source_target_pairs={{0,4},{1,3},{4,8},{5,1},{8,12},{9,5},{12,14},{13,9},{14,10},{15,13... | collective-permute-start | bytes 909320 | tf_op jit(solution)/shard_map/ppermute | solution.py:78
  37.9 21.9 %collective-permute-start.16 = (bf16[592,256]{1,0:T(8,128)(2,1)S(1)}, bf16[592,256]{1,0:T(8,128)(2,1)S(1)}, u32[]{:S(2)}, u32[]{:S(2)}) collective-permute-start(bf16[592,256]{1,0:T(8,128)(2,1)S(1)} %extract.1), channel_id=1, source_target_pairs={{1,4},{0,3},{5,8},{4,1},{9,12},{8,5},{13,14},{12,9},{15,10},{14,13... | collective-permute-start | bytes 909320 | tf_op jit(solution)/shard_map/ppermute | solution.py:78
  59.8 15.8 %collective-permute-start.20 = (bf16[2,432,256]{2,1,0:T(8,128)(2,1)S(1)}, bf16[2,432,256]{2,1,0:T(8,128)(2,1)S(1)}, u32[]{:S(2)}, u32[]{:S(2)}) collective-permute-start(bf16[2,432,256]{2,1,0:T(8,128)(2,1)S(1)} %get-tuple-element.51), channel_id=1, source_target_pairs={{0,1},{1,0},{2,3},{3,2},{4,5},{5,4},{6,7},{7,6},{8,9},{9,8},{10,11... | collective-permute-start | bytes 1327112 | tf_op jit(solution)/shard_map/ppermute | solution.py:82
  60.3 14.7 %collective-permute-start.23 = (bf16[592,256]{1,0:T(8,128)(2,1)S(1)}, bf16[592,256]{1,0:T(8,128)(2,1)S(1)}, u32[]{:S(2)}, u32[]{:S(2)}) collective-permute-start(bf16[592,256]{1,0:T(8,128)(2,1)S(1)} %collective-permute-done.16), channel_id=1, source_target_pairs={{0,4},{1,3},{4,8},{5,1},{8,12},{9,5},{12,14},{13,9},{14,10},{15,13... | collective-permute-start | bytes 909320 | tf_op jit(solution)/shard_map/ppermute | solution.py:78
  60.9 14.2 %collective-permute-start.22 = (bf16[592,256]{1,0:T(8,128)(2,1)S(1)}, bf16[592,256]{1,0:T(8,128)(2,1)S(1)}, u32[]{:S(2)}, u32[]{:S(2)}) collective-permute-start(bf16[592,256]{1,0:T(8,128)(2,1)S(1)} %collective-permute-done.15), channel_id=1, source_target_pairs={{0,4},{1,3},{4,8},{5,1},{8,12},{9,5},{12,14},{13,9},{14,10},{15,13... | collective-permute-start | bytes 909320 | tf_op jit(solution)/shard_map/ppermute | solution.py:78
  63.3 13.7 %collective-permute-start.21 = (bf16[432,256]{1,0:T(8,128)(2,1)S(1)}, bf16[432,256]{1,0:T(8,128)(2,1)S(1)}, u32[]{:S(2)}, u32[]{:S(2)}) collective-permute-start(bf16[432,256]{1,0:T(8,128)(2,1)S(1)} %get-tuple-element.70), channel_id=1, source_target_pairs={{0,4},{1,5},{4,8},{5,9},{8,12},{9,13},{12,14},{13,15},{14,10},{15,... | collective-permute-start | bytes 663560 | tf_op jit(solution)/shard_map/ppermute | solution.py:78
  63.8 13.2 %collective-permute-start.38 = (bf16[432,256]{1,0:T(8,128)(2,1)S(1)}, bf16[432,256]{1,0:T(8,128)(2,1)S(1)}, u32[]{:S(2)}, u32[]{:S(2)}) collective-permute-start(bf16[432,256]{1,0:T(8,128)(2,1)S(1)} %get-tuple-element.69), channel_id=1, source_target_pairs={{0,2},{1,3},{4,0},{5,1},{8,4},{9,5},{12,8},{13,9},{14,12},{15,13},... | collective-permute-start | bytes 663560 | tf_op jit(solution)/shard_map/ppermute | solution.py:78
  75.0 13.0 %collective-permute-start.19 = (bf16[2,432,256]{2,1,0:T(8,128)(2,1)S(1)}, bf16[2,432,256]{2,1,0:T(8,128)(2,1)S(1)}, u32[]{:S(2)}, u32[]{:S(2)}) collective-permute-start(bf16[2,432,256]{2,1,0:T(8,128)(2,1)S(1)} %get-tuple-element.49), channel_id=1, source_target_pairs={{0,1},{1,0},{2,3},{3,2},{4,5},{5,4},{6,7},{7,6},{8,9},{9,8},{10,11... | collective-permute-start | bytes 1327112 | tf_op jit(solution)/shard_map/ppermute | solution.py:82
  75.1 12.9 %collective-permute-start.26 = (bf16[592,256]{1,0:T(8,128)(2,1)S(1)}, bf16[592,256]{1,0:T(8,128)(2,1)S(1)}, u32[]{:S(2)}, u32[]{:S(2)}) collective-permute-start(bf16[592,256]{1,0:T(8,128)(2,1)S(1)} %collective-permute-done.23), channel_id=1, source_target_pairs={{0,4},{1,3},{4,8},{5,1},{8,12},{9,5},{12,14},{13,9},{14,10},{15,13... | collective-permute-start | bytes 909320 | tf_op jit(solution)/shard_map/ppermute | solution.py:78
  75.6 12.0 %collective-permute-start.25 = (bf16[592,256]{1,0:T(8,128)(2,1)S(1)}, bf16[592,256]{1,0:T(8,128)(2,1)S(1)}, u32[]{:S(2)}, u32[]{:S(2)}) collective-permute-start(bf16[592,256]{1,0:T(8,128)(2,1)S(1)} %collective-permute-done.22), channel_id=1, source_target_pairs={{0,4},{1,3},{4,8},{5,1},{8,12},{9,5},{12,14},{13,9},{14,10},{15,13... | collective-permute-start | bytes 909320 | tf_op jit(solution)/shard_map/ppermute | solution.py:78
  77.2 12.7 %collective-permute-start.24 = (bf16[432,256]{1,0:T(8,128)(2,1)S(1)}, bf16[432,256]{1,0:T(8,128)(2,1)S(1)}, u32[]{:S(2)}, u32[]{:S(2)}) collective-permute-start(bf16[432,256]{1,0:T(8,128)(2,1)S(1)} %get-tuple-element.54), channel_id=1, source_target_pairs={{0,4},{1,5},{4,8},{5,9},{8,12},{9,13},{12,14},{13,15},{14,10},{15,... | collective-permute-start | bytes 663560 | tf_op jit(solution)/shard_map/ppermute | solution.py:78
  77.9 12.0 %collective-permute-start.39 = (bf16[432,256]{1,0:T(8,128)(2,1)S(1)}, bf16[432,256]{1,0:T(8,128)(2,1)S(1)}, u32[]{:S(2)}, u32[]{:S(2)}) collective-permute-start(bf16[432,256]{1,0:T(8,128)(2,1)S(1)} %get-tuple-element.63), channel_id=1, source_target_pairs={{0,2},{1,3},{4,0},{5,1},{8,4},{9,5},{12,8},{13,9},{14,12},{15,13},... | collective-permute-start | bytes 663560 | tf_op jit(solution)/shard_map/ppermute | solution.py:78
  95.4 7.3 %collective-permute-start.36 = (bf16[592,256]{1,0:T(8,128)(2,1)S(1)}, bf16[592,256]{1,0:T(8,128)(2,1)S(1)}, u32[]{:S(2)}, u32[]{:S(2)}) collective-permute-start(bf16[592,256]{1,0:T(8,128)(2,1)S(1)} %collective-permute-done.26), channel_id=1, source_target_pairs={{0,1},{1,0},{2,3},{3,2},{4,5},{5,4},{6,7},{7,6},{8,9},{9,8},{10,11... | collective-permute-start | bytes 909320 | tf_op jit(solution)/shard_map/ppermute | solution.py:82
  95.4 7.2 %collective-permute-start.32 = (bf16[592,256]{1,0:T(8,128)(2,1)S(1)}, bf16[592,256]{1,0:T(8,128)(2,1)S(1)}, u32[]{:S(2)}, u32[]{:S(2)}) collective-permute-start(bf16[592,256]{1,0:T(8,128)(2,1)S(1)} %collective-permute-done.25), channel_id=1, source_target_pairs={{0,1},{1,0},{2,3},{3,2},{4,5},{5,4},{6,7},{7,6},{8,9},{9,8},{10,11... | collective-permute-start | bytes 909320 | tf_op jit(solution)/shard_map/ppermute | solution.py:82
  100.6 15.2 %collective-permute-start.40 = (bf16[432,256]{1,0:T(8,128)(2,1)S(1)}, bf16[432,256]{1,0:T(8,128)(2,1)S(1)}, u32[]{:S(2)}, u32[]{:S(2)}) collective-permute-start(bf16[432,256]{1,0:T(8,128)(2,1)S(1)} %get-tuple-element.64), channel_id=1, source_target_pairs={{0,2},{1,3},{4,0},{5,1},{8,4},{9,5},{12,8},{13,9},{14,12},{15,13},... | collective-permute-start | bytes 663560 | tf_op jit(solution)/shard_map/ppermute | solution.py:78
  100.9 14.8 %collective-permute-start.37 = (bf16[432,256]{1,0:T(8,128)(2,1)S(1)}, bf16[432,256]{1,0:T(8,128)(2,1)S(1)}, u32[]{:S(2)}, u32[]{:S(2)}) collective-permute-start(bf16[432,256]{1,0:T(8,128)(2,1)S(1)} %fusion.5), channel_id=1, source_target_pairs={{0,4},{1,5},{4,8},{5,9},{8,12},{9,13},{12,14},{13,15},{14,10},{15,... | collective-permute-start | bytes 663560 | tf_op jit(solution)/shard_map/ppermute | solution.py:78
  (28 other events, 250.3 us)

commit v20 on v19

--- a/solution.py
+++ b/solution.py
@@ -23,7 +23,7 @@
 
 
 HB = 24
-VMEM_LIMIT = 40 * 1024 * 1024
+VMEM_LIMIT = 52 * 1024 * 1024
 DIRECTIONS = [
     (i, j, l)
     for i in (-1, 0, 1)

time: 117 us -> 110 us (0.940); the launches traced: 117 us -> 108 us
  Pallas kernels: 40.6 us -> 31.6 us
  waiting for transfers between devices: 37.1 us -> 35.8 us
  starting transfers between devices: 30.2 us -> 31.5 us
    pallas_call x1, Pallas kernels: 19.5 us -> 11.9 us  [local(): call(functools.partial(weight_grad_body, slots, factor, peers, count), (s...]
    ppermute x21, waiting for transfers between devices: 37 us -> 35.7 us  [ring_step(): return lax.ppermute(x, 'morton', pairs)]
    ppermute x21, starting transfers between devices: 26.4 us -> 27.7 us  [ring_step(): return lax.ppermute(x, 'morton', pairs)]
    unnamed x22 -> x66, local copies, waits for them, and re-layouts: 5.76 us -> 4.87 us
  transfers between devices with their start and end apart: 41 -> 41, of which waited for: 10 -> 10; matrix products, arithmetic and copies ran while one was open for 1% -> 2% of each run, Pallas kernels for 34% -> 28%
where the time goes in v20:
time: 110 us; the launch traced here: 108 us
  waiting for transfers between devices  35.8 us (33%)
  Pallas kernels  31.6 us (29%)
  starting transfers between devices  31.5 us (29%)
  local copies, waits for them, and re-layouts  5.56 us (5%)
  other arithmetic  2.58 us (2%)
    ppermute x21, waiting for transfers between devices, ring_step(): return lax.ppermute(x, 'morton', pairs)  35.7 us
    ppermute x21, starting transfers between devices, ring_step(): return lax.ppermute(x, 'morton', pairs)  27.7 us
    pallas_call x1, Pallas kernels, local(): call(functools.partial(weight_grad_body, slots, factor, peers, count), (s...  11.9 us
    pallas_call x1, Pallas kernels, local(): call(functools.partial(input_grad_body, slots, peers, count), sds((per_de...  11.9 us
    pallas_call x1, Pallas kernels, local(): call(mix_body, sds((per_device, channels), BF16), [HBM, HBM, VMEM], [pltp...  6.65 us
    unnamed x66, local copies, waits for them, and re-layouts  4.87 us
    ppermute x20, starting transfers between devices, swap_cores(): return lax.ppermute(x, 'morton', [(m, m ^ 1) for m in range(peers)])  3.82 us
  transfers between devices with their start and end apart: 41, of which 10 were waited for; matrix products, arithmetic and copies ran while one was open for 2% of the time, Pallas kernels for 28%

profile of v20, /device:TPU:0, one launch (start us, length us, event | category | flops | bytes accessed | tf_op | source)
XLA Modules:
  0.0 108.1 jit_solution(10867514631052052348)
XLA Ops:
  3.7 1.1 %norm.1 = (bf16[1024,256]{1,0:T(8,128)(2,1)S(1)}, bf16[608,256]{1,0:T(8,128)(2,1)S(1)}) custom-call(s32[2,26]{1,0:T(2,128)S(1)} %copy-done.3, s32[1,64]{1,0:T(1,128)S(1)} %copy-done.7, bf16[1024,256]{1,0:T(8,128)(2,1)S(1)} %copy-done, f32[1,256]{1,0:T(1,128)S(1)} %bitcast.75), custom_call_target="tpu_custom_call" | custom-call | flops 2000000000 | tf_op jit(solution)/shard_map/norm/pallas_call | solution.py:634
  4.9 3.1 %collective-permute-start.1 = (bf16[608,256]{1,0:T(8,128)(2,1)S(1)}, bf16[608,256]{1,0:T(8,128)(2,1)S(1)}, u32[]{:S(2)}, u32[]{:S(2)}) collective-permute-start(bf16[608,256]{1,0:T(8,128)(2,1)S(1)} %get-tuple-element.35), channel_id=1, source_target_pairs={{0,4},{1,3},{4,8},{5,1},{8,12},{9,5},{12,14},{13,9},{14,10},{15,13... | collective-permute-start | bytes 933896 | tf_op jit(solution)/shard_map/ppermute | solution.py:78
  8.7 6.0 %collective-permute-done.1 = bf16[608,256]{1,0:T(8,128)(2,1)S(1)} collective-permute-done((bf16[608,256]{1,0:T(8,128)(2,1)S(1)}, bf16[608,256]{1,0:T(8,128)(2,1)S(1)}, u32[]{:S(2)}, u32[]{:S(2)}) %collective-permute-start.1) | collective-permute-done | bytes 311328 | tf_op jit(solution)/shard_map/ppermute | solution.py:78
  14.7 2.5 %collective-permute-start.2 = (bf16[608,256]{1,0:T(8,128)(2,1)S(1)}, bf16[608,256]{1,0:T(8,128)(2,1)S(1)}, u32[]{:S(2)}, u32[]{:S(2)}) collective-permute-start(bf16[608,256]{1,0:T(8,128)(2,1)S(1)} %collective-permute-done.1), channel_id=1, source_target_pairs={{0,4},{1,3},{4,8},{5,1},{8,12},{9,5},{12,14},{13,9},{14,10},{15,13... | collective-permute-start | bytes 933896 | tf_op jit(solution)/shard_map/ppermute | solution.py:78
  17.9 1.6 %collective-permute-start.6 = (bf16[608,256]{1,0:T(8,128)(2,1)S(1)}, bf16[608,256]{1,0:T(8,128)(2,1)S(1)}, u32[]{:S(2)}, u32[]{:S(2)}) collective-permute-start(bf16[608,256]{1,0:T(8,128)(2,1)S(1)} %collective-permute-done.5), channel_id=1, source_target_pairs={{0,4},{1,3},{4,8},{5,1},{8,12},{9,5},{12,14},{13,9},{14,10},{15,13... | collective-permute-start | bytes 933896 | tf_op jit(solution)/shard_map/ppermute | solution.py:78
  19.5 3.5 %collective-permute-done.2 = bf16[608,256]{1,0:T(8,128)(2,1)S(1)} collective-permute-done((bf16[608,256]{1,0:T(8,128)(2,1)S(1)}, bf16[608,256]{1,0:T(8,128)(2,1)S(1)}, u32[]{:S(2)}, u32[]{:S(2)}) %collective-permute-start.2) | collective-permute-done | bytes 311328 | tf_op jit(solution)/shard_map/ppermute | solution.py:78
  24.6 1.7 %collective-permute-done.6 = bf16[608,256]{1,0:T(8,128)(2,1)S(1)} collective-permute-done((bf16[608,256]{1,0:T(8,128)(2,1)S(1)}, bf16[608,256]{1,0:T(8,128)(2,1)S(1)}, u32[]{:S(2)}, u32[]{:S(2)}) %collective-permute-start.6) | collective-permute-done | bytes 311328 | tf_op jit(solution)/shard_map/ppermute | solution.py:78
  27.4 2.5 %collective-permute-done.3 = bf16[608,256]{1,0:T(8,128)(2,1)S(1)} collective-permute-done((bf16[608,256]{1,0:T(8,128)(2,1)S(1)}, bf16[608,256]{1,0:T(8,128)(2,1)S(1)}, u32[]{:S(2)}, u32[]{:S(2)}) %collective-permute-start.3) | collective-permute-done | bytes 311328 | tf_op jit(solution)/shard_map/ppermute | solution.py:78
  31.6 1.6 %collective-permute-done.7 = bf16[608,256]{1,0:T(8,128)(2,1)S(1)} collective-permute-done((bf16[608,256]{1,0:T(8,128)(2,1)S(1)}, bf16[608,256]{1,0:T(8,128)(2,1)S(1)}, u32[]{:S(2)}, u32[]{:S(2)}) %collective-permute-start.7) | collective-permute-done | bytes 311328 | tf_op jit(solution)/shard_map/ppermute | solution.py:78
  33.2 3.6 %collective-permute-done.4 = bf16[608,256]{1,0:T(8,128)(2,1)S(1)} collective-permute-done((bf16[608,256]{1,0:T(8,128)(2,1)S(1)}, bf16[608,256]{1,0:T(8,128)(2,1)S(1)}, u32[]{:S(2)}, u32[]{:S(2)}) %collective-permute-start.4) | collective-permute-done | bytes 311328 | tf_op jit(solution)/shard_map/ppermute | solution.py:78
  36.8 1.1 %collective-permute-start.15 = (bf16[592,256]{1,0:T(8,128)(2,1)S(1)}, bf16[592,256]{1,0:T(8,128)(2,1)S(1)}, u32[]{:S(2)}, u32[]{:S(2)}) collective-permute-start(bf16[592,256]{1,0:T(8,128)(2,1)S(1)} %extract.1), channel_id=1, source_target_pairs={{0,4},{1,3},{4,8},{5,1},{8,12},{9,5},{12,14},{13,9},{14,10},{15,13... | collective-permute-start | bytes 909320 | tf_op jit(solution)/shard_map/ppermute | solution.py:78
  37.9 2.3 %collective-permute-start.16 = (bf16[592,256]{1,0:T(8,128)(2,1)S(1)}, bf16[592,256]{1,0:T(8,128)(2,1)S(1)}, u32[]{:S(2)}, u32[]{:S(2)}) collective-permute-start(bf16[592,256]{1,0:T(8,128)(2,1)S(1)} %extract.1), channel_id=1, source_target_pairs={{1,4},{0,3},{5,8},{4,1},{9,12},{8,5},{13,14},{12,9},{15,10},{14,13... | collective-permute-start | bytes 909320 | tf_op jit(solution)/shard_map/ppermute | solution.py:78
  41.2 11.9 %weight_grad.1 = (f32[8,432,256]{2,1,0:T(8,128)}, bf16[2,432,256]{2,1,0:T(8,128)(2,1)}, bf16[2,432,256]{2,1,0:T(8,128)(2,1)}, bf16[2,432,256]{2,1,0:T(8,128)(2,1...) custom-call(s32[2,26]{1,0:T(2,128)S(1)} %copy-done.4, ...), custom_call_target="tpu_custom_call" | custom-call | flops 8999999488 | tf_op jit(solution)/shard_map/weight_grad/pallas_call | solution.py:665
  54.3 2.3 %collective-permute-start.22 = (bf16[592,256]{1,0:T(8,128)(2,1)S(1)}, bf16[592,256]{1,0:T(8,128)(2,1)S(1)}, u32[]{:S(2)}, u32[]{:S(2)}) collective-permute-start(bf16[592,256]{1,0:T(8,128)(2,1)S(1)} %collective-permute-done.15), channel_id=1, source_target_pairs={{0,4},{1,3},{4,8},{5,1},{8,12},{9,5},{12,14},{13,9},{14,10},{15,13... | collective-permute-start | bytes 909320 | tf_op jit(solution)/shard_map/ppermute | solution.py:78
  56.6 1.3 %fusion.7 = (bf16[432,256]{1,0:T(8,128)(2,1)S(1)}, bf16[432,256]{1,0:T(8,128)(2,1)S(1)}) fusion(f32[8,432,256]{2,1,0:T(8,128)} %get-tuple-element.39, bf16[2,432,256]{2,1,0:T(8,128)(2,1)S(1)} %collective-permute-done.17), kind=kLoop, calls=%fused_computation.15 | loop fusion | flops 663552 | bytes 1769472 | tf_op jit(solution)/shard_map/convert_element_type | solution.py:138
  58.4 1.6 %collective-permute-start.38 = (bf16[432,256]{1,0:T(8,128)(2,1)S(1)}, bf16[432,256]{1,0:T(8,128)(2,1)S(1)}, u32[]{:S(2)}, u32[]{:S(2)}) collective-permute-start(bf16[432,256]{1,0:T(8,128)(2,1)S(1)} %get-tuple-element.69), channel_id=1, source_target_pairs={{0,2},{1,3},{4,0},{5,1},{8,4},{9,5},{12,8},{13,9},{14,12},{15,13},... | collective-permute-start | bytes 663560 | tf_op jit(solution)/shard_map/ppermute | solution.py:78
  60.0 6.7 %mix.1 = bf16[1024,256]{1,0:T(8,128)(2,1)} custom-call(bf16[20,64,2304]{2,1,0:T(8,128)(2,1)} %get-tuple-element.44.cols_ref, bf16[6912,256]{1,0:T(8,128)(2,1)} %refs_6_.1, bf16[1024,256]{1,0:T(8,128)(2,1)S(1)} %copy-done.1), custom_call_target="tpu_custom_call" | custom-call | flops 6000000000 | tf_op jit(solution)/shard_map/mix/pallas_call | solution.py:706
  67.7 1.3 %collective-permute-start.25 = (bf16[592,256]{1,0:T(8,128)(2,1)S(1)}, bf16[592,256]{1,0:T(8,128)(2,1)S(1)}, u32[]{:S(2)}, u32[]{:S(2)}) collective-permute-start(bf16[592,256]{1,0:T(8,128)(2,1)S(1)} %collective-permute-done.22), channel_id=1, source_target_pairs={{0,4},{1,3},{4,8},{5,1},{8,12},{9,5},{12,14},{13,9},{14,10},{15,13... | collective-permute-start | bytes 909320 | tf_op jit(solution)/shard_map/ppermute | solution.py:78
  69.7 1.6 %collective-permute-start.39 = (bf16[432,256]{1,0:T(8,128)(2,1)S(1)}, bf16[432,256]{1,0:T(8,128)(2,1)S(1)}, u32[]{:S(2)}, u32[]{:S(2)}) collective-permute-start(bf16[432,256]{1,0:T(8,128)(2,1)S(1)} %get-tuple-element.63), channel_id=1, source_target_pairs={{0,2},{1,3},{4,0},{5,1},{8,4},{9,5},{12,8},{13,9},{14,12},{15,13},... | collective-permute-start | bytes 663560 | tf_op jit(solution)/shard_map/ppermute | solution.py:78
  71.3 8.0 %collective-permute-done.25 = bf16[592,256]{1,0:T(8,128)(2,1)S(1)} collective-permute-done((bf16[592,256]{1,0:T(8,128)(2,1)S(1)}, bf16[592,256]{1,0:T(8,128)(2,1)S(1)}, u32[]{:S(2)}, u32[]{:S(2)}) %collective-permute-start.25) | collective-permute-done | bytes 303136 | tf_op jit(solution)/shard_map/ppermute | solution.py:78
  82.3 3.8 %collective-permute-done.28 = bf16[592,256]{1,0:T(8,128)(2,1)S(1)} collective-permute-done((bf16[592,256]{1,0:T(8,128)(2,1)S(1)}, bf16[592,256]{1,0:T(8,128)(2,1)S(1)}, u32[]{:S(2)}, u32[]{:S(2)}) %collective-permute-start.28) | collective-permute-done | bytes 303136 | tf_op jit(solution)/shard_map/ppermute | solution.py:78
  88.0 4.2 %collective-permute-done.27 = bf16[432,256]{1,0:T(8,128)(2,1)S(1)} collective-permute-done((bf16[432,256]{1,0:T(8,128)(2,1)S(1)}, bf16[432,256]{1,0:T(8,128)(2,1)S(1)}, u32[]{:S(2)}, u32[]{:S(2)}) %collective-permute-start.27) | collective-permute-done | bytes 221216 | tf_op jit(solution)/shard_map/ppermute | solution.py:78
  92.9 1.4 %collective-permute-start.37 = (bf16[432,256]{1,0:T(8,128)(2,1)S(1)}, bf16[432,256]{1,0:T(8,128)(2,1)S(1)}, u32[]{:S(2)}, u32[]{:S(2)}) collective-permute-start(bf16[432,256]{1,0:T(8,128)(2,1)S(1)} %fusion.5), channel_id=1, source_target_pairs={{0,4},{1,5},{4,8},{5,9},{8,12},{9,13},{12,14},{13,15},{14,10},{15,... | collective-permute-start | bytes 663560 | tf_op jit(solution)/shard_map/ppermute | solution.py:78
  95.3 11.9 %input_grad.1 = bf16[1024,256]{1,0:T(8,128)(2,1)} custom-call(s32[16,256]{1,0:T(8,128)S(1)} %get-tuple-element.57.refs_0_, s32[1,64]{1,0:T(1,128)S(1)} %copy-done.8, s32[33]{0:T(128)S(1)} %dynamic-slice_bitcast_fusion.refs_1_.refs_2_, bf16[1024,256]{1,0:T(8,128)(2,1)} %refs_3_.3, bf16[1024,256]{1,0:T(8,128)(2,1)} %refs_4_.1, f32[1,256]{1,0:T(1,128)S(1)} %bitcast.76, ...), custom_call_target="tpu_custom_call" | custom-call | flops 12999999488 | tf_op jit(solution)/shard_map/input_grad/pallas_call | solution.py:724
  (135 shorter events, 20.6 us)
Async XLA Ops:
  4.9 9.8 %collective-permute-start.1 = (bf16[608,256]{1,0:T(8,128)(2,1)S(1)}, bf16[608,256]{1,0:T(8,128)(2,1)S(1)}, u32[]{:S(2)}, u32[]{:S(2)}) collective-permute-start(bf16[608,256]{1,0:T(8,128)(2,1)S(1)} %get-tuple-element.35), channel_id=1, source_target_pairs={{0,4},{1,3},{4,8},{5,1},{8,12},{9,5},{12,14},{13,9},{14,10},{15,13... | collective-permute-start | bytes 933896 | tf_op jit(solution)/shard_map/ppermute | solution.py:78
  7.9 9.9 %collective-permute-start.5 = (bf16[608,256]{1,0:T(8,128)(2,1)S(1)}, bf16[608,256]{1,0:T(8,128)(2,1)S(1)}, u32[]{:S(2)}, u32[]{:S(2)}) collective-permute-start(bf16[608,256]{1,0:T(8,128)(2,1)S(1)} %get-tuple-element.35), channel_id=1, source_target_pairs={{1,4},{0,3},{5,8},{4,1},{9,12},{8,5},{13,14},{12,9},{15,10},{14,13... | collective-permute-start | bytes 933896 | tf_op jit(solution)/shard_map/ppermute | solution.py:78
  14.7 8.3 %collective-permute-start.2 = (bf16[608,256]{1,0:T(8,128)(2,1)S(1)}, bf16[608,256]{1,0:T(8,128)(2,1)S(1)}, u32[]{:S(2)}, u32[]{:S(2)}) collective-permute-start(bf16[608,256]{1,0:T(8,128)(2,1)S(1)} %collective-permute-done.1), channel_id=1, source_target_pairs={{0,4},{1,3},{4,8},{5,1},{8,12},{9,5},{12,14},{13,9},{14,10},{15,13... | collective-permute-start | bytes 933896 | tf_op jit(solution)/shard_map/ppermute | solution.py:78
  17.9 8.5 %collective-permute-start.6 = (bf16[608,256]{1,0:T(8,128)(2,1)S(1)}, bf16[608,256]{1,0:T(8,128)(2,1)S(1)}, u32[]{:S(2)}, u32[]{:S(2)}) collective-permute-start(bf16[608,256]{1,0:T(8,128)(2,1)S(1)} %collective-permute-done.5), channel_id=1, source_target_pairs={{0,4},{1,3},{4,8},{5,1},{8,12},{9,5},{12,14},{13,9},{14,10},{15,13... | collective-permute-start | bytes 933896 | tf_op jit(solution)/shard_map/ppermute | solution.py:78
  24.1 6.9 %collective-permute-start = (bf16[608,256]{1,0:T(8,128)(2,1)S(1)}, bf16[608,256]{1,0:T(8,128)(2,1)S(1)}, u32[]{:S(2)}, u32[]{:S(2)}) collective-permute-start(bf16[608,256]{1,0:T(8,128)(2,1)S(1)} %get-tuple-element.35), channel_id=1, source_target_pairs={{0,1},{1,0},{2,3},{3,2},{4,5},{5,4},{6,7},{7,6},{8,9},{9,8},{10,11... | collective-permute-start | bytes 933896 | tf_op jit(solution)/shard_map/ppermute | solution.py:82
  24.1 6.9 %collective-permute-start.8 = (bf16[608,256]{1,0:T(8,128)(2,1)S(1)}, bf16[608,256]{1,0:T(8,128)(2,1)S(1)}, u32[]{:S(2)}, u32[]{:S(2)}) collective-permute-start(bf16[608,256]{1,0:T(8,128)(2,1)S(1)} %collective-permute-done.1), channel_id=1, source_target_pairs={{0,1},{1,0},{2,3},{3,2},{4,5},{5,4},{6,7},{7,6},{8,9},{9,8},{10,11... | collective-permute-start | bytes 933896 | tf_op jit(solution)/shard_map/ppermute | solution.py:82
  24.6 6.9 %collective-permute-start.12 = (bf16[608,256]{1,0:T(8,128)(2,1)S(1)}, bf16[608,256]{1,0:T(8,128)(2,1)S(1)}, u32[]{:S(2)}, u32[]{:S(2)}) collective-permute-start(bf16[608,256]{1,0:T(8,128)(2,1)S(1)} %collective-permute-done.5), channel_id=1, source_target_pairs={{0,1},{1,0},{2,3},{3,2},{4,5},{5,4},{6,7},{7,6},{8,9},{9,8},{10,11... | collective-permute-start | bytes 933896 | tf_op jit(solution)/shard_map/ppermute | solution.py:82
  31.0 6.9 %collective-permute-start.13 = (bf16[608,256]{1,0:T(8,128)(2,1)S(1)}, bf16[608,256]{1,0:T(8,128)(2,1)S(1)}, u32[]{:S(2)}, u32[]{:S(2)}) collective-permute-start(bf16[608,256]{1,0:T(8,128)(2,1)S(1)} %collective-permute-done.6), channel_id=1, source_target_pairs={{0,1},{1,0},{2,3},{3,2},{4,5},{5,4},{6,7},{7,6},{8,9},{9,8},{10,11... | collective-permute-start | bytes 933896 | tf_op jit(solution)/shard_map/ppermute | solution.py:82
  31.5 8.7 %collective-permute-start.10 = (bf16[608,256]{1,0:T(8,128)(2,1)S(1)}, bf16[608,256]{1,0:T(8,128)(2,1)S(1)}, u32[]{:S(2)}, u32[]{:S(2)}) collective-permute-start(bf16[608,256]{1,0:T(8,128)(2,1)S(1)} %collective-permute-done.3), channel_id=1, source_target_pairs={{0,1},{1,0},{2,3},{3,2},{4,5},{5,4},{6,7},{7,6},{8,9},{9,8},{10,11... | collective-permute-start | bytes 933896 | tf_op jit(solution)/shard_map/ppermute | solution.py:82
  33.2 7.0 %collective-permute-start.14 = (bf16[608,256]{1,0:T(8,128)(2,1)S(1)}, bf16[608,256]{1,0:T(8,128)(2,1)S(1)}, u32[]{:S(2)}, u32[]{:S(2)}) collective-permute-start(bf16[608,256]{1,0:T(8,128)(2,1)S(1)} %collective-permute-done.7), channel_id=1, source_target_pairs={{0,1},{1,0},{2,3},{3,2},{4,5},{5,4},{6,7},{7,6},{8,9},{9,8},{10,11... | collective-permute-start | bytes 933896 | tf_op jit(solution)/shard_map/ppermute | solution.py:82
  36.8 16.3 %collective-permute-start.15 = (bf16[592,256]{1,0:T(8,128)(2,1)S(1)}, bf16[592,256]{1,0:T(8,128)(2,1)S(1)}, u32[]{:S(2)}, u32[]{:S(2)}) collective-permute-start(bf16[592,256]{1,0:T(8,128)(2,1)S(1)} %extract.1), channel_id=1, source_target_pairs={{0,4},{1,3},{4,8},{5,1},{8,12},{9,5},{12,14},{13,9},{14,10},{15,13... | collective-permute-start | bytes 909320 | tf_op jit(solution)/shard_map/ppermute | solution.py:78
  37.9 15.2 %collective-permute-start.16 = (bf16[592,256]{1,0:T(8,128)(2,1)S(1)}, bf16[592,256]{1,0:T(8,128)(2,1)S(1)}, u32[]{:S(2)}, u32[]{:S(2)}) collective-permute-start(bf16[592,256]{1,0:T(8,128)(2,1)S(1)} %extract.1), channel_id=1, source_target_pairs={{1,4},{0,3},{5,8},{4,1},{9,12},{8,5},{13,14},{12,9},{15,10},{14,13... | collective-permute-start | bytes 909320 | tf_op jit(solution)/shard_map/ppermute | solution.py:78
  53.2 14.5 %collective-permute-start.20 = (bf16[2,432,256]{2,1,0:T(8,128)(2,1)}, bf16[2,432,256]{2,1,0:T(8,128)(2,1)S(1)}, u32[]{:S(2)}, u32[]{:S(2)}) collective-permute-start(bf16[2,432,256]{2,1,0:T(8,128)(2,1)} %get-tuple-element.51), channel_id=1, source_target_pairs={{0,1},{1,0},{2,3},{3,2},{4,5},{5,4},{6,7},{7,6},{8,9},{9,8},{10,11... | collective-permute-start | bytes 1327112 | tf_op jit(solution)/shard_map/ppermute | solution.py:82
  53.7 13.0 %collective-permute-start.23 = (bf16[592,256]{1,0:T(8,128)(2,1)S(1)}, bf16[592,256]{1,0:T(8,128)(2,1)S(1)}, u32[]{:S(2)}, u32[]{:S(2)}) collective-permute-start(bf16[592,256]{1,0:T(8,128)(2,1)S(1)} %collective-permute-done.16), channel_id=1, source_target_pairs={{0,4},{1,3},{4,8},{5,1},{8,12},{9,5},{12,14},{13,9},{14,10},{15,13... | collective-permute-start | bytes 909320 | tf_op jit(solution)/shard_map/ppermute | solution.py:78
  54.3 12.5 %collective-permute-start.22 = (bf16[592,256]{1,0:T(8,128)(2,1)S(1)}, bf16[592,256]{1,0:T(8,128)(2,1)S(1)}, u32[]{:S(2)}, u32[]{:S(2)}) collective-permute-start(bf16[592,256]{1,0:T(8,128)(2,1)S(1)} %collective-permute-done.15), channel_id=1, source_target_pairs={{0,4},{1,3},{4,8},{5,1},{8,12},{9,5},{12,14},{13,9},{14,10},{15,13... | collective-permute-start | bytes 909320 | tf_op jit(solution)/shard_map/ppermute | solution.py:78
  57.9 11.2 %collective-permute-start.21 = (bf16[432,256]{1,0:T(8,128)(2,1)S(1)}, bf16[432,256]{1,0:T(8,128)(2,1)S(1)}, u32[]{:S(2)}, u32[]{:S(2)}) collective-permute-start(bf16[432,256]{1,0:T(8,128)(2,1)S(1)} %get-tuple-element.70), channel_id=1, source_target_pairs={{0,4},{1,5},{4,8},{5,9},{8,12},{9,13},{12,14},{13,15},{14,10},{15,... | collective-permute-start | bytes 663560 | tf_op jit(solution)/shard_map/ppermute | solution.py:78
  58.4 10.7 %collective-permute-start.38 = (bf16[432,256]{1,0:T(8,128)(2,1)S(1)}, bf16[432,256]{1,0:T(8,128)(2,1)S(1)}, u32[]{:S(2)}, u32[]{:S(2)}) collective-permute-start(bf16[432,256]{1,0:T(8,128)(2,1)S(1)} %get-tuple-element.69), channel_id=1, source_target_pairs={{0,2},{1,3},{4,0},{5,1},{8,4},{9,5},{12,8},{13,9},{14,12},{15,13},... | collective-permute-start | bytes 663560 | tf_op jit(solution)/shard_map/ppermute | solution.py:78
  66.7 13.4 %collective-permute-start.19 = (bf16[2,432,256]{2,1,0:T(8,128)(2,1)S(1)}, bf16[2,432,256]{2,1,0:T(8,128)(2,1)S(1)}, u32[]{:S(2)}, u32[]{:S(2)}) collective-permute-start(bf16[2,432,256]{2,1,0:T(8,128)(2,1)S(1)} %copy-done.12), channel_id=1, source_target_pairs={{0,1},{1,0},{2,3},{3,2},{4,5},{5,4},{6,7},{7,6},{8,9},{9,8},{10,11... | collective-permute-start | bytes 1327112 | tf_op jit(solution)/shard_map/ppermute | solution.py:82
  66.8 13.4 %collective-permute-start.26 = (bf16[592,256]{1,0:T(8,128)(2,1)S(1)}, bf16[592,256]{1,0:T(8,128)(2,1)S(1)}, u32[]{:S(2)}, u32[]{:S(2)}) collective-permute-start(bf16[592,256]{1,0:T(8,128)(2,1)S(1)} %collective-permute-done.23), channel_id=1, source_target_pairs={{0,4},{1,3},{4,8},{5,1},{8,12},{9,5},{12,14},{13,9},{14,10},{15,13... | collective-permute-start | bytes 909320 | tf_op jit(solution)/shard_map/ppermute | solution.py:78
  67.7 11.6 %collective-permute-start.25 = (bf16[592,256]{1,0:T(8,128)(2,1)S(1)}, bf16[592,256]{1,0:T(8,128)(2,1)S(1)}, u32[]{:S(2)}, u32[]{:S(2)}) collective-permute-start(bf16[592,256]{1,0:T(8,128)(2,1)S(1)} %collective-permute-done.22), channel_id=1, source_target_pairs={{0,4},{1,3},{4,8},{5,1},{8,12},{9,5},{12,14},{13,9},{14,10},{15,13... | collective-permute-start | bytes 909320 | tf_op jit(solution)/shard_map/ppermute | solution.py:78
  69.2 12.4 %collective-permute-start.24 = (bf16[432,256]{1,0:T(8,128)(2,1)S(1)}, bf16[432,256]{1,0:T(8,128)(2,1)S(1)}, u32[]{:S(2)}, u32[]{:S(2)}) collective-permute-start(bf16[432,256]{1,0:T(8,128)(2,1)S(1)} %get-tuple-element.54), channel_id=1, source_target_pairs={{0,4},{1,5},{4,8},{5,9},{8,12},{9,13},{12,14},{13,15},{14,10},{15,... | collective-permute-start | bytes 663560 | tf_op jit(solution)/shard_map/ppermute | solution.py:78
  69.7 11.9 %collective-permute-start.39 = (bf16[432,256]{1,0:T(8,128)(2,1)S(1)}, bf16[432,256]{1,0:T(8,128)(2,1)S(1)}, u32[]{:S(2)}, u32[]{:S(2)}) collective-permute-start(bf16[432,256]{1,0:T(8,128)(2,1)S(1)} %get-tuple-element.63), channel_id=1, source_target_pairs={{0,2},{1,3},{4,0},{5,1},{8,4},{9,5},{12,8},{13,9},{14,12},{15,13},... | collective-permute-start | bytes 663560 | tf_op jit(solution)/shard_map/ppermute | solution.py:78
  92.2 14.9 %collective-permute-start.40 = (bf16[432,256]{1,0:T(8,128)(2,1)S(1)}, bf16[432,256]{1,0:T(8,128)(2,1)S(1)}, u32[]{:S(2)}, u32[]{:S(2)}) collective-permute-start(bf16[432,256]{1,0:T(8,128)(2,1)S(1)} %get-tuple-element.64), channel_id=1, source_target_pairs={{0,2},{1,3},{4,0},{5,1},{8,4},{9,5},{12,8},{13,9},{14,12},{15,13},... | collective-permute-start | bytes 663560 | tf_op jit(solution)/shard_map/ppermute | solution.py:78
  92.9 14.3 %collective-permute-start.37 = (bf16[432,256]{1,0:T(8,128)(2,1)S(1)}, bf16[432,256]{1,0:T(8,128)(2,1)S(1)}, u32[]{:S(2)}, u32[]{:S(2)}) collective-permute-start(bf16[432,256]{1,0:T(8,128)(2,1)S(1)} %fusion.5), channel_id=1, source_target_pairs={{0,4},{1,5},{4,8},{5,9},{8,12},{9,13},{12,14},{13,15},{14,10},{15,... | collective-permute-start | bytes 663560 | tf_op jit(solution)/shard_map/ppermute | solution.py:78
  (50 other events, 425.0 us)
